TPU v7x, 32 devices: a whole 2x2x4 slice. The times are simulated.
32 devices in a mesh: groups: 2 (over y), mem: 4 (over x, core), heads: 4 (over z).
Axes of the slice: x: 2, y: 2, z: 4, core: 2. Of those that a mesh axis runs over, the one named last changes fastest.
Arguments:
- hidden: bfloat16 [32, 8192], P(('groups', 'heads')), parts along dimension 0, may hold values from -6 to 6
- norm_gain: bfloat16 [8192], P('mem'), may hold values from 0.5 to 1.5
- q_weight: bfloat16 [8192, 8192], P('mem', 'heads'), may hold values from -0.0625 to 0.0625
- k_weight: bfloat16 [8192, 1024], P('mem', 'heads'), may hold values from -1 to 1, as said below
- v_weight: bfloat16 [8192, 1024], P('mem', 'heads'), may hold values from -1 to 1, as said below
- o_weight: bfloat16 [8192, 8192], P('heads', 'mem'), may hold values from -0.0625 to 0.0625
- k_cache: bfloat16 [384, 8, 128, 128], P(('groups', 'mem'), 'heads'), parts along dimension 0, may hold values from -40 to 40, as said below
- v_cache: bfloat16 [384, 8, 128, 128], P(('groups', 'mem'), 'heads'), parts along dimension 0, may hold values from -6 to 6, as said below
- page_table: int32 [16, 24], P('groups'), parts along dimension 0, may hold values from 0 to 191, as said below
- attend_list: int32 [16, 8], P('groups'), parts along dimension 0, may hold values from 0 to 23, as said below
- lengths: int32 [16], P('groups'), parts along dimension 0, may hold values from 1409 to 3072, as said below
Outputs:
- layer_out: bfloat16 [32, 8192], P(('groups', 'heads'), 'mem'), parts along dimension 0
There are 2 independent parts, one for each index of `groups`. A program takes and returns all parts, laid end to end along the dimension named above; an argument that names none is the same for every part. Nothing has to cross between parts.
Inputs may be any that keep to these rules, and one draw needn't show every extreme that they name: `page_table`: A permutation of the pool slots 0 to 191 laid out as 8 rows of 24. The blocks named by attend_list lie at most 32 in any one range of slots m * 48 to (m + 1) * 48 - 1, and exactly 32 in some such range. `attend_list`: each row names 8 distinct blocks, all below ceil(lengths[r] / 128), among them its last block ceil(lengths[r] / 128) - 1. `lengths`: some row holds 3072 steps. `k_cache`: each key-value head is stored 1 times, the copies equal. `v_cache`: each key-value head is stored 1 times, the copies equal. `k_weight`: the 1 column blocks of each key-value head are equal. `v_weight`: the 1 column blocks of each key-value head are equal.
All inputs are finite; a program needn't handle non-finite values.
Results may differ from a plain program's by a relative error of at most 0.007.
The roundings to bfloat16 on the way count: a program that leaves them out, or rounds other values in their place, can miss the bound.
Values may be sent and summed in bfloat16 or wider, within the bound.
No kernel may reach another device: no remote copies, remote signals or barrier semaphores. Data moves between devices by JAX's collectives and lax.ppermute only.
A program may use at most 64 MiB of HBM per device.

v0:
```python
import jax
import jax.numpy as jnp
from jax import lax
from jax.sharding import PartitionSpec as P

NEG_FILL = -1e30
EPSILON = 1e-05


def fold_owners(running, shard_piece):
    piece_peak, piece_total, piece_accum = shard_piece
    run_peak, run_total, run_accum = running
    joint_peak = jnp.maximum(run_peak, jnp.max(piece_peak, axis=0))
    piece_factor = jnp.exp(piece_peak - joint_peak[None])
    joint_total = jnp.sum(piece_total * piece_factor, axis=0)
    joint_accum = jnp.sum(piece_accum * piece_factor[..., None], axis=0)
    return (joint_peak, joint_total, joint_accum)


def shards(
    hidden,
    norm_gain,
    q_weight,
    k_weight,
    v_weight,
    o_weight,
    k_cache,
    v_cache,
    page_table,
    attend_list,
    lengths,
):
    highest = lax.Precision.HIGHEST
    mem_count = lax.axis_size("mem")
    mem_index = lax.axis_index("mem")
    feature_cols = norm_gain.shape[0]
    hidden_f = hidden.astype(jnp.float32)
    mean_sq = jnp.mean(hidden_f * hidden_f, axis=-1, keepdims=True)
    own_cols = lax.dynamic_slice_in_dim(hidden_f, mem_index * feature_cols, feature_cols, 1)
    normed = (own_cols * lax.rsqrt(mean_sq + EPSILON) * norm_gain.astype(jnp.float32)).astype(
        jnp.bfloat16
    )
    shard_piece = lax.all_gather(normed, "heads", axis=0, tiled=True)
    partial_value = jnp.concatenate(
        [
            jnp.dot(shard_piece, q_weight, preferred_element_type=jnp.float32),
            jnp.dot(shard_piece, k_weight, preferred_element_type=jnp.float32),
            jnp.dot(shard_piece, v_weight, preferred_element_type=jnp.float32),
        ],
        axis=1,
    )
    summed = lax.psum(partial_value, "mem")
    query_cols = q_weight.shape[1]
    value_cols = k_weight.shape[1]
    pool_blocks = k_cache.shape[0]
    local_kv = k_cache.shape[1]
    block_size = k_cache.shape[2]
    head_dim = k_cache.shape[3]
    row_count = lengths.shape[0]
    token_count = summed.shape[0]
    step_count = token_count // row_count
    local_heads = query_cols // head_dim
    per_kv = local_heads // local_kv
    query_count = step_count * per_kv
    scale_factor = head_dim ** (-0.5)
    queries = summed[:, :query_cols].astype(jnp.bfloat16)
    queries = queries.reshape(row_count, step_count, local_kv, per_kv, head_dim).transpose(
        0, 2, 1, 3, 4
    )
    queries = queries.reshape(row_count, local_kv, query_count, head_dim)
    new_keys = summed[:, query_cols : query_cols + value_cols].astype(jnp.bfloat16)
    new_keys = new_keys.reshape(row_count, step_count, local_kv, head_dim).transpose(0, 2, 1, 3)
    new_values = summed[:, query_cols + value_cols :].astype(jnp.bfloat16)
    new_values = new_values.reshape(row_count, step_count, local_kv, head_dim).transpose(0, 2, 1, 3)
    history = page_table.shape[1]
    pair_count = row_count * history
    block_ids = jnp.arange(history, dtype=jnp.int32)
    attended = jnp.any(attend_list[:, :, None] == block_ids[None, None, :], axis=1).reshape(
        pair_count
    )
    slot_global = mem_index * pool_blocks + jnp.arange(pool_blocks, dtype=jnp.int32)
    owner_hit = page_table.reshape(pair_count)[None, :] == slot_global[:, None]
    pair_of_slot = jnp.sum(
        jnp.where(owner_hit, jnp.arange(pair_count, dtype=jnp.int32)[None, :], 0), axis=1
    )
    slot_row = pair_of_slot // history
    slot_block = pair_of_slot % history
    slot_live = jnp.take(attended, pair_of_slot)
    capacity = 2 * row_count * attend_list.shape[1] // mem_count
    running_pos = jnp.cumsum(slot_live.astype(jnp.int32)) - 1
    picked = slot_live[None, :] & (
        running_pos[None, :] == jnp.arange(capacity, dtype=jnp.int32)[:, None]
    )
    chosen = jnp.sum(
        jnp.where(picked, jnp.arange(pool_blocks, dtype=jnp.int32)[None, :], 0), axis=1
    )
    block_keys = jnp.take(k_cache, chosen, axis=0)
    block_values = jnp.take(v_cache, chosen, axis=0)
    block_row = jnp.take(slot_row, chosen)
    block_index = jnp.take(slot_block, chosen)
    block_live = jnp.any(picked, axis=1)
    row_onehot = block_row[:, None] == jnp.arange(row_count, dtype=jnp.int32)[None, :]
    block_queries = jnp.take(queries, block_row, axis=0)
    scores = (
        jnp.einsum("cgqd,cgkd->cgqk", block_queries, block_keys, preferred_element_type=jnp.float32)
        * scale_factor
    )
    positions = block_index[:, None] * block_size + jnp.arange(block_size, dtype=jnp.int32)[None, :]
    valid = (block_live[:, None] & (positions < jnp.take(lengths, block_row)[:, None]))[
        :, None, None, :
    ]
    scores = jnp.where(valid, scores, NEG_FILL)
    block_peak = jnp.max(scores, axis=-1)
    row_peak = jnp.max(
        jnp.where(row_onehot[:, :, None, None], block_peak[:, None], NEG_FILL), axis=0
    )
    weights = jnp.where(
        valid, jnp.exp(scores - jnp.take(row_peak, block_row, axis=0)[..., None]), 0.0
    )
    weights_high = weights.astype(jnp.bfloat16)
    weights_low = (weights - weights_high.astype(jnp.float32)).astype(jnp.bfloat16)
    block_accum = jnp.einsum(
        "cgqk,cgkd->cgqd", weights_high, block_values, preferred_element_type=jnp.float32
    )
    block_accum = block_accum + jnp.einsum(
        "cgqk,cgkd->cgqd", weights_low, block_values, preferred_element_type=jnp.float32
    )
    onehot_f = row_onehot.astype(jnp.float32)
    row_sums = jnp.einsum("cr,cgq->rgq", onehot_f, jnp.sum(weights, axis=-1), precision=highest)
    row_accum = jnp.einsum("cr,cgqd->rgqd", onehot_f, block_accum, precision=highest)
    fresh_scores = (
        jnp.einsum("rgqd,rgtd->rgqt", queries, new_keys, preferred_element_type=jnp.float32)
        * scale_factor
    )
    causal = (
        jnp.arange(step_count, dtype=jnp.int32)[None, :]
        <= (jnp.arange(query_count, dtype=jnp.int32) // per_kv)[:, None]
    )
    fresh_scores = jnp.where(causal, fresh_scores, NEG_FILL)
    start_state = (
        jnp.full_like(row_peak, NEG_FILL),
        jnp.zeros_like(row_sums),
        jnp.zeros_like(row_accum),
    )
    cache_peak, cache_sum, cache_accum = fold_owners(
        start_state,
        (
            lax.all_gather(row_peak[None], "mem", axis=0, tiled=True),
            lax.all_gather(row_sums[None], "mem", axis=0, tiled=True),
            lax.all_gather(row_accum[None], "mem", axis=0, tiled=True),
        ),
    )
    final_peak = jnp.maximum(cache_peak, jnp.max(fresh_scores, axis=-1))
    carried = jnp.exp(cache_peak - final_peak)
    fresh_weights = jnp.where(causal, jnp.exp(fresh_scores - final_peak[..., None]), 0.0)
    final_sum = cache_sum * carried + jnp.sum(fresh_weights, axis=-1)
    final_accum = cache_accum * carried[..., None] + jnp.einsum(
        "rgqt,rgtd->rgqd", fresh_weights, new_values.astype(jnp.float32), precision=highest
    )
    attended_out = (final_accum / final_sum[..., None]).astype(jnp.bfloat16)
    attended_out = attended_out.reshape(
        row_count, local_kv, step_count, per_kv, head_dim
    ).transpose(0, 2, 1, 3, 4)
    attended_out = attended_out.reshape(token_count, query_cols)
    projected = lax.psum_scatter(
        jnp.dot(attended_out, o_weight, preferred_element_type=jnp.float32),
        "heads",
        scatter_dimension=0,
        tiled=True,
    )
    return projected.astype(jnp.bfloat16)


def solution(mesh):
    in_specs = (
        P(("groups", "heads"), None),
        P("mem"),
        P("mem", "heads"),
        P("mem", "heads"),
        P("mem", "heads"),
        P("heads", "mem"),
        P(("groups", "mem"), "heads", None, None),
        P(("groups", "mem"), "heads", None, None),
        P("groups", None),
        P("groups", None),
        P("groups"),
    )
    out_specs = P(("groups", "heads"), "mem")
    return jax.shard_map(shards, mesh=mesh, in_specs=in_specs, out_specs=out_specs, check_vma=False)
```

profile of v0, /device:TPU:0, one launch (start us, length us, event | category | flops | bytes accessed | tf_op | source)
XLA Modules:
  0.0 102.7 jit_solution(13370720556598059067)
XLA Ops:
  0.0 0.9 eq.60
  1.2 0.8 fusion.34
  2.0 0.8 gather_fusion
  3.3 0.7 gather_fusion.5
  4.0 0.7 gather_fusion.4
  4.7 0.7 gather_fusion.1
  6.0 14.9 %all-gather.3 = bf16[4,4,2048]{2,1,0:T(4,128)(2,1)S(1)} all-gather(bf16[1,4,2048]{2,1,0:T(4,128)(2,1)S(1)} %fusion.35), channel_id=1, replica_groups=mesh['groups'=2,'mem'=4,'heads'=4] {'heads'}, dimensions={0}, use_global_device_ids=true | all-gather | bytes 81920 | tf_op jit(solution)/shard_map/all_gather | solution.py:43
  20.9 4.7 %fusion.62 = f32[16,2048]{1,0:T(8,128)S(1)} fusion(bf16[16,2048]{1,0:T(8,128)(2,1)S(1)} %reshape.322, bf16[2048,2048]{1,0:T(8,128)(2,1)} %param.17), kind=kOutput, calls=%fused_computation.117 | convolution fusion | flops 134217728 | bytes 8585216 | tf_op jit(solution)/shard_map/dot_general | solution.py:46
  26.2 11.7 %all-reduce.3 = bf16[16,2560]{1,0:T(8,128)(2,1)S(1)} all-reduce(f32[16,2560]{1,0:T(8,128)S(1)} %pad_maximum_fusion), channel_id=1, replica_groups=mesh['groups'=2,'mem'=4,'heads'=4] {'mem'}, use_global_device_ids=true, to_apply=%region_6.8 | all-reduce | flops 40960 | bytes 245760 | tf_op jit(solution)/shard_map/psum | solution.py:52
  38.0 1.3 %gather_fusion.2 = bf16[32,2,16,128]{3,2,1,0:T(8,128)(2,1)} fusion(bf16[8,2,16,128]{3,2,1,0:T(8,128)(2,1)S(1)} %bitcast.67, s32[1024]{0:T(1024)S(1)} %pad_clamp_fusion), kind=kCustom, calls=%fused_computation.6 | custom fusion | bytes 524416 | tf_op jit(solution)/shard_map/jit(_take)/gather | solution.py:103
  39.3 2.2 %gather_fusion.6 = bf16[32,2,128,128]{3,2,1,0:T(8,128)(2,1)} fusion(bf16[48,2,128,128]{3,2,1,0:T(8,128)(2,1)S(1)} %copy-done, s32[1024]{0:T(1024)S(1)} %pad_clamp_fusion.1), kind=kCustom, calls=%fused_computation.1.clone | custom fusion | bytes 4194432 | tf_op jit(solution)/shard_map/jit(_take)/gather | solution.py:97
  41.4 3.8 %fusion.60 = (f32[32,2,16]{2,1,0:T(2,128)S(1)}, f32[32,2,16,128]{3,2,1,0:T(8,128)}) fusion(bf16[32,2,128,128]{3,2,1,0:T(8,128)(2,1)} %gather_fusion.6, pred[32]{0:T(512)(128)(4,1)S(1)} %get-tuple-element.12, bf16[32,2,16,128]{3,2,1,0:T(8,128)(2,1)} %gather_fusion.2, pred[32]{0:T(512)(128)(4,1)S(1)} %get-tuple-element.14, pred[32,128]{1,0:T(8,128)(4,1)S(1)} %fusion.38), kind=kOutput, calls=%fused_computation.115 | convolution fusion | flops 35126272 | bytes 2891840 | tf_op jit(solution)/shard_map/cgqd,cgkd->cgqk/dot_general | solution.py:105
  45.4 5.3 %all-gather.1 = f32[32,2,16]{2,1,0:T(2,128)S(1)} all-gather(f32[8,2,16]{2,1,0:T(2,128)S(1)} %select_reduce_fusion), channel_id=3, replica_groups=mesh['groups'=2,'mem'=4,'heads'=4] {'mem'}, dimensions={0}, use_global_device_ids=true | all-gather | bytes 5120 | tf_op jit(solution)/shard_map/all_gather | solution.py:148
  51.1 0.6 gather_fusion.3
  51.8 1.4 %fusion.18 = f32[32,2,16]{2,1,0:T(2,128)S(1)} fusion(f32[32,2,16,128]{3,2,1,0:T(8,128)} %get-tuple-element.24, f32[32,2,16]{2,1,0:T(2,128)S(1)} %broadcast_select_fusion.3, pred[32,128]{1,0:T(8,128)(4,1)S(1)} %fusion.38), kind=kLoop, calls=%fused_computation.29 | loop fusion | flops 392192 | bytes 536576 | tf_op jit(solution)/shard_map/reduce_sum | solution.py:129
  53.4 5.4 %all-gather.2 = f32[32,2,16]{2,0,1:T(8,128)S(1)} all-gather(f32[8,2,16]{2,0,1:T(8,128)S(1)} %fusion.31), channel_id=4, replica_groups=mesh['groups'=2,'mem'=4,'heads'=4] {'mem'}, dimensions={0}, use_global_device_ids=true | all-gather | bytes 5120 | tf_op jit(solution)/shard_map/all_gather | solution.py:149
  58.9 4.1 %gather_fusion.7 = bf16[32,2,128,128]{3,2,1,0:T(8,128)(2,1)} fusion(bf16[48,2,128,128]{3,2,1,0:T(8,128)(2,1)} %param.22, s32[1024]{0:T(1024)S(1)} %pad_clamp_fusion.1), kind=kCustom, calls=%fused_computation.3.clone | custom fusion | bytes 4194432 | tf_op jit(solution)/shard_map/jit(_take)/gather | solution.py:98
  63.0 2.6 %fusion.14 = f32[32,2,16,128]{3,2,1,0:T(8,128)S(1)} fusion(bf16[32,2,128,128]{3,2,1,0:T(8,128)(2,1)} %gather_fusion.7, pred[32]{0:T(512)(128)(4,1)S(1)} %get-tuple-element.12, f32[32,2,16,128]{3,2,1,0:T(8,128)} %get-tuple-element.24, f32[32,2,16]{2,1,0:T(2,128)S(1)} %broadcast_select_fusion.3, pred[32,128]{1,0:T(8,128)(4,1)S(1)} %fusion.38), kind=kOutput, calls=%fused_computation.22 | convolution fusion | flops 34996224 | bytes 3153952 | tf_op jit(solution)/shard_map/cgqk,cgkd->cgqd/dot_general | solution.py:122
  65.6 0.7 convolution_add_fusion
  66.3 0.6 fusion.16
  66.9 7.4 %all-gather = f32[32,2,16,128]{3,0,2,1:T(8,128)S(1)} all-gather(f32[8,2,16,128]{3,0,2,1:T(8,128)S(1)} %fusion.16), channel_id=2, replica_groups=mesh['groups'=2,'mem'=4,'heads'=4] {'mem'}, dimensions={0}, use_global_device_ids=true | all-gather | bytes 655360 | tf_op jit(solution)/shard_map/all_gather | solution.py:150
  75.0 4.6 %fusion.65 = f32[16,2048]{1,0:T(8,128)S(1)} fusion(bf16[16,2048]{1,0:T(8,128)(2,1)S(1)} %reshape.246, bf16[2048,2048]{1,0:T(8,128)(2,1)} %param.20), kind=kOutput, calls=%fused_computation.120 | convolution fusion | flops 134217728 | bytes 8585216 | tf_op jit(solution)/shard_map/dot_general | solution.py:166
  79.6 21.3 %all-reduce.4 = bf16[16,2048]{1,0:T(8,128)(2,1)S(1)} all-reduce(f32[16,2048]{1,0:T(8,128)S(1)} %fusion.65), channel_id=5, replica_groups=mesh['groups'=2,'mem'=4,'heads'=4] {'heads'}, use_global_device_ids=true, to_apply=%region_15.18.clone | all-reduce | flops 32768 | bytes 196608
  102.1 0.6 dynamic-slice_convert_fusion
  (73 shorter events, 3.9 us)
Async XLA Ops:
  0.0 39.3 %copy-start = (bf16[48,2,128,128]{3,2,1,0:T(8,128)(2,1)S(1)}, bf16[48,2,128,128]{3,2,1,0:T(8,128)(2,1)}, u32[]{:S(2)}) copy-start(bf16[48,2,128,128]{3,2,1,0:T(8,128)(2,1)} %param.21) | copy-start | bytes 9437188
  0.0 4.7 %copy-start.1 = (s32[8]{0:T(128)S(1)}, s32[8]{0:T(128)}, u32[]{:S(2)}) copy-start(s32[8]{0:T(128)} %param.25) | copy-start | bytes 100
  0.0 5.6 %copy-start.6 = (bf16[4,8192]{1,0:T(4,128)(2,1)S(1)}, bf16[4,8192]{1,0:T(4,128)(2,1)}, u32[]{:S(2)}) copy-start(bf16[4,8192]{1,0:T(4,128)(2,1)} %param.15) | copy-start | bytes 196612
  0.0 5.7 %copy-start.7 = (bf16[2048]{0:T(1024)(128)(2,1)S(1)}, bf16[2048]{0:T(1024)(128)(2,1)}, u32[]{:S(2)}) copy-start(bf16[2048]{0:T(1024)(128)(2,1)} %param.16) | copy-start | bytes 12292
  20.9 4.7 %copy-start.3 = (bf16[2048,256]{1,0:T(8,128)(2,1)S(1)}, bf16[2048,256]{1,0:T(8,128)(2,1)}, u32[]{:S(2)}) copy-start(bf16[2048,256]{1,0:T(8,128)(2,1)} %param.18) | copy-start | bytes 3145732
  20.9 5.0 %copy-start.4 = (bf16[2048,256]{1,0:T(8,128)(2,1)S(1)}, bf16[2048,256]{1,0:T(8,128)(2,1)}, u32[]{:S(2)}) copy-start(bf16[2048,256]{1,0:T(8,128)(2,1)} %param.19) | copy-start | bytes 3145732
  63.0 2.6 %copy-start.2 = (bf16[32,2,128,128]{3,2,1,0:T(8,128)(2,1)S(1)}, bf16[32,2,128,128]{3,2,1,0:T(8,128)(2,1)}, u32[]{:S(2)}) copy-start(bf16[32,2,128,128]{3,2,1,0:T(8,128)(2,1)} %gather_fusion.7) | copy-start | bytes 6291460
  63.0 2.6 %copy-start.5 = (f32[32,2,16,128]{3,2,1,0:T(8,128)S(1)}, f32[32,2,16,128]{3,2,1,0:T(8,128)}, u32[]{:S(2)}) copy-start(f32[32,2,16,128]{3,2,1,0:T(8,128)} %get-tuple-element.24) | copy-start | bytes 1572868
  75.0 25.9 %copy-start.8 = (u32[32]{0:T(128)S(1)}, u32[32]{0:T(128)}, u32[]{:S(2)}) copy-start(u32[32]{0:T(128)} %constant.151) | copy-start | bytes 388
where the time goes:
time: 103 us
  blocking collectives  66.1 us (64%)
  matrix products  18.2 us (18%)
  local copies, waits for them, and re-layouts  13.6 us (13%)
  other arithmetic  3.86 us (4%)
    unnamed x1, blocking collectives  21.3 us
    all_gather x1, blocking collectives, shards(): shard_piece = lax.all_gather(normed, 'heads', axis=0, tiled=True)  14.9 us
    psum x1, blocking collectives, shards(): summed = lax.psum(partial_value, 'mem')  11.7 us
    all_gather x1, blocking collectives, shards(): lax.all_gather(row_accum[None], 'mem', axis=0, tiled=True)  7.41 us
    all_gather x1, blocking collectives, shards(): lax.all_gather(row_sums[None], 'mem', axis=0, tiled=True)  5.41 us
    all_gather x1, blocking collectives, shards(): lax.all_gather(row_peak[None], 'mem', axis=0, tiled=True)  5.32 us
    dot_general x1, matrix products, shards(): jnp.dot(shard_piece, q_weight, preferred_element_type=jnp.float32)  4.72 us
    dot_general x1, matrix products, shards(): jnp.dot(attended_out, o_weight, preferred_element_type=jnp.float32)  4.58 us

commit v1 on v0

v1 whole, which is shorter than its diff:
```python
import functools

import jax
import jax.numpy as jnp
from jax import lax
from jax.experimental import pallas as pl
from jax.experimental.pallas import tpu as pltpu
from jax.sharding import PartitionSpec as P

NEG_FILL = -1e30
EPSILON = 1e-05
LANES = 128
MIB = 1 << 20
IN_VMEM = pl.BlockSpec(memory_space=pltpu.VMEM)
IN_SMEM = pl.BlockSpec(memory_space=pltpu.SMEM)


def swap(array, axis, distance):
    count = lax.axis_size(axis)
    return lax.ppermute(array, axis, [(i, i ^ distance) for i in range(count)])


def kernel_call(body, name, outs, ins, vmem_mib, flops, scratch=()):
    return pl.pallas_call(
        body,
        out_shape=outs,
        in_specs=ins,
        out_specs=jax.tree.map(lambda _: IN_VMEM, outs),
        scratch_shapes=list(scratch),
        name=name,
        compiler_params=pltpu.CompilerParams(vmem_limit_bytes=vmem_mib * MIB),
        cost_estimate=pl.CostEstimate(flops=int(flops), bytes_accessed=MIB, transcendentals=0),
    )


def norm_body(hidden_ref, gain_ref, out_ref):
    cols = gain_ref.shape[1]
    start = pl.multiple_of(lax.axis_index("mem") * cols, cols)
    hidden = hidden_ref[...].astype(jnp.float32)
    mean_sq = jnp.mean(hidden * hidden, axis=-1, keepdims=True)
    own = hidden_ref[:, pl.ds(start, cols)].astype(jnp.float32)
    normed = own * lax.rsqrt(mean_sq + EPSILON) * gain_ref[...].astype(jnp.float32)
    out_ref[...] = normed.astype(jnp.bfloat16)


def project_body(parts, tile, *refs):
    chunks, (q_ref, k_ref, v_ref, out_ref) = refs[:parts], refs[parts:]
    rows = jnp.concatenate([c[...].astype(jnp.float32) for c in chunks], axis=0)
    rows = rows.astype(jnp.bfloat16)
    at = 0
    for weight in (q_ref, k_ref, v_ref):
        width = min(tile, weight.shape[1])
        for col in range(0, weight.shape[1], width):
            out_ref[:, at : at + width] = jnp.dot(
                rows, weight[:, col : col + width], preferred_element_type=jnp.float32
            )
            at += width


def output_body(tile, rows_ref, weight_ref, *out_refs):
    rows = rows_ref[...]
    chunk = out_refs[0].shape[0]
    for col in range(0, weight_ref.shape[1], tile):
        product = jnp.dot(
            rows, weight_ref[:, col : col + tile], preferred_element_type=jnp.float32
        )
        for i, out_ref in enumerate(out_refs):
            out_ref[:, col : col + tile] = product[i * chunk : (i + 1) * chunk]


def split_dot(weights, values):
    high = weights.astype(jnp.bfloat16)
    low = (weights - high.astype(jnp.float32)).astype(jnp.bfloat16)
    both = jnp.dot(
        jnp.concatenate([high, low], axis=0), values, preferred_element_type=jnp.float32
    )
    return both[: weights.shape[0]] + both[weights.shape[0] :]


def group_lanes(query_count):
    lane = lax.broadcasted_iota(jnp.int32, (query_count, LANES), 1)
    row = lax.broadcasted_iota(jnp.int32, (query_count, LANES), 0)
    return lane - row


def pack_columns(columns, query_count):
    per_row = LANES // query_count
    offset = group_lanes(query_count)
    rows = []
    for first in range(0, len(columns), per_row):
        row = jnp.zeros((query_count, LANES), jnp.float32)
        for i, column in enumerate(columns[first : first + per_row]):
            row = jnp.where(offset == i * query_count, column, row)
        rows.append(jnp.sum(row, axis=0, keepdims=True))
    return rows


def unpack_column(row, place, query_count):
    spread = jnp.broadcast_to(row, (query_count, LANES))
    picked = jnp.where(group_lanes(query_count) == place * query_count, spread, 0.0)
    return jnp.sum(picked, axis=1, keepdims=True)


def attend_body(
    chunk,
    steps,
    scale,
    table_ref,
    list_ref,
    lengths_ref,
    query_ref,
    new_key_ref,
    new_value_ref,
    key_ref,
    value_ref,
    out_ref,
    slot_ref,
    row_ref,
    valid_ref,
    score_ref,
    peak_ref,
    total_ref,
    accum_ref,
):
    mem = lax.axis_index("mem")
    head_shard = lax.axis_index("heads")
    row_count, kv_heads, query_count, head_dim = query_ref.shape
    pool, block = key_ref.shape[0], key_ref.shape[2]
    selected = list_ref.shape[1]
    capacity = score_ref.shape[0]

    def place_of(row):
        first = row * steps
        return (lax.bitwise_xor(first // chunk, head_shard) * chunk + first % chunk) // steps

    def add_pair(row, i, count):
        index = list_ref[row, i]
        slot = table_ref[row, index] - mem * pool
        slot_ref[count] = slot
        row_ref[count] = place_of(row)
        valid_ref[count] = lengths_ref[row] - index * block
        return count + ((slot >= 0) & (slot < pool)).astype(jnp.int32)

    count = jnp.int32(0)
    for row in range(row_count):
        for i in range(selected):
            count = add_pair(row, i, count)

    def block_of(c):
        live = c < count
        slot = jnp.where(live, slot_ref[c], 0)
        row = jnp.where(live, row_ref[c], row_count)
        valid = jnp.where(live, valid_ref[c], 0)
        return slot, row, valid

    lane = lax.broadcasted_iota(jnp.int32, (query_count, LANES), 1)
    peak_ref[...] = jnp.full(peak_ref.shape, NEG_FILL, jnp.float32)
    total_ref[...] = jnp.zeros(total_ref.shape, jnp.float32)
    accum_ref[...] = jnp.zeros(accum_ref.shape, jnp.float32)
    contract_last = (((1,), (1,)), ((), ()))
    for c in range(capacity):
        slot, row, valid = block_of(c)
        read_row = jnp.minimum(row, row_count - 1)
        for g in range(kv_heads):
            score = lax.dot_general(
                query_ref[read_row, g],
                key_ref[slot, g],
                contract_last,
                preferred_element_type=jnp.float32,
            )
            score = jnp.where(lane < valid, score * scale, NEG_FILL)
            score_ref[c, g] = score
            peak_ref[row, g] = jnp.maximum(peak_ref[row, g], score)

    tokens = new_key_ref.shape[1]
    shape = (row_count * query_count, tokens)
    per_kv = query_count // steps
    query_row = lax.broadcasted_iota(jnp.int32, shape, 0)
    query_place = query_row // query_count * steps + query_row % query_count // per_kv
    key_place = lax.broadcasted_iota(jnp.int32, shape, 1)

    def token_of(place):
        return lax.bitwise_xor(place // chunk, head_shard) * chunk + place % chunk

    query_token, key_token = token_of(query_place), token_of(key_place)
    seen = (
        (query_token // steps == key_token // steps)
        & (key_token <= query_token)
        & (query_token // steps % lax.axis_size("mem") == mem)
    )
    peaks = [None] * (row_count * kv_heads)
    totals = [None] * (row_count * kv_heads)
    for g in range(kv_heads):
        score = lax.dot_general(
            query_ref[:, g].reshape(row_count * query_count, head_dim),
            new_key_ref[g],
            contract_last,
            preferred_element_type=jnp.float32,
        )
        score = jnp.where(seen, score * scale, NEG_FILL)
        old = jnp.max(
            peak_ref[:row_count, g].reshape(row_count * query_count, LANES), axis=1, keepdims=True
        )
        peak = jnp.maximum(old, jnp.max(score, axis=1, keepdims=True))
        weights = jnp.where(seen, jnp.exp(score - peak), 0.0)
        accum = split_dot(weights, new_value_ref[g]).reshape(row_count, query_count, head_dim)
        total = jnp.sum(weights, axis=1, keepdims=True)
        wide = jnp.broadcast_to(peak, (row_count * query_count, LANES))
        wide = wide.reshape(row_count, query_count, LANES)
        peak_ref[:row_count, g] = wide
        accum_ref[:row_count, g] = accum
        total = jnp.broadcast_to(total, (row_count * query_count, LANES))
        total = total.reshape(row_count, query_count, LANES)
        for row in range(row_count):
            peaks[row * kv_heads + g] = wide[row]
            totals[row * kv_heads + g] = total[row]

    for c in range(capacity):
        slot, row, valid = block_of(c)
        for g in range(kv_heads):
            weights = jnp.exp(score_ref[c, g] - peak_ref[row, g])
            weights = jnp.where(lane < valid, weights, 0.0)
            total_ref[row, g] += weights
            accum_ref[row, g] += split_dot(weights, value_ref[slot, g])

    for row in range(row_count):
        for g in range(kv_heads):
            group = row * kv_heads + g
            totals[group] = totals[group] + jnp.sum(total_ref[row, g], axis=1, keepdims=True)
    groups = row_count * kv_heads
    height = groups * query_count
    out_ref[:height] = accum_ref[:row_count].reshape(height, head_dim)
    packed = pack_columns(peaks, query_count) + pack_columns(totals, query_count)
    spare = out_ref.shape[0] - height - len(packed)
    packed.append(jnp.zeros((spare, LANES), jnp.float32))
    out_ref[height:] = jnp.concatenate(packed, axis=0)


def combine_body(query_count, last, own_ref, other_ref, out_ref):
    per_row = LANES // query_count
    height = own_ref.shape[0] - 8
    groups = height // query_count
    rows = -(-groups // per_row)
    own_peak, other_peak = own_ref[height : height + rows], other_ref[height : height + rows]
    peak = jnp.maximum(own_peak, other_peak)
    own_factor, other_factor = jnp.exp(own_peak - peak), jnp.exp(other_peak - peak)
    total = (
        own_ref[height + rows : height + 2 * rows] * own_factor
        + other_ref[height + rows : height + 2 * rows] * other_factor
    )
    if last:
        own_factor, other_factor = own_factor / total, other_factor / total
    else:
        spare = jnp.zeros((8 - 2 * rows, LANES), jnp.float32)
        out_ref[height:] = jnp.concatenate([peak, total, spare], axis=0)
    for group in range(groups):
        row, place = divmod(group, per_row)
        at = slice(group * query_count, (group + 1) * query_count)
        merged = own_ref[at] * unpack_column(
            own_factor[row : row + 1], place, query_count
        ) + other_ref[at] * unpack_column(other_factor[row : row + 1], place, query_count)
        out_ref[at] = merged.astype(out_ref.dtype)


def shards(
    hidden,
    norm_gain,
    q_weight,
    k_weight,
    v_weight,
    o_weight,
    k_cache,
    v_cache,
    page_table,
    attend_list,
    lengths,
):
    mem_count, head_count = lax.axis_size("mem"), lax.axis_size("heads")
    chunk = hidden.shape[0]
    feature_cols = norm_gain.shape[0]
    query_cols, value_cols = q_weight.shape[1], k_weight.shape[1]
    _, kv_heads, block, head_dim = k_cache.shape
    row_count, selected = attend_list.shape
    token_count = chunk * head_count
    steps = token_count // row_count
    per_kv = query_cols // head_dim // kv_heads
    query_count = steps * per_kv
    capacity = 2 * row_count * selected // mem_count
    f32, bf16 = jnp.float32, jnp.bfloat16

    normed = kernel_call(
        norm_body,
        "norm",
        jax.ShapeDtypeStruct((chunk, feature_cols), bf16),
        [IN_VMEM] * 2,
        2,
        1e10,
    )(hidden, norm_gain.reshape(1, feature_cols))
    pieces = [normed] + [swap(normed, "heads", d) for d in range(1, head_count)]

    width = query_cols + 2 * value_cols
    summed = kernel_call(
        functools.partial(project_body, head_count, 512),
        "project",
        jax.ShapeDtypeStruct((token_count, width), f32),
        [IN_VMEM] * (head_count + 3),
        8,
        2 * token_count * feature_cols * width,
    )(*pieces, q_weight, k_weight, v_weight)
    distance = 1
    while distance < mem_count:
        summed = summed + swap(summed, "mem", distance)
        distance *= 2

    queries = summed[:, :query_cols].astype(bf16)
    queries = queries.reshape(row_count, steps, kv_heads, per_kv, head_dim)
    queries = queries.transpose(0, 2, 1, 3, 4).reshape(row_count, kv_heads, query_count, head_dim)
    fresh = summed[:, query_cols:].astype(bf16).reshape(token_count, 2, kv_heads, head_dim)
    fresh = fresh.transpose(1, 2, 0, 3)

    height = row_count * kv_heads * query_count
    partial = kernel_call(
        functools.partial(attend_body, chunk, steps, head_dim ** (-0.5)),
        "attend",
        jax.ShapeDtypeStruct((height + 8, LANES), f32),
        [IN_SMEM] * 3 + [IN_VMEM] * 5,
        8,
        1e10,
        [pltpu.SMEM((capacity + 1,), jnp.int32)] * 3
        + [pltpu.VMEM((capacity, kv_heads, query_count, LANES), f32)]
        + [pltpu.VMEM((row_count + 1, kv_heads, query_count, LANES), f32)] * 3,
    )(page_table, attend_list, lengths, queries, fresh[0], fresh[1], k_cache, v_cache)

    distance = 1
    while distance < mem_count:
        last = 2 * distance == mem_count
        partial = kernel_call(
            functools.partial(combine_body, query_count, last),
            "combine",
            jax.ShapeDtypeStruct((height, LANES), bf16)
            if last
            else jax.ShapeDtypeStruct(partial.shape, f32),
            [IN_VMEM] * 2,
            4,
            1e7,
        )(partial, swap(partial, "mem", distance))
        distance *= 2

    attended = partial.reshape(row_count, kv_heads, steps, per_kv, head_dim)
    attended = attended.transpose(0, 2, 1, 3, 4).reshape(token_count, query_cols)
    projected = kernel_call(
        functools.partial(output_body, 512),
        "output",
        [jax.ShapeDtypeStruct((chunk, o_weight.shape[1]), f32)] * head_count,
        [IN_VMEM] * 2,
        8,
        2 * token_count * query_cols * o_weight.shape[1],
    )(attended, o_weight)
    total = projected[0]
    for d in range(1, head_count):
        total = total + swap(projected[d], "heads", d)
    return total.astype(bf16)


def solution(mesh):
    in_specs = (
        P(("groups", "heads"), None),
        P("mem"),
        P("mem", "heads"),
        P("mem", "heads"),
        P("mem", "heads"),
        P("heads", "mem"),
        P(("groups", "mem"), "heads", None, None),
        P(("groups", "mem"), "heads", None, None),
        P("groups", None),
        P("groups", None),
        P("groups"),
    )
    out_specs = P(("groups", "heads"), "mem")
    return jax.shard_map(shards, mesh=mesh, in_specs=in_specs, out_specs=out_specs, check_vma=False)
```

time: 103 us -> 46.8 us (0.45)
  blocking collectives: 66.1 us -> 0 us
  waiting for transfers between devices: 0 us -> 19 us
  matrix products: 18.2 us -> 0 us
  starting transfers between devices: 0 us -> 13.3 us
  local copies, waits for them, and re-layouts: 13.6 us -> 6.93 us
  Pallas kernels: 0 us -> 6.4 us
  other arithmetic: 3.86 us -> 0.67 us
    all_gather x4 -> x0, blocking collectives: 33.1 us -> none  [the longest x1 14.9 us: shards(): shard_piece = lax.all_gather(normed, 'heads', axis=0, tiled=True)]
    unnamed x1 -> x0, blocking collectives: 21.3 us -> none
    ppermute x0 -> x10, waiting for transfers between devices: none -> 19 us  [swap(): return lax.ppermute(array, axis, [(i, i ^ distance) for i in range(count)])]
    dot_general x11 -> x0, matrix products: 18.2 us -> none  [the longest x1 4.72 us: shards(): jnp.dot(shard_piece, q_weight, preferred_element_type=jnp.float32)]
    ppermute x0 -> x10, starting transfers between devices: none -> 13.3 us  [swap(): return lax.ppermute(array, axis, [(i, i ^ distance) for i in range(count)])]
    psum x1 -> x0, blocking collectives: 11.7 us -> none  [shards(): summed = lax.psum(partial_value, 'mem')]
    gather x8 -> x0, local copies, waits for them, and re-layouts: 11 us -> none  [the longest x1 4.06 us: shards(): block_values = jnp.take(v_cache, chosen, axis=0)]
    pallas_call x0 -> x6, Pallas kernels: none -> 6.4 us  [the longest x1 3.28 us: shards(): kernel_call(functools.partial(attend_body, chunk, steps, head_dim ** (-0....]
  transfers between devices with their start and end apart: 0 -> 10, of which waited for: 0 -> 8; matrix products, arithmetic and copies ran while one was open for 0% -> 0% of each run, Pallas kernels for 0% -> 0%
where the time goes in v1:
time: 46.8 us; the launch traced here: 46.6 us
  waiting for transfers between devices  19 us (41%)
  starting transfers between devices  13.3 us (28%)
  local copies, waits for them, and re-layouts  6.93 us (15%)
  Pallas kernels  6.4 us (14%)
  other arithmetic  0.67 us (1%)
    ppermute x10, waiting for transfers between devices, swap(): return lax.ppermute(array, axis, [(i, i ^ distance) for i in range(count)])  19 us
    ppermute x10, starting transfers between devices, swap(): return lax.ppermute(array, axis, [(i, i ^ distance) for i in range(count)])  13.3 us
    unnamed x22, local copies, waits for them, and re-layouts  6.15 us
    pallas_call x1, Pallas kernels, shards(): kernel_call(functools.partial(attend_body, chunk, steps, head_dim ** (-0....  3.28 us
    pallas_call x1, Pallas kernels, shards(): kernel_call(functools.partial(project_body, head_count, 512), 'project',...  1.46 us
    pallas_call x1, Pallas kernels, shards(): kernel_call(functools.partial(output_body, 512), 'output', [jax.ShapeDtyp...  1.19 us
  transfers between devices with their start and end apart: 10, of which 8 were waited for; matrix products, arithmetic and copies ran while one was open for 0% of the time, Pallas kernels for 0%

profile of v1, /device:TPU:0, one launch (start us, length us, event | category | flops | bytes accessed | tf_op | source)
XLA Modules:
  0.0 46.6 jit_solution(6576126398008363049)
XLA Ops:
  0.0 0.7 %reshape.18.gain_ref = bf16[1,2048]{1,0:T(2,128)(2,1)S(1)} reshape(bf16[2048]{0:T(1024)(128)(2,1)} %param.12) | data formatting | bytes 8192 | tf_op jit(solution)/shard_map/reshape | solution.py:298
  0.7 0.8 %copy-done.6 = bf16[4,8192]{1,0:T(4,128)(2,1)S(1)} copy-done((bf16[4,8192]{1,0:T(4,128)(2,1)S(1)}, bf16[4,8192]{1,0:T(4,128)(2,1)}, u32[]{:S(2)}) %copy-start.6) | copy-done | bytes 65560
  1.5 0.2 norm.1.refs_0_
  1.7 5.1 %collective-permute-start.2 = (bf16[4,2048]{1,0:T(4,128)(2,1)S(1)}, bf16[4,2048]{1,0:T(4,128)(2,1)S(1)}, u32[]{:S(2)}, u32[]{:S(2)}) collective-permute-start(bf16[4,2048]{1,0:T(4,128)(2,1)S(1)} %norm.1.refs_0_), channel_id=1, source_target_pairs={{0,3},{1,2},{2,1},{3,0},{4,7},{5,6},{6,5},{7,4},{8,11},{9,10},{10,... | collective-permute-start | bytes 49160 | tf_op jit(solution)/shard_map/ppermute | solution.py:20
  6.9 0.6 %collective-permute-start = (bf16[4,2048]{1,0:T(4,128)(2,1)S(1)}, bf16[4,2048]{1,0:T(4,128)(2,1)S(1)}, u32[]{:S(2)}, u32[]{:S(2)}) collective-permute-start(bf16[4,2048]{1,0:T(4,128)(2,1)S(1)} %norm.1.refs_0_), channel_id=1, source_target_pairs={{0,1},{1,0},{2,3},{3,2},{4,5},{5,4},{6,7},{7,6},{8,9},{9,8},{10,11... | collective-permute-start | bytes 49160 | tf_op jit(solution)/shard_map/ppermute | solution.py:20
  7.5 1.1 %collective-permute-done.2.refs_3_ = bf16[4,2048]{1,0:T(4,128)(2,1)S(1)} collective-permute-done((bf16[4,2048]{1,0:T(4,128)(2,1)S(1)}, bf16[4,2048]{1,0:T(4,128)(2,1)S(1)}, u32[]{:S(2)}, u32[]{:S(2)}) %collective-permute-start.2) | collective-permute-done | bytes 16416 | tf_op jit(solution)/shard_map/ppermute | solution.py:20
  8.6 2.9 %collective-permute-done.1.refs_2_ = bf16[4,2048]{1,0:T(4,128)(2,1)S(1)} collective-permute-done((bf16[4,2048]{1,0:T(4,128)(2,1)S(1)}, bf16[4,2048]{1,0:T(4,128)(2,1)S(1)}, u32[]{:S(2)}, u32[]{:S(2)}) %collective-permute-start.1) | collective-permute-done | bytes 16416 | tf_op jit(solution)/shard_map/ppermute | solution.py:20
  11.5 1.5 %project.1 = f32[16,2560]{1,0:T(8,128)S(1)} custom-call(bf16[4,2048]{1,0:T(4,128)(2,1)S(1)} %norm.1.refs_0_, bf16[4,2048]{1,0:T(4,128)(2,1)S(1)} %collective-permute-done.refs_1_, bf16[4,2048]{1,0:T(4,128)(2,1)S(1)} %collective-permute-done.1.refs_2_, bf16[4,2048]{1,0:T(4,128)(2,1)S(1)} %collective-permute-done.2.refs_3_, bf16[2048,2048]{1,0:T(8,128)(2,1)S(1)} %copy-done, ...), custom_call_target="tpu_custom_call" | custom-call | flops 167772160 | bytes 1048576 | tf_op jit(solution)/shard_map/project/pallas_call | solution.py:302
  13.0 1.4 %collective-permute-done.3 = f32[16,2560]{1,0:T(8,128)S(1)} collective-permute-done((f32[16,2560]{1,0:T(8,128)S(1)}, f32[16,2560]{1,0:T(8,128)S(1)}, u32[]{:S(2)}, u32[]{:S(2)}) %collective-permute-start.3) | collective-permute-done | bytes 163872 | tf_op jit(solution)/shard_map/ppermute | solution.py:20
  14.4 1.6 %collective-permute-start.4 = (f32[16,2560]{1,0:T(8,128)S(1)}, f32[16,2560]{1,0:T(8,128)S(1)}, u32[]{:S(2)}, u32[]{:S(2)}) collective-permute-start(f32[16,2560]{1,0:T(8,128)S(1)} %add.15), channel_id=1, source_target_pairs={{0,8},{4,12},{8,0},{12,4},{1,9},{5,13},{9,1},{13,5},{2,10},{6,14},... | collective-permute-start | bytes 491528 | tf_op jit(solution)/shard_map/ppermute | solution.py:20
  16.0 4.8 %collective-permute-done.4 = f32[16,2560]{1,0:T(8,128)S(1)} collective-permute-done((f32[16,2560]{1,0:T(8,128)S(1)}, f32[16,2560]{1,0:T(8,128)S(1)}, u32[]{:S(2)}, u32[]{:S(2)}) %collective-permute-start.4) | collective-permute-done | bytes 163872 | tf_op jit(solution)/shard_map/ppermute | solution.py:20
  20.9 1.9 %copy-done.5 = bf16[48,2,128,128]{3,2,1,0:T(8,128)(2,1)S(1)} copy-done((bf16[48,2,128,128]{3,2,1,0:T(8,128)(2,1)S(1)}, bf16[48,2,128,128]{3,2,1,0:T(8,128)(2,1)}, u32[]{:S(2)}) %copy-start.5) | copy-done | bytes 3145752
  22.8 3.3 %attend.1.own_ref = f32[264,128]{1,0:T(8,128)S(1)} custom-call(s32[8,24]{1,0:T(8,128)S(1)} %copy-done.7, s32[8,8]{1,0:T(8,128)S(1)} %copy-done.8, s32[8]{0:T(128)S(1)} %copy-done.9, bf16[8,2,16,128]{3,2,1,0:T(8,128)(2,1)S(1)} %bitcast.23, bf16[2,16,128]{2,1,0:T(8,128)(2,1)S(1)} %get-tuple-element.14.new_key_ref, ...), custom_call_target="tpu_custom_call" | custom-call | flops 10000000000 | bytes 1048576 | tf_op jit(solution)/shard_map/attend/pallas_call | solution.py:322
  26.2 1.3 %collective-permute-done.5.other_ref = f32[264,128]{1,0:T(8,128)S(1)} collective-permute-done((f32[264,128]{1,0:T(8,128)S(1)}, f32[264,128]{1,0:T(8,128)S(1)}, u32[]{:S(2)}, u32[]{:S(2)}) %collective-permute-start.5) | collective-permute-done | bytes 135200 | tf_op jit(solution)/shard_map/ppermute | solution.py:20
  27.7 1.6 %collective-permute-start.6 = (f32[264,128]{1,0:T(8,128)S(1)}, f32[264,128]{1,0:T(8,128)S(1)}, u32[]{:S(2)}, u32[]{:S(2)}) collective-permute-start(f32[264,128]{1,0:T(8,128)S(1)} %combine.2.own_ref), channel_id=1, source_target_pairs={{0,8},{4,12},{8,0},{12,4},{1,9},{5,13},{9,1},{13,5},{2,10},{6,14},... | collective-permute-start | bytes 405512 | tf_op jit(solution)/shard_map/ppermute | solution.py:20
  29.2 4.1 %collective-permute-done.6.other_ref = f32[264,128]{1,0:T(8,128)S(1)} collective-permute-done((f32[264,128]{1,0:T(8,128)S(1)}, f32[264,128]{1,0:T(8,128)S(1)}, u32[]{:S(2)}, u32[]{:S(2)}) %collective-permute-start.6) | collective-permute-done | bytes 135200 | tf_op jit(solution)/shard_map/ppermute | solution.py:20
  33.4 0.2 combine.3
  33.6 3.4 %copy-done.1 = bf16[2048,2048]{1,0:T(8,128)(2,1)S(1)} copy-done((bf16[2048,2048]{1,0:T(8,128)(2,1)S(1)}, bf16[2048,2048]{1,0:T(8,128)(2,1)}, u32[]{:S(2)}) %copy-start.1) | copy-done | bytes 8388632
  37.0 1.2 %output.1 = (f32[4,2048]{1,0:T(4,128)S(1)}, f32[4,2048]{1,0:T(4,128)S(1)}, f32[4,2048]{1,0:T(4,128)S(1)}, f32[4,2048]{1,0:T(4,128)S(1)}) custom-call(bf16[16,2048]{1,0:T(8,128)(2,1)S(1)} %reshape.23.rows_ref, bf16[2048,2048]{1,0:T(8,128)(2,1)S(1)} %copy-done.1), custom_call_target="tpu_custom_call" | custom-call | flops 134217728 | bytes 1048576 | tf_op jit(solution)/shard_map/output/pallas_call | solution.py:351
  38.2 2.1 %collective-permute-start.8 = (f32[4,2048]{1,0:T(4,128)S(1)}, f32[4,2048]{1,0:T(4,128)S(1)}, u32[]{:S(2)}, u32[]{:S(2)}) collective-permute-start(f32[4,2048]{1,0:T(4,128)S(1)} %get-tuple-element.11), channel_id=1, source_target_pairs={{0,2},{1,3},{2,0},{3,1},{4,6},{5,7},{6,4},{7,5},{8,10},{9,11},{10,... | collective-permute-start | bytes 98312 | tf_op jit(solution)/shard_map/ppermute | solution.py:20
  40.2 2.3 %collective-permute-start.9 = (f32[4,2048]{1,0:T(4,128)S(1)}, f32[4,2048]{1,0:T(4,128)S(1)}, u32[]{:S(2)}, u32[]{:S(2)}) collective-permute-start(f32[4,2048]{1,0:T(4,128)S(1)} %get-tuple-element.12), channel_id=1, source_target_pairs={{0,3},{1,2},{2,1},{3,0},{4,7},{5,6},{6,5},{7,4},{8,11},{9,10},{10,... | collective-permute-start | bytes 98312 | tf_op jit(solution)/shard_map/ppermute | solution.py:20
  42.6 0.5 %collective-permute-done.8 = f32[4,2048]{1,0:T(4,128)S(1)} collective-permute-done((f32[4,2048]{1,0:T(4,128)S(1)}, f32[4,2048]{1,0:T(4,128)S(1)}, u32[]{:S(2)}, u32[]{:S(2)}) %collective-permute-start.8) | collective-permute-done | bytes 32800 | tf_op jit(solution)/shard_map/ppermute | solution.py:20
  43.0 2.9 %collective-permute-done.9 = f32[4,2048]{1,0:T(4,128)S(1)} collective-permute-done((f32[4,2048]{1,0:T(4,128)S(1)}, f32[4,2048]{1,0:T(4,128)S(1)}, u32[]{:S(2)}, u32[]{:S(2)}) %collective-permute-start.9) | collective-permute-done | bytes 32800 | tf_op jit(solution)/shard_map/ppermute | solution.py:20
  45.9 0.6 %add_convert_fusion.1 = bf16[4,2048]{1,0:T(4,128)(2,1)} fusion(f32[4,2048]{1,0:T(4,128)S(1)} %collective-permute-done.9, f32[4,2048]{1,0:T(4,128)S(1)} %collective-permute-done.8, f32[4,2048]{1,0:T(4,128)S(1)} %get-tuple-element.9, f32[4,2048]{1,0:T(4,128)S(1)} %collective-permute-done.7), kind=kLoop, calls=%fused_computation.4 | loop fusion | flops 32768 | bytes 147456 | tf_op jit(solution)/shard_map/convert_element_type | solution.py:362
  (35 shorter events, 0.4 us)
Async XLA Ops:
  0.7 0.8 %copy-start.6 = (bf16[4,8192]{1,0:T(4,128)(2,1)S(1)}, bf16[4,8192]{1,0:T(4,128)(2,1)}, u32[]{:S(2)}) copy-start(bf16[4,8192]{1,0:T(4,128)(2,1)} %hidden_ref.1) | copy-start | bytes 196612
  1.5 10.0 %copy-start = (bf16[2048,2048]{1,0:T(8,128)(2,1)S(1)}, bf16[2048,2048]{1,0:T(8,128)(2,1)}, u32[]{:S(2)}) copy-start(bf16[2048,2048]{1,0:T(8,128)(2,1)} %refs_4_.1) | copy-start | bytes 25165828
  1.5 10.0 %copy-start.2 = (bf16[2048,256]{1,0:T(8,128)(2,1)S(1)}, bf16[2048,256]{1,0:T(8,128)(2,1)}, u32[]{:S(2)}) copy-start(bf16[2048,256]{1,0:T(8,128)(2,1)} %refs_5_.1) | copy-start | bytes 3145732
  1.5 10.0 %copy-start.3 = (bf16[2048,256]{1,0:T(8,128)(2,1)S(1)}, bf16[2048,256]{1,0:T(8,128)(2,1)}, u32[]{:S(2)}) copy-start(bf16[2048,256]{1,0:T(8,128)(2,1)} %refs_6_.1) | copy-start | bytes 3145732
  1.7 19.2 %copy-start.4 = (bf16[48,2,128,128]{3,2,1,0:T(8,128)(2,1)S(1)}, bf16[48,2,128,128]{3,2,1,0:T(8,128)(2,1)}, u32[]{:S(2)}) copy-start(bf16[48,2,128,128]{3,2,1,0:T(8,128)(2,1)} %key_ref.1) | copy-start | bytes 9437188
  1.7 19.2 %copy-start.7 = (s32[8,24]{1,0:T(8,128)S(1)}, s32[8,24]{1,0:T(8,128)}, u32[]{:S(2)}) copy-start(s32[8,24]{1,0:T(8,128)} %table_ref.1) | copy-start | bytes 2308
  1.7 19.2 %copy-start.8 = (s32[8,8]{1,0:T(8,128)S(1)}, s32[8,8]{1,0:T(8,128)}, u32[]{:S(2)}) copy-start(s32[8,8]{1,0:T(8,128)} %list_ref.1) | copy-start | bytes 772
  1.7 19.2 %copy-start.9 = (s32[8]{0:T(128)S(1)}, s32[8]{0:T(128)}, u32[]{:S(2)}) copy-start(s32[8]{0:T(128)} %lengths_ref.1) | copy-start | bytes 100
  1.7 6.8 %collective-permute-start.2 = (bf16[4,2048]{1,0:T(4,128)(2,1)S(1)}, bf16[4,2048]{1,0:T(4,128)(2,1)S(1)}, u32[]{:S(2)}, u32[]{:S(2)}) collective-permute-start(bf16[4,2048]{1,0:T(4,128)(2,1)S(1)} %norm.1.refs_0_), channel_id=1, source_target_pairs={{0,3},{1,2},{2,1},{3,0},{4,7},{5,6},{6,5},{7,4},{8,11},{9,10},{10,... | collective-permute-start | bytes 49160 | tf_op jit(solution)/shard_map/ppermute | solution.py:20
  6.9 4.6 %collective-permute-start.1 = (bf16[4,2048]{1,0:T(4,128)(2,1)S(1)}, bf16[4,2048]{1,0:T(4,128)(2,1)S(1)}, u32[]{:S(2)}, u32[]{:S(2)}) collective-permute-start(bf16[4,2048]{1,0:T(4,128)(2,1)S(1)} %norm.1.refs_0_), channel_id=1, source_target_pairs={{0,2},{1,3},{2,0},{3,1},{4,6},{5,7},{6,4},{7,5},{8,10},{9,11},{10,... | collective-permute-start | bytes 49160 | tf_op jit(solution)/shard_map/ppermute | solution.py:20
  6.9 4.6 %collective-permute-start = (bf16[4,2048]{1,0:T(4,128)(2,1)S(1)}, bf16[4,2048]{1,0:T(4,128)(2,1)S(1)}, u32[]{:S(2)}, u32[]{:S(2)}) collective-permute-start(bf16[4,2048]{1,0:T(4,128)(2,1)S(1)} %norm.1.refs_0_), channel_id=1, source_target_pairs={{0,1},{1,0},{2,3},{3,2},{4,5},{5,4},{6,7},{7,6},{8,9},{9,8},{10,11... | collective-permute-start | bytes 49160 | tf_op jit(solution)/shard_map/ppermute | solution.py:20
  13.0 1.4 %collective-permute-start.3 = (f32[16,2560]{1,0:T(8,128)S(1)}, f32[16,2560]{1,0:T(8,128)S(1)}, u32[]{:S(2)}, u32[]{:S(2)}) collective-permute-start(f32[16,2560]{1,0:T(8,128)S(1)} %project.1), channel_id=1, source_target_pairs={{0,4},{4,0},{8,12},{12,8},{1,5},{5,1},{9,13},{13,9},{2,6},{6,2},{1... | collective-permute-start | bytes 491528 | tf_op jit(solution)/shard_map/ppermute | solution.py:20
  14.4 6.3 %collective-permute-start.4 = (f32[16,2560]{1,0:T(8,128)S(1)}, f32[16,2560]{1,0:T(8,128)S(1)}, u32[]{:S(2)}, u32[]{:S(2)}) collective-permute-start(f32[16,2560]{1,0:T(8,128)S(1)} %add.15), channel_id=1, source_target_pairs={{0,8},{4,12},{8,0},{12,4},{1,9},{5,13},{9,1},{13,5},{2,10},{6,14},... | collective-permute-start | bytes 491528 | tf_op jit(solution)/shard_map/ppermute | solution.py:20
  20.9 1.9 %copy-start.5 = (bf16[48,2,128,128]{3,2,1,0:T(8,128)(2,1)S(1)}, bf16[48,2,128,128]{3,2,1,0:T(8,128)(2,1)}, u32[]{:S(2)}) copy-start(bf16[48,2,128,128]{3,2,1,0:T(8,128)(2,1)} %value_ref.1) | copy-start | bytes 9437188
  26.1 1.4 %collective-permute-start.5 = (f32[264,128]{1,0:T(8,128)S(1)}, f32[264,128]{1,0:T(8,128)S(1)}, u32[]{:S(2)}, u32[]{:S(2)}) collective-permute-start(f32[264,128]{1,0:T(8,128)S(1)} %attend.1.own_ref), channel_id=1, source_target_pairs={{0,4},{4,0},{8,12},{12,8},{1,5},{5,1},{9,13},{13,9},{2,6},{6,2},{1... | collective-permute-start | bytes 405512 | tf_op jit(solution)/shard_map/ppermute | solution.py:20
  27.7 5.7 %collective-permute-start.6 = (f32[264,128]{1,0:T(8,128)S(1)}, f32[264,128]{1,0:T(8,128)S(1)}, u32[]{:S(2)}, u32[]{:S(2)}) collective-permute-start(f32[264,128]{1,0:T(8,128)S(1)} %combine.2.own_ref), channel_id=1, source_target_pairs={{0,8},{4,12},{8,0},{12,4},{1,9},{5,13},{9,1},{13,5},{2,10},{6,14},... | collective-permute-start | bytes 405512 | tf_op jit(solution)/shard_map/ppermute | solution.py:20
  33.6 3.4 %copy-start.1 = (bf16[2048,2048]{1,0:T(8,128)(2,1)S(1)}, bf16[2048,2048]{1,0:T(8,128)(2,1)}, u32[]{:S(2)}) copy-start(bf16[2048,2048]{1,0:T(8,128)(2,1)} %weight_ref.1) | copy-start | bytes 25165828
  38.2 4.4 %collective-permute-start.7 = (f32[4,2048]{1,0:T(4,128)S(1)}, f32[4,2048]{1,0:T(4,128)S(1)}, u32[]{:S(2)}, u32[]{:S(2)}) collective-permute-start(f32[4,2048]{1,0:T(4,128)S(1)} %get-tuple-element.10), channel_id=1, source_target_pairs={{0,1},{1,0},{2,3},{3,2},{4,5},{5,4},{6,7},{7,6},{8,9},{9,8},{10,11... | collective-permute-start | bytes 98312 | tf_op jit(solution)/shard_map/ppermute | solution.py:20
  38.2 4.9 %collective-permute-start.8 = (f32[4,2048]{1,0:T(4,128)S(1)}, f32[4,2048]{1,0:T(4,128)S(1)}, u32[]{:S(2)}, u32[]{:S(2)}) collective-permute-start(f32[4,2048]{1,0:T(4,128)S(1)} %get-tuple-element.11), channel_id=1, source_target_pairs={{0,2},{1,3},{2,0},{3,1},{4,6},{5,7},{6,4},{7,5},{8,10},{9,11},{10,... | collective-permute-start | bytes 98312 | tf_op jit(solution)/shard_map/ppermute | solution.py:20
  40.2 5.7 %collective-permute-start.9 = (f32[4,2048]{1,0:T(4,128)S(1)}, f32[4,2048]{1,0:T(4,128)S(1)}, u32[]{:S(2)}, u32[]{:S(2)}) collective-permute-start(f32[4,2048]{1,0:T(4,128)S(1)} %get-tuple-element.12), channel_id=1, source_target_pairs={{0,3},{1,2},{2,1},{3,0},{4,7},{5,6},{6,5},{7,4},{8,11},{9,10},{10,... | collective-permute-start | bytes 98312 | tf_op jit(solution)/shard_map/ppermute | solution.py:20

commit v2 on v1

v2 whole, which is shorter than its diff:
```python
import functools

import jax
import jax.numpy as jnp
from jax import lax
from jax.experimental import pallas as pl
from jax.experimental.pallas import tpu as pltpu
from jax.sharding import PartitionSpec as P

NEG_FILL = -1e30
EPSILON = 1e-05
LANES = 128
MIB = 1 << 20
IN_VMEM = pl.BlockSpec(memory_space=pltpu.VMEM)
IN_SMEM = pl.BlockSpec(memory_space=pltpu.SMEM)


def swap(array, axis, distance):
    count = lax.axis_size(axis)
    return lax.ppermute(array, axis, [(i, i ^ distance) for i in range(count)])


def kernel_call(body, name, outs, ins, vmem_mib, flops, scratch=(), out_space=IN_VMEM):
    return pl.pallas_call(
        body,
        out_shape=outs,
        in_specs=ins,
        out_specs=jax.tree.map(lambda _: out_space, outs),
        scratch_shapes=list(scratch),
        name=name,
        compiler_params=pltpu.CompilerParams(vmem_limit_bytes=vmem_mib * MIB),
        cost_estimate=pl.CostEstimate(flops=int(flops), bytes_accessed=1024, transcendentals=0),
    )


def norm_body(hidden_hbm, gain_hbm, out_ref, hidden_ref, gain_ref, sems):
    copies = [
        pltpu.make_async_copy(hidden_hbm, hidden_ref, sems.at[0]),
        pltpu.make_async_copy(gain_hbm, gain_ref, sems.at[1]),
    ]
    for copy in copies:
        copy.start()
    for copy in copies:
        copy.wait()
    cols = gain_ref.shape[0]
    start = pl.multiple_of(lax.axis_index("mem") * cols, cols)
    hidden = hidden_ref[...].astype(jnp.float32)
    mean_sq = jnp.mean(hidden * hidden, axis=-1, keepdims=True)
    own = hidden_ref[:, pl.ds(start, cols)].astype(jnp.float32)
    gain = gain_ref[...].astype(jnp.float32).reshape(1, cols)
    normed = own * lax.rsqrt(mean_sq + EPSILON) * gain
    out_ref[...] = normed.astype(jnp.bfloat16)


def select_body(chunk, steps, pool, block, table_ref, list_ref, lengths_ref, slot_ref, row_ref, valid_ref):
    mem = lax.axis_index("mem")
    head_shard = lax.axis_index("heads")
    row_count, selected = list_ref.shape
    count = jnp.int32(0)
    for row in range(row_count):
        first = row * steps
        place = (lax.bitwise_xor(first // chunk, head_shard) * chunk + first % chunk) // steps
        length = lengths_ref[row]
        for i in range(selected):
            index = list_ref[row, i]
            slot = table_ref[row, index] - mem * pool
            slot_ref[count] = slot
            row_ref[count] = place
            valid_ref[count] = length - index * block
            count += ((slot >= 0) & (slot < pool)).astype(jnp.int32)
    for c in range(slot_ref.shape[0] - 1):
        live = c < count
        slot_ref[c] = jnp.where(live, slot_ref[c], 0)
        row_ref[c] = jnp.where(live, row_ref[c], row_count)
        valid_ref[c] = jnp.where(live, valid_ref[c], 0)


def project_body(places, tile, *refs):
    q_ref, k_ref, v_ref, out_ref = refs[len(places) :]
    chunks = [refs[places.index(i)] for i in range(len(places))]
    rows = jnp.concatenate([c[...].astype(jnp.float32) for c in chunks], axis=0)
    rows = rows.astype(jnp.bfloat16)
    at = 0
    for weight in (q_ref, k_ref, v_ref):
        width = min(tile, weight.shape[1])
        for col in range(0, weight.shape[1], width):
            product = jnp.dot(
                rows, weight[:, col : col + width], preferred_element_type=jnp.float32
            )
            for lane in range(0, width, LANES):
                out_ref[at : at + rows.shape[0]] = product[:, lane : lane + LANES]
                at += rows.shape[0]


def add_body(own_ref, other_ref, out_ref, *sent_refs):
    total = own_ref[...] + other_ref[...]
    for ref in (out_ref, *sent_refs):
        ref[...] = total.astype(ref.dtype)


def split_dot(weights, values):
    high = weights.astype(jnp.bfloat16)
    low = (weights - high.astype(jnp.float32)).astype(jnp.bfloat16)
    both = jnp.dot(
        jnp.concatenate([high, low], axis=0), values, preferred_element_type=jnp.float32
    )
    return both[: weights.shape[0]] + both[weights.shape[0] :]


def to_pieces(rows):
    pieces = []
    for _ in range(3):
        pieces.append(rows.astype(jnp.bfloat16))
        rows = rows - pieces[-1].astype(jnp.float32)
    return pieces


def from_pieces(pieces):
    high, middle, low = [piece.astype(jnp.float32) for piece in pieces]
    return low + middle + high


def group_lanes(query_count):
    lane = lax.broadcasted_iota(jnp.int32, (query_count, LANES), 1)
    row = lax.broadcasted_iota(jnp.int32, (query_count, LANES), 0)
    return lane - row


def pack_columns(columns, query_count):
    per_row = LANES // query_count
    offset = group_lanes(query_count)
    rows = []
    for first in range(0, len(columns), per_row):
        row = jnp.zeros((query_count, LANES), jnp.float32)
        for i, column in enumerate(columns[first : first + per_row]):
            row = jnp.where(offset == i * query_count, column, row)
        rows.append(jnp.sum(row, axis=0, keepdims=True))
    return rows


def unpack_column(row, place, query_count):
    spread = jnp.broadcast_to(row, (query_count, LANES))
    picked = jnp.where(group_lanes(query_count) == place * query_count, spread, 0.0)
    return jnp.sum(picked, axis=1, keepdims=True)


def attend_body(
    chunk,
    steps,
    scale,
    slot_ref,
    row_ref,
    valid_ref,
    own_ref,
    other_ref,
    key_ref,
    value_ref,
    out_ref,
    wide_ref,
    query_ref,
    score_ref,
    peak_ref,
    total_ref,
    accum_ref,
):
    mem = lax.axis_index("mem")
    head_shard = lax.axis_index("heads")
    row_count, kv_heads, query_count, head_dim = query_ref.shape
    capacity = score_ref.shape[0]
    tokens = row_count * steps
    per_kv = query_count // steps

    projected = (own_ref[...] + other_ref[...].astype(jnp.float32)).astype(jnp.bfloat16)
    wide_ref[...] = projected.astype(jnp.float32)
    for row in range(row_count):
        for g in range(kv_heads):
            first = g * per_kv * tokens + row * steps
            parts = [wide_ref[pl.ds(first + s, per_kv, stride=tokens)] for s in range(steps)]
            query_ref[row, g] = jnp.concatenate(parts, axis=0).astype(jnp.bfloat16)
    fresh_at = kv_heads * per_kv * tokens
    fresh = [
        projected[fresh_at + i * tokens : fresh_at + (i + 1) * tokens] for i in range(2 * kv_heads)
    ]
    new_keys, new_values = fresh[:kv_heads], fresh[kv_heads:]

    lane = lax.broadcasted_iota(jnp.int32, (query_count, LANES), 1)
    peak_ref[...] = jnp.full(peak_ref.shape, NEG_FILL, jnp.float32)
    total_ref[...] = jnp.zeros(total_ref.shape, jnp.float32)
    accum_ref[...] = jnp.zeros(accum_ref.shape, jnp.float32)
    contract_last = (((1,), (1,)), ((), ()))
    for c in range(capacity):
        slot, row, valid = slot_ref[c], row_ref[c], valid_ref[c]
        read_row = jnp.minimum(row, row_count - 1)
        for g in range(kv_heads):
            score = lax.dot_general(
                query_ref[read_row, g],
                key_ref[slot, g],
                contract_last,
                preferred_element_type=jnp.float32,
            )
            score = jnp.where(lane < valid, score * scale, NEG_FILL)
            score_ref[c, g] = score
            peak_ref[row, g] = jnp.maximum(peak_ref[row, g], score)

    shape = (row_count * query_count, tokens)
    query_row = lax.broadcasted_iota(jnp.int32, shape, 0)
    query_place = query_row // query_count * steps + query_row % query_count // per_kv
    key_place = lax.broadcasted_iota(jnp.int32, shape, 1)

    def token_of(place):
        return lax.bitwise_xor(place // chunk, head_shard) * chunk + place % chunk

    query_token, key_token = token_of(query_place), token_of(key_place)
    seen = (
        (query_token // steps == key_token // steps)
        & (key_token <= query_token)
        & (query_token // steps % lax.axis_size("mem") == mem)
    )
    peaks = [None] * (row_count * kv_heads)
    totals = [None] * (row_count * kv_heads)
    for g in range(kv_heads):
        score = lax.dot_general(
            query_ref[:, g].reshape(row_count * query_count, head_dim),
            new_keys[g],
            contract_last,
            preferred_element_type=jnp.float32,
        )
        score = jnp.where(seen, score * scale, NEG_FILL)
        old = jnp.max(
            peak_ref[:row_count, g].reshape(row_count * query_count, LANES), axis=1, keepdims=True
        )
        peak = jnp.maximum(old, jnp.max(score, axis=1, keepdims=True))
        weights = jnp.where(seen, jnp.exp(score - peak), 0.0)
        accum = split_dot(weights, new_values[g]).reshape(row_count, query_count, head_dim)
        total = jnp.sum(weights, axis=1, keepdims=True)
        wide = jnp.broadcast_to(peak, (row_count * query_count, LANES))
        wide = wide.reshape(row_count, query_count, LANES)
        peak_ref[:row_count, g] = wide
        accum_ref[:row_count, g] = accum
        total = jnp.broadcast_to(total, (row_count * query_count, LANES))
        total = total.reshape(row_count, query_count, LANES)
        for row in range(row_count):
            peaks[row * kv_heads + g] = wide[row]
            totals[row * kv_heads + g] = total[row]

    for c in range(capacity):
        slot, row, valid = slot_ref[c], row_ref[c], valid_ref[c]
        for g in range(kv_heads):
            weights = jnp.exp(score_ref[c, g] - peak_ref[row, g])
            weights = jnp.where(lane < valid, weights, 0.0)
            total_ref[row, g] += weights
            accum_ref[row, g] += split_dot(weights, value_ref[slot, g])

    for row in range(row_count):
        for g in range(kv_heads):
            group = row * kv_heads + g
            totals[group] = totals[group] + jnp.sum(total_ref[row, g], axis=1, keepdims=True)
    groups = row_count * kv_heads
    height = groups * query_count
    out_ref[:height] = accum_ref[:row_count].reshape(height, head_dim)
    packed = pack_columns(peaks, query_count) + pack_columns(totals, query_count)
    spare = out_ref.shape[0] - height - len(packed)
    packed.append(jnp.zeros((spare, LANES), jnp.float32))
    out_ref[height:] = jnp.concatenate(packed, axis=0)


def state_rows(groups, query_count):
    return -(-groups // (LANES // query_count))


def merge_states(query_count, groups, last, own_ref, other_ref):
    per_row = LANES // query_count
    height = groups * query_count
    rows = state_rows(groups, query_count)
    own_peak, own_total = (own_ref[height + i * rows : height + (i + 1) * rows] for i in range(2))
    if other_ref.dtype == jnp.bfloat16:
        tail = other_ref[height:]
        pieces = [tail[i * rows : (i + 1) * rows] for i in range(6)]
        other_peak, other_total = from_pieces(pieces[:3]), from_pieces(pieces[3:])
    else:
        other_peak, other_total = (
            other_ref[height + i * rows : height + (i + 1) * rows] for i in range(2)
        )
    peak = jnp.maximum(own_peak, other_peak)
    own_factor, other_factor = jnp.exp(own_peak - peak), jnp.exp(other_peak - peak)
    total = own_total * own_factor + other_total * other_factor
    if last:
        own_factor, other_factor = own_factor / total, other_factor / total
    values = []
    for group in range(groups):
        row, place = divmod(group, per_row)
        at = slice(group * query_count, (group + 1) * query_count)
        values.append(
            own_ref[at] * unpack_column(own_factor[row : row + 1], place, query_count)
            + other_ref[at].astype(jnp.float32)
            * unpack_column(other_factor[row : row + 1], place, query_count)
        )
    return peak, total, values


def combine_body(query_count, groups, own_ref, other_ref, *out_refs):
    height = groups * query_count
    peak, total, values = merge_states(query_count, groups, False, own_ref, other_ref)
    for ref in out_refs:
        tail = [peak, total]
        if ref.dtype == jnp.bfloat16:
            tail = to_pieces(peak) + to_pieces(total)
        spare = ref.shape[0] - height - len(tail) * peak.shape[0]
        tail.append(jnp.zeros((spare, LANES), ref.dtype))
        ref[height:] = jnp.concatenate(tail, axis=0)
        for group, value in enumerate(values):
            ref[group * query_count : (group + 1) * query_count] = value.astype(ref.dtype)


def output_body(kv_heads, steps, tile, own_ref, other_ref, weight_ref, *refs):
    out_refs, wide_ref = refs[:-1], refs[-1]
    heads = weight_ref.shape[0] // LANES
    per_kv = heads // kv_heads
    tokens = wide_ref.shape[0] // heads
    groups = tokens // steps * kv_heads
    _, _, values = merge_states(steps * per_kv, groups, True, own_ref, other_ref)
    for group, value in enumerate(values):
        row, g = divmod(group, kv_heads)
        for s in range(steps):
            first = g * per_kv * tokens + row * steps + s
            wide_ref[pl.ds(first, per_kv, stride=tokens)] = value[s * per_kv : (s + 1) * per_kv]
    rows = jnp.concatenate(
        [wide_ref[j * tokens : (j + 1) * tokens].astype(jnp.bfloat16) for j in range(heads)], axis=1
    )
    chunk = out_refs[0].shape[0]
    for col in range(0, weight_ref.shape[1], tile):
        product = jnp.dot(
            rows, weight_ref[:, col : col + tile], preferred_element_type=jnp.float32
        )
        for i, out_ref in enumerate(out_refs):
            out_ref[:, col : col + tile] = product[i * chunk : (i + 1) * chunk]


def shards(
    hidden,
    norm_gain,
    q_weight,
    k_weight,
    v_weight,
    o_weight,
    k_cache,
    v_cache,
    page_table,
    attend_list,
    lengths,
):
    mem_count, head_count = lax.axis_size("mem"), lax.axis_size("heads")
    chunk = hidden.shape[0]
    feature_cols = norm_gain.shape[0]
    query_cols, value_cols = q_weight.shape[1], k_weight.shape[1]
    pool, kv_heads, block, head_dim = k_cache.shape
    row_count, selected = attend_list.shape
    token_count = chunk * head_count
    steps = token_count // row_count
    per_kv = query_cols // head_dim // kv_heads
    query_count = steps * per_kv
    capacity = 2 * row_count * selected // mem_count
    f32, bf16 = jnp.float32, jnp.bfloat16

    normed = kernel_call(
        norm_body,
        "norm",
        jax.ShapeDtypeStruct((chunk, feature_cols), bf16),
        [pl.BlockSpec(memory_space=pltpu.HBM)] * 2,
        2,
        1e10,
        [pltpu.VMEM(hidden.shape, bf16), pltpu.VMEM(norm_gain.shape, bf16)]
        + [pltpu.SemaphoreType.DMA((2,))],
    )(*[pltpu.with_memory_space_constraint(a, pltpu.HBM) for a in (hidden, norm_gain)])
    distances = [*range(2, head_count), 1]
    pieces = [normed] + [swap(normed, "heads", d) for d in distances]

    chosen = kernel_call(
        functools.partial(select_body, chunk, steps, pool, block),
        "select",
        [jax.ShapeDtypeStruct((capacity + 1,), jnp.int32)] * 3,
        [IN_SMEM] * 3,
        2,
        1e10,
        out_space=IN_SMEM,
    )(page_table, attend_list, lengths)

    width = query_cols + 2 * value_cols
    summed = kernel_call(
        functools.partial(project_body, (0, *distances), 512),
        "project",
        jax.ShapeDtypeStruct((width // LANES * token_count, LANES), f32),
        [IN_VMEM] * (head_count + 3),
        4,
        2 * token_count * feature_cols * width,
    )(*pieces, q_weight, k_weight, v_weight)
    sent = summed
    distance = 1
    while 2 * distance < mem_count:
        added = kernel_call(
            add_body,
            "add",
            [jax.ShapeDtypeStruct(summed.shape, f32)],
            [IN_VMEM] * 2,
            2,
            1e10,
        )(summed, swap(sent, "mem", distance))
        summed, sent = added[0], added[-1]
        distance *= 2

    groups = row_count * kv_heads
    height = groups * query_count
    state = (kv_heads, query_count, LANES)
    partial = kernel_call(
        functools.partial(attend_body, chunk, steps, head_dim ** (-0.5)),
        "attend",
        jax.ShapeDtypeStruct((height + 8, LANES), f32),
        [IN_SMEM] * 3 + [IN_VMEM] * 4,
        4,
        1e10,
        [pltpu.VMEM(summed.shape, f32), pltpu.VMEM((row_count, *state), bf16)]
        + [pltpu.VMEM((capacity, *state), f32)]
        + [pltpu.VMEM((row_count + 1, *state), f32)] * 3,
    )(*chosen, summed, swap(sent.astype(jnp.float16), "mem", distance).astype(f32), k_cache, v_cache)

    sent = partial
    distance = 1
    while 2 * distance < mem_count:
        outs = [jax.ShapeDtypeStruct(partial.shape, f32)]
        if 4 * distance == mem_count:
            pad = -(-6 * state_rows(groups, query_count) // 16) * 16
            outs.append(jax.ShapeDtypeStruct((height + pad, LANES), bf16))
        merged = kernel_call(
            functools.partial(combine_body, query_count, groups),
            "combine",
            outs,
            [IN_VMEM] * 2,
            2,
            1e10,
        )(partial, swap(sent, "mem", distance))
        partial, sent = merged[0], merged[-1]
        distance *= 2

    out_cols = o_weight.shape[1]
    projected = kernel_call(
        functools.partial(output_body, kv_heads, steps, min(512, out_cols)),
        "output",
        [jax.ShapeDtypeStruct((chunk, out_cols), f32)] * head_count,
        [IN_VMEM] * 3,
        4,
        2 * token_count * query_cols * out_cols,
        [pltpu.VMEM((query_cols // LANES * token_count, LANES), f32)],
    )(partial, swap(sent, "mem", distance), o_weight)
    total = projected[0]
    for d in distances:
        total = total + swap(projected[d], "heads", d)
    return total.astype(bf16)


def solution(mesh):
    in_specs = (
        P(("groups", "heads"), None),
        P("mem"),
        P("mem", "heads"),
        P("mem", "heads"),
        P("mem", "heads"),
        P("heads", "mem"),
        P(("groups", "mem"), "heads", None, None),
        P(("groups", "mem"), "heads", None, None),
        P("groups", None),
        P("groups", None),
        P("groups"),
    )
    out_specs = P(("groups", "heads"), "mem")
    return jax.shard_map(shards, mesh=mesh, in_specs=in_specs, out_specs=out_specs, check_vma=False)
```

time: 46.8 us -> 36.3 us (0.78)
  local copies, waits for them, and re-layouts: 6.93 us -> 0.05 us
  waiting for transfers between devices: 19 us -> 14.1 us
  Pallas kernels: 6.4 us -> 8.72 us
  starting transfers between devices: 13.3 us -> 12.4 us
    unnamed x22 -> x20, local copies, waits for them, and re-layouts: 6.15 us -> 0.05 us
    ppermute x10, waiting for transfers between devices: 19 us -> 14.1 us  [swap(): return lax.ppermute(array, axis, [(i, i ^ distance) for i in range(count)])]
    pallas_call x4 -> x5, Pallas kernels: 2.96 us -> 4.76 us  [the longest x1 1.81 us: shards(): kernel_call(functools.partial(select_body, chunk, steps, pool, block), 's...]
    pallas_call x1, Pallas kernels: 0.16 us -> 1.17 us  [shards(): kernel_call(norm_body, 'norm', jax.ShapeDtypeStruct((chunk, feature_cols)...]
    ppermute x10, starting transfers between devices: 13.3 us -> 12.4 us  [swap(): return lax.ppermute(array, axis, [(i, i ^ distance) for i in range(count)])]
    reshape x6 -> x0, local copies, waits for them, and re-layouts: 0.76 us -> none  [the longest x1 0.69 us: shards(): norm_gain.reshape(1, feature_cols)]
    pallas_call x1, Pallas kernels: 3.28 us -> 2.79 us  [shards(): kernel_call(functools.partial(attend_body, chunk, steps, head_dim ** (-0....]
  transfers between devices with their start and end apart: 10 -> 10, of which waited for: 8 -> 8; matrix products, arithmetic and copies ran while one was open for 0% -> 0% of each run, Pallas kernels for 0% -> 5%
where the time goes in v2:
time: 36.3 us; the launch traced here: 36.1 us
  waiting for transfers between devices  14.1 us (39%)
  starting transfers between devices  12.4 us (34%)
  Pallas kernels  8.72 us (24%)
  other arithmetic  0.65 us (2%)
    ppermute x10, waiting for transfers between devices, swap(): return lax.ppermute(array, axis, [(i, i ^ distance) for i in range(count)])  14.1 us
    ppermute x10, starting transfers between devices, swap(): return lax.ppermute(array, axis, [(i, i ^ distance) for i in range(count)])  12.4 us
    pallas_call x1, Pallas kernels, shards(): kernel_call(functools.partial(attend_body, chunk, steps, head_dim ** (-0....  2.79 us
    pallas_call x1, Pallas kernels, shards(): kernel_call(functools.partial(select_body, chunk, steps, pool, block), 's...  1.81 us
    pallas_call x1, Pallas kernels, shards(): kernel_call(functools.partial(project_body, (0, *distances), 512), 'proje...  1.46 us
    pallas_call x1, Pallas kernels, shards(): kernel_call(functools.partial(output_body, kv_heads, steps, min(512, out_...  1.32 us
    pallas_call x1, Pallas kernels, shards(): kernel_call(norm_body, 'norm', jax.ShapeDtypeStruct((chunk, feature_cols)...  1.17 us
  transfers between devices with their start and end apart: 10, of which 8 were waited for; matrix products, arithmetic and copies ran while one was open for 0% of the time, Pallas kernels for 5%

profile of v2, /device:TPU:0, one launch (start us, length us, event | category | flops | bytes accessed | tf_op | source)
XLA Modules:
  0.0 36.1 jit_solution(8480345947543967834)
XLA Ops:
  0.0 1.2 %norm.1.refs_0_ = bf16[4,2048]{1,0:T(4,128)(2,1)S(1)} custom-call(bf16[4,8192]{1,0:T(4,128)(2,1)} %hidden_hbm.1, bf16[2048]{0:T(1024)(128)(2,1)} %gain_hbm.1), custom_call_target="tpu_custom_call" | custom-call | flops 10000000000 | bytes 1024 | tf_op jit(solution)/shard_map/norm/pallas_call | solution.py:365
  1.2 4.1 %collective-permute-start = (bf16[4,2048]{1,0:T(4,128)(2,1)S(1)}, bf16[4,2048]{1,0:T(4,128)(2,1)S(1)}, u32[]{:S(2)}, u32[]{:S(2)}) collective-permute-start(bf16[4,2048]{1,0:T(4,128)(2,1)S(1)} %norm.1.refs_0_), channel_id=1, source_target_pairs={{0,2},{1,3},{2,0},{3,1},{4,6},{5,7},{6,4},{7,5},{8,10},{9,11},{10,... | collective-permute-start | bytes 49160 | tf_op jit(solution)/shard_map/ppermute | solution.py:20
  5.3 1.3 %collective-permute-start.1 = (bf16[4,2048]{1,0:T(4,128)(2,1)S(1)}, bf16[4,2048]{1,0:T(4,128)(2,1)S(1)}, u32[]{:S(2)}, u32[]{:S(2)}) collective-permute-start(bf16[4,2048]{1,0:T(4,128)(2,1)S(1)} %norm.1.refs_0_), channel_id=1, source_target_pairs={{0,3},{1,2},{2,1},{3,0},{4,7},{5,6},{6,5},{7,4},{8,11},{9,10},{10,... | collective-permute-start | bytes 49160 | tf_op jit(solution)/shard_map/ppermute | solution.py:20
  6.6 0.2 collective-permute-start.2
  6.9 0.1 collective-permute-done.refs_1_
  7.0 3.8 %collective-permute-done.1.refs_2_ = bf16[4,2048]{1,0:T(4,128)(2,1)S(1)} collective-permute-done((bf16[4,2048]{1,0:T(4,128)(2,1)S(1)}, bf16[4,2048]{1,0:T(4,128)(2,1)S(1)}, u32[]{:S(2)}, u32[]{:S(2)}) %collective-permute-start.1) | collective-permute-done | bytes 16416 | tf_op jit(solution)/shard_map/ppermute | solution.py:20
  10.8 1.5 %project.1.own_ref = f32[320,128]{1,0:T(8,128)S(1)} custom-call(bf16[4,2048]{1,0:T(4,128)(2,1)S(1)} %norm.1.refs_0_, bf16[4,2048]{1,0:T(4,128)(2,1)S(1)} %collective-permute-done.refs_1_, bf16[4,2048]{1,0:T(4,128)(2,1)S(1)} %collective-permute-done.1.refs_2_, bf16[4,2048]{1,0:T(4,128)(2,1)S(1)} %collective-permute-done.2.refs_3_, ...), custom_call_target="tpu_custom_call" | custom-call | flops 167772160 | bytes 1024 | tf_op jit(solution)/shard_map/project/pallas_call | solution.py:389
  12.4 1.4 %collective-permute-done.3.other_ref = f32[320,128]{1,0:T(8,128)S(1)} collective-permute-done((f32[320,128]{1,0:T(8,128)S(1)}, f32[320,128]{1,0:T(8,128)S(1)}, u32[]{:S(2)}, u32[]{:S(2)}) %collective-permute-start.3) | collective-permute-done | bytes 163872 | tf_op jit(solution)/shard_map/ppermute | solution.py:20
  13.8 1.6 %collective-permute-start.4 = (f16[320,128]{1,0:T(8,128)(2,1)S(1)}, f16[320,128]{1,0:T(8,128)(2,1)S(1)}, u32[]{:S(2)}, u32[]{:S(2)}) collective-permute-start(f16[320,128]{1,0:T(8,128)(2,1)S(1)} %convert_element_type.9), channel_id=1, source_target_pairs={{0,8},{4,12},{8,0},{12,4},{1,9},{5,13},{9,1},{13,5},{2,10},{6,14},... | collective-permute-start | bytes 245768 | tf_op jit(solution)/shard_map/ppermute | solution.py:20
  15.4 1.8 %select.1 = (s32[33]{0:T(128)S(1)}, s32[33]{0:T(128)S(1)}, s32[33]{0:T(128)S(1)}) custom-call(s32[8,24]{1,0:T(8,128)S(1)} %copy-done.5, s32[8,8]{1,0:T(8,128)S(1)} %copy-done.6, s32[8]{0:T(128)S(1)} %copy-done.7), custom_call_target="tpu_custom_call" | custom-call | flops 10000000000 | bytes 1024 | tf_op jit(solution)/shard_map/select/pallas_call | solution.py:378
  17.2 1.2 %collective-permute-done.4 = f16[320,128]{1,0:T(8,128)(2,1)S(1)} collective-permute-done((f16[320,128]{1,0:T(8,128)(2,1)S(1)}, f16[320,128]{1,0:T(8,128)(2,1)S(1)}, u32[]{:S(2)}, u32[]{:S(2)}) %collective-permute-start.4) | collective-permute-done | bytes 81952 | tf_op jit(solution)/shard_map/ppermute | solution.py:20
  18.4 2.8 %attend.1.own_ref = f32[264,128]{1,0:T(8,128)S(1)} custom-call(s32[33]{0:T(128)S(1)} %get-tuple-element.14.slot_ref, s32[33]{0:T(128)S(1)} %get-tuple-element.15.row_ref, s32[33]{0:T(128)S(1)} %get-tuple-element.16.valid_ref, f32[320,128]{1,0:T(8,128)S(1)} %add.16.own_ref, f32[320,128]{1,0:T(8,128)S(1)} %convert_element_type.10.other_ref, ...), custom_call_target="tpu_custom_call" | custom-call | flops 10000000000 | bytes 1024 | tf_op jit(solution)/shard_map/attend/pallas_call | solution.py:414
  21.2 0.1 collective-permute-start.5
  21.3 1.3 %collective-permute-done.5.other_ref = f32[264,128]{1,0:T(8,128)S(1)} collective-permute-done((f32[264,128]{1,0:T(8,128)S(1)}, f32[264,128]{1,0:T(8,128)S(1)}, u32[]{:S(2)}, u32[]{:S(2)}) %collective-permute-start.5) | collective-permute-done | bytes 135200 | tf_op jit(solution)/shard_map/ppermute | solution.py:20
  22.7 0.2 combine.1
  22.8 1.6 %collective-permute-start.6 = (bf16[272,128]{1,0:T(8,128)(2,1)S(1)}, bf16[272,128]{1,0:T(8,128)(2,1)S(1)}, u32[]{:S(2)}, u32[]{:S(2)}) collective-permute-start(bf16[272,128]{1,0:T(8,128)(2,1)S(1)} %get-tuple-element.18), channel_id=1, source_target_pairs={{0,8},{4,12},{8,0},{12,4},{1,9},{5,13},{9,1},{13,5},{2,10},{6,14},... | collective-permute-start | bytes 208904 | tf_op jit(solution)/shard_map/ppermute | solution.py:20
  24.4 2.8 %collective-permute-done.6.other_ref = bf16[272,128]{1,0:T(8,128)(2,1)S(1)} collective-permute-done((bf16[272,128]{1,0:T(8,128)(2,1)S(1)}, bf16[272,128]{1,0:T(8,128)(2,1)S(1)}, u32[]{:S(2)}, u32[]{:S(2)}) %collective-permute-start.6) | collective-permute-done | bytes 69664 | tf_op jit(solution)/shard_map/ppermute | solution.py:20
  27.2 1.3 %output.1 = (f32[4,2048]{1,0:T(4,128)S(1)}, f32[4,2048]{1,0:T(4,128)S(1)}, f32[4,2048]{1,0:T(4,128)S(1)}, f32[4,2048]{1,0:T(4,128)S(1)}) custom-call(f32[264,128]{1,0:T(8,128)S(1)} %get-tuple-element.17.own_ref, bf16[272,128]{1,0:T(8,128)(2,1)S(1)} %collective-permute-done.6.other_ref, bf16[2048,2048]{1,0:T(8,128)(2,1)S(1)} %bitcast.1), custom_call_target="tpu_custom_call" | custom-call | flops 134217728 | bytes 1024 | tf_op jit(solution)/shard_map/output/pallas_call | solution.py:445
  28.5 1.2 %collective-permute-start.7 = (f32[4,2048]{1,0:T(4,128)S(1)}, f32[4,2048]{1,0:T(4,128)S(1)}, u32[]{:S(2)}, u32[]{:S(2)}) collective-permute-start(f32[4,2048]{1,0:T(4,128)S(1)} %get-tuple-element.20), channel_id=1, source_target_pairs={{0,2},{1,3},{2,0},{3,1},{4,6},{5,7},{6,4},{7,5},{8,10},{9,11},{10,... | collective-permute-start | bytes 98312 | tf_op jit(solution)/shard_map/ppermute | solution.py:20
  29.8 0.9 %collective-permute-start.8 = (f32[4,2048]{1,0:T(4,128)S(1)}, f32[4,2048]{1,0:T(4,128)S(1)}, u32[]{:S(2)}, u32[]{:S(2)}) collective-permute-start(f32[4,2048]{1,0:T(4,128)S(1)} %get-tuple-element.21), channel_id=1, source_target_pairs={{0,3},{1,2},{2,1},{3,0},{4,7},{5,6},{6,5},{7,4},{8,11},{9,10},{10,... | collective-permute-start | bytes 98312 | tf_op jit(solution)/shard_map/ppermute | solution.py:20
  30.7 1.3 %collective-permute-start.9 = (f32[4,2048]{1,0:T(4,128)S(1)}, f32[4,2048]{1,0:T(4,128)S(1)}, u32[]{:S(2)}, u32[]{:S(2)}) collective-permute-start(f32[4,2048]{1,0:T(4,128)S(1)} %get-tuple-element.22), channel_id=1, source_target_pairs={{0,1},{1,0},{2,3},{3,2},{4,5},{5,4},{6,7},{7,6},{8,9},{9,8},{10,11... | collective-permute-start | bytes 98312 | tf_op jit(solution)/shard_map/ppermute | solution.py:20
  32.0 1.6 %collective-permute-done.7 = f32[4,2048]{1,0:T(4,128)S(1)} collective-permute-done((f32[4,2048]{1,0:T(4,128)S(1)}, f32[4,2048]{1,0:T(4,128)S(1)}, u32[]{:S(2)}, u32[]{:S(2)}) %collective-permute-start.7) | collective-permute-done | bytes 32800 | tf_op jit(solution)/shard_map/ppermute | solution.py:20
  33.6 1.9 %collective-permute-done.8 = f32[4,2048]{1,0:T(4,128)S(1)} collective-permute-done((f32[4,2048]{1,0:T(4,128)S(1)}, f32[4,2048]{1,0:T(4,128)S(1)}, u32[]{:S(2)}, u32[]{:S(2)}) %collective-permute-start.8) | collective-permute-done | bytes 32800 | tf_op jit(solution)/shard_map/ppermute | solution.py:20
  35.5 0.6 %add_convert_fusion = bf16[4,2048]{1,0:T(4,128)(2,1)} fusion(f32[4,2048]{1,0:T(4,128)S(1)} %collective-permute-done.9, f32[4,2048]{1,0:T(4,128)S(1)} %collective-permute-done.8, f32[4,2048]{1,0:T(4,128)S(1)} %get-tuple-element.19, f32[4,2048]{1,0:T(4,128)S(1)} %collective-permute-done.7), kind=kLoop, calls=%fused_computation | loop fusion | flops 32768 | bytes 147456 | tf_op jit(solution)/shard_map/convert_element_type | solution.py:457
  (27 shorter events, 0.2 us)
Async XLA Ops:
  0.0 10.8 %copy-start = (bf16[2048,2048]{1,0:T(8,128)(2,1)S(1)}, bf16[2048,2048]{1,0:T(8,128)(2,1)}, u32[]{:S(2)}) copy-start(bf16[2048,2048]{1,0:T(8,128)(2,1)} %refs_4_.1) | copy-start | bytes 25165828
  0.0 10.8 %copy-start.1 = (bf16[2048,256]{1,0:T(8,128)(2,1)S(1)}, bf16[2048,256]{1,0:T(8,128)(2,1)}, u32[]{:S(2)}) copy-start(bf16[2048,256]{1,0:T(8,128)(2,1)} %refs_5_.1) | copy-start | bytes 3145732
  0.0 10.8 %copy-start.2 = (bf16[2048,256]{1,0:T(8,128)(2,1)S(1)}, bf16[2048,256]{1,0:T(8,128)(2,1)}, u32[]{:S(2)}) copy-start(bf16[2048,256]{1,0:T(8,128)(2,1)} %refs_6_.1) | copy-start | bytes 3145732
  1.2 5.8 %collective-permute-start = (bf16[4,2048]{1,0:T(4,128)(2,1)S(1)}, bf16[4,2048]{1,0:T(4,128)(2,1)S(1)}, u32[]{:S(2)}, u32[]{:S(2)}) collective-permute-start(bf16[4,2048]{1,0:T(4,128)(2,1)S(1)} %norm.1.refs_0_), channel_id=1, source_target_pairs={{0,2},{1,3},{2,0},{3,1},{4,6},{5,7},{6,4},{7,5},{8,10},{9,11},{10,... | collective-permute-start | bytes 49160 | tf_op jit(solution)/shard_map/ppermute | solution.py:20
  5.3 5.5 %collective-permute-start.1 = (bf16[4,2048]{1,0:T(4,128)(2,1)S(1)}, bf16[4,2048]{1,0:T(4,128)(2,1)S(1)}, u32[]{:S(2)}, u32[]{:S(2)}) collective-permute-start(bf16[4,2048]{1,0:T(4,128)(2,1)S(1)} %norm.1.refs_0_), channel_id=1, source_target_pairs={{0,3},{1,2},{2,1},{3,0},{4,7},{5,6},{6,5},{7,4},{8,11},{9,10},{10,... | collective-permute-start | bytes 49160 | tf_op jit(solution)/shard_map/ppermute | solution.py:20
  6.6 4.2 %collective-permute-start.2 = (bf16[4,2048]{1,0:T(4,128)(2,1)S(1)}, bf16[4,2048]{1,0:T(4,128)(2,1)S(1)}, u32[]{:S(2)}, u32[]{:S(2)}) collective-permute-start(bf16[4,2048]{1,0:T(4,128)(2,1)S(1)} %norm.1.refs_0_), channel_id=1, source_target_pairs={{0,1},{1,0},{2,3},{3,2},{4,5},{5,4},{6,7},{7,6},{8,9},{9,8},{10,11... | collective-permute-start | bytes 49160 | tf_op jit(solution)/shard_map/ppermute | solution.py:20
  12.3 3.1 %copy-start.5 = (s32[8,24]{1,0:T(8,128)S(1)}, s32[8,24]{1,0:T(8,128)}, u32[]{:S(2)}) copy-start(s32[8,24]{1,0:T(8,128)} %table_ref.1) | copy-start | bytes 2308
  12.3 3.1 %copy-start.6 = (s32[8,8]{1,0:T(8,128)S(1)}, s32[8,8]{1,0:T(8,128)}, u32[]{:S(2)}) copy-start(s32[8,8]{1,0:T(8,128)} %list_ref.1) | copy-start | bytes 772
  12.3 3.1 %copy-start.7 = (s32[8]{0:T(128)S(1)}, s32[8]{0:T(128)}, u32[]{:S(2)}) copy-start(s32[8]{0:T(128)} %lengths_ref.1) | copy-start | bytes 100
  12.3 1.4 %collective-permute-start.3 = (f32[320,128]{1,0:T(8,128)S(1)}, f32[320,128]{1,0:T(8,128)S(1)}, u32[]{:S(2)}, u32[]{:S(2)}) collective-permute-start(f32[320,128]{1,0:T(8,128)S(1)} %project.1.own_ref), channel_id=1, source_target_pairs={{0,4},{4,0},{8,12},{12,8},{1,5},{5,1},{9,13},{13,9},{2,6},{6,2},{1... | collective-permute-start | bytes 491528 | tf_op jit(solution)/shard_map/ppermute | solution.py:20
  13.8 4.6 %copy-start.3 = (bf16[48,2,128,128]{3,2,1,0:T(8,128)(2,1)S(1)}, bf16[48,2,128,128]{3,2,1,0:T(8,128)(2,1)}, u32[]{:S(2)}) copy-start(bf16[48,2,128,128]{3,2,1,0:T(8,128)(2,1)} %key_ref.1) | copy-start | bytes 9437188
  13.8 4.6 %copy-start.4 = (bf16[48,2,128,128]{3,2,1,0:T(8,128)(2,1)S(1)}, bf16[48,2,128,128]{3,2,1,0:T(8,128)(2,1)}, u32[]{:S(2)}) copy-start(bf16[48,2,128,128]{3,2,1,0:T(8,128)(2,1)} %value_ref.1) | copy-start | bytes 9437188
  13.8 4.6 %collective-permute-start.4 = (f16[320,128]{1,0:T(8,128)(2,1)S(1)}, f16[320,128]{1,0:T(8,128)(2,1)S(1)}, u32[]{:S(2)}, u32[]{:S(2)}) collective-permute-start(f16[320,128]{1,0:T(8,128)(2,1)S(1)} %convert_element_type.9), channel_id=1, source_target_pairs={{0,8},{4,12},{8,0},{12,4},{1,9},{5,13},{9,1},{13,5},{2,10},{6,14},... | collective-permute-start | bytes 245768 | tf_op jit(solution)/shard_map/ppermute | solution.py:20
  18.4 8.8 %slice-start = ((s8[8388608]{0:T(1024)(128)(4,1)}), s8[4194304]{0:T(1024)(128)(4,1)S(1)}, s32[]{:S(2)}) async-start(s8[8388608]{0:T(1024)(128)(4,1)} %bitcast), calls=%async_computation | async-start | bytes 8388608
  21.2 6.0 %slice-start.1 = ((s8[8388608]{0:T(1024)(128)(4,1)}), s8[4194304]{0:T(1024)(128)(4,1)S(1)}, s32[]{:S(2)}) async-start(s8[8388608]{0:T(1024)(128)(4,1)} %bitcast), calls=%async_computation.1 | async-start | bytes 8388608
  21.2 1.4 %collective-permute-start.5 = (f32[264,128]{1,0:T(8,128)S(1)}, f32[264,128]{1,0:T(8,128)S(1)}, u32[]{:S(2)}, u32[]{:S(2)}) collective-permute-start(f32[264,128]{1,0:T(8,128)S(1)} %attend.1.own_ref), channel_id=1, source_target_pairs={{0,4},{4,0},{8,12},{12,8},{1,5},{5,1},{9,13},{13,9},{2,6},{6,2},{1... | collective-permute-start | bytes 405512 | tf_op jit(solution)/shard_map/ppermute | solution.py:20
  22.8 4.4 %collective-permute-start.6 = (bf16[272,128]{1,0:T(8,128)(2,1)S(1)}, bf16[272,128]{1,0:T(8,128)(2,1)S(1)}, u32[]{:S(2)}, u32[]{:S(2)}) collective-permute-start(bf16[272,128]{1,0:T(8,128)(2,1)S(1)} %get-tuple-element.18), channel_id=1, source_target_pairs={{0,8},{4,12},{8,0},{12,4},{1,9},{5,13},{9,1},{13,5},{2,10},{6,14},... | collective-permute-start | bytes 208904 | tf_op jit(solution)/shard_map/ppermute | solution.py:20
  28.5 5.1 %collective-permute-start.7 = (f32[4,2048]{1,0:T(4,128)S(1)}, f32[4,2048]{1,0:T(4,128)S(1)}, u32[]{:S(2)}, u32[]{:S(2)}) collective-permute-start(f32[4,2048]{1,0:T(4,128)S(1)} %get-tuple-element.20), channel_id=1, source_target_pairs={{0,2},{1,3},{2,0},{3,1},{4,6},{5,7},{6,4},{7,5},{8,10},{9,11},{10,... | collective-permute-start | bytes 98312 | tf_op jit(solution)/shard_map/ppermute | solution.py:20
  29.8 5.7 %collective-permute-start.8 = (f32[4,2048]{1,0:T(4,128)S(1)}, f32[4,2048]{1,0:T(4,128)S(1)}, u32[]{:S(2)}, u32[]{:S(2)}) collective-permute-start(f32[4,2048]{1,0:T(4,128)S(1)} %get-tuple-element.21), channel_id=1, source_target_pairs={{0,3},{1,2},{2,1},{3,0},{4,7},{5,6},{6,5},{7,4},{8,11},{9,10},{10,... | collective-permute-start | bytes 98312 | tf_op jit(solution)/shard_map/ppermute | solution.py:20
  30.7 4.8 %collective-permute-start.9 = (f32[4,2048]{1,0:T(4,128)S(1)}, f32[4,2048]{1,0:T(4,128)S(1)}, u32[]{:S(2)}, u32[]{:S(2)}) collective-permute-start(f32[4,2048]{1,0:T(4,128)S(1)} %get-tuple-element.22), channel_id=1, source_target_pairs={{0,1},{1,0},{2,3},{3,2},{4,5},{5,4},{6,7},{7,6},{8,9},{9,8},{10,11... | collective-permute-start | bytes 98312 | tf_op jit(solution)/shard_map/ppermute | solution.py:20

commit v3 on v2

--- a/solution.py
+++ b/solution.py
@@ -25,7 +25,7 @@
         body,
         out_shape=outs,
         in_specs=ins,
-        out_specs=jax.tree.map(lambda _: out_space, outs),
+        out_specs=out_space if isinstance(out_space, list) else jax.tree.map(lambda _: out_space, outs),
         scratch_shapes=list(scratch),
         name=name,
         compiler_params=pltpu.CompilerParams(vmem_limit_bytes=vmem_mib * MIB),
@@ -52,10 +52,14 @@
     out_ref[...] = normed.astype(jnp.bfloat16)
 
 
-def select_body(chunk, steps, pool, block, table_ref, list_ref, lengths_ref, slot_ref, row_ref, valid_ref):
+def select_body(
+    chunk, steps, pool, block, per_kv, table_ref, list_ref, lengths_ref,
+    chosen_ref, seen_ref,
+):
     mem = lax.axis_index("mem")
     head_shard = lax.axis_index("heads")
     row_count, selected = list_ref.shape
+    stride = chosen_ref.shape[0] // 3
     count = jnp.int32(0)
     for row in range(row_count):
         first = row * steps
@@ -64,23 +68,49 @@
         for i in range(selected):
             index = list_ref[row, i]
             slot = table_ref[row, index] - mem * pool
-            slot_ref[count] = slot
-            row_ref[count] = place
-            valid_ref[count] = length - index * block
+            chosen_ref[count] = slot
+            chosen_ref[stride + count] = place
+            chosen_ref[2 * stride + count] = length - index * block
             count += ((slot >= 0) & (slot < pool)).astype(jnp.int32)
-    for c in range(slot_ref.shape[0] - 1):
+    for c in range(stride - 1):
         live = c < count
-        slot_ref[c] = jnp.where(live, slot_ref[c], 0)
-        row_ref[c] = jnp.where(live, row_ref[c], row_count)
-        valid_ref[c] = jnp.where(live, valid_ref[c], 0)
-
-
-def project_body(places, tile, *refs):
+        for at, blank in ((c, 0), (stride + c, row_count), (2 * stride + c, 0)):
+            chosen_ref[at] = jnp.where(live, chosen_ref[at], blank)
+
+    def token_of(place):
+        return lax.bitwise_xor(place // chunk, head_shard) * chunk + place % chunk
+
+    tokens = row_count * steps
+    group_rows = steps * per_kv
+    row_height = seen_ref.shape[0] // row_count
+    at = lax.broadcasted_iota(jnp.int32, seen_ref.shape, 0)
+    query_token = token_of(at // row_height * steps + at % group_rows // per_kv)
+    query_head = at % row_height // group_rows
+    lane = lax.broadcasted_iota(jnp.int32, seen_ref.shape, 1)
+    key_head, key = lane // tokens, lane % tokens
+    key_token = token_of(key % row_count * steps + key // row_count)
+    seen = (
+        (query_head == key_head)
+        & (query_token // steps == key_token // steps)
+        & (key_token <= query_token)
+        & (query_token // steps % lax.axis_size("mem") == mem)
+    )
+    seen_ref[...] = seen.astype(jnp.float32)
+
+
+def project_body(places, steps, kv_heads, tile, *refs):
     q_ref, k_ref, v_ref, out_ref = refs[len(places) :]
-    chunks = [refs[places.index(i)] for i in range(len(places))]
-    rows = jnp.concatenate([c[...].astype(jnp.float32) for c in chunks], axis=0)
-    rows = rows.astype(jnp.bfloat16)
-    at = 0
+    chunks = [refs[places.index(i)][...].astype(jnp.float32) for i in range(len(places))]
+    rows = jnp.concatenate(chunks, axis=0).astype(jnp.bfloat16)
+    tokens = rows.shape[0]
+    row_count = tokens // steps
+    to = lax.broadcasted_iota(jnp.int32, (tokens, tokens), 0)
+    come = lax.broadcasted_iota(jnp.int32, (tokens, tokens), 1)
+    order = (to % row_count * steps + to // row_count == come).astype(jnp.bfloat16)
+    rows = jnp.dot(order, rows, preferred_element_type=jnp.float32).astype(jnp.bfloat16)
+    heads = q_ref.shape[1] // LANES
+    per_kv = heads // kv_heads
+    head = 0
     for weight in (q_ref, k_ref, v_ref):
         width = min(tile, weight.shape[1])
         for col in range(0, weight.shape[1], width):
@@ -88,8 +118,16 @@
                 rows, weight[:, col : col + width], preferred_element_type=jnp.float32
             )
             for lane in range(0, width, LANES):
-                out_ref[at : at + rows.shape[0]] = product[:, lane : lane + LANES]
-                at += rows.shape[0]
+                columns = product[:, lane : lane + LANES]
+                if head < heads:
+                    for s in range(steps):
+                        at = (head // per_kv * steps + s) * per_kv + head % per_kv
+                        out_ref[pl.ds(at, row_count, stride=heads * steps)] = columns[
+                            s * row_count : (s + 1) * row_count
+                        ]
+                else:
+                    out_ref[head * tokens : (head + 1) * tokens] = columns
+                head += 1
 
 
 def add_body(own_ref, other_ref, out_ref, *sent_refs):
@@ -126,14 +164,16 @@
     return lane - row
 
 
-def pack_columns(columns, query_count):
+def pack_columns(column, query_count):
     per_row = LANES // query_count
     offset = group_lanes(query_count)
+    groups = column.shape[0] // query_count
     rows = []
-    for first in range(0, len(columns), per_row):
+    for first in range(0, groups, per_row):
         row = jnp.zeros((query_count, LANES), jnp.float32)
-        for i, column in enumerate(columns[first : first + per_row]):
-            row = jnp.where(offset == i * query_count, column, row)
+        for i in range(min(per_row, groups - first)):
+            at = (first + i) * query_count
+            row = jnp.where(offset == i * query_count, column[at : at + query_count], row)
         rows.append(jnp.sum(row, axis=0, keepdims=True))
     return rows
 
@@ -145,120 +185,105 @@
 
 
 def attend_body(
-    chunk,
-    steps,
     scale,
-    slot_ref,
-    row_ref,
-    valid_ref,
+    chosen_ref,
+    seen_ref,
     own_ref,
     other_ref,
     key_ref,
     value_ref,
     out_ref,
-    wide_ref,
     query_ref,
     score_ref,
-    peak_ref,
     total_ref,
     accum_ref,
+    *peak_refs,
 ):
-    mem = lax.axis_index("mem")
-    head_shard = lax.axis_index("heads")
-    row_count, kv_heads, query_count, head_dim = query_ref.shape
+    row_count, row_height, head_dim = query_ref.shape
+    kv_heads = key_ref.shape[1]
+    query_count = row_height // kv_heads
     capacity = score_ref.shape[0]
-    tokens = row_count * steps
-    per_kv = query_count // steps
-
-    projected = (own_ref[...] + other_ref[...].astype(jnp.float32)).astype(jnp.bfloat16)
-    wide_ref[...] = projected.astype(jnp.float32)
-    for row in range(row_count):
-        for g in range(kv_heads):
-            first = g * per_kv * tokens + row * steps
-            parts = [wide_ref[pl.ds(first + s, per_kv, stride=tokens)] for s in range(steps)]
-            query_ref[row, g] = jnp.concatenate(parts, axis=0).astype(jnp.bfloat16)
-    fresh_at = kv_heads * per_kv * tokens
-    fresh = [
-        projected[fresh_at + i * tokens : fresh_at + (i + 1) * tokens] for i in range(2 * kv_heads)
-    ]
-    new_keys, new_values = fresh[:kv_heads], fresh[kv_heads:]
-
-    lane = lax.broadcasted_iota(jnp.int32, (query_count, LANES), 1)
-    peak_ref[...] = jnp.full(peak_ref.shape, NEG_FILL, jnp.float32)
-    total_ref[...] = jnp.zeros(total_ref.shape, jnp.float32)
-    accum_ref[...] = jnp.zeros(accum_ref.shape, jnp.float32)
+    height = row_count * row_height
     contract_last = (((1,), (1,)), ((), ()))
+
+    projected = (own_ref[...] + other_ref[...]).astype(jnp.bfloat16)
+    queries = projected[:height]
+    query_ref[...] = queries.reshape(query_ref.shape)
+    fresh = projected[height:]
+    count = fresh.shape[0] // 2
+    spare = jnp.zeros((LANES - count, head_dim), jnp.bfloat16)
+    seen = seen_ref[...] > 0
+    fresh_score = lax.dot_general(
+        queries,
+        jnp.concatenate([fresh[:count], spare], axis=0),
+        contract_last,
+        preferred_element_type=jnp.float32,
+    )
+    fresh_score = jnp.where(seen, fresh_score * scale, NEG_FILL)
+    peak_ref = peak_refs[0]
+    peak_ref[:row_count] = fresh_score.reshape(row_count, row_height, LANES)
+    peak_ref[row_count] = jnp.full((row_height, LANES), NEG_FILL, jnp.float32)
+    for ref in peak_refs[1:]:
+        ref[...] = jnp.full(ref.shape, NEG_FILL, jnp.float32)
+    stride = chosen_ref.shape[0] // 3
+
+    lane = lax.broadcasted_iota(jnp.int32, (row_height, LANES), 1)
     for c in range(capacity):
-        slot, row, valid = slot_ref[c], row_ref[c], valid_ref[c]
-        read_row = jnp.minimum(row, row_count - 1)
-        for g in range(kv_heads):
-            score = lax.dot_general(
-                query_ref[read_row, g],
-                key_ref[slot, g],
-                contract_last,
-                preferred_element_type=jnp.float32,
-            )
-            score = jnp.where(lane < valid, score * scale, NEG_FILL)
-            score_ref[c, g] = score
-            peak_ref[row, g] = jnp.maximum(peak_ref[row, g], score)
-
-    shape = (row_count * query_count, tokens)
-    query_row = lax.broadcasted_iota(jnp.int32, shape, 0)
-    query_place = query_row // query_count * steps + query_row % query_count // per_kv
-    key_place = lax.broadcasted_iota(jnp.int32, shape, 1)
-
-    def token_of(place):
-        return lax.bitwise_xor(place // chunk, head_shard) * chunk + place % chunk
-
-    query_token, key_token = token_of(query_place), token_of(key_place)
-    seen = (
-        (query_token // steps == key_token // steps)
-        & (key_token <= query_token)
-        & (query_token // steps % lax.axis_size("mem") == mem)
-    )
-    peaks = [None] * (row_count * kv_heads)
-    totals = [None] * (row_count * kv_heads)
-    for g in range(kv_heads):
-        score = lax.dot_general(
-            query_ref[:, g].reshape(row_count * query_count, head_dim),
-            new_keys[g],
+        slot, row, valid = (chosen_ref[i * stride + c] for i in range(3))
+        every = lax.dot_general(
+            query_ref[jnp.minimum(row, row_count - 1)],
+            key_ref[slot].reshape(kv_heads * LANES, head_dim),
             contract_last,
             preferred_element_type=jnp.float32,
         )
-        score = jnp.where(seen, score * scale, NEG_FILL)
-        old = jnp.max(
-            peak_ref[:row_count, g].reshape(row_count * query_count, LANES), axis=1, keepdims=True
+        score = jnp.concatenate(
+            [
+                every[g * query_count : (g + 1) * query_count, g * LANES : (g + 1) * LANES]
+                for g in range(kv_heads)
+            ],
+            axis=0,
         )
-        peak = jnp.maximum(old, jnp.max(score, axis=1, keepdims=True))
-        weights = jnp.where(seen, jnp.exp(score - peak), 0.0)
-        accum = split_dot(weights, new_values[g]).reshape(row_count, query_count, head_dim)
-        total = jnp.sum(weights, axis=1, keepdims=True)
-        wide = jnp.broadcast_to(peak, (row_count * query_count, LANES))
-        wide = wide.reshape(row_count, query_count, LANES)
-        peak_ref[:row_count, g] = wide
-        accum_ref[:row_count, g] = accum
-        total = jnp.broadcast_to(total, (row_count * query_count, LANES))
-        total = total.reshape(row_count, query_count, LANES)
-        for row in range(row_count):
-            peaks[row * kv_heads + g] = wide[row]
-            totals[row * kv_heads + g] = total[row]
+        score = jnp.where(lane < valid, score * scale, NEG_FILL)
+        score_ref[c] = score
+        ref = peak_refs[c % len(peak_refs)]
+        ref[row] = jnp.maximum(ref[row], score)
+
+    peak = functools.reduce(jnp.maximum, [ref[:row_count] for ref in peak_refs])
+    peak = jnp.max(peak.reshape(height, LANES), axis=1, keepdims=True)
+    peak = jnp.broadcast_to(peak, (height, LANES))
+    peak_ref[:row_count] = peak.reshape(row_count, row_height, LANES)
+    weights = jnp.where(seen, jnp.exp(fresh_score - peak), 0.0)
+    total_ref[:row_count] = weights.reshape(row_count, row_height, LANES)
+    total_ref[row_count] = jnp.zeros((row_height, LANES), jnp.float32)
+    accum = split_dot(weights, jnp.concatenate([fresh[count:], spare], axis=0))
+    accum_ref[:row_count] = accum.reshape(row_count, row_height, head_dim)
+    accum_ref[row_count] = jnp.zeros((row_height, head_dim), jnp.float32)
 
     for c in range(capacity):
-        slot, row, valid = slot_ref[c], row_ref[c], valid_ref[c]
+        slot, row = chosen_ref[c], chosen_ref[stride + c]
+        weights = jnp.exp(score_ref[c] - peak_ref[row])
+        total_ref[row] += weights
+        high = weights.astype(jnp.bfloat16)
+        low = (weights - high.astype(jnp.float32)).astype(jnp.bfloat16)
+        split = []
         for g in range(kv_heads):
-            weights = jnp.exp(score_ref[c, g] - peak_ref[row, g])
-            weights = jnp.where(lane < valid, weights, 0.0)
-            total_ref[row, g] += weights
-            accum_ref[row, g] += split_dot(weights, value_ref[slot, g])
-
-    for row in range(row_count):
-        for g in range(kv_heads):
-            group = row * kv_heads + g
-            totals[group] = totals[group] + jnp.sum(total_ref[row, g], axis=1, keepdims=True)
-    groups = row_count * kv_heads
-    height = groups * query_count
+            at = slice(g * query_count, (g + 1) * query_count)
+            half = jnp.concatenate([high[at], low[at]], axis=0)
+            blank = jnp.zeros_like(half)
+            split.append(
+                jnp.concatenate([half if i == g else blank for i in range(kv_heads)], axis=1)
+            )
+        both = jnp.dot(
+            jnp.concatenate(split, axis=0),
+            value_ref[slot].reshape(kv_heads * LANES, head_dim),
+            preferred_element_type=jnp.float32,
+        ).reshape(kv_heads, 2, query_count, head_dim)
+        accum_ref[row] += (both[:, 0] + both[:, 1]).reshape(row_height, head_dim)
+
+    total = jnp.sum(total_ref[:row_count].reshape(height, LANES), axis=1, keepdims=True)
+    total = jnp.broadcast_to(total, (height, LANES))
     out_ref[:height] = accum_ref[:row_count].reshape(height, head_dim)
-    packed = pack_columns(peaks, query_count) + pack_columns(totals, query_count)
+    packed = pack_columns(peak, query_count) + pack_columns(total, query_count)
     spare = out_ref.shape[0] - height - len(packed)
     packed.append(jnp.zeros((spare, LANES), jnp.float32))
     out_ref[height:] = jnp.concatenate(packed, axis=0)
@@ -360,6 +385,8 @@
     per_kv = query_cols // head_dim // kv_heads
     query_count = steps * per_kv
     capacity = 2 * row_count * selected // mem_count
+    groups = row_count * kv_heads
+    height = groups * query_count
     f32, bf16 = jnp.float32, jnp.bfloat16
 
     normed = kernel_call(
@@ -376,18 +403,21 @@
     pieces = [normed] + [swap(normed, "heads", d) for d in distances]
 
     chosen = kernel_call(
-        functools.partial(select_body, chunk, steps, pool, block),
+        functools.partial(select_body, chunk, steps, pool, block, per_kv),
         "select",
-        [jax.ShapeDtypeStruct((capacity + 1,), jnp.int32)] * 3,
+        [
+            pltpu.SMEM((3 * (capacity + 1),), jnp.int32),
+            jax.ShapeDtypeStruct((height, LANES), f32),
+        ],
         [IN_SMEM] * 3,
         2,
         1e10,
-        out_space=IN_SMEM,
+        out_space=[IN_SMEM, IN_VMEM],
     )(page_table, attend_list, lengths)
 
     width = query_cols + 2 * value_cols
     summed = kernel_call(
-        functools.partial(project_body, (0, *distances), 512),
+        functools.partial(project_body, (0, *distances), steps, kv_heads, 512),
         "project",
         jax.ShapeDtypeStruct((width // LANES * token_count, LANES), f32),
         [IN_VMEM] * (head_count + 3),
@@ -408,20 +438,17 @@
         summed, sent = added[0], added[-1]
         distance *= 2
 
-    groups = row_count * kv_heads
-    height = groups * query_count
-    state = (kv_heads, query_count, LANES)
+    state = (kv_heads * query_count, LANES)
     partial = kernel_call(
-        functools.partial(attend_body, chunk, steps, head_dim ** (-0.5)),
+        functools.partial(attend_body, head_dim ** (-0.5)),
         "attend",
         jax.ShapeDtypeStruct((height + 8, LANES), f32),
-        [IN_SMEM] * 3 + [IN_VMEM] * 4,
+        [IN_SMEM] + [IN_VMEM] * 5,
         4,
         1e10,
-        [pltpu.VMEM(summed.shape, f32), pltpu.VMEM((row_count, *state), bf16)]
-        + [pltpu.VMEM((capacity, *state), f32)]
-        + [pltpu.VMEM((row_count + 1, *state), f32)] * 3,
-    )(*chosen, summed, swap(sent.astype(jnp.float16), "mem", distance).astype(f32), k_cache, v_cache)
+        [pltpu.VMEM((row_count, *state), bf16), pltpu.VMEM((capacity, *state), f32)]
+        + [pltpu.VMEM((row_count + 1, *state), f32)] * 6,
+    )(pltpu.with_memory_space_constraint(chosen[0], pltpu.SMEM), chosen[1], summed, swap(sent.astype(jnp.float16), "mem", distance).astype(f32), k_cache, v_cache)
 
     sent = partial
     distance = 1

time: 36.3 us -> 35.1 us (0.967)
  Pallas kernels: 8.72 us -> 7.17 us
  waiting for transfers between devices: 14.1 us -> 14.5 us
    pallas_call x3, Pallas kernels: 6.06 us -> 4.52 us  [the longest x1 1.57 us: shards(): kernel_call(functools.partial(project_body, (0, *distances), steps, kv_he...]
    ppermute x10, waiting for transfers between devices: 14.1 us -> 14.5 us  [swap(): return lax.ppermute(array, axis, [(i, i ^ distance) for i in range(count)])]
  transfers between devices with their start and end apart: 10 -> 10, of which waited for: 8 -> 8; matrix products, arithmetic and copies ran while one was open for 0% -> 0% of each run, Pallas kernels for 5% -> 4%
where the time goes in v3:
time: 35.1 us; the launch traced here: 35 us
  waiting for transfers between devices  14.5 us (41%)
  starting transfers between devices  12.4 us (35%)
  Pallas kernels  7.17 us (20%)
  other arithmetic  0.65 us (2%)
    ppermute x10, waiting for transfers between devices, swap(): return lax.ppermute(array, axis, [(i, i ^ distance) for i in range(count)])  14.5 us
    ppermute x10, starting transfers between devices, swap(): return lax.ppermute(array, axis, [(i, i ^ distance) for i in range(count)])  12.4 us
    pallas_call x1, Pallas kernels, shards(): kernel_call(functools.partial(project_body, (0, *distances), steps, kv_he...  1.57 us
    pallas_call x1, Pallas kernels, shards(): kernel_call(functools.partial(attend_body, head_dim ** (-0.5)), 'attend',...  1.51 us
    pallas_call x1, Pallas kernels, shards(): kernel_call(functools.partial(select_body, chunk, steps, pool, block, per...  1.43 us
    pallas_call x1, Pallas kernels, shards(): kernel_call(functools.partial(output_body, kv_heads, steps, min(512, out_...  1.32 us
    pallas_call x1, Pallas kernels, shards(): kernel_call(norm_body, 'norm', jax.ShapeDtypeStruct((chunk, feature_cols)...  1.17 us
  transfers between devices with their start and end apart: 10, of which 8 were waited for; matrix products, arithmetic and copies ran while one was open for 0% of the time, Pallas kernels for 4%

profile of v3, /device:TPU:0, one launch (start us, length us, event | category | flops | bytes accessed | tf_op | source)
XLA Modules:
  0.0 35.0 jit_solution(11315174240070081440)
XLA Ops:
  0.0 1.2 %norm.1.refs_0_ = bf16[4,2048]{1,0:T(4,128)(2,1)S(1)} custom-call(bf16[4,8192]{1,0:T(4,128)(2,1)} %hidden_hbm.1, bf16[2048]{0:T(1024)(128)(2,1)} %gain_hbm.1), custom_call_target="tpu_custom_call" | custom-call | flops 10000000000 | bytes 1024 | tf_op jit(solution)/shard_map/norm/pallas_call | solution.py:392
  1.2 4.1 %collective-permute-start = (bf16[4,2048]{1,0:T(4,128)(2,1)S(1)}, bf16[4,2048]{1,0:T(4,128)(2,1)S(1)}, u32[]{:S(2)}, u32[]{:S(2)}) collective-permute-start(bf16[4,2048]{1,0:T(4,128)(2,1)S(1)} %norm.1.refs_0_), channel_id=1, source_target_pairs={{0,2},{1,3},{2,0},{3,1},{4,6},{5,7},{6,4},{7,5},{8,10},{9,11},{10,... | collective-permute-start | bytes 49160 | tf_op jit(solution)/shard_map/ppermute | solution.py:20
  5.3 1.3 %collective-permute-start.1 = (bf16[4,2048]{1,0:T(4,128)(2,1)S(1)}, bf16[4,2048]{1,0:T(4,128)(2,1)S(1)}, u32[]{:S(2)}, u32[]{:S(2)}) collective-permute-start(bf16[4,2048]{1,0:T(4,128)(2,1)S(1)} %norm.1.refs_0_), channel_id=1, source_target_pairs={{0,3},{1,2},{2,1},{3,0},{4,7},{5,6},{6,5},{7,4},{8,11},{9,10},{10,... | collective-permute-start | bytes 49160 | tf_op jit(solution)/shard_map/ppermute | solution.py:20
  6.6 0.2 collective-permute-start.2
  6.9 0.1 collective-permute-done.refs_1_
  7.0 3.8 %collective-permute-done.1.refs_2_ = bf16[4,2048]{1,0:T(4,128)(2,1)S(1)} collective-permute-done((bf16[4,2048]{1,0:T(4,128)(2,1)S(1)}, bf16[4,2048]{1,0:T(4,128)(2,1)S(1)}, u32[]{:S(2)}, u32[]{:S(2)}) %collective-permute-start.1) | collective-permute-done | bytes 16416 | tf_op jit(solution)/shard_map/ppermute | solution.py:20
  10.8 1.6 %project.1.own_ref = f32[320,128]{1,0:T(8,128)S(1)} custom-call(bf16[4,2048]{1,0:T(4,128)(2,1)S(1)} %norm.1.refs_0_, bf16[4,2048]{1,0:T(4,128)(2,1)S(1)} %collective-permute-done.refs_1_, bf16[4,2048]{1,0:T(4,128)(2,1)S(1)} %collective-permute-done.1.refs_2_, bf16[4,2048]{1,0:T(4,128)(2,1)S(1)} %collective-permute-done.2.refs_3_, ...), custom_call_target="tpu_custom_call" | custom-call | flops 167772160 | bytes 1024 | tf_op jit(solution)/shard_map/project/pallas_call | solution.py:419
  12.5 1.4 %collective-permute-done.3.other_ref = f32[320,128]{1,0:T(8,128)S(1)} collective-permute-done((f32[320,128]{1,0:T(8,128)S(1)}, f32[320,128]{1,0:T(8,128)S(1)}, u32[]{:S(2)}, u32[]{:S(2)}) %collective-permute-start.3) | collective-permute-done | bytes 163872 | tf_op jit(solution)/shard_map/ppermute | solution.py:20
  14.0 1.6 %collective-permute-start.4 = (f16[320,128]{1,0:T(8,128)(2,1)S(1)}, f16[320,128]{1,0:T(8,128)(2,1)S(1)}, u32[]{:S(2)}, u32[]{:S(2)}) collective-permute-start(f16[320,128]{1,0:T(8,128)(2,1)S(1)} %convert_element_type.9), channel_id=1, source_target_pairs={{0,8},{4,12},{8,0},{12,4},{1,9},{5,13},{9,1},{13,5},{2,10},{6,14},... | collective-permute-start | bytes 245768 | tf_op jit(solution)/shard_map/ppermute | solution.py:20
  15.5 1.4 %select.1 = (s32[99]{0:T(128)S(4)}, f32[256,128]{1,0:T(8,128)S(1)}) custom-call(s32[8,24]{1,0:T(8,128)S(1)} %copy-done.5, s32[8,8]{1,0:T(8,128)S(1)} %copy-done.6, s32[8]{0:T(128)S(1)} %copy-done.7), custom_call_target="tpu_custom_call" | custom-call | flops 10000000000 | bytes 1024 | tf_op jit(solution)/shard_map/select/pallas_call | solution.py:405
  17.0 1.6 %collective-permute-done.4 = f16[320,128]{1,0:T(8,128)(2,1)S(1)} collective-permute-done((f16[320,128]{1,0:T(8,128)(2,1)S(1)}, f16[320,128]{1,0:T(8,128)(2,1)S(1)}, u32[]{:S(2)}, u32[]{:S(2)}) %collective-permute-start.4) | collective-permute-done | bytes 81952 | tf_op jit(solution)/shard_map/ppermute | solution.py:20
  18.6 1.5 %attend.1.own_ref = f32[264,128]{1,0:T(8,128)S(1)} custom-call(s32[99]{0:T(128)S(4)} %get-tuple-element.13.chosen_ref, f32[256,128]{1,0:T(8,128)S(1)} %get-tuple-element.14.seen_ref, f32[320,128]{1,0:T(8,128)S(1)} %add.16.own_ref, f32[320,128]{1,0:T(8,128)S(1)} %convert_element_type.10.other_ref, bf16[48,2,128,128]{3,2,1,0:T(8,128)(2,1)S(1)} %copy-done.3, ...), custom_call_target="tpu_custom_call" | custom-call | flops 10000000000 | bytes 1024 | tf_op jit(solution)/shard_map/attend/pallas_call | solution.py:442
  20.1 0.1 collective-permute-start.5
  20.2 1.3 %collective-permute-done.5.other_ref = f32[264,128]{1,0:T(8,128)S(1)} collective-permute-done((f32[264,128]{1,0:T(8,128)S(1)}, f32[264,128]{1,0:T(8,128)S(1)}, u32[]{:S(2)}, u32[]{:S(2)}) %collective-permute-start.5) | collective-permute-done | bytes 135200 | tf_op jit(solution)/shard_map/ppermute | solution.py:20
  21.5 0.2 combine.1
  21.7 1.6 %collective-permute-start.6 = (bf16[272,128]{1,0:T(8,128)(2,1)S(1)}, bf16[272,128]{1,0:T(8,128)(2,1)S(1)}, u32[]{:S(2)}, u32[]{:S(2)}) collective-permute-start(bf16[272,128]{1,0:T(8,128)(2,1)S(1)} %get-tuple-element.16), channel_id=1, source_target_pairs={{0,8},{4,12},{8,0},{12,4},{1,9},{5,13},{9,1},{13,5},{2,10},{6,14},... | collective-permute-start | bytes 208904 | tf_op jit(solution)/shard_map/ppermute | solution.py:20
  23.2 2.8 %collective-permute-done.6.other_ref = bf16[272,128]{1,0:T(8,128)(2,1)S(1)} collective-permute-done((bf16[272,128]{1,0:T(8,128)(2,1)S(1)}, bf16[272,128]{1,0:T(8,128)(2,1)S(1)}, u32[]{:S(2)}, u32[]{:S(2)}) %collective-permute-start.6) | collective-permute-done | bytes 69664 | tf_op jit(solution)/shard_map/ppermute | solution.py:20
  26.1 1.3 %output.1 = (f32[4,2048]{1,0:T(4,128)S(1)}, f32[4,2048]{1,0:T(4,128)S(1)}, f32[4,2048]{1,0:T(4,128)S(1)}, f32[4,2048]{1,0:T(4,128)S(1)}) custom-call(f32[264,128]{1,0:T(8,128)S(1)} %get-tuple-element.15.own_ref, bf16[272,128]{1,0:T(8,128)(2,1)S(1)} %collective-permute-done.6.other_ref, bf16[2048,2048]{1,0:T(8,128)(2,1)S(1)} %bitcast.1), custom_call_target="tpu_custom_call" | custom-call | flops 134217728 | bytes 1024 | tf_op jit(solution)/shard_map/output/pallas_call | solution.py:472
  27.4 1.2 %collective-permute-start.7 = (f32[4,2048]{1,0:T(4,128)S(1)}, f32[4,2048]{1,0:T(4,128)S(1)}, u32[]{:S(2)}, u32[]{:S(2)}) collective-permute-start(f32[4,2048]{1,0:T(4,128)S(1)} %get-tuple-element.18), channel_id=1, source_target_pairs={{0,2},{1,3},{2,0},{3,1},{4,6},{5,7},{6,4},{7,5},{8,10},{9,11},{10,... | collective-permute-start | bytes 98312 | tf_op jit(solution)/shard_map/ppermute | solution.py:20
  28.6 0.9 %collective-permute-start.8 = (f32[4,2048]{1,0:T(4,128)S(1)}, f32[4,2048]{1,0:T(4,128)S(1)}, u32[]{:S(2)}, u32[]{:S(2)}) collective-permute-start(f32[4,2048]{1,0:T(4,128)S(1)} %get-tuple-element.19), channel_id=1, source_target_pairs={{0,3},{1,2},{2,1},{3,0},{4,7},{5,6},{6,5},{7,4},{8,11},{9,10},{10,... | collective-permute-start | bytes 98312 | tf_op jit(solution)/shard_map/ppermute | solution.py:20
  29.5 1.4 %collective-permute-start.9 = (f32[4,2048]{1,0:T(4,128)S(1)}, f32[4,2048]{1,0:T(4,128)S(1)}, u32[]{:S(2)}, u32[]{:S(2)}) collective-permute-start(f32[4,2048]{1,0:T(4,128)S(1)} %get-tuple-element.20), channel_id=1, source_target_pairs={{0,1},{1,0},{2,3},{3,2},{4,5},{5,4},{6,7},{7,6},{8,9},{9,8},{10,11... | collective-permute-start | bytes 98312 | tf_op jit(solution)/shard_map/ppermute | solution.py:20
  30.9 1.5 %collective-permute-done.7 = f32[4,2048]{1,0:T(4,128)S(1)} collective-permute-done((f32[4,2048]{1,0:T(4,128)S(1)}, f32[4,2048]{1,0:T(4,128)S(1)}, u32[]{:S(2)}, u32[]{:S(2)}) %collective-permute-start.7) | collective-permute-done | bytes 32800 | tf_op jit(solution)/shard_map/ppermute | solution.py:20
  32.4 1.9 %collective-permute-done.8 = f32[4,2048]{1,0:T(4,128)S(1)} collective-permute-done((f32[4,2048]{1,0:T(4,128)S(1)}, f32[4,2048]{1,0:T(4,128)S(1)}, u32[]{:S(2)}, u32[]{:S(2)}) %collective-permute-start.8) | collective-permute-done | bytes 32800 | tf_op jit(solution)/shard_map/ppermute | solution.py:20
  34.3 0.6 %add_convert_fusion = bf16[4,2048]{1,0:T(4,128)(2,1)} fusion(f32[4,2048]{1,0:T(4,128)S(1)} %collective-permute-done.9, f32[4,2048]{1,0:T(4,128)S(1)} %collective-permute-done.8, f32[4,2048]{1,0:T(4,128)S(1)} %get-tuple-element.17, f32[4,2048]{1,0:T(4,128)S(1)} %collective-permute-done.7), kind=kLoop, calls=%fused_computation | loop fusion | flops 32768 | bytes 147456 | tf_op jit(solution)/shard_map/convert_element_type | solution.py:484
  (27 shorter events, 0.2 us)
Async XLA Ops:
  0.0 10.8 %copy-start = (bf16[2048,2048]{1,0:T(8,128)(2,1)S(1)}, bf16[2048,2048]{1,0:T(8,128)(2,1)}, u32[]{:S(2)}) copy-start(bf16[2048,2048]{1,0:T(8,128)(2,1)} %refs_4_.1) | copy-start | bytes 25165828
  0.0 10.8 %copy-start.1 = (bf16[2048,256]{1,0:T(8,128)(2,1)S(1)}, bf16[2048,256]{1,0:T(8,128)(2,1)}, u32[]{:S(2)}) copy-start(bf16[2048,256]{1,0:T(8,128)(2,1)} %refs_5_.1) | copy-start | bytes 3145732
  0.0 10.8 %copy-start.2 = (bf16[2048,256]{1,0:T(8,128)(2,1)S(1)}, bf16[2048,256]{1,0:T(8,128)(2,1)}, u32[]{:S(2)}) copy-start(bf16[2048,256]{1,0:T(8,128)(2,1)} %refs_6_.1) | copy-start | bytes 3145732
  1.2 5.8 %collective-permute-start = (bf16[4,2048]{1,0:T(4,128)(2,1)S(1)}, bf16[4,2048]{1,0:T(4,128)(2,1)S(1)}, u32[]{:S(2)}, u32[]{:S(2)}) collective-permute-start(bf16[4,2048]{1,0:T(4,128)(2,1)S(1)} %norm.1.refs_0_), channel_id=1, source_target_pairs={{0,2},{1,3},{2,0},{3,1},{4,6},{5,7},{6,4},{7,5},{8,10},{9,11},{10,... | collective-permute-start | bytes 49160 | tf_op jit(solution)/shard_map/ppermute | solution.py:20
  5.3 5.5 %collective-permute-start.1 = (bf16[4,2048]{1,0:T(4,128)(2,1)S(1)}, bf16[4,2048]{1,0:T(4,128)(2,1)S(1)}, u32[]{:S(2)}, u32[]{:S(2)}) collective-permute-start(bf16[4,2048]{1,0:T(4,128)(2,1)S(1)} %norm.1.refs_0_), channel_id=1, source_target_pairs={{0,3},{1,2},{2,1},{3,0},{4,7},{5,6},{6,5},{7,4},{8,11},{9,10},{10,... | collective-permute-start | bytes 49160 | tf_op jit(solution)/shard_map/ppermute | solution.py:20
  6.6 4.2 %collective-permute-start.2 = (bf16[4,2048]{1,0:T(4,128)(2,1)S(1)}, bf16[4,2048]{1,0:T(4,128)(2,1)S(1)}, u32[]{:S(2)}, u32[]{:S(2)}) collective-permute-start(bf16[4,2048]{1,0:T(4,128)(2,1)S(1)} %norm.1.refs_0_), channel_id=1, source_target_pairs={{0,1},{1,0},{2,3},{3,2},{4,5},{5,4},{6,7},{7,6},{8,9},{9,8},{10,11... | collective-permute-start | bytes 49160 | tf_op jit(solution)/shard_map/ppermute | solution.py:20
  12.4 3.1 %copy-start.5 = (s32[8,24]{1,0:T(8,128)S(1)}, s32[8,24]{1,0:T(8,128)}, u32[]{:S(2)}) copy-start(s32[8,24]{1,0:T(8,128)} %table_ref.1) | copy-start | bytes 2308
  12.4 3.1 %copy-start.6 = (s32[8,8]{1,0:T(8,128)S(1)}, s32[8,8]{1,0:T(8,128)}, u32[]{:S(2)}) copy-start(s32[8,8]{1,0:T(8,128)} %list_ref.1) | copy-start | bytes 772
  12.4 3.1 %copy-start.7 = (s32[8]{0:T(128)S(1)}, s32[8]{0:T(128)}, u32[]{:S(2)}) copy-start(s32[8]{0:T(128)} %lengths_ref.1) | copy-start | bytes 100
  12.4 1.5 %collective-permute-start.3 = (f32[320,128]{1,0:T(8,128)S(1)}, f32[320,128]{1,0:T(8,128)S(1)}, u32[]{:S(2)}, u32[]{:S(2)}) collective-permute-start(f32[320,128]{1,0:T(8,128)S(1)} %project.1.own_ref), channel_id=1, source_target_pairs={{0,4},{4,0},{8,12},{12,8},{1,5},{5,1},{9,13},{13,9},{2,6},{6,2},{1... | collective-permute-start | bytes 491528 | tf_op jit(solution)/shard_map/ppermute | solution.py:20
  13.9 4.6 %copy-start.3 = (bf16[48,2,128,128]{3,2,1,0:T(8,128)(2,1)S(1)}, bf16[48,2,128,128]{3,2,1,0:T(8,128)(2,1)}, u32[]{:S(2)}) copy-start(bf16[48,2,128,128]{3,2,1,0:T(8,128)(2,1)} %key_ref.1) | copy-start | bytes 9437188
  14.0 4.6 %copy-start.4 = (bf16[48,2,128,128]{3,2,1,0:T(8,128)(2,1)S(1)}, bf16[48,2,128,128]{3,2,1,0:T(8,128)(2,1)}, u32[]{:S(2)}) copy-start(bf16[48,2,128,128]{3,2,1,0:T(8,128)(2,1)} %value_ref.1) | copy-start | bytes 9437188
  14.0 4.6 %collective-permute-start.4 = (f16[320,128]{1,0:T(8,128)(2,1)S(1)}, f16[320,128]{1,0:T(8,128)(2,1)S(1)}, u32[]{:S(2)}, u32[]{:S(2)}) collective-permute-start(f16[320,128]{1,0:T(8,128)(2,1)S(1)} %convert_element_type.9), channel_id=1, source_target_pairs={{0,8},{4,12},{8,0},{12,4},{1,9},{5,13},{9,1},{13,5},{2,10},{6,14},... | collective-permute-start | bytes 245768 | tf_op jit(solution)/shard_map/ppermute | solution.py:20
  18.6 7.5 %slice-start = ((s8[8388608]{0:T(1024)(128)(4,1)}), s8[4194304]{0:T(1024)(128)(4,1)S(1)}, s32[]{:S(2)}) async-start(s8[8388608]{0:T(1024)(128)(4,1)} %bitcast), calls=%async_computation | async-start | bytes 8388608
  20.1 6.0 %slice-start.1 = ((s8[8388608]{0:T(1024)(128)(4,1)}), s8[4194304]{0:T(1024)(128)(4,1)S(1)}, s32[]{:S(2)}) async-start(s8[8388608]{0:T(1024)(128)(4,1)} %bitcast), calls=%async_computation.1 | async-start | bytes 8388608
  20.1 1.4 %collective-permute-start.5 = (f32[264,128]{1,0:T(8,128)S(1)}, f32[264,128]{1,0:T(8,128)S(1)}, u32[]{:S(2)}, u32[]{:S(2)}) collective-permute-start(f32[264,128]{1,0:T(8,128)S(1)} %attend.1.own_ref), channel_id=1, source_target_pairs={{0,4},{4,0},{8,12},{12,8},{1,5},{5,1},{9,13},{13,9},{2,6},{6,2},{1... | collective-permute-start | bytes 405512 | tf_op jit(solution)/shard_map/ppermute | solution.py:20
  21.7 4.4 %collective-permute-start.6 = (bf16[272,128]{1,0:T(8,128)(2,1)S(1)}, bf16[272,128]{1,0:T(8,128)(2,1)S(1)}, u32[]{:S(2)}, u32[]{:S(2)}) collective-permute-start(bf16[272,128]{1,0:T(8,128)(2,1)S(1)} %get-tuple-element.16), channel_id=1, source_target_pairs={{0,8},{4,12},{8,0},{12,4},{1,9},{5,13},{9,1},{13,5},{2,10},{6,14},... | collective-permute-start | bytes 208904 | tf_op jit(solution)/shard_map/ppermute | solution.py:20
  27.4 5.0 %collective-permute-start.7 = (f32[4,2048]{1,0:T(4,128)S(1)}, f32[4,2048]{1,0:T(4,128)S(1)}, u32[]{:S(2)}, u32[]{:S(2)}) collective-permute-start(f32[4,2048]{1,0:T(4,128)S(1)} %get-tuple-element.18), channel_id=1, source_target_pairs={{0,2},{1,3},{2,0},{3,1},{4,6},{5,7},{6,4},{7,5},{8,10},{9,11},{10,... | collective-permute-start | bytes 98312 | tf_op jit(solution)/shard_map/ppermute | solution.py:20
  28.6 5.7 %collective-permute-start.8 = (f32[4,2048]{1,0:T(4,128)S(1)}, f32[4,2048]{1,0:T(4,128)S(1)}, u32[]{:S(2)}, u32[]{:S(2)}) collective-permute-start(f32[4,2048]{1,0:T(4,128)S(1)} %get-tuple-element.19), channel_id=1, source_target_pairs={{0,3},{1,2},{2,1},{3,0},{4,7},{5,6},{6,5},{7,4},{8,11},{9,10},{10,... | collective-permute-start | bytes 98312 | tf_op jit(solution)/shard_map/ppermute | solution.py:20
  29.5 4.8 %collective-permute-start.9 = (f32[4,2048]{1,0:T(4,128)S(1)}, f32[4,2048]{1,0:T(4,128)S(1)}, u32[]{:S(2)}, u32[]{:S(2)}) collective-permute-start(f32[4,2048]{1,0:T(4,128)S(1)} %get-tuple-element.20), channel_id=1, source_target_pairs={{0,1},{1,0},{2,3},{3,2},{4,5},{5,4},{6,7},{7,6},{8,9},{9,8},{10,11... | collective-permute-start | bytes 98312 | tf_op jit(solution)/shard_map/ppermute | solution.py:20

commit v4 on v3

--- a/solution.py
+++ b/solution.py
@@ -18,6 +18,17 @@
 def swap(array, axis, distance):
     count = lax.axis_size(axis)
     return lax.ppermute(array, axis, [(i, i ^ distance) for i in range(count)])
+
+
+def crossing(distance):
+    return distance if distance == 1 else distance + 1
+
+
+def swap_across(array, distance):
+    heads = lax.axis_size("heads")
+    count = lax.axis_size("mem") * heads
+    pairs = [(i, i ^ heads ^ distance) for i in range(count)]
+    return lax.ppermute(array, ("mem", "heads"), pairs)
 
 
 def kernel_call(body, name, outs, ins, vmem_mib, flops, scratch=(), out_space=IN_VMEM):
@@ -33,23 +44,22 @@
     )
 
 
-def norm_body(hidden_hbm, gain_hbm, out_ref, hidden_ref, gain_ref, sems):
-    copies = [
-        pltpu.make_async_copy(hidden_hbm, hidden_ref, sems.at[0]),
-        pltpu.make_async_copy(gain_hbm, gain_ref, sems.at[1]),
-    ]
-    for copy in copies:
-        copy.start()
-    for copy in copies:
-        copy.wait()
-    cols = gain_ref.shape[0]
-    start = pl.multiple_of(lax.axis_index("mem") * cols, cols)
+def norm_body(hidden_hbm, own_ref, mate_ref, hidden_ref, sem):
+    copy = pltpu.make_async_copy(hidden_hbm, hidden_ref, sem)
+    copy.start()
+    copy.wait()
+    cols = own_ref.shape[1] - LANES
+    mem = lax.axis_index("mem")
     hidden = hidden_ref[...].astype(jnp.float32)
-    mean_sq = jnp.mean(hidden * hidden, axis=-1, keepdims=True)
-    own = hidden_ref[:, pl.ds(start, cols)].astype(jnp.float32)
-    gain = gain_ref[...].astype(jnp.float32).reshape(1, cols)
-    normed = own * lax.rsqrt(mean_sq + EPSILON) * gain
-    out_ref[...] = normed.astype(jnp.bfloat16)
+    factor = lax.rsqrt(jnp.mean(hidden * hidden, axis=-1, keepdims=True) + EPSILON)
+    lane = lax.broadcasted_iota(jnp.int32, (hidden.shape[0], LANES), 1)
+    tail = jnp.zeros((hidden.shape[0], LANES), jnp.float32)
+    for i, piece in enumerate(to_pieces(factor)):
+        tail = jnp.where(lane == i, piece.astype(jnp.float32), tail)
+    for ref, index in ((own_ref, mem), (mate_ref, lax.bitwise_xor(mem, 1))):
+        start = pl.multiple_of(index * cols, cols)
+        ref[:, :cols] = hidden_ref[:, pl.ds(start, cols)]
+        ref[:, cols:] = tail.astype(ref.dtype)
 
 
 def select_body(
@@ -99,9 +109,13 @@
 
 
 def project_body(places, steps, kv_heads, tile, *refs):
-    q_ref, k_ref, v_ref, out_ref = refs[len(places) :]
+    gain_ref, q_ref, k_ref, v_ref, out_ref = refs[len(places) :]
     chunks = [refs[places.index(i)][...].astype(jnp.float32) for i in range(len(places))]
-    rows = jnp.concatenate(chunks, axis=0).astype(jnp.bfloat16)
+    rows = jnp.concatenate(chunks, axis=0)
+    cols = gain_ref.shape[0]
+    factor = from_pieces([rows[:, cols + i : cols + i + 1] for i in range(3)])
+    gain = gain_ref[...].astype(jnp.float32).reshape(1, cols)
+    rows = (rows[:, :cols] * factor * gain).astype(jnp.bfloat16)
     tokens = rows.shape[0]
     row_count = tokens // steps
     to = lax.broadcasted_iota(jnp.int32, (tokens, tokens), 0)
@@ -389,18 +403,17 @@
     height = groups * query_count
     f32, bf16 = jnp.float32, jnp.bfloat16
 
-    normed = kernel_call(
+    own, mate = kernel_call(
         norm_body,
         "norm",
-        jax.ShapeDtypeStruct((chunk, feature_cols), bf16),
-        [pl.BlockSpec(memory_space=pltpu.HBM)] * 2,
+        [jax.ShapeDtypeStruct((chunk, feature_cols + LANES), bf16)] * 2,
+        [pl.BlockSpec(memory_space=pltpu.HBM)],
         2,
         1e10,
-        [pltpu.VMEM(hidden.shape, bf16), pltpu.VMEM(norm_gain.shape, bf16)]
-        + [pltpu.SemaphoreType.DMA((2,))],
-    )(*[pltpu.with_memory_space_constraint(a, pltpu.HBM) for a in (hidden, norm_gain)])
+        [pltpu.VMEM(hidden.shape, bf16), pltpu.SemaphoreType.DMA],
+    )(pltpu.with_memory_space_constraint(hidden, pltpu.HBM))
     distances = [*range(2, head_count), 1]
-    pieces = [normed] + [swap(normed, "heads", d) for d in distances]
+    pieces = [own] + [swap_across(mate, d) for d in distances]
 
     chosen = kernel_call(
         functools.partial(select_body, chunk, steps, pool, block, per_kv),
@@ -420,10 +433,10 @@
         functools.partial(project_body, (0, *distances), steps, kv_heads, 512),
         "project",
         jax.ShapeDtypeStruct((width // LANES * token_count, LANES), f32),
-        [IN_VMEM] * (head_count + 3),
+        [IN_VMEM] * (head_count + 4),
         4,
         2 * token_count * feature_cols * width,
-    )(*pieces, q_weight, k_weight, v_weight)
+    )(*pieces, norm_gain, q_weight, k_weight, v_weight)
     sent = summed
     distance = 1
     while 2 * distance < mem_count:
@@ -434,7 +447,7 @@
             [IN_VMEM] * 2,
             2,
             1e10,
-        )(summed, swap(sent, "mem", distance))
+        )(summed, swap(sent, "mem", crossing(distance)))
         summed, sent = added[0], added[-1]
         distance *= 2
 
@@ -448,7 +461,7 @@
         1e10,
         [pltpu.VMEM((row_count, *state), bf16), pltpu.VMEM((capacity, *state), f32)]
         + [pltpu.VMEM((row_count + 1, *state), f32)] * 6,
-    )(pltpu.with_memory_space_constraint(chosen[0], pltpu.SMEM), chosen[1], summed, swap(sent.astype(jnp.float16), "mem", distance).astype(f32), k_cache, v_cache)
+    )(pltpu.with_memory_space_constraint(chosen[0], pltpu.SMEM), chosen[1], summed, swap(sent.astype(jnp.float16), "mem", crossing(distance)).astype(f32), k_cache, v_cache)
 
     sent = partial
     distance = 1
@@ -464,7 +477,7 @@
             [IN_VMEM] * 2,
             2,
             1e10,
-        )(partial, swap(sent, "mem", distance))
+        )(partial, swap(sent, "mem", crossing(distance)))
         partial, sent = merged[0], merged[-1]
         distance *= 2
 
@@ -477,7 +490,7 @@
         4,
         2 * token_count * query_cols * out_cols,
         [pltpu.VMEM((query_cols // LANES * token_count, LANES), f32)],
-    )(partial, swap(sent, "mem", distance), o_weight)
+    )(partial, swap(sent, "mem", crossing(distance)), o_weight)
     total = projected[0]
     for d in distances:
         total = total + swap(projected[d], "heads", d)

time: 35.1 us -> 34.4 us (0.980)
  waiting for transfers between devices: 14.5 us -> 13 us
  starting transfers between devices: 12.4 us -> 13 us
    ppermute x0 -> x3, starting transfers between devices: none -> 5.41 us  [swap_across(): return lax.ppermute(array, ('mem', 'heads'), pairs)]
    ppermute x10 -> x7, starting transfers between devices: 12.4 us -> 7.61 us  [swap(): return lax.ppermute(array, axis, [(i, i ^ distance) for i in range(count)])]
    ppermute x10 -> x7, waiting for transfers between devices: 14.5 us -> 9.91 us  [swap(): return lax.ppermute(array, axis, [(i, i ^ distance) for i in range(count)])]
    ppermute x0 -> x3, waiting for transfers between devices: none -> 3.13 us  [swap_across(): return lax.ppermute(array, ('mem', 'heads'), pairs)]
  transfers between devices with their start and end apart: 10 -> 10, of which waited for: 8 -> 7; matrix products, arithmetic and copies ran while one was open for 0% -> 0% of each run, Pallas kernels for 4% -> 4%
where the time goes in v4:
time: 34.4 us; the launch traced here: 34.2 us
  starting transfers between devices  13 us (38%)
  waiting for transfers between devices  13 us (38%)
  Pallas kernels  7.31 us (21%)
  other arithmetic  0.65 us (2%)
    ppermute x7, waiting for transfers between devices, swap(): return lax.ppermute(array, axis, [(i, i ^ distance) for i in range(count)])  9.91 us
    ppermute x7, starting transfers between devices, swap(): return lax.ppermute(array, axis, [(i, i ^ distance) for i in range(count)])  7.61 us
    ppermute x3, starting transfers between devices, swap_across(): return lax.ppermute(array, ('mem', 'heads'), pairs)  5.41 us
    ppermute x3, waiting for transfers between devices, swap_across(): return lax.ppermute(array, ('mem', 'heads'), pairs)  3.13 us
    pallas_call x1, Pallas kernels, shards(): kernel_call(functools.partial(project_body, (0, *distances), steps, kv_he...  1.72 us
    pallas_call x1, Pallas kernels, shards(): kernel_call(functools.partial(attend_body, head_dim ** (-0.5)), 'attend',...  1.51 us
    pallas_call x1, Pallas kernels, shards(): kernel_call(functools.partial(select_body, chunk, steps, pool, block, per...  1.43 us
    pallas_call x1, Pallas kernels, shards(): kernel_call(functools.partial(output_body, kv_heads, steps, min(512, out_...  1.32 us
  transfers between devices with their start and end apart: 10, of which 7 were waited for; matrix products, arithmetic and copies ran while one was open for 0% of the time, Pallas kernels for 4%

profile of v4, /device:TPU:0, one launch (start us, length us, event | category | flops | bytes accessed | tf_op | source)
XLA Modules:
  0.0 34.2 jit_solution(7795981582703527320)
XLA Ops:
  0.0 1.2 %norm.1 = (bf16[4,2176]{1,0:T(4,128)(2,1)S(1)}, bf16[4,2176]{1,0:T(4,128)(2,1)S(1)}) custom-call(bf16[4,8192]{1,0:T(4,128)(2,1)} %hidden_hbm.1), custom_call_target="tpu_custom_call" | custom-call | flops 10000000000 | bytes 1024 | tf_op jit(solution)/shard_map/norm/pallas_call | solution.py:406
  1.2 3.6 %collective-permute-start = (bf16[4,2176]{1,0:T(4,128)(2,1)S(1)}, bf16[4,2176]{1,0:T(4,128)(2,1)S(1)}, u32[]{:S(2)}, u32[]{:S(2)}) collective-permute-start(bf16[4,2176]{1,0:T(4,128)(2,1)S(1)} %get-tuple-element.18), channel_id=1, source_target_pairs={{0,6},{1,7},{2,4},{3,5},{4,2},{5,3},{6,0},{7,1},{8,14},{9,15},{10,... | collective-permute-start | bytes 52232 | tf_op jit(solution)/shard_map/ppermute | solution.py:31
  4.7 1.6 %collective-permute-start.1 = (bf16[4,2176]{1,0:T(4,128)(2,1)S(1)}, bf16[4,2176]{1,0:T(4,128)(2,1)S(1)}, u32[]{:S(2)}, u32[]{:S(2)}) collective-permute-start(bf16[4,2176]{1,0:T(4,128)(2,1)S(1)} %get-tuple-element.18), channel_id=1, source_target_pairs={{0,7},{1,6},{2,5},{3,4},{4,3},{5,2},{6,1},{7,0},{8,15},{9,14},{10,... | collective-permute-start | bytes 52232 | tf_op jit(solution)/shard_map/ppermute | solution.py:31
  6.4 0.2 collective-permute-start.2
  6.6 3.1 %collective-permute-done.1.refs_2_ = bf16[4,2176]{1,0:T(4,128)(2,1)S(1)} collective-permute-done((bf16[4,2176]{1,0:T(4,128)(2,1)S(1)}, bf16[4,2176]{1,0:T(4,128)(2,1)S(1)}, u32[]{:S(2)}, u32[]{:S(2)}) %collective-permute-start.1) | collective-permute-done | bytes 17440 | tf_op jit(solution)/shard_map/ppermute | solution.py:31
  9.8 1.7 %project.1.own_ref = f32[320,128]{1,0:T(8,128)S(1)} custom-call(bf16[4,2176]{1,0:T(4,128)(2,1)S(1)} %get-tuple-element.17.refs_0_, bf16[4,2176]{1,0:T(4,128)(2,1)S(1)} %collective-permute-done.refs_1_, bf16[4,2176]{1,0:T(4,128)(2,1)S(1)} %collective-permute-done.1.refs_2_, bf16[4,2176]{1,0:T(4,128)(2,1)S(1)} %collective-permute-done.2.refs_3_, ...), custom_call_target="tpu_custom_call" | custom-call | flops 167772160 | bytes 1024 | tf_op jit(solution)/shard_map/project/pallas_call | solution.py:432
  11.5 0.8 %collective-permute-start.3 = (f32[320,128]{1,0:T(8,128)S(1)}, f32[320,128]{1,0:T(8,128)S(1)}, u32[]{:S(2)}, u32[]{:S(2)}) collective-permute-start(f32[320,128]{1,0:T(8,128)S(1)} %project.1.own_ref), channel_id=1, source_target_pairs={{0,4},{4,0},{8,12},{12,8},{1,5},{5,1},{9,13},{13,9},{2,6},{6,2},{1... | collective-permute-start | bytes 491528 | tf_op jit(solution)/shard_map/ppermute | solution.py:20
  12.3 1.0 %collective-permute-done.3.other_ref = f32[320,128]{1,0:T(8,128)S(1)} collective-permute-done((f32[320,128]{1,0:T(8,128)S(1)}, f32[320,128]{1,0:T(8,128)S(1)}, u32[]{:S(2)}, u32[]{:S(2)}) %collective-permute-start.3) | collective-permute-done | bytes 163872 | tf_op jit(solution)/shard_map/ppermute | solution.py:20
  13.4 1.5 %collective-permute-start.4 = (f16[320,128]{1,0:T(8,128)(2,1)S(1)}, f16[320,128]{1,0:T(8,128)(2,1)S(1)}, u32[]{:S(2)}, u32[]{:S(2)}) collective-permute-start(f16[320,128]{1,0:T(8,128)(2,1)S(1)} %convert_element_type.9), channel_id=1, source_target_pairs={{0,12},{4,8},{8,4},{12,0},{1,13},{5,9},{9,5},{13,1},{2,14},{6,10},... | collective-permute-start | bytes 245768 | tf_op jit(solution)/shard_map/ppermute | solution.py:20
  14.9 1.4 %select.1 = (s32[99]{0:T(128)S(4)}, f32[256,128]{1,0:T(8,128)S(1)}) custom-call(s32[8,24]{1,0:T(8,128)S(1)} %copy-done.6, s32[8,8]{1,0:T(8,128)S(1)} %copy-done.7, s32[8]{0:T(128)S(1)} %copy-done.8), custom_call_target="tpu_custom_call" | custom-call | flops 10000000000 | bytes 1024 | tf_op jit(solution)/shard_map/select/pallas_call | solution.py:418
  16.4 1.4 %collective-permute-done.4 = f16[320,128]{1,0:T(8,128)(2,1)S(1)} collective-permute-done((f16[320,128]{1,0:T(8,128)(2,1)S(1)}, f16[320,128]{1,0:T(8,128)(2,1)S(1)}, u32[]{:S(2)}, u32[]{:S(2)}) %collective-permute-start.4) | collective-permute-done | bytes 81952 | tf_op jit(solution)/shard_map/ppermute | solution.py:20
  17.8 1.5 %attend.1.own_ref = f32[264,128]{1,0:T(8,128)S(1)} custom-call(s32[99]{0:T(128)S(4)} %get-tuple-element.15.chosen_ref, f32[256,128]{1,0:T(8,128)S(1)} %get-tuple-element.16.seen_ref, f32[320,128]{1,0:T(8,128)S(1)} %add.16.own_ref, f32[320,128]{1,0:T(8,128)S(1)} %convert_element_type.10.other_ref, bf16[48,2,128,128]{3,2,1,0:T(8,128)(2,1)S(1)} %copy-done.4, ...), custom_call_target="tpu_custom_call" | custom-call | flops 10000000000 | bytes 1024 | tf_op jit(solution)/shard_map/attend/pallas_call | solution.py:455
  19.3 0.3 collective-permute-start.5
  19.7 1.1 %collective-permute-done.5.other_ref = f32[264,128]{1,0:T(8,128)S(1)} collective-permute-done((f32[264,128]{1,0:T(8,128)S(1)}, f32[264,128]{1,0:T(8,128)S(1)}, u32[]{:S(2)}, u32[]{:S(2)}) %collective-permute-start.5) | collective-permute-done | bytes 135200 | tf_op jit(solution)/shard_map/ppermute | solution.py:20
  20.7 0.2 combine.1
  20.9 1.4 %collective-permute-start.6 = (bf16[272,128]{1,0:T(8,128)(2,1)S(1)}, bf16[272,128]{1,0:T(8,128)(2,1)S(1)}, u32[]{:S(2)}, u32[]{:S(2)}) collective-permute-start(bf16[272,128]{1,0:T(8,128)(2,1)S(1)} %get-tuple-element.20), channel_id=1, source_target_pairs={{0,12},{4,8},{8,4},{12,0},{1,13},{5,9},{9,5},{13,1},{2,14},{6,10},... | collective-permute-start | bytes 208904 | tf_op jit(solution)/shard_map/ppermute | solution.py:20
  22.4 2.7 %collective-permute-done.6.other_ref = bf16[272,128]{1,0:T(8,128)(2,1)S(1)} collective-permute-done((bf16[272,128]{1,0:T(8,128)(2,1)S(1)}, bf16[272,128]{1,0:T(8,128)(2,1)S(1)}, u32[]{:S(2)}, u32[]{:S(2)}) %collective-permute-start.6) | collective-permute-done | bytes 69664 | tf_op jit(solution)/shard_map/ppermute | solution.py:20
  25.1 1.3 %output.1 = (f32[4,2048]{1,0:T(4,128)S(1)}, f32[4,2048]{1,0:T(4,128)S(1)}, f32[4,2048]{1,0:T(4,128)S(1)}, f32[4,2048]{1,0:T(4,128)S(1)}) custom-call(f32[264,128]{1,0:T(8,128)S(1)} %get-tuple-element.19.own_ref, bf16[272,128]{1,0:T(8,128)(2,1)S(1)} %collective-permute-done.6.other_ref, bf16[2048,2048]{1,0:T(8,128)(2,1)S(1)} %bitcast.1), custom_call_target="tpu_custom_call" | custom-call | flops 134217728 | bytes 1024 | tf_op jit(solution)/shard_map/output/pallas_call | solution.py:485
  26.4 1.5 %collective-permute-start.7 = (f32[4,2048]{1,0:T(4,128)S(1)}, f32[4,2048]{1,0:T(4,128)S(1)}, u32[]{:S(2)}, u32[]{:S(2)}) collective-permute-start(f32[4,2048]{1,0:T(4,128)S(1)} %get-tuple-element.22), channel_id=1, source_target_pairs={{0,2},{1,3},{2,0},{3,1},{4,6},{5,7},{6,4},{7,5},{8,10},{9,11},{10,... | collective-permute-start | bytes 98312 | tf_op jit(solution)/shard_map/ppermute | solution.py:20
  27.9 0.9 %collective-permute-start.8 = (f32[4,2048]{1,0:T(4,128)S(1)}, f32[4,2048]{1,0:T(4,128)S(1)}, u32[]{:S(2)}, u32[]{:S(2)}) collective-permute-start(f32[4,2048]{1,0:T(4,128)S(1)} %get-tuple-element.23), channel_id=1, source_target_pairs={{0,3},{1,2},{2,1},{3,0},{4,7},{5,6},{6,5},{7,4},{8,11},{9,10},{10,... | collective-permute-start | bytes 98312 | tf_op jit(solution)/shard_map/ppermute | solution.py:20
  28.8 1.1 %collective-permute-start.9 = (f32[4,2048]{1,0:T(4,128)S(1)}, f32[4,2048]{1,0:T(4,128)S(1)}, u32[]{:S(2)}, u32[]{:S(2)}) collective-permute-start(f32[4,2048]{1,0:T(4,128)S(1)} %get-tuple-element.24), channel_id=1, source_target_pairs={{0,1},{1,0},{2,3},{3,2},{4,5},{5,4},{6,7},{7,6},{8,9},{9,8},{10,11... | collective-permute-start | bytes 98312 | tf_op jit(solution)/shard_map/ppermute | solution.py:20
  29.9 1.3 %collective-permute-done.7 = f32[4,2048]{1,0:T(4,128)S(1)} collective-permute-done((f32[4,2048]{1,0:T(4,128)S(1)}, f32[4,2048]{1,0:T(4,128)S(1)}, u32[]{:S(2)}, u32[]{:S(2)}) %collective-permute-start.7) | collective-permute-done | bytes 32800 | tf_op jit(solution)/shard_map/ppermute | solution.py:20
  31.2 2.4 %collective-permute-done.8 = f32[4,2048]{1,0:T(4,128)S(1)} collective-permute-done((f32[4,2048]{1,0:T(4,128)S(1)}, f32[4,2048]{1,0:T(4,128)S(1)}, u32[]{:S(2)}, u32[]{:S(2)}) %collective-permute-start.8) | collective-permute-done | bytes 32800 | tf_op jit(solution)/shard_map/ppermute | solution.py:20
  33.6 0.6 %add_convert_fusion = bf16[4,2048]{1,0:T(4,128)(2,1)} fusion(f32[4,2048]{1,0:T(4,128)S(1)} %collective-permute-done.9, f32[4,2048]{1,0:T(4,128)S(1)} %collective-permute-done.8, f32[4,2048]{1,0:T(4,128)S(1)} %get-tuple-element.21, f32[4,2048]{1,0:T(4,128)S(1)} %collective-permute-done.7), kind=kLoop, calls=%fused_computation | loop fusion | flops 32768 | bytes 147456 | tf_op jit(solution)/shard_map/convert_element_type | solution.py:497
  (29 shorter events, 0.1 us)
Async XLA Ops:
  0.0 9.7 %copy-start.3 = (bf16[2048]{0:T(1024)(128)(2,1)S(1)}, bf16[2048]{0:T(1024)(128)(2,1)}, u32[]{:S(2)}) copy-start(bf16[2048]{0:T(1024)(128)(2,1)} %refs_4_.1) | copy-start | bytes 12292
  0.0 9.7 %copy-start = (bf16[2048,2048]{1,0:T(8,128)(2,1)S(1)}, bf16[2048,2048]{1,0:T(8,128)(2,1)}, u32[]{:S(2)}) copy-start(bf16[2048,2048]{1,0:T(8,128)(2,1)} %refs_5_.1) | copy-start | bytes 25165828
  0.0 9.7 %copy-start.1 = (bf16[2048,256]{1,0:T(8,128)(2,1)S(1)}, bf16[2048,256]{1,0:T(8,128)(2,1)}, u32[]{:S(2)}) copy-start(bf16[2048,256]{1,0:T(8,128)(2,1)} %refs_6_.1) | copy-start | bytes 3145732
  0.0 9.7 %copy-start.2 = (bf16[2048,256]{1,0:T(8,128)(2,1)S(1)}, bf16[2048,256]{1,0:T(8,128)(2,1)}, u32[]{:S(2)}) copy-start(bf16[2048,256]{1,0:T(8,128)(2,1)} %refs_7_.1) | copy-start | bytes 3145732
  1.2 5.4 %collective-permute-start = (bf16[4,2176]{1,0:T(4,128)(2,1)S(1)}, bf16[4,2176]{1,0:T(4,128)(2,1)S(1)}, u32[]{:S(2)}, u32[]{:S(2)}) collective-permute-start(bf16[4,2176]{1,0:T(4,128)(2,1)S(1)} %get-tuple-element.18), channel_id=1, source_target_pairs={{0,6},{1,7},{2,4},{3,5},{4,2},{5,3},{6,0},{7,1},{8,14},{9,15},{10,... | collective-permute-start | bytes 52232 | tf_op jit(solution)/shard_map/ppermute | solution.py:31
  4.7 5.0 %collective-permute-start.1 = (bf16[4,2176]{1,0:T(4,128)(2,1)S(1)}, bf16[4,2176]{1,0:T(4,128)(2,1)S(1)}, u32[]{:S(2)}, u32[]{:S(2)}) collective-permute-start(bf16[4,2176]{1,0:T(4,128)(2,1)S(1)} %get-tuple-element.18), channel_id=1, source_target_pairs={{0,7},{1,6},{2,5},{3,4},{4,3},{5,2},{6,1},{7,0},{8,15},{9,14},{10,... | collective-permute-start | bytes 52232 | tf_op jit(solution)/shard_map/ppermute | solution.py:31
  6.4 3.4 %collective-permute-start.2 = (bf16[4,2176]{1,0:T(4,128)(2,1)S(1)}, bf16[4,2176]{1,0:T(4,128)(2,1)S(1)}, u32[]{:S(2)}, u32[]{:S(2)}) collective-permute-start(bf16[4,2176]{1,0:T(4,128)(2,1)S(1)} %get-tuple-element.18), channel_id=1, source_target_pairs={{0,5},{1,4},{2,7},{3,6},{4,1},{5,0},{6,3},{7,2},{8,13},{9,12},{10,... | collective-permute-start | bytes 52232 | tf_op jit(solution)/shard_map/ppermute | solution.py:31
  11.5 3.4 %copy-start.6 = (s32[8,24]{1,0:T(8,128)S(1)}, s32[8,24]{1,0:T(8,128)}, u32[]{:S(2)}) copy-start(s32[8,24]{1,0:T(8,128)} %table_ref.1) | copy-start | bytes 2308
  11.5 3.4 %copy-start.7 = (s32[8,8]{1,0:T(8,128)S(1)}, s32[8,8]{1,0:T(8,128)}, u32[]{:S(2)}) copy-start(s32[8,8]{1,0:T(8,128)} %list_ref.1) | copy-start | bytes 772
  11.5 3.4 %copy-start.8 = (s32[8]{0:T(128)S(1)}, s32[8]{0:T(128)}, u32[]{:S(2)}) copy-start(s32[8]{0:T(128)} %lengths_ref.1) | copy-start | bytes 100
  11.5 1.8 %collective-permute-start.3 = (f32[320,128]{1,0:T(8,128)S(1)}, f32[320,128]{1,0:T(8,128)S(1)}, u32[]{:S(2)}, u32[]{:S(2)}) collective-permute-start(f32[320,128]{1,0:T(8,128)S(1)} %project.1.own_ref), channel_id=1, source_target_pairs={{0,4},{4,0},{8,12},{12,8},{1,5},{5,1},{9,13},{13,9},{2,6},{6,2},{1... | collective-permute-start | bytes 491528 | tf_op jit(solution)/shard_map/ppermute | solution.py:20
  13.4 4.4 %copy-start.4 = (bf16[48,2,128,128]{3,2,1,0:T(8,128)(2,1)S(1)}, bf16[48,2,128,128]{3,2,1,0:T(8,128)(2,1)}, u32[]{:S(2)}) copy-start(bf16[48,2,128,128]{3,2,1,0:T(8,128)(2,1)} %key_ref.1) | copy-start | bytes 9437188
  13.4 4.4 %copy-start.5 = (bf16[48,2,128,128]{3,2,1,0:T(8,128)(2,1)S(1)}, bf16[48,2,128,128]{3,2,1,0:T(8,128)(2,1)}, u32[]{:S(2)}) copy-start(bf16[48,2,128,128]{3,2,1,0:T(8,128)(2,1)} %value_ref.1) | copy-start | bytes 9437188
  13.4 4.4 %collective-permute-start.4 = (f16[320,128]{1,0:T(8,128)(2,1)S(1)}, f16[320,128]{1,0:T(8,128)(2,1)S(1)}, u32[]{:S(2)}, u32[]{:S(2)}) collective-permute-start(f16[320,128]{1,0:T(8,128)(2,1)S(1)} %convert_element_type.9), channel_id=1, source_target_pairs={{0,12},{4,8},{8,4},{12,0},{1,13},{5,9},{9,5},{13,1},{2,14},{6,10},... | collective-permute-start | bytes 245768 | tf_op jit(solution)/shard_map/ppermute | solution.py:20
  17.8 7.3 %slice-start = ((s8[8388608]{0:T(1024)(128)(4,1)}), s8[4194304]{0:T(1024)(128)(4,1)S(1)}, s32[]{:S(2)}) async-start(s8[8388608]{0:T(1024)(128)(4,1)} %bitcast), calls=%async_computation | async-start | bytes 8388608
  19.3 5.8 %slice-start.1 = ((s8[8388608]{0:T(1024)(128)(4,1)}), s8[4194304]{0:T(1024)(128)(4,1)S(1)}, s32[]{:S(2)}) async-start(s8[8388608]{0:T(1024)(128)(4,1)} %bitcast), calls=%async_computation.1 | async-start | bytes 8388608
  19.3 1.4 %collective-permute-start.5 = (f32[264,128]{1,0:T(8,128)S(1)}, f32[264,128]{1,0:T(8,128)S(1)}, u32[]{:S(2)}, u32[]{:S(2)}) collective-permute-start(f32[264,128]{1,0:T(8,128)S(1)} %attend.1.own_ref), channel_id=1, source_target_pairs={{0,4},{4,0},{8,12},{12,8},{1,5},{5,1},{9,13},{13,9},{2,6},{6,2},{1... | collective-permute-start | bytes 405512 | tf_op jit(solution)/shard_map/ppermute | solution.py:20
  20.9 4.2 %collective-permute-start.6 = (bf16[272,128]{1,0:T(8,128)(2,1)S(1)}, bf16[272,128]{1,0:T(8,128)(2,1)S(1)}, u32[]{:S(2)}, u32[]{:S(2)}) collective-permute-start(bf16[272,128]{1,0:T(8,128)(2,1)S(1)} %get-tuple-element.20), channel_id=1, source_target_pairs={{0,12},{4,8},{8,4},{12,0},{1,13},{5,9},{9,5},{13,1},{2,14},{6,10},... | collective-permute-start | bytes 208904 | tf_op jit(solution)/shard_map/ppermute | solution.py:20
  26.4 4.8 %collective-permute-start.7 = (f32[4,2048]{1,0:T(4,128)S(1)}, f32[4,2048]{1,0:T(4,128)S(1)}, u32[]{:S(2)}, u32[]{:S(2)}) collective-permute-start(f32[4,2048]{1,0:T(4,128)S(1)} %get-tuple-element.22), channel_id=1, source_target_pairs={{0,2},{1,3},{2,0},{3,1},{4,6},{5,7},{6,4},{7,5},{8,10},{9,11},{10,... | collective-permute-start | bytes 98312 | tf_op jit(solution)/shard_map/ppermute | solution.py:20
  27.9 5.7 %collective-permute-start.8 = (f32[4,2048]{1,0:T(4,128)S(1)}, f32[4,2048]{1,0:T(4,128)S(1)}, u32[]{:S(2)}, u32[]{:S(2)}) collective-permute-start(f32[4,2048]{1,0:T(4,128)S(1)} %get-tuple-element.23), channel_id=1, source_target_pairs={{0,3},{1,2},{2,1},{3,0},{4,7},{5,6},{6,5},{7,4},{8,11},{9,10},{10,... | collective-permute-start | bytes 98312 | tf_op jit(solution)/shard_map/ppermute | solution.py:20
  28.8 4.8 %collective-permute-start.9 = (f32[4,2048]{1,0:T(4,128)S(1)}, f32[4,2048]{1,0:T(4,128)S(1)}, u32[]{:S(2)}, u32[]{:S(2)}) collective-permute-start(f32[4,2048]{1,0:T(4,128)S(1)} %get-tuple-element.24), channel_id=1, source_target_pairs={{0,1},{1,0},{2,3},{3,2},{4,5},{5,4},{6,7},{7,6},{8,9},{9,8},{10,11... | collective-permute-start | bytes 98312 | tf_op jit(solution)/shard_map/ppermute | solution.py:20

commit v5 on v4

--- a/solution.py
+++ b/solution.py
@@ -63,9 +63,9 @@
 
 
 def select_body(
-    chunk, steps, pool, block, per_kv, table_ref, list_ref, lengths_ref,
-    chosen_ref, seen_ref,
+    chunk, steps, per_kv, table_ref, list_ref, lengths_ref, key_ref, chosen_ref, seen_ref, turned_ref
 ):
+    pool, kv_heads, block, head_dim = key_ref.shape
     mem = lax.axis_index("mem")
     head_shard = lax.axis_index("heads")
     row_count, selected = list_ref.shape
@@ -86,19 +86,21 @@
         live = c < count
         for at, blank in ((c, 0), (stride + c, row_count), (2 * stride + c, 0)):
             chosen_ref[at] = jnp.where(live, chosen_ref[at], blank)
+        keys = key_ref[chosen_ref[c]]
+        for g in range(kv_heads):
+            turned_ref[c, :, g * block : (g + 1) * block] = keys[g].T
 
     def token_of(place):
         return lax.bitwise_xor(place // chunk, head_shard) * chunk + place % chunk
 
     tokens = row_count * steps
-    group_rows = steps * per_kv
-    row_height = seen_ref.shape[0] // row_count
+    heads = kv_heads * per_kv
     at = lax.broadcasted_iota(jnp.int32, seen_ref.shape, 0)
-    query_token = token_of(at // row_height * steps + at % group_rows // per_kv)
-    query_head = at % row_height // group_rows
+    query_token = token_of(at // heads)
+    query_head = at % heads // per_kv
     lane = lax.broadcasted_iota(jnp.int32, seen_ref.shape, 1)
     key_head, key = lane // tokens, lane % tokens
-    key_token = token_of(key % row_count * steps + key // row_count)
+    key_token = token_of(key)
     seen = (
         (query_head == key_head)
         & (query_token // steps == key_token // steps)
@@ -108,7 +110,7 @@
     seen_ref[...] = seen.astype(jnp.float32)
 
 
-def project_body(places, steps, kv_heads, tile, *refs):
+def project_body(places, tile, *refs):
     gain_ref, q_ref, k_ref, v_ref, out_ref = refs[len(places) :]
     chunks = [refs[places.index(i)][...].astype(jnp.float32) for i in range(len(places))]
     rows = jnp.concatenate(chunks, axis=0)
@@ -117,13 +119,7 @@
     gain = gain_ref[...].astype(jnp.float32).reshape(1, cols)
     rows = (rows[:, :cols] * factor * gain).astype(jnp.bfloat16)
     tokens = rows.shape[0]
-    row_count = tokens // steps
-    to = lax.broadcasted_iota(jnp.int32, (tokens, tokens), 0)
-    come = lax.broadcasted_iota(jnp.int32, (tokens, tokens), 1)
-    order = (to % row_count * steps + to // row_count == come).astype(jnp.bfloat16)
-    rows = jnp.dot(order, rows, preferred_element_type=jnp.float32).astype(jnp.bfloat16)
     heads = q_ref.shape[1] // LANES
-    per_kv = heads // kv_heads
     head = 0
     for weight in (q_ref, k_ref, v_ref):
         width = min(tile, weight.shape[1])
@@ -134,11 +130,7 @@
             for lane in range(0, width, LANES):
                 columns = product[:, lane : lane + LANES]
                 if head < heads:
-                    for s in range(steps):
-                        at = (head // per_kv * steps + s) * per_kv + head % per_kv
-                        out_ref[pl.ds(at, row_count, stride=heads * steps)] = columns[
-                            s * row_count : (s + 1) * row_count
-                        ]
+                    out_ref[pl.ds(head, tokens, stride=heads)] = columns
                 else:
                     out_ref[head * tokens : (head + 1) * tokens] = columns
                 head += 1
@@ -200,11 +192,13 @@
 
 def attend_body(
     scale,
+    heads,
+    query_count,
     chosen_ref,
     seen_ref,
     own_ref,
     other_ref,
-    key_ref,
+    turned_ref,
     value_ref,
     out_ref,
     query_ref,
@@ -214,8 +208,7 @@
     *peak_refs,
 ):
     row_count, row_height, head_dim = query_ref.shape
-    kv_heads = key_ref.shape[1]
-    query_count = row_height // kv_heads
+    kv_heads = value_ref.shape[1]
     capacity = score_ref.shape[0]
     height = row_count * row_height
     contract_last = (((1,), (1,)), ((), ()))
@@ -242,21 +235,17 @@
     stride = chosen_ref.shape[0] // 3
 
     lane = lax.broadcasted_iota(jnp.int32, (row_height, LANES), 1)
+    head_of = lax.broadcasted_iota(jnp.int32, (row_height, LANES), 0) % heads // (heads // kv_heads)
     for c in range(capacity):
         slot, row, valid = (chosen_ref[i * stride + c] for i in range(3))
-        every = lax.dot_general(
+        every = jnp.dot(
             query_ref[jnp.minimum(row, row_count - 1)],
-            key_ref[slot].reshape(kv_heads * LANES, head_dim),
-            contract_last,
+            turned_ref[c],
             preferred_element_type=jnp.float32,
         )
-        score = jnp.concatenate(
-            [
-                every[g * query_count : (g + 1) * query_count, g * LANES : (g + 1) * LANES]
-                for g in range(kv_heads)
-            ],
-            axis=0,
-        )
+        score = every[:, :LANES]
+        for g in range(1, kv_heads):
+            score = jnp.where(head_of == g, every[:, g * LANES : (g + 1) * LANES], score)
         score = jnp.where(lane < valid, score * scale, NEG_FILL)
         score_ref[c] = score
         ref = peak_refs[c % len(peak_refs)]
@@ -277,22 +266,10 @@
         slot, row = chosen_ref[c], chosen_ref[stride + c]
         weights = jnp.exp(score_ref[c] - peak_ref[row])
         total_ref[row] += weights
-        high = weights.astype(jnp.bfloat16)
-        low = (weights - high.astype(jnp.float32)).astype(jnp.bfloat16)
-        split = []
-        for g in range(kv_heads):
-            at = slice(g * query_count, (g + 1) * query_count)
-            half = jnp.concatenate([high[at], low[at]], axis=0)
-            blank = jnp.zeros_like(half)
-            split.append(
-                jnp.concatenate([half if i == g else blank for i in range(kv_heads)], axis=1)
-            )
-        both = jnp.dot(
-            jnp.concatenate(split, axis=0),
-            value_ref[slot].reshape(kv_heads * LANES, head_dim),
-            preferred_element_type=jnp.float32,
-        ).reshape(kv_heads, 2, query_count, head_dim)
-        accum_ref[row] += (both[:, 0] + both[:, 1]).reshape(row_height, head_dim)
+        spread = [jnp.where(head_of == g, weights, 0.0) for g in range(kv_heads)]
+        accum_ref[row] += split_dot(
+            jnp.concatenate(spread, axis=1), value_ref[slot].reshape(kv_heads * LANES, head_dim)
+        )
 
     total = jnp.sum(total_ref[:row_count].reshape(height, LANES), axis=1, keepdims=True)
     total = jnp.broadcast_to(total, (height, LANES))
@@ -351,21 +328,16 @@
             ref[group * query_count : (group + 1) * query_count] = value.astype(ref.dtype)
 
 
-def output_body(kv_heads, steps, tile, own_ref, other_ref, weight_ref, *refs):
+def output_body(query_count, tile, own_ref, other_ref, weight_ref, *refs):
     out_refs, wide_ref = refs[:-1], refs[-1]
     heads = weight_ref.shape[0] // LANES
-    per_kv = heads // kv_heads
     tokens = wide_ref.shape[0] // heads
-    groups = tokens // steps * kv_heads
-    _, _, values = merge_states(steps * per_kv, groups, True, own_ref, other_ref)
+    groups = wide_ref.shape[0] // query_count
+    _, _, values = merge_states(query_count, groups, True, own_ref, other_ref)
     for group, value in enumerate(values):
-        row, g = divmod(group, kv_heads)
-        for s in range(steps):
-            first = g * per_kv * tokens + row * steps + s
-            wide_ref[pl.ds(first, per_kv, stride=tokens)] = value[s * per_kv : (s + 1) * per_kv]
-    rows = jnp.concatenate(
-        [wide_ref[j * tokens : (j + 1) * tokens].astype(jnp.bfloat16) for j in range(heads)], axis=1
-    )
+        wide_ref[group * query_count : (group + 1) * query_count] = value
+    rows = [wide_ref[pl.ds(head, tokens, stride=heads)] for head in range(heads)]
+    rows = jnp.concatenate(rows, axis=1).astype(jnp.bfloat16)
     chunk = out_refs[0].shape[0]
     for col in range(0, weight_ref.shape[1], tile):
         product = jnp.dot(
@@ -413,24 +385,26 @@
         [pltpu.VMEM(hidden.shape, bf16), pltpu.SemaphoreType.DMA],
     )(pltpu.with_memory_space_constraint(hidden, pltpu.HBM))
     distances = [*range(2, head_count), 1]
-    pieces = [own] + [swap_across(mate, d) for d in distances]
-
-    chosen = kernel_call(
-        functools.partial(select_body, chunk, steps, pool, block, per_kv),
+    gathered = distances[::-1]
+    pieces = [own] + [swap_across(mate, d) for d in gathered]
+
+    chosen, seen, turned = kernel_call(
+        functools.partial(select_body, chunk, steps, per_kv),
         "select",
         [
             pltpu.SMEM((3 * (capacity + 1),), jnp.int32),
             jax.ShapeDtypeStruct((height, LANES), f32),
+            jax.ShapeDtypeStruct((capacity, head_dim, kv_heads * block), bf16),
         ],
-        [IN_SMEM] * 3,
-        2,
+        [IN_SMEM] * 3 + [IN_VMEM],
+        4,
         1e10,
-        out_space=[IN_SMEM, IN_VMEM],
-    )(page_table, attend_list, lengths)
+        out_space=[IN_SMEM, IN_VMEM, IN_VMEM],
+    )(page_table, attend_list, lengths, k_cache)
 
     width = query_cols + 2 * value_cols
     summed = kernel_call(
-        functools.partial(project_body, (0, *distances), steps, kv_heads, 512),
+        functools.partial(project_body, (0, *gathered), 512),
         "project",
         jax.ShapeDtypeStruct((width // LANES * token_count, LANES), f32),
         [IN_VMEM] * (head_count + 4),
@@ -453,7 +427,7 @@
 
     state = (kv_heads * query_count, LANES)
     partial = kernel_call(
-        functools.partial(attend_body, head_dim ** (-0.5)),
+        functools.partial(attend_body, head_dim ** (-0.5), kv_heads * per_kv, query_count),
         "attend",
         jax.ShapeDtypeStruct((height + 8, LANES), f32),
         [IN_SMEM] + [IN_VMEM] * 5,
@@ -461,7 +435,14 @@
         1e10,
         [pltpu.VMEM((row_count, *state), bf16), pltpu.VMEM((capacity, *state), f32)]
         + [pltpu.VMEM((row_count + 1, *state), f32)] * 6,
-    )(pltpu.with_memory_space_constraint(chosen[0], pltpu.SMEM), chosen[1], summed, swap(sent.astype(jnp.float16), "mem", crossing(distance)).astype(f32), k_cache, v_cache)
+    )(
+        pltpu.with_memory_space_constraint(chosen, pltpu.SMEM),
+        seen,
+        summed,
+        swap(sent.astype(jnp.float16), "mem", crossing(distance)).astype(f32),
+        turned,
+        v_cache,
+    )
 
     sent = partial
     distance = 1
@@ -483,7 +464,7 @@
 
     out_cols = o_weight.shape[1]
     projected = kernel_call(
-        functools.partial(output_body, kv_heads, steps, min(512, out_cols)),
+        functools.partial(output_body, query_count, min(512, out_cols)),
         "output",
         [jax.ShapeDtypeStruct((chunk, out_cols), f32)] * head_count,
         [IN_VMEM] * 3,

time: 34.4 us -> 33.9 us (0.985)
    ppermute x7, waiting for transfers between devices: 9.91 us -> 9.52 us  [swap(): return lax.ppermute(array, axis, [(i, i ^ distance) for i in range(count)])]
  transfers between devices with their start and end apart: 10 -> 10, of which waited for: 7 -> 7; matrix products, arithmetic and copies ran while one was open for 0% -> 0% of each run, Pallas kernels for 4% -> 5%
where the time goes in v5:
time: 33.9 us; the launch traced here: 33.7 us
  starting transfers between devices  13 us (38%)
  waiting for transfers between devices  12.7 us (37%)
  Pallas kernels  7.22 us (21%)
  other arithmetic  0.65 us (2%)
    ppermute x7, waiting for transfers between devices, swap(): return lax.ppermute(array, axis, [(i, i ^ distance) for i in range(count)])  9.52 us
    ppermute x7, starting transfers between devices, swap(): return lax.ppermute(array, axis, [(i, i ^ distance) for i in range(count)])  7.62 us
    ppermute x3, starting transfers between devices, swap_across(): return lax.ppermute(array, ('mem', 'heads'), pairs)  5.41 us
    ppermute x3, waiting for transfers between devices, swap_across(): return lax.ppermute(array, ('mem', 'heads'), pairs)  3.13 us
    pallas_call x1, Pallas kernels, shards(): kernel_call(functools.partial(select_body, chunk, steps, per_kv), 'select...  1.81 us
    pallas_call x1, Pallas kernels, shards(): kernel_call(functools.partial(project_body, (0, *gathered), 512), 'projec...  1.59 us
    pallas_call x1, Pallas kernels, shards(): kernel_call(functools.partial(output_body, query_count, min(512, out_cols...  1.31 us
    pallas_call x1, Pallas kernels, shards(): kernel_call(functools.partial(attend_body, head_dim ** (-0.5), kv_heads *...  1.18 us
  transfers between devices with their start and end apart: 10, of which 7 were waited for; matrix products, arithmetic and copies ran while one was open for 0% of the time, Pallas kernels for 5%

profile of v5, /device:TPU:0, one launch (start us, length us, event | category | flops | bytes accessed | tf_op | source)
XLA Modules:
  0.0 33.7 jit_solution(16617669813440269067)
XLA Ops:
  0.0 1.2 %norm.1 = (bf16[4,2176]{1,0:T(4,128)(2,1)S(1)}, bf16[4,2176]{1,0:T(4,128)(2,1)S(1)}) custom-call(bf16[4,8192]{1,0:T(4,128)(2,1)} %hidden_hbm.1), custom_call_target="tpu_custom_call" | custom-call | flops 10000000000 | bytes 1024 | tf_op jit(solution)/shard_map/norm/pallas_call | solution.py:378
  1.2 3.6 %collective-permute-start.2 = (bf16[4,2176]{1,0:T(4,128)(2,1)S(1)}, bf16[4,2176]{1,0:T(4,128)(2,1)S(1)}, u32[]{:S(2)}, u32[]{:S(2)}) collective-permute-start(bf16[4,2176]{1,0:T(4,128)(2,1)S(1)} %get-tuple-element.19), channel_id=1, source_target_pairs={{0,6},{1,7},{2,4},{3,5},{4,2},{5,3},{6,0},{7,1},{8,14},{9,15},{10,... | collective-permute-start | bytes 52232 | tf_op jit(solution)/shard_map/ppermute | solution.py:31
  4.7 1.6 %collective-permute-start.1 = (bf16[4,2176]{1,0:T(4,128)(2,1)S(1)}, bf16[4,2176]{1,0:T(4,128)(2,1)S(1)}, u32[]{:S(2)}, u32[]{:S(2)}) collective-permute-start(bf16[4,2176]{1,0:T(4,128)(2,1)S(1)} %get-tuple-element.19), channel_id=1, source_target_pairs={{0,7},{1,6},{2,5},{3,4},{4,3},{5,2},{6,1},{7,0},{8,15},{9,14},{10,... | collective-permute-start | bytes 52232 | tf_op jit(solution)/shard_map/ppermute | solution.py:31
  6.4 0.2 collective-permute-start
  6.6 3.1 %collective-permute-done.1.refs_2_ = bf16[4,2176]{1,0:T(4,128)(2,1)S(1)} collective-permute-done((bf16[4,2176]{1,0:T(4,128)(2,1)S(1)}, bf16[4,2176]{1,0:T(4,128)(2,1)S(1)}, u32[]{:S(2)}, u32[]{:S(2)}) %collective-permute-start.1) | collective-permute-done | bytes 17440 | tf_op jit(solution)/shard_map/ppermute | solution.py:31
  9.8 1.6 %project.1.own_ref = f32[320,128]{1,0:T(8,128)S(1)} custom-call(bf16[4,2176]{1,0:T(4,128)(2,1)S(1)} %get-tuple-element.18.refs_0_, bf16[4,2176]{1,0:T(4,128)(2,1)S(1)} %collective-permute-done.refs_1_, bf16[4,2176]{1,0:T(4,128)(2,1)S(1)} %collective-permute-done.1.refs_2_, bf16[4,2176]{1,0:T(4,128)(2,1)S(1)} %collective-permute-done.2.refs_3_, ...), custom_call_target="tpu_custom_call" | custom-call | flops 167772160 | bytes 1024 | tf_op jit(solution)/shard_map/project/pallas_call | solution.py:406
  11.4 0.8 %collective-permute-start.3 = (f32[320,128]{1,0:T(8,128)S(1)}, f32[320,128]{1,0:T(8,128)S(1)}, u32[]{:S(2)}, u32[]{:S(2)}) collective-permute-start(f32[320,128]{1,0:T(8,128)S(1)} %project.1.own_ref), channel_id=1, source_target_pairs={{0,4},{4,0},{8,12},{12,8},{1,5},{5,1},{9,13},{13,9},{2,6},{6,2},{1... | collective-permute-start | bytes 491528 | tf_op jit(solution)/shard_map/ppermute | solution.py:20
  12.2 1.0 %collective-permute-done.3.other_ref = f32[320,128]{1,0:T(8,128)S(1)} collective-permute-done((f32[320,128]{1,0:T(8,128)S(1)}, f32[320,128]{1,0:T(8,128)S(1)}, u32[]{:S(2)}, u32[]{:S(2)}) %collective-permute-start.3) | collective-permute-done | bytes 163872 | tf_op jit(solution)/shard_map/ppermute | solution.py:20
  13.2 1.5 %collective-permute-start.4 = (f16[320,128]{1,0:T(8,128)(2,1)S(1)}, f16[320,128]{1,0:T(8,128)(2,1)S(1)}, u32[]{:S(2)}, u32[]{:S(2)}) collective-permute-start(f16[320,128]{1,0:T(8,128)(2,1)S(1)} %convert_element_type.9), channel_id=1, source_target_pairs={{0,12},{4,8},{8,4},{12,0},{1,13},{5,9},{9,5},{13,1},{2,14},{6,10},... | collective-permute-start | bytes 245768 | tf_op jit(solution)/shard_map/ppermute | solution.py:20
  14.8 1.8 %select.1 = (s32[99]{0:T(128)S(4)}, f32[256,128]{1,0:T(8,128)S(1)}, bf16[32,128,256]{2,1,0:T(8,128)(2,1)S(1)}) custom-call(s32[8,24]{1,0:T(8,128)S(1)} %copy-done.6, s32[8,8]{1,0:T(8,128)S(1)} %copy-done.7, s32[8]{0:T(128)S(1)} %copy-done.8, bf16[48,2,128,128]{3,2,1,0:T(8,128)(2,1)S(1)} %copy-done.4), custom_call_target="tpu_custom_call" | custom-call | flops 10000000000 | bytes 1024 | tf_op jit(solution)/shard_map/select/pallas_call | solution.py:391
  16.6 1.0 %collective-permute-done.4 = f16[320,128]{1,0:T(8,128)(2,1)S(1)} collective-permute-done((f16[320,128]{1,0:T(8,128)(2,1)S(1)}, f16[320,128]{1,0:T(8,128)(2,1)S(1)}, u32[]{:S(2)}, u32[]{:S(2)}) %collective-permute-start.4) | collective-permute-done | bytes 81952 | tf_op jit(solution)/shard_map/ppermute | solution.py:20
  17.6 1.2 %attend.1.own_ref = f32[264,128]{1,0:T(8,128)S(1)} custom-call(s32[99]{0:T(128)S(4)} %get-tuple-element.16.chosen_ref, f32[256,128]{1,0:T(8,128)S(1)} %get-tuple-element.17.seen_ref, f32[320,128]{1,0:T(8,128)S(1)} %add.16.own_ref, f32[320,128]{1,0:T(8,128)S(1)} %convert_element_type.10.other_ref, bf16[32,128,256]{2,1,0:T(8,128)(2,1)S(1)} %get-tuple-element.20.turned_ref, ...), custom_call_target="tpu_custom_call" | custom-call | flops 10000000000 | bytes 1024 | tf_op jit(solution)/shard_map/attend/pallas_call | solution.py:429
  18.8 0.3 %collective-permute-start.5 = (f32[264,128]{1,0:T(8,128)S(1)}, f32[264,128]{1,0:T(8,128)S(1)}, u32[]{:S(2)}, u32[]{:S(2)}) collective-permute-start(f32[264,128]{1,0:T(8,128)S(1)} %attend.1.own_ref), channel_id=1, source_target_pairs={{0,4},{4,0},{8,12},{12,8},{1,5},{5,1},{9,13},{13,9},{2,6},{6,2},{1... | collective-permute-start | bytes 405512 | tf_op jit(solution)/shard_map/ppermute | solution.py:20
  19.2 1.1 %collective-permute-done.5.other_ref = f32[264,128]{1,0:T(8,128)S(1)} collective-permute-done((f32[264,128]{1,0:T(8,128)S(1)}, f32[264,128]{1,0:T(8,128)S(1)}, u32[]{:S(2)}, u32[]{:S(2)}) %collective-permute-start.5) | collective-permute-done | bytes 135200 | tf_op jit(solution)/shard_map/ppermute | solution.py:20
  20.3 0.2 combine.1
  20.4 1.4 %collective-permute-start.6 = (bf16[272,128]{1,0:T(8,128)(2,1)S(1)}, bf16[272,128]{1,0:T(8,128)(2,1)S(1)}, u32[]{:S(2)}, u32[]{:S(2)}) collective-permute-start(bf16[272,128]{1,0:T(8,128)(2,1)S(1)} %get-tuple-element.22), channel_id=1, source_target_pairs={{0,12},{4,8},{8,4},{12,0},{1,13},{5,9},{9,5},{13,1},{2,14},{6,10},... | collective-permute-start | bytes 208904 | tf_op jit(solution)/shard_map/ppermute | solution.py:20
  21.9 2.7 %collective-permute-done.6.other_ref = bf16[272,128]{1,0:T(8,128)(2,1)S(1)} collective-permute-done((bf16[272,128]{1,0:T(8,128)(2,1)S(1)}, bf16[272,128]{1,0:T(8,128)(2,1)S(1)}, u32[]{:S(2)}, u32[]{:S(2)}) %collective-permute-start.6) | collective-permute-done | bytes 69664 | tf_op jit(solution)/shard_map/ppermute | solution.py:20
  24.6 1.3 %output.1 = (f32[4,2048]{1,0:T(4,128)S(1)}, f32[4,2048]{1,0:T(4,128)S(1)}, f32[4,2048]{1,0:T(4,128)S(1)}, f32[4,2048]{1,0:T(4,128)S(1)}) custom-call(f32[264,128]{1,0:T(8,128)S(1)} %get-tuple-element.21.own_ref, bf16[272,128]{1,0:T(8,128)(2,1)S(1)} %collective-permute-done.6.other_ref, bf16[2048,2048]{1,0:T(8,128)(2,1)S(1)} %bitcast.1), custom_call_target="tpu_custom_call" | custom-call | flops 134217728 | bytes 1024 | tf_op jit(solution)/shard_map/output/pallas_call | solution.py:466
  25.9 1.5 %collective-permute-start.7 = (f32[4,2048]{1,0:T(4,128)S(1)}, f32[4,2048]{1,0:T(4,128)S(1)}, u32[]{:S(2)}, u32[]{:S(2)}) collective-permute-start(f32[4,2048]{1,0:T(4,128)S(1)} %get-tuple-element.24), channel_id=1, source_target_pairs={{0,2},{1,3},{2,0},{3,1},{4,6},{5,7},{6,4},{7,5},{8,10},{9,11},{10,... | collective-permute-start | bytes 98312 | tf_op jit(solution)/shard_map/ppermute | solution.py:20
  27.4 0.9 %collective-permute-start.8 = (f32[4,2048]{1,0:T(4,128)S(1)}, f32[4,2048]{1,0:T(4,128)S(1)}, u32[]{:S(2)}, u32[]{:S(2)}) collective-permute-start(f32[4,2048]{1,0:T(4,128)S(1)} %get-tuple-element.25), channel_id=1, source_target_pairs={{0,3},{1,2},{2,1},{3,0},{4,7},{5,6},{6,5},{7,4},{8,11},{9,10},{10,... | collective-permute-start | bytes 98312 | tf_op jit(solution)/shard_map/ppermute | solution.py:20
  28.3 1.1 %collective-permute-start.9 = (f32[4,2048]{1,0:T(4,128)S(1)}, f32[4,2048]{1,0:T(4,128)S(1)}, u32[]{:S(2)}, u32[]{:S(2)}) collective-permute-start(f32[4,2048]{1,0:T(4,128)S(1)} %get-tuple-element.26), channel_id=1, source_target_pairs={{0,1},{1,0},{2,3},{3,2},{4,5},{5,4},{6,7},{7,6},{8,9},{9,8},{10,11... | collective-permute-start | bytes 98312 | tf_op jit(solution)/shard_map/ppermute | solution.py:20
  29.4 1.3 %collective-permute-done.7 = f32[4,2048]{1,0:T(4,128)S(1)} collective-permute-done((f32[4,2048]{1,0:T(4,128)S(1)}, f32[4,2048]{1,0:T(4,128)S(1)}, u32[]{:S(2)}, u32[]{:S(2)}) %collective-permute-start.7) | collective-permute-done | bytes 32800 | tf_op jit(solution)/shard_map/ppermute | solution.py:20
  30.7 2.4 %collective-permute-done.8 = f32[4,2048]{1,0:T(4,128)S(1)} collective-permute-done((f32[4,2048]{1,0:T(4,128)S(1)}, f32[4,2048]{1,0:T(4,128)S(1)}, u32[]{:S(2)}, u32[]{:S(2)}) %collective-permute-start.8) | collective-permute-done | bytes 32800 | tf_op jit(solution)/shard_map/ppermute | solution.py:20
  33.1 0.6 %add_convert_fusion = bf16[4,2048]{1,0:T(4,128)(2,1)} fusion(f32[4,2048]{1,0:T(4,128)S(1)} %collective-permute-done.9, f32[4,2048]{1,0:T(4,128)S(1)} %collective-permute-done.8, f32[4,2048]{1,0:T(4,128)S(1)} %get-tuple-element.23, f32[4,2048]{1,0:T(4,128)S(1)} %collective-permute-done.7), kind=kLoop, calls=%fused_computation | loop fusion | flops 32768 | bytes 147456 | tf_op jit(solution)/shard_map/convert_element_type | solution.py:478
  (29 shorter events, 0.1 us)
Async XLA Ops:
  0.0 9.7 %copy-start.2 = (bf16[2048,256]{1,0:T(8,128)(2,1)S(1)}, bf16[2048,256]{1,0:T(8,128)(2,1)}, u32[]{:S(2)}) copy-start(bf16[2048,256]{1,0:T(8,128)(2,1)} %refs_7_.1) | copy-start | bytes 3145732
  0.0 9.7 %copy-start.1 = (bf16[2048,256]{1,0:T(8,128)(2,1)S(1)}, bf16[2048,256]{1,0:T(8,128)(2,1)}, u32[]{:S(2)}) copy-start(bf16[2048,256]{1,0:T(8,128)(2,1)} %refs_6_.1) | copy-start | bytes 3145732
  0.0 9.7 %copy-start.3 = (bf16[2048]{0:T(1024)(128)(2,1)S(1)}, bf16[2048]{0:T(1024)(128)(2,1)}, u32[]{:S(2)}) copy-start(bf16[2048]{0:T(1024)(128)(2,1)} %refs_4_.1) | copy-start | bytes 12292
  0.0 9.7 %copy-start = (bf16[2048,2048]{1,0:T(8,128)(2,1)S(1)}, bf16[2048,2048]{1,0:T(8,128)(2,1)}, u32[]{:S(2)}) copy-start(bf16[2048,2048]{1,0:T(8,128)(2,1)} %refs_5_.1) | copy-start | bytes 25165828
  1.2 5.4 %collective-permute-start.2 = (bf16[4,2176]{1,0:T(4,128)(2,1)S(1)}, bf16[4,2176]{1,0:T(4,128)(2,1)S(1)}, u32[]{:S(2)}, u32[]{:S(2)}) collective-permute-start(bf16[4,2176]{1,0:T(4,128)(2,1)S(1)} %get-tuple-element.19), channel_id=1, source_target_pairs={{0,6},{1,7},{2,4},{3,5},{4,2},{5,3},{6,0},{7,1},{8,14},{9,15},{10,... | collective-permute-start | bytes 52232 | tf_op jit(solution)/shard_map/ppermute | solution.py:31
  4.7 5.0 %collective-permute-start.1 = (bf16[4,2176]{1,0:T(4,128)(2,1)S(1)}, bf16[4,2176]{1,0:T(4,128)(2,1)S(1)}, u32[]{:S(2)}, u32[]{:S(2)}) collective-permute-start(bf16[4,2176]{1,0:T(4,128)(2,1)S(1)} %get-tuple-element.19), channel_id=1, source_target_pairs={{0,7},{1,6},{2,5},{3,4},{4,3},{5,2},{6,1},{7,0},{8,15},{9,14},{10,... | collective-permute-start | bytes 52232 | tf_op jit(solution)/shard_map/ppermute | solution.py:31
  6.4 3.4 %collective-permute-start = (bf16[4,2176]{1,0:T(4,128)(2,1)S(1)}, bf16[4,2176]{1,0:T(4,128)(2,1)S(1)}, u32[]{:S(2)}, u32[]{:S(2)}) collective-permute-start(bf16[4,2176]{1,0:T(4,128)(2,1)S(1)} %get-tuple-element.19), channel_id=1, source_target_pairs={{0,5},{1,4},{2,7},{3,6},{4,1},{5,0},{6,3},{7,2},{8,13},{9,12},{10,... | collective-permute-start | bytes 52232 | tf_op jit(solution)/shard_map/ppermute | solution.py:31
  11.3 3.4 %copy-start.4 = (bf16[48,2,128,128]{3,2,1,0:T(8,128)(2,1)S(1)}, bf16[48,2,128,128]{3,2,1,0:T(8,128)(2,1)}, u32[]{:S(2)}) copy-start(bf16[48,2,128,128]{3,2,1,0:T(8,128)(2,1)} %key_ref.1) | copy-start | bytes 9437188
  11.3 3.4 %copy-start.6 = (s32[8,24]{1,0:T(8,128)S(1)}, s32[8,24]{1,0:T(8,128)}, u32[]{:S(2)}) copy-start(s32[8,24]{1,0:T(8,128)} %table_ref.1) | copy-start | bytes 2308
  11.3 3.4 %copy-start.7 = (s32[8,8]{1,0:T(8,128)S(1)}, s32[8,8]{1,0:T(8,128)}, u32[]{:S(2)}) copy-start(s32[8,8]{1,0:T(8,128)} %list_ref.1) | copy-start | bytes 772
  11.3 3.4 %copy-start.8 = (s32[8]{0:T(128)S(1)}, s32[8]{0:T(128)}, u32[]{:S(2)}) copy-start(s32[8]{0:T(128)} %lengths_ref.1) | copy-start | bytes 100
  11.4 1.8 %collective-permute-start.3 = (f32[320,128]{1,0:T(8,128)S(1)}, f32[320,128]{1,0:T(8,128)S(1)}, u32[]{:S(2)}, u32[]{:S(2)}) collective-permute-start(f32[320,128]{1,0:T(8,128)S(1)} %project.1.own_ref), channel_id=1, source_target_pairs={{0,4},{4,0},{8,12},{12,8},{1,5},{5,1},{9,13},{13,9},{2,6},{6,2},{1... | collective-permute-start | bytes 491528 | tf_op jit(solution)/shard_map/ppermute | solution.py:20
  13.2 4.4 %copy-start.5 = (bf16[48,2,128,128]{3,2,1,0:T(8,128)(2,1)S(1)}, bf16[48,2,128,128]{3,2,1,0:T(8,128)(2,1)}, u32[]{:S(2)}) copy-start(bf16[48,2,128,128]{3,2,1,0:T(8,128)(2,1)} %value_ref.1) | copy-start | bytes 9437188
  13.2 4.4 %collective-permute-start.4 = (f16[320,128]{1,0:T(8,128)(2,1)S(1)}, f16[320,128]{1,0:T(8,128)(2,1)S(1)}, u32[]{:S(2)}, u32[]{:S(2)}) collective-permute-start(f16[320,128]{1,0:T(8,128)(2,1)S(1)} %convert_element_type.9), channel_id=1, source_target_pairs={{0,12},{4,8},{8,4},{12,0},{1,13},{5,9},{9,5},{13,1},{2,14},{6,10},... | collective-permute-start | bytes 245768 | tf_op jit(solution)/shard_map/ppermute | solution.py:20
  17.6 7.0 %slice-start = ((s8[8388608]{0:T(1024)(128)(4,1)}), s8[4194304]{0:T(1024)(128)(4,1)S(1)}, s32[]{:S(2)}) async-start(s8[8388608]{0:T(1024)(128)(4,1)} %bitcast), calls=%async_computation | async-start | bytes 8388608
  18.8 5.8 %slice-start.1 = ((s8[8388608]{0:T(1024)(128)(4,1)}), s8[4194304]{0:T(1024)(128)(4,1)S(1)}, s32[]{:S(2)}) async-start(s8[8388608]{0:T(1024)(128)(4,1)} %bitcast), calls=%async_computation.1 | async-start | bytes 8388608
  18.8 1.4 %collective-permute-start.5 = (f32[264,128]{1,0:T(8,128)S(1)}, f32[264,128]{1,0:T(8,128)S(1)}, u32[]{:S(2)}, u32[]{:S(2)}) collective-permute-start(f32[264,128]{1,0:T(8,128)S(1)} %attend.1.own_ref), channel_id=1, source_target_pairs={{0,4},{4,0},{8,12},{12,8},{1,5},{5,1},{9,13},{13,9},{2,6},{6,2},{1... | collective-permute-start | bytes 405512 | tf_op jit(solution)/shard_map/ppermute | solution.py:20
  20.4 4.2 %collective-permute-start.6 = (bf16[272,128]{1,0:T(8,128)(2,1)S(1)}, bf16[272,128]{1,0:T(8,128)(2,1)S(1)}, u32[]{:S(2)}, u32[]{:S(2)}) collective-permute-start(bf16[272,128]{1,0:T(8,128)(2,1)S(1)} %get-tuple-element.22), channel_id=1, source_target_pairs={{0,12},{4,8},{8,4},{12,0},{1,13},{5,9},{9,5},{13,1},{2,14},{6,10},... | collective-permute-start | bytes 208904 | tf_op jit(solution)/shard_map/ppermute | solution.py:20
  25.9 4.8 %collective-permute-start.7 = (f32[4,2048]{1,0:T(4,128)S(1)}, f32[4,2048]{1,0:T(4,128)S(1)}, u32[]{:S(2)}, u32[]{:S(2)}) collective-permute-start(f32[4,2048]{1,0:T(4,128)S(1)} %get-tuple-element.24), channel_id=1, source_target_pairs={{0,2},{1,3},{2,0},{3,1},{4,6},{5,7},{6,4},{7,5},{8,10},{9,11},{10,... | collective-permute-start | bytes 98312 | tf_op jit(solution)/shard_map/ppermute | solution.py:20
  27.4 5.7 %collective-permute-start.8 = (f32[4,2048]{1,0:T(4,128)S(1)}, f32[4,2048]{1,0:T(4,128)S(1)}, u32[]{:S(2)}, u32[]{:S(2)}) collective-permute-start(f32[4,2048]{1,0:T(4,128)S(1)} %get-tuple-element.25), channel_id=1, source_target_pairs={{0,3},{1,2},{2,1},{3,0},{4,7},{5,6},{6,5},{7,4},{8,11},{9,10},{10,... | collective-permute-start | bytes 98312 | tf_op jit(solution)/shard_map/ppermute | solution.py:20
  28.3 4.8 %collective-permute-start.9 = (f32[4,2048]{1,0:T(4,128)S(1)}, f32[4,2048]{1,0:T(4,128)S(1)}, u32[]{:S(2)}, u32[]{:S(2)}) collective-permute-start(f32[4,2048]{1,0:T(4,128)S(1)} %get-tuple-element.26), channel_id=1, source_target_pairs={{0,1},{1,0},{2,3},{3,2},{4,5},{5,4},{6,7},{7,6},{8,9},{9,8},{10,11... | collective-permute-start | bytes 98312 | tf_op jit(solution)/shard_map/ppermute | solution.py:20

commit v6 on v5

--- a/solution.py
+++ b/solution.py
@@ -344,7 +344,7 @@
             rows, weight_ref[:, col : col + tile], preferred_element_type=jnp.float32
         )
         for i, out_ref in enumerate(out_refs):
-            out_ref[:, col : col + tile] = product[i * chunk : (i + 1) * chunk]
+            out_ref[:, col : col + tile] = product[i * chunk : (i + 1) * chunk].astype(out_ref.dtype)
 
 
 def shards(
@@ -466,7 +466,7 @@
     projected = kernel_call(
         functools.partial(output_body, query_count, min(512, out_cols)),
         "output",
-        [jax.ShapeDtypeStruct((chunk, out_cols), f32)] * head_count,
+        [jax.ShapeDtypeStruct((chunk, out_cols), bf16 if i else f32) for i in range(head_count)],
         [IN_VMEM] * 3,
         4,
         2 * token_count * query_cols * out_cols,
@@ -474,7 +474,7 @@
     )(partial, swap(sent, "mem", crossing(distance)), o_weight)
     total = projected[0]
     for d in distances:
-        total = total + swap(projected[d], "heads", d)
+        total = total + swap(projected[d], "heads", d).astype(f32)
     return total.astype(bf16)
 
 

time: 33.9 us -> 33.7 us (level)
  no operation moved by 1% of the time
where the time goes in v6:
time: 33.7 us; the launch traced here: 33.6 us
  starting transfers between devices  13 us (39%)
  waiting for transfers between devices  12.5 us (37%)
  Pallas kernels  7.22 us (21%)
  other arithmetic  0.65 us (2%)
    ppermute x7, waiting for transfers between devices, swap(): return lax.ppermute(array, axis, [(i, i ^ distance) for i in range(count)])  9.34 us
    ppermute x7, starting transfers between devices, swap(): return lax.ppermute(array, axis, [(i, i ^ distance) for i in range(count)])  7.63 us
    ppermute x3, starting transfers between devices, swap_across(): return lax.ppermute(array, ('mem', 'heads'), pairs)  5.41 us
    ppermute x3, waiting for transfers between devices, swap_across(): return lax.ppermute(array, ('mem', 'heads'), pairs)  3.13 us
    pallas_call x1, Pallas kernels, shards(): kernel_call(functools.partial(select_body, chunk, steps, per_kv), 'select...  1.81 us
    pallas_call x1, Pallas kernels, shards(): kernel_call(functools.partial(project_body, (0, *gathered), 512), 'projec...  1.59 us
    pallas_call x1, Pallas kernels, shards(): kernel_call(functools.partial(output_body, query_count, min(512, out_cols...  1.31 us
    pallas_call x1, Pallas kernels, shards(): kernel_call(functools.partial(attend_body, head_dim ** (-0.5), kv_heads *...  1.18 us
  transfers between devices with their start and end apart: 10, of which 7 were waited for; matrix products, arithmetic and copies ran while one was open for 0% of the time, Pallas kernels for 5%

profile of v6, /device:TPU:0, one launch (start us, length us, event | category | flops | bytes accessed | tf_op | source)
XLA Modules:
  0.0 33.6 jit_solution(3467335188639082287)
XLA Ops:
  0.0 1.2 %norm.1 = (bf16[4,2176]{1,0:T(4,128)(2,1)S(1)}, bf16[4,2176]{1,0:T(4,128)(2,1)S(1)}) custom-call(bf16[4,8192]{1,0:T(4,128)(2,1)} %hidden_hbm.1), custom_call_target="tpu_custom_call" | custom-call | flops 10000000000 | bytes 1024 | tf_op jit(solution)/shard_map/norm/pallas_call | solution.py:378
  1.2 3.6 %collective-permute-start.2 = (bf16[4,2176]{1,0:T(4,128)(2,1)S(1)}, bf16[4,2176]{1,0:T(4,128)(2,1)S(1)}, u32[]{:S(2)}, u32[]{:S(2)}) collective-permute-start(bf16[4,2176]{1,0:T(4,128)(2,1)S(1)} %get-tuple-element.19), channel_id=1, source_target_pairs={{0,6},{1,7},{2,4},{3,5},{4,2},{5,3},{6,0},{7,1},{8,14},{9,15},{10,... | collective-permute-start | bytes 52232 | tf_op jit(solution)/shard_map/ppermute | solution.py:31
  4.7 1.6 %collective-permute-start.1 = (bf16[4,2176]{1,0:T(4,128)(2,1)S(1)}, bf16[4,2176]{1,0:T(4,128)(2,1)S(1)}, u32[]{:S(2)}, u32[]{:S(2)}) collective-permute-start(bf16[4,2176]{1,0:T(4,128)(2,1)S(1)} %get-tuple-element.19), channel_id=1, source_target_pairs={{0,7},{1,6},{2,5},{3,4},{4,3},{5,2},{6,1},{7,0},{8,15},{9,14},{10,... | collective-permute-start | bytes 52232 | tf_op jit(solution)/shard_map/ppermute | solution.py:31
  6.4 0.2 collective-permute-start
  6.6 3.1 %collective-permute-done.1.refs_2_ = bf16[4,2176]{1,0:T(4,128)(2,1)S(1)} collective-permute-done((bf16[4,2176]{1,0:T(4,128)(2,1)S(1)}, bf16[4,2176]{1,0:T(4,128)(2,1)S(1)}, u32[]{:S(2)}, u32[]{:S(2)}) %collective-permute-start.1) | collective-permute-done | bytes 17440 | tf_op jit(solution)/shard_map/ppermute | solution.py:31
  9.8 1.6 %project.1.own_ref = f32[320,128]{1,0:T(8,128)S(1)} custom-call(bf16[4,2176]{1,0:T(4,128)(2,1)S(1)} %get-tuple-element.18.refs_0_, bf16[4,2176]{1,0:T(4,128)(2,1)S(1)} %collective-permute-done.refs_1_, bf16[4,2176]{1,0:T(4,128)(2,1)S(1)} %collective-permute-done.1.refs_2_, bf16[4,2176]{1,0:T(4,128)(2,1)S(1)} %collective-permute-done.2.refs_3_, ...), custom_call_target="tpu_custom_call" | custom-call | flops 167772160 | bytes 1024 | tf_op jit(solution)/shard_map/project/pallas_call | solution.py:406
  11.4 0.8 %collective-permute-start.3 = (f32[320,128]{1,0:T(8,128)S(1)}, f32[320,128]{1,0:T(8,128)S(1)}, u32[]{:S(2)}, u32[]{:S(2)}) collective-permute-start(f32[320,128]{1,0:T(8,128)S(1)} %project.1.own_ref), channel_id=1, source_target_pairs={{0,4},{4,0},{8,12},{12,8},{1,5},{5,1},{9,13},{13,9},{2,6},{6,2},{1... | collective-permute-start | bytes 491528 | tf_op jit(solution)/shard_map/ppermute | solution.py:20
  12.2 1.0 %collective-permute-done.3.other_ref = f32[320,128]{1,0:T(8,128)S(1)} collective-permute-done((f32[320,128]{1,0:T(8,128)S(1)}, f32[320,128]{1,0:T(8,128)S(1)}, u32[]{:S(2)}, u32[]{:S(2)}) %collective-permute-start.3) | collective-permute-done | bytes 163872 | tf_op jit(solution)/shard_map/ppermute | solution.py:20
  13.2 1.5 %collective-permute-start.4 = (f16[320,128]{1,0:T(8,128)(2,1)S(1)}, f16[320,128]{1,0:T(8,128)(2,1)S(1)}, u32[]{:S(2)}, u32[]{:S(2)}) collective-permute-start(f16[320,128]{1,0:T(8,128)(2,1)S(1)} %convert_element_type.18), channel_id=1, source_target_pairs={{0,12},{4,8},{8,4},{12,0},{1,13},{5,9},{9,5},{13,1},{2,14},{6,10},... | collective-permute-start | bytes 245768 | tf_op jit(solution)/shard_map/ppermute | solution.py:20
  14.8 1.8 %select.1 = (s32[99]{0:T(128)S(4)}, f32[256,128]{1,0:T(8,128)S(1)}, bf16[32,128,256]{2,1,0:T(8,128)(2,1)S(1)}) custom-call(s32[8,24]{1,0:T(8,128)S(1)} %copy-done.6, s32[8,8]{1,0:T(8,128)S(1)} %copy-done.7, s32[8]{0:T(128)S(1)} %copy-done.8, bf16[48,2,128,128]{3,2,1,0:T(8,128)(2,1)S(1)} %copy-done.4), custom_call_target="tpu_custom_call" | custom-call | flops 10000000000 | bytes 1024 | tf_op jit(solution)/shard_map/select/pallas_call | solution.py:391
  16.6 1.0 %collective-permute-done.4 = f16[320,128]{1,0:T(8,128)(2,1)S(1)} collective-permute-done((f16[320,128]{1,0:T(8,128)(2,1)S(1)}, f16[320,128]{1,0:T(8,128)(2,1)S(1)}, u32[]{:S(2)}, u32[]{:S(2)}) %collective-permute-start.4) | collective-permute-done | bytes 81952 | tf_op jit(solution)/shard_map/ppermute | solution.py:20
  17.6 1.2 %attend.1.own_ref = f32[264,128]{1,0:T(8,128)S(1)} custom-call(s32[99]{0:T(128)S(4)} %get-tuple-element.16.chosen_ref, f32[256,128]{1,0:T(8,128)S(1)} %get-tuple-element.17.seen_ref, f32[320,128]{1,0:T(8,128)S(1)} %add.16.own_ref, f32[320,128]{1,0:T(8,128)S(1)} %convert_element_type.19.other_ref, bf16[32,128,256]{2,1,0:T(8,128)(2,1)S(1)} %get-tuple-element.20.turned_ref, ...), custom_call_target="tpu_custom_call" | custom-call | flops 10000000000 | bytes 1024 | tf_op jit(solution)/shard_map/attend/pallas_call | solution.py:429
  18.8 0.4 %collective-permute-start.5 = (f32[264,128]{1,0:T(8,128)S(1)}, f32[264,128]{1,0:T(8,128)S(1)}, u32[]{:S(2)}, u32[]{:S(2)}) collective-permute-start(f32[264,128]{1,0:T(8,128)S(1)} %attend.1.own_ref), channel_id=1, source_target_pairs={{0,4},{4,0},{8,12},{12,8},{1,5},{5,1},{9,13},{13,9},{2,6},{6,2},{1... | collective-permute-start | bytes 405512 | tf_op jit(solution)/shard_map/ppermute | solution.py:20
  19.2 1.1 %collective-permute-done.5.other_ref = f32[264,128]{1,0:T(8,128)S(1)} collective-permute-done((f32[264,128]{1,0:T(8,128)S(1)}, f32[264,128]{1,0:T(8,128)S(1)}, u32[]{:S(2)}, u32[]{:S(2)}) %collective-permute-start.5) | collective-permute-done | bytes 135200 | tf_op jit(solution)/shard_map/ppermute | solution.py:20
  20.3 0.2 combine.1
  20.4 1.4 %collective-permute-start.6 = (bf16[272,128]{1,0:T(8,128)(2,1)S(1)}, bf16[272,128]{1,0:T(8,128)(2,1)S(1)}, u32[]{:S(2)}, u32[]{:S(2)}) collective-permute-start(bf16[272,128]{1,0:T(8,128)(2,1)S(1)} %get-tuple-element.22), channel_id=1, source_target_pairs={{0,12},{4,8},{8,4},{12,0},{1,13},{5,9},{9,5},{13,1},{2,14},{6,10},... | collective-permute-start | bytes 208904 | tf_op jit(solution)/shard_map/ppermute | solution.py:20
  21.9 2.7 %collective-permute-done.6.other_ref = bf16[272,128]{1,0:T(8,128)(2,1)S(1)} collective-permute-done((bf16[272,128]{1,0:T(8,128)(2,1)S(1)}, bf16[272,128]{1,0:T(8,128)(2,1)S(1)}, u32[]{:S(2)}, u32[]{:S(2)}) %collective-permute-start.6) | collective-permute-done | bytes 69664 | tf_op jit(solution)/shard_map/ppermute | solution.py:20
  24.6 1.3 %output.1 = (f32[4,2048]{1,0:T(4,128)S(1)}, bf16[4,2048]{1,0:T(4,128)(2,1)S(1)}, bf16[4,2048]{1,0:T(4,128)(2,1)S(1)}, bf16[4,2048]{1,0:T(4,128)(2,1)S(1)}) custom-call(f32[264,128]{1,0:T(8,128)S(1)} %get-tuple-element.21.own_ref, bf16[272,128]{1,0:T(8,128)(2,1)S(1)} %collective-permute-done.6.other_ref, bf16[2048,2048]{1,0:T(8,128)(2,1)S(1)} %bitcast.1), custom_call_target="tpu_custom_call" | custom-call | flops 134217728 | bytes 1024 | tf_op jit(solution)/shard_map/output/pallas_call | solution.py:466
  25.9 1.5 %collective-permute-start.7 = (bf16[4,2048]{1,0:T(4,128)(2,1)S(1)}, bf16[4,2048]{1,0:T(4,128)(2,1)S(1)}, u32[]{:S(2)}, u32[]{:S(2)}) collective-permute-start(bf16[4,2048]{1,0:T(4,128)(2,1)S(1)} %get-tuple-element.24), channel_id=1, source_target_pairs={{0,2},{1,3},{2,0},{3,1},{4,6},{5,7},{6,4},{7,5},{8,10},{9,11},{10,... | collective-permute-start | bytes 49160 | tf_op jit(solution)/shard_map/ppermute | solution.py:20
  27.4 0.9 %collective-permute-start.8 = (bf16[4,2048]{1,0:T(4,128)(2,1)S(1)}, bf16[4,2048]{1,0:T(4,128)(2,1)S(1)}, u32[]{:S(2)}, u32[]{:S(2)}) collective-permute-start(bf16[4,2048]{1,0:T(4,128)(2,1)S(1)} %get-tuple-element.25), channel_id=1, source_target_pairs={{0,3},{1,2},{2,1},{3,0},{4,7},{5,6},{6,5},{7,4},{8,11},{9,10},{10,... | collective-permute-start | bytes 49160 | tf_op jit(solution)/shard_map/ppermute | solution.py:20
  28.3 1.1 %collective-permute-start.9 = (bf16[4,2048]{1,0:T(4,128)(2,1)S(1)}, bf16[4,2048]{1,0:T(4,128)(2,1)S(1)}, u32[]{:S(2)}, u32[]{:S(2)}) collective-permute-start(bf16[4,2048]{1,0:T(4,128)(2,1)S(1)} %get-tuple-element.26), channel_id=1, source_target_pairs={{0,1},{1,0},{2,3},{3,2},{4,5},{5,4},{6,7},{7,6},{8,9},{9,8},{10,11... | collective-permute-start | bytes 49160 | tf_op jit(solution)/shard_map/ppermute | solution.py:20
  29.4 1.1 %collective-permute-done.7 = bf16[4,2048]{1,0:T(4,128)(2,1)S(1)} collective-permute-done((bf16[4,2048]{1,0:T(4,128)(2,1)S(1)}, bf16[4,2048]{1,0:T(4,128)(2,1)S(1)}, u32[]{:S(2)}, u32[]{:S(2)}) %collective-permute-start.7) | collective-permute-done | bytes 16416 | tf_op jit(solution)/shard_map/ppermute | solution.py:20
  30.5 2.4 %collective-permute-done.8 = bf16[4,2048]{1,0:T(4,128)(2,1)S(1)} collective-permute-done((bf16[4,2048]{1,0:T(4,128)(2,1)S(1)}, bf16[4,2048]{1,0:T(4,128)(2,1)S(1)}, u32[]{:S(2)}, u32[]{:S(2)}) %collective-permute-start.8) | collective-permute-done | bytes 16416 | tf_op jit(solution)/shard_map/ppermute | solution.py:20
  32.9 0.6 %add_convert_fusion = bf16[4,2048]{1,0:T(4,128)(2,1)} fusion(bf16[4,2048]{1,0:T(4,128)(2,1)S(1)} %collective-permute-done.9, bf16[4,2048]{1,0:T(4,128)(2,1)S(1)} %collective-permute-done.8, f32[4,2048]{1,0:T(4,128)S(1)} %get-tuple-element.23, bf16[4,2048]{1,0:T(4,128)(2,1)S(1)} %collective-permute-done.7), kind=kLoop, calls=%fused_computation | loop fusion | flops 57344 | bytes 98304 | tf_op jit(solution)/shard_map/convert_element_type | solution.py:478
  (29 shorter events, 0.1 us)
Async XLA Ops:
  0.0 9.7 %copy-start.2 = (bf16[2048,256]{1,0:T(8,128)(2,1)S(1)}, bf16[2048,256]{1,0:T(8,128)(2,1)}, u32[]{:S(2)}) copy-start(bf16[2048,256]{1,0:T(8,128)(2,1)} %refs_7_.1) | copy-start | bytes 3145732
  0.0 9.7 %copy-start.1 = (bf16[2048,256]{1,0:T(8,128)(2,1)S(1)}, bf16[2048,256]{1,0:T(8,128)(2,1)}, u32[]{:S(2)}) copy-start(bf16[2048,256]{1,0:T(8,128)(2,1)} %refs_6_.1) | copy-start | bytes 3145732
  0.0 9.7 %copy-start.3 = (bf16[2048]{0:T(1024)(128)(2,1)S(1)}, bf16[2048]{0:T(1024)(128)(2,1)}, u32[]{:S(2)}) copy-start(bf16[2048]{0:T(1024)(128)(2,1)} %refs_4_.1) | copy-start | bytes 12292
  0.0 9.7 %copy-start = (bf16[2048,2048]{1,0:T(8,128)(2,1)S(1)}, bf16[2048,2048]{1,0:T(8,128)(2,1)}, u32[]{:S(2)}) copy-start(bf16[2048,2048]{1,0:T(8,128)(2,1)} %refs_5_.1) | copy-start | bytes 25165828
  1.2 5.4 %collective-permute-start.2 = (bf16[4,2176]{1,0:T(4,128)(2,1)S(1)}, bf16[4,2176]{1,0:T(4,128)(2,1)S(1)}, u32[]{:S(2)}, u32[]{:S(2)}) collective-permute-start(bf16[4,2176]{1,0:T(4,128)(2,1)S(1)} %get-tuple-element.19), channel_id=1, source_target_pairs={{0,6},{1,7},{2,4},{3,5},{4,2},{5,3},{6,0},{7,1},{8,14},{9,15},{10,... | collective-permute-start | bytes 52232 | tf_op jit(solution)/shard_map/ppermute | solution.py:31
  4.7 5.0 %collective-permute-start.1 = (bf16[4,2176]{1,0:T(4,128)(2,1)S(1)}, bf16[4,2176]{1,0:T(4,128)(2,1)S(1)}, u32[]{:S(2)}, u32[]{:S(2)}) collective-permute-start(bf16[4,2176]{1,0:T(4,128)(2,1)S(1)} %get-tuple-element.19), channel_id=1, source_target_pairs={{0,7},{1,6},{2,5},{3,4},{4,3},{5,2},{6,1},{7,0},{8,15},{9,14},{10,... | collective-permute-start | bytes 52232 | tf_op jit(solution)/shard_map/ppermute | solution.py:31
  6.4 3.4 %collective-permute-start = (bf16[4,2176]{1,0:T(4,128)(2,1)S(1)}, bf16[4,2176]{1,0:T(4,128)(2,1)S(1)}, u32[]{:S(2)}, u32[]{:S(2)}) collective-permute-start(bf16[4,2176]{1,0:T(4,128)(2,1)S(1)} %get-tuple-element.19), channel_id=1, source_target_pairs={{0,5},{1,4},{2,7},{3,6},{4,1},{5,0},{6,3},{7,2},{8,13},{9,12},{10,... | collective-permute-start | bytes 52232 | tf_op jit(solution)/shard_map/ppermute | solution.py:31
  11.3 3.4 %copy-start.4 = (bf16[48,2,128,128]{3,2,1,0:T(8,128)(2,1)S(1)}, bf16[48,2,128,128]{3,2,1,0:T(8,128)(2,1)}, u32[]{:S(2)}) copy-start(bf16[48,2,128,128]{3,2,1,0:T(8,128)(2,1)} %key_ref.1) | copy-start | bytes 9437188
  11.3 3.4 %copy-start.6 = (s32[8,24]{1,0:T(8,128)S(1)}, s32[8,24]{1,0:T(8,128)}, u32[]{:S(2)}) copy-start(s32[8,24]{1,0:T(8,128)} %table_ref.1) | copy-start | bytes 2308
  11.3 3.4 %copy-start.7 = (s32[8,8]{1,0:T(8,128)S(1)}, s32[8,8]{1,0:T(8,128)}, u32[]{:S(2)}) copy-start(s32[8,8]{1,0:T(8,128)} %list_ref.1) | copy-start | bytes 772
  11.3 3.4 %copy-start.8 = (s32[8]{0:T(128)S(1)}, s32[8]{0:T(128)}, u32[]{:S(2)}) copy-start(s32[8]{0:T(128)} %lengths_ref.1) | copy-start | bytes 100
  11.4 1.8 %collective-permute-start.3 = (f32[320,128]{1,0:T(8,128)S(1)}, f32[320,128]{1,0:T(8,128)S(1)}, u32[]{:S(2)}, u32[]{:S(2)}) collective-permute-start(f32[320,128]{1,0:T(8,128)S(1)} %project.1.own_ref), channel_id=1, source_target_pairs={{0,4},{4,0},{8,12},{12,8},{1,5},{5,1},{9,13},{13,9},{2,6},{6,2},{1... | collective-permute-start | bytes 491528 | tf_op jit(solution)/shard_map/ppermute | solution.py:20
  13.2 4.4 %copy-start.5 = (bf16[48,2,128,128]{3,2,1,0:T(8,128)(2,1)S(1)}, bf16[48,2,128,128]{3,2,1,0:T(8,128)(2,1)}, u32[]{:S(2)}) copy-start(bf16[48,2,128,128]{3,2,1,0:T(8,128)(2,1)} %value_ref.1) | copy-start | bytes 9437188
  13.2 4.4 %collective-permute-start.4 = (f16[320,128]{1,0:T(8,128)(2,1)S(1)}, f16[320,128]{1,0:T(8,128)(2,1)S(1)}, u32[]{:S(2)}, u32[]{:S(2)}) collective-permute-start(f16[320,128]{1,0:T(8,128)(2,1)S(1)} %convert_element_type.18), channel_id=1, source_target_pairs={{0,12},{4,8},{8,4},{12,0},{1,13},{5,9},{9,5},{13,1},{2,14},{6,10},... | collective-permute-start | bytes 245768 | tf_op jit(solution)/shard_map/ppermute | solution.py:20
  17.6 7.0 %slice-start = ((s8[8388608]{0:T(1024)(128)(4,1)}), s8[4194304]{0:T(1024)(128)(4,1)S(1)}, s32[]{:S(2)}) async-start(s8[8388608]{0:T(1024)(128)(4,1)} %bitcast), calls=%async_computation | async-start | bytes 8388608
  18.8 5.8 %slice-start.1 = ((s8[8388608]{0:T(1024)(128)(4,1)}), s8[4194304]{0:T(1024)(128)(4,1)S(1)}, s32[]{:S(2)}) async-start(s8[8388608]{0:T(1024)(128)(4,1)} %bitcast), calls=%async_computation.1 | async-start | bytes 8388608
  18.8 1.4 %collective-permute-start.5 = (f32[264,128]{1,0:T(8,128)S(1)}, f32[264,128]{1,0:T(8,128)S(1)}, u32[]{:S(2)}, u32[]{:S(2)}) collective-permute-start(f32[264,128]{1,0:T(8,128)S(1)} %attend.1.own_ref), channel_id=1, source_target_pairs={{0,4},{4,0},{8,12},{12,8},{1,5},{5,1},{9,13},{13,9},{2,6},{6,2},{1... | collective-permute-start | bytes 405512 | tf_op jit(solution)/shard_map/ppermute | solution.py:20
  20.4 4.2 %collective-permute-start.6 = (bf16[272,128]{1,0:T(8,128)(2,1)S(1)}, bf16[272,128]{1,0:T(8,128)(2,1)S(1)}, u32[]{:S(2)}, u32[]{:S(2)}) collective-permute-start(bf16[272,128]{1,0:T(8,128)(2,1)S(1)} %get-tuple-element.22), channel_id=1, source_target_pairs={{0,12},{4,8},{8,4},{12,0},{1,13},{5,9},{9,5},{13,1},{2,14},{6,10},... | collective-permute-start | bytes 208904 | tf_op jit(solution)/shard_map/ppermute | solution.py:20
  25.9 4.6 %collective-permute-start.7 = (bf16[4,2048]{1,0:T(4,128)(2,1)S(1)}, bf16[4,2048]{1,0:T(4,128)(2,1)S(1)}, u32[]{:S(2)}, u32[]{:S(2)}) collective-permute-start(bf16[4,2048]{1,0:T(4,128)(2,1)S(1)} %get-tuple-element.24), channel_id=1, source_target_pairs={{0,2},{1,3},{2,0},{3,1},{4,6},{5,7},{6,4},{7,5},{8,10},{9,11},{10,... | collective-permute-start | bytes 49160 | tf_op jit(solution)/shard_map/ppermute | solution.py:20
  27.4 5.5 %collective-permute-start.8 = (bf16[4,2048]{1,0:T(4,128)(2,1)S(1)}, bf16[4,2048]{1,0:T(4,128)(2,1)S(1)}, u32[]{:S(2)}, u32[]{:S(2)}) collective-permute-start(bf16[4,2048]{1,0:T(4,128)(2,1)S(1)} %get-tuple-element.25), channel_id=1, source_target_pairs={{0,3},{1,2},{2,1},{3,0},{4,7},{5,6},{6,5},{7,4},{8,11},{9,10},{10,... | collective-permute-start | bytes 49160 | tf_op jit(solution)/shard_map/ppermute | solution.py:20
  28.3 4.6 %collective-permute-start.9 = (bf16[4,2048]{1,0:T(4,128)(2,1)S(1)}, bf16[4,2048]{1,0:T(4,128)(2,1)S(1)}, u32[]{:S(2)}, u32[]{:S(2)}) collective-permute-start(bf16[4,2048]{1,0:T(4,128)(2,1)S(1)} %get-tuple-element.26), channel_id=1, source_target_pairs={{0,1},{1,0},{2,3},{3,2},{4,5},{5,4},{6,7},{7,6},{8,9},{9,8},{10,11... | collective-permute-start | bytes 49160 | tf_op jit(solution)/shard_map/ppermute | solution.py:20

commit v7 on v6

--- a/solution.py
+++ b/solution.py
@@ -48,18 +48,16 @@
     copy = pltpu.make_async_copy(hidden_hbm, hidden_ref, sem)
     copy.start()
     copy.wait()
-    cols = own_ref.shape[1] - LANES
+    cols = own_ref.shape[1] - 3 * LANES
     mem = lax.axis_index("mem")
     hidden = hidden_ref[...].astype(jnp.float32)
     factor = lax.rsqrt(jnp.mean(hidden * hidden, axis=-1, keepdims=True) + EPSILON)
-    lane = lax.broadcasted_iota(jnp.int32, (hidden.shape[0], LANES), 1)
-    tail = jnp.zeros((hidden.shape[0], LANES), jnp.float32)
-    for i, piece in enumerate(to_pieces(factor)):
-        tail = jnp.where(lane == i, piece.astype(jnp.float32), tail)
+    wide = jnp.broadcast_to(factor, (hidden.shape[0], LANES))
+    tail = jnp.concatenate(to_pieces(wide), axis=1)
     for ref, index in ((own_ref, mem), (mate_ref, lax.bitwise_xor(mem, 1))):
         start = pl.multiple_of(index * cols, cols)
         ref[:, :cols] = hidden_ref[:, pl.ds(start, cols)]
-        ref[:, cols:] = tail.astype(ref.dtype)
+        ref[:, cols:] = tail
 
 
 def select_body(
@@ -110,13 +108,18 @@
     seen_ref[...] = seen.astype(jnp.float32)
 
 
+def pass_body(in_ref, out_ref):
+    out_ref[...] = in_ref[...]
+
+
 def project_body(places, tile, *refs):
     gain_ref, q_ref, k_ref, v_ref, out_ref = refs[len(places) :]
     chunks = [refs[places.index(i)][...].astype(jnp.float32) for i in range(len(places))]
     rows = jnp.concatenate(chunks, axis=0)
     cols = gain_ref.shape[0]
-    factor = from_pieces([rows[:, cols + i : cols + i + 1] for i in range(3)])
     gain = gain_ref[...].astype(jnp.float32).reshape(1, cols)
+    tail = [rows[:, cols + i * LANES : cols + (i + 1) * LANES] for i in range(3)]
+    factor = jnp.concatenate([from_pieces(tail)] * (cols // LANES), axis=1)
     rows = (rows[:, :cols] * factor * gain).astype(jnp.bfloat16)
     tokens = rows.shape[0]
     heads = q_ref.shape[1] // LANES
@@ -378,12 +381,20 @@
     own, mate = kernel_call(
         norm_body,
         "norm",
-        [jax.ShapeDtypeStruct((chunk, feature_cols + LANES), bf16)] * 2,
+        [jax.ShapeDtypeStruct((chunk, feature_cols + 3 * LANES), bf16)] * 2,
         [pl.BlockSpec(memory_space=pltpu.HBM)],
         2,
-        1e10,
+        1,
         [pltpu.VMEM(hidden.shape, bf16), pltpu.SemaphoreType.DMA],
     )(pltpu.with_memory_space_constraint(hidden, pltpu.HBM))
+    mate = kernel_call(
+        pass_body,
+        "pass",
+        jax.ShapeDtypeStruct(mate.shape, bf16),
+        [IN_VMEM],
+        1,
+        1e10,
+    )(mate)
     distances = [*range(2, head_count), 1]
     gathered = distances[::-1]
     pieces = [own] + [swap_across(mate, d) for d in gathered]

time: 33.7 us -> 33.6 us (level)
  no operation moved by 1% of the time
where the time goes in v7:
time: 33.6 us; the launch traced here: 33.4 us
  starting transfers between devices  13 us (39%)
  waiting for transfers between devices  12.5 us (37%)
  Pallas kernels  6.95 us (21%)
  other arithmetic  0.65 us (2%)
    ppermute x7, waiting for transfers between devices, swap(): return lax.ppermute(array, axis, [(i, i ^ distance) for i in range(count)])  9.35 us
    ppermute x7, starting transfers between devices, swap(): return lax.ppermute(array, axis, [(i, i ^ distance) for i in range(count)])  7.62 us
    ppermute x3, starting transfers between devices, swap_across(): return lax.ppermute(array, ('mem', 'heads'), pairs)  5.4 us
    ppermute x3, waiting for transfers between devices, swap_across(): return lax.ppermute(array, ('mem', 'heads'), pairs)  3.18 us
    pallas_call x1, Pallas kernels, shards(): kernel_call(functools.partial(select_body, chunk, steps, per_kv), 'select...  1.81 us
    pallas_call x1, Pallas kernels, shards(): kernel_call(functools.partial(project_body, (0, *gathered), 512), 'projec...  1.46 us
    pallas_call x1, Pallas kernels, shards(): kernel_call(functools.partial(output_body, query_count, min(512, out_cols...  1.31 us
    pallas_call x1, Pallas kernels, shards(): kernel_call(functools.partial(attend_body, head_dim ** (-0.5), kv_heads *...  1.18 us
  transfers between devices with their start and end apart: 10, of which 7 were waited for; matrix products, arithmetic and copies ran while one was open for 0% of the time, Pallas kernels for 5%

profile of v7, /device:TPU:0, one launch (start us, length us, event | category | flops | bytes accessed | tf_op | source)
XLA Modules:
  0.0 33.4 jit_solution(8277498949302565468)
XLA Ops:
  0.0 1.0 %norm.1 = (bf16[4,2432]{1,0:T(4,128)(2,1)S(1)}, bf16[4,2432]{1,0:T(4,128)(2,1)S(1)}) custom-call(bf16[4,8192]{1,0:T(4,128)(2,1)} %hidden_hbm.1), custom_call_target="tpu_custom_call" | custom-call | flops 1 | bytes 1024 | tf_op jit(solution)/shard_map/norm/pallas_call | solution.py:381
  1.1 3.5 %collective-permute-start.2 = (bf16[4,2432]{1,0:T(4,128)(2,1)S(1)}, bf16[4,2432]{1,0:T(4,128)(2,1)S(1)}, u32[]{:S(2)}, u32[]{:S(2)}) collective-permute-start(bf16[4,2432]{1,0:T(4,128)(2,1)S(1)} %pass.1), channel_id=1, source_target_pairs={{0,6},{1,7},{2,4},{3,5},{4,2},{5,3},{6,0},{7,1},{8,14},{9,15},{10,... | collective-permute-start | bytes 58376 | tf_op jit(solution)/shard_map/ppermute | solution.py:31
  4.6 1.6 %collective-permute-start.1 = (bf16[4,2432]{1,0:T(4,128)(2,1)S(1)}, bf16[4,2432]{1,0:T(4,128)(2,1)S(1)}, u32[]{:S(2)}, u32[]{:S(2)}) collective-permute-start(bf16[4,2432]{1,0:T(4,128)(2,1)S(1)} %pass.1), channel_id=1, source_target_pairs={{0,7},{1,6},{2,5},{3,4},{4,3},{5,2},{6,1},{7,0},{8,15},{9,14},{10,... | collective-permute-start | bytes 58376 | tf_op jit(solution)/shard_map/ppermute | solution.py:31
  6.3 0.2 collective-permute-start
  6.5 3.2 %collective-permute-done.1.refs_2_ = bf16[4,2432]{1,0:T(4,128)(2,1)S(1)} collective-permute-done((bf16[4,2432]{1,0:T(4,128)(2,1)S(1)}, bf16[4,2432]{1,0:T(4,128)(2,1)S(1)}, u32[]{:S(2)}, u32[]{:S(2)}) %collective-permute-start.1) | collective-permute-done | bytes 19488 | tf_op jit(solution)/shard_map/ppermute | solution.py:31
  9.7 1.5 %project.1.own_ref = f32[320,128]{1,0:T(8,128)S(1)} custom-call(bf16[4,2432]{1,0:T(4,128)(2,1)S(1)} %get-tuple-element.18.refs_0_, bf16[4,2432]{1,0:T(4,128)(2,1)S(1)} %collective-permute-done.refs_1_, bf16[4,2432]{1,0:T(4,128)(2,1)S(1)} %collective-permute-done.1.refs_2_, bf16[4,2432]{1,0:T(4,128)(2,1)S(1)} %collective-permute-done.2.refs_3_, ...), custom_call_target="tpu_custom_call" | custom-call | flops 167772160 | bytes 1024 | tf_op jit(solution)/shard_map/project/pallas_call | solution.py:417
  11.2 0.8 %collective-permute-start.3 = (f32[320,128]{1,0:T(8,128)S(1)}, f32[320,128]{1,0:T(8,128)S(1)}, u32[]{:S(2)}, u32[]{:S(2)}) collective-permute-start(f32[320,128]{1,0:T(8,128)S(1)} %project.1.own_ref), channel_id=1, source_target_pairs={{0,4},{4,0},{8,12},{12,8},{1,5},{5,1},{9,13},{13,9},{2,6},{6,2},{1... | collective-permute-start | bytes 491528 | tf_op jit(solution)/shard_map/ppermute | solution.py:20
  12.0 1.0 %collective-permute-done.3.other_ref = f32[320,128]{1,0:T(8,128)S(1)} collective-permute-done((f32[320,128]{1,0:T(8,128)S(1)}, f32[320,128]{1,0:T(8,128)S(1)}, u32[]{:S(2)}, u32[]{:S(2)}) %collective-permute-start.3) | collective-permute-done | bytes 163872 | tf_op jit(solution)/shard_map/ppermute | solution.py:20
  13.1 1.5 %collective-permute-start.4 = (f16[320,128]{1,0:T(8,128)(2,1)S(1)}, f16[320,128]{1,0:T(8,128)(2,1)S(1)}, u32[]{:S(2)}, u32[]{:S(2)}) collective-permute-start(f16[320,128]{1,0:T(8,128)(2,1)S(1)} %convert_element_type.18), channel_id=1, source_target_pairs={{0,12},{4,8},{8,4},{12,0},{1,13},{5,9},{9,5},{13,1},{2,14},{6,10},... | collective-permute-start | bytes 245768 | tf_op jit(solution)/shard_map/ppermute | solution.py:20
  14.6 1.8 %select.1 = (s32[99]{0:T(128)S(4)}, f32[256,128]{1,0:T(8,128)S(1)}, bf16[32,128,256]{2,1,0:T(8,128)(2,1)S(1)}) custom-call(s32[8,24]{1,0:T(8,128)S(1)} %copy-done.5, s32[8,8]{1,0:T(8,128)S(1)} %copy-done.6, s32[8]{0:T(128)S(1)} %copy-done.7, bf16[48,2,128,128]{3,2,1,0:T(8,128)(2,1)S(1)} %copy-done.3), custom_call_target="tpu_custom_call" | custom-call | flops 10000000000 | bytes 1024 | tf_op jit(solution)/shard_map/select/pallas_call | solution.py:402
  16.5 1.0 %collective-permute-done.4 = f16[320,128]{1,0:T(8,128)(2,1)S(1)} collective-permute-done((f16[320,128]{1,0:T(8,128)(2,1)S(1)}, f16[320,128]{1,0:T(8,128)(2,1)S(1)}, u32[]{:S(2)}, u32[]{:S(2)}) %collective-permute-start.4) | collective-permute-done | bytes 81952 | tf_op jit(solution)/shard_map/ppermute | solution.py:20
  17.5 1.2 %attend.1.own_ref = f32[264,128]{1,0:T(8,128)S(1)} custom-call(s32[99]{0:T(128)S(4)} %get-tuple-element.16.chosen_ref, f32[256,128]{1,0:T(8,128)S(1)} %get-tuple-element.17.seen_ref, f32[320,128]{1,0:T(8,128)S(1)} %add.16.own_ref, f32[320,128]{1,0:T(8,128)S(1)} %convert_element_type.19.other_ref, bf16[32,128,256]{2,1,0:T(8,128)(2,1)S(1)} %get-tuple-element.20.turned_ref, ...), custom_call_target="tpu_custom_call" | custom-call | flops 10000000000 | bytes 1024 | tf_op jit(solution)/shard_map/attend/pallas_call | solution.py:440
  18.7 0.3 %collective-permute-start.5 = (f32[264,128]{1,0:T(8,128)S(1)}, f32[264,128]{1,0:T(8,128)S(1)}, u32[]{:S(2)}, u32[]{:S(2)}) collective-permute-start(f32[264,128]{1,0:T(8,128)S(1)} %attend.1.own_ref), channel_id=1, source_target_pairs={{0,4},{4,0},{8,12},{12,8},{1,5},{5,1},{9,13},{13,9},{2,6},{6,2},{1... | collective-permute-start | bytes 405512 | tf_op jit(solution)/shard_map/ppermute | solution.py:20
  19.0 1.1 %collective-permute-done.5.other_ref = f32[264,128]{1,0:T(8,128)S(1)} collective-permute-done((f32[264,128]{1,0:T(8,128)S(1)}, f32[264,128]{1,0:T(8,128)S(1)}, u32[]{:S(2)}, u32[]{:S(2)}) %collective-permute-start.5) | collective-permute-done | bytes 135200 | tf_op jit(solution)/shard_map/ppermute | solution.py:20
  20.1 0.2 combine.1
  20.3 1.4 %collective-permute-start.6 = (bf16[272,128]{1,0:T(8,128)(2,1)S(1)}, bf16[272,128]{1,0:T(8,128)(2,1)S(1)}, u32[]{:S(2)}, u32[]{:S(2)}) collective-permute-start(bf16[272,128]{1,0:T(8,128)(2,1)S(1)} %get-tuple-element.22), channel_id=1, source_target_pairs={{0,12},{4,8},{8,4},{12,0},{1,13},{5,9},{9,5},{13,1},{2,14},{6,10},... | collective-permute-start | bytes 208904 | tf_op jit(solution)/shard_map/ppermute | solution.py:20
  21.7 2.7 %collective-permute-done.6.other_ref = bf16[272,128]{1,0:T(8,128)(2,1)S(1)} collective-permute-done((bf16[272,128]{1,0:T(8,128)(2,1)S(1)}, bf16[272,128]{1,0:T(8,128)(2,1)S(1)}, u32[]{:S(2)}, u32[]{:S(2)}) %collective-permute-start.6) | collective-permute-done | bytes 69664 | tf_op jit(solution)/shard_map/ppermute | solution.py:20
  24.4 1.3 %output.1 = (f32[4,2048]{1,0:T(4,128)S(1)}, bf16[4,2048]{1,0:T(4,128)(2,1)S(1)}, bf16[4,2048]{1,0:T(4,128)(2,1)S(1)}, bf16[4,2048]{1,0:T(4,128)(2,1)S(1)}) custom-call(f32[264,128]{1,0:T(8,128)S(1)} %get-tuple-element.21.own_ref, bf16[272,128]{1,0:T(8,128)(2,1)S(1)} %collective-permute-done.6.other_ref, bf16[2048,2048]{1,0:T(8,128)(2,1)S(1)} %bitcast.1), custom_call_target="tpu_custom_call" | custom-call | flops 134217728 | bytes 1024 | tf_op jit(solution)/shard_map/output/pallas_call | solution.py:477
  25.7 1.5 %collective-permute-start.7 = (bf16[4,2048]{1,0:T(4,128)(2,1)S(1)}, bf16[4,2048]{1,0:T(4,128)(2,1)S(1)}, u32[]{:S(2)}, u32[]{:S(2)}) collective-permute-start(bf16[4,2048]{1,0:T(4,128)(2,1)S(1)} %get-tuple-element.24), channel_id=1, source_target_pairs={{0,2},{1,3},{2,0},{3,1},{4,6},{5,7},{6,4},{7,5},{8,10},{9,11},{10,... | collective-permute-start | bytes 49160 | tf_op jit(solution)/shard_map/ppermute | solution.py:20
  27.2 0.9 %collective-permute-start.8 = (bf16[4,2048]{1,0:T(4,128)(2,1)S(1)}, bf16[4,2048]{1,0:T(4,128)(2,1)S(1)}, u32[]{:S(2)}, u32[]{:S(2)}) collective-permute-start(bf16[4,2048]{1,0:T(4,128)(2,1)S(1)} %get-tuple-element.25), channel_id=1, source_target_pairs={{0,3},{1,2},{2,1},{3,0},{4,7},{5,6},{6,5},{7,4},{8,11},{9,10},{10,... | collective-permute-start | bytes 49160 | tf_op jit(solution)/shard_map/ppermute | solution.py:20
  28.2 1.1 %collective-permute-start.9 = (bf16[4,2048]{1,0:T(4,128)(2,1)S(1)}, bf16[4,2048]{1,0:T(4,128)(2,1)S(1)}, u32[]{:S(2)}, u32[]{:S(2)}) collective-permute-start(bf16[4,2048]{1,0:T(4,128)(2,1)S(1)} %get-tuple-element.26), channel_id=1, source_target_pairs={{0,1},{1,0},{2,3},{3,2},{4,5},{5,4},{6,7},{7,6},{8,9},{9,8},{10,11... | collective-permute-start | bytes 49160 | tf_op jit(solution)/shard_map/ppermute | solution.py:20
  29.2 1.1 %collective-permute-done.7 = bf16[4,2048]{1,0:T(4,128)(2,1)S(1)} collective-permute-done((bf16[4,2048]{1,0:T(4,128)(2,1)S(1)}, bf16[4,2048]{1,0:T(4,128)(2,1)S(1)}, u32[]{:S(2)}, u32[]{:S(2)}) %collective-permute-start.7) | collective-permute-done | bytes 16416 | tf_op jit(solution)/shard_map/ppermute | solution.py:20
  30.4 2.4 %collective-permute-done.8 = bf16[4,2048]{1,0:T(4,128)(2,1)S(1)} collective-permute-done((bf16[4,2048]{1,0:T(4,128)(2,1)S(1)}, bf16[4,2048]{1,0:T(4,128)(2,1)S(1)}, u32[]{:S(2)}, u32[]{:S(2)}) %collective-permute-start.8) | collective-permute-done | bytes 16416 | tf_op jit(solution)/shard_map/ppermute | solution.py:20
  32.8 0.6 %add_convert_fusion = bf16[4,2048]{1,0:T(4,128)(2,1)} fusion(bf16[4,2048]{1,0:T(4,128)(2,1)S(1)} %collective-permute-done.9, bf16[4,2048]{1,0:T(4,128)(2,1)S(1)} %collective-permute-done.8, f32[4,2048]{1,0:T(4,128)S(1)} %get-tuple-element.23, bf16[4,2048]{1,0:T(4,128)(2,1)S(1)} %collective-permute-done.7), kind=kLoop, calls=%fused_computation | loop fusion | flops 57344 | bytes 98304 | tf_op jit(solution)/shard_map/convert_element_type | solution.py:489
  (33 shorter events, 0.1 us)
Async XLA Ops:
  1.0 8.7 %slice-start.2 = ((s8[8388608]{0:T(1024)(128)(4,1)}), s8[4194304]{0:T(1024)(128)(4,1)S(1)}, s32[]{:S(2)}) async-start(s8[8388608]{0:T(1024)(128)(4,1)} %bitcast.2), calls=%async_computation.2 | async-start | bytes 8388608
  1.0 8.6 %slice-start.3 = ((s8[8388608]{0:T(1024)(128)(4,1)}), s8[4194304]{0:T(1024)(128)(4,1)S(1)}, s32[]{:S(2)}) async-start(s8[8388608]{0:T(1024)(128)(4,1)} %bitcast.2), calls=%async_computation.3 | async-start | bytes 8388608
  1.0 8.6 %copy-start = (bf16[2048,256]{1,0:T(8,128)(2,1)S(1)}, bf16[2048,256]{1,0:T(8,128)(2,1)}, u32[]{:S(2)}) copy-start(bf16[2048,256]{1,0:T(8,128)(2,1)} %refs_6_.1) | copy-start | bytes 3145732
  1.1 8.6 %copy-start.1 = (bf16[2048,256]{1,0:T(8,128)(2,1)S(1)}, bf16[2048,256]{1,0:T(8,128)(2,1)}, u32[]{:S(2)}) copy-start(bf16[2048,256]{1,0:T(8,128)(2,1)} %refs_7_.1) | copy-start | bytes 3145732
  1.1 8.6 %copy-start.2 = (bf16[2048]{0:T(1024)(128)(2,1)S(1)}, bf16[2048]{0:T(1024)(128)(2,1)}, u32[]{:S(2)}) copy-start(bf16[2048]{0:T(1024)(128)(2,1)} %refs_4_.1) | copy-start | bytes 12292
  1.1 5.4 %collective-permute-start.2 = (bf16[4,2432]{1,0:T(4,128)(2,1)S(1)}, bf16[4,2432]{1,0:T(4,128)(2,1)S(1)}, u32[]{:S(2)}, u32[]{:S(2)}) collective-permute-start(bf16[4,2432]{1,0:T(4,128)(2,1)S(1)} %pass.1), channel_id=1, source_target_pairs={{0,6},{1,7},{2,4},{3,5},{4,2},{5,3},{6,0},{7,1},{8,14},{9,15},{10,... | collective-permute-start | bytes 58376 | tf_op jit(solution)/shard_map/ppermute | solution.py:31
  4.6 5.0 %collective-permute-start.1 = (bf16[4,2432]{1,0:T(4,128)(2,1)S(1)}, bf16[4,2432]{1,0:T(4,128)(2,1)S(1)}, u32[]{:S(2)}, u32[]{:S(2)}) collective-permute-start(bf16[4,2432]{1,0:T(4,128)(2,1)S(1)} %pass.1), channel_id=1, source_target_pairs={{0,7},{1,6},{2,5},{3,4},{4,3},{5,2},{6,1},{7,0},{8,15},{9,14},{10,... | collective-permute-start | bytes 58376 | tf_op jit(solution)/shard_map/ppermute | solution.py:31
  6.3 3.4 %collective-permute-start = (bf16[4,2432]{1,0:T(4,128)(2,1)S(1)}, bf16[4,2432]{1,0:T(4,128)(2,1)S(1)}, u32[]{:S(2)}, u32[]{:S(2)}) collective-permute-start(bf16[4,2432]{1,0:T(4,128)(2,1)S(1)} %pass.1), channel_id=1, source_target_pairs={{0,5},{1,4},{2,7},{3,6},{4,1},{5,0},{6,3},{7,2},{8,13},{9,12},{10,... | collective-permute-start | bytes 58376 | tf_op jit(solution)/shard_map/ppermute | solution.py:31
  11.2 3.4 %copy-start.3 = (bf16[48,2,128,128]{3,2,1,0:T(8,128)(2,1)S(1)}, bf16[48,2,128,128]{3,2,1,0:T(8,128)(2,1)}, u32[]{:S(2)}) copy-start(bf16[48,2,128,128]{3,2,1,0:T(8,128)(2,1)} %key_ref.1) | copy-start | bytes 9437188
  11.2 3.4 %copy-start.5 = (s32[8,24]{1,0:T(8,128)S(1)}, s32[8,24]{1,0:T(8,128)}, u32[]{:S(2)}) copy-start(s32[8,24]{1,0:T(8,128)} %table_ref.1) | copy-start | bytes 2308
  11.2 3.4 %copy-start.6 = (s32[8,8]{1,0:T(8,128)S(1)}, s32[8,8]{1,0:T(8,128)}, u32[]{:S(2)}) copy-start(s32[8,8]{1,0:T(8,128)} %list_ref.1) | copy-start | bytes 772
  11.2 3.4 %copy-start.7 = (s32[8]{0:T(128)S(1)}, s32[8]{0:T(128)}, u32[]{:S(2)}) copy-start(s32[8]{0:T(128)} %lengths_ref.1) | copy-start | bytes 100
  11.2 1.8 %collective-permute-start.3 = (f32[320,128]{1,0:T(8,128)S(1)}, f32[320,128]{1,0:T(8,128)S(1)}, u32[]{:S(2)}, u32[]{:S(2)}) collective-permute-start(f32[320,128]{1,0:T(8,128)S(1)} %project.1.own_ref), channel_id=1, source_target_pairs={{0,4},{4,0},{8,12},{12,8},{1,5},{5,1},{9,13},{13,9},{2,6},{6,2},{1... | collective-permute-start | bytes 491528 | tf_op jit(solution)/shard_map/ppermute | solution.py:20
  13.1 4.4 %copy-start.4 = (bf16[48,2,128,128]{3,2,1,0:T(8,128)(2,1)S(1)}, bf16[48,2,128,128]{3,2,1,0:T(8,128)(2,1)}, u32[]{:S(2)}) copy-start(bf16[48,2,128,128]{3,2,1,0:T(8,128)(2,1)} %value_ref.1) | copy-start | bytes 9437188
  13.1 4.4 %collective-permute-start.4 = (f16[320,128]{1,0:T(8,128)(2,1)S(1)}, f16[320,128]{1,0:T(8,128)(2,1)S(1)}, u32[]{:S(2)}, u32[]{:S(2)}) collective-permute-start(f16[320,128]{1,0:T(8,128)(2,1)S(1)} %convert_element_type.18), channel_id=1, source_target_pairs={{0,12},{4,8},{8,4},{12,0},{1,13},{5,9},{9,5},{13,1},{2,14},{6,10},... | collective-permute-start | bytes 245768 | tf_op jit(solution)/shard_map/ppermute | solution.py:20
  17.5 7.0 %slice-start = ((s8[8388608]{0:T(1024)(128)(4,1)}), s8[4194304]{0:T(1024)(128)(4,1)S(1)}, s32[]{:S(2)}) async-start(s8[8388608]{0:T(1024)(128)(4,1)} %bitcast), calls=%async_computation | async-start | bytes 8388608
  18.7 5.8 %slice-start.1 = ((s8[8388608]{0:T(1024)(128)(4,1)}), s8[4194304]{0:T(1024)(128)(4,1)S(1)}, s32[]{:S(2)}) async-start(s8[8388608]{0:T(1024)(128)(4,1)} %bitcast), calls=%async_computation.1 | async-start | bytes 8388608
  18.7 1.4 %collective-permute-start.5 = (f32[264,128]{1,0:T(8,128)S(1)}, f32[264,128]{1,0:T(8,128)S(1)}, u32[]{:S(2)}, u32[]{:S(2)}) collective-permute-start(f32[264,128]{1,0:T(8,128)S(1)} %attend.1.own_ref), channel_id=1, source_target_pairs={{0,4},{4,0},{8,12},{12,8},{1,5},{5,1},{9,13},{13,9},{2,6},{6,2},{1... | collective-permute-start | bytes 405512 | tf_op jit(solution)/shard_map/ppermute | solution.py:20
  20.3 4.2 %collective-permute-start.6 = (bf16[272,128]{1,0:T(8,128)(2,1)S(1)}, bf16[272,128]{1,0:T(8,128)(2,1)S(1)}, u32[]{:S(2)}, u32[]{:S(2)}) collective-permute-start(bf16[272,128]{1,0:T(8,128)(2,1)S(1)} %get-tuple-element.22), channel_id=1, source_target_pairs={{0,12},{4,8},{8,4},{12,0},{1,13},{5,9},{9,5},{13,1},{2,14},{6,10},... | collective-permute-start | bytes 208904 | tf_op jit(solution)/shard_map/ppermute | solution.py:20
  25.7 4.6 %collective-permute-start.7 = (bf16[4,2048]{1,0:T(4,128)(2,1)S(1)}, bf16[4,2048]{1,0:T(4,128)(2,1)S(1)}, u32[]{:S(2)}, u32[]{:S(2)}) collective-permute-start(bf16[4,2048]{1,0:T(4,128)(2,1)S(1)} %get-tuple-element.24), channel_id=1, source_target_pairs={{0,2},{1,3},{2,0},{3,1},{4,6},{5,7},{6,4},{7,5},{8,10},{9,11},{10,... | collective-permute-start | bytes 49160 | tf_op jit(solution)/shard_map/ppermute | solution.py:20
  27.2 5.5 %collective-permute-start.8 = (bf16[4,2048]{1,0:T(4,128)(2,1)S(1)}, bf16[4,2048]{1,0:T(4,128)(2,1)S(1)}, u32[]{:S(2)}, u32[]{:S(2)}) collective-permute-start(bf16[4,2048]{1,0:T(4,128)(2,1)S(1)} %get-tuple-element.25), channel_id=1, source_target_pairs={{0,3},{1,2},{2,1},{3,0},{4,7},{5,6},{6,5},{7,4},{8,11},{9,10},{10,... | collective-permute-start | bytes 49160 | tf_op jit(solution)/shard_map/ppermute | solution.py:20
  28.2 4.6 %collective-permute-start.9 = (bf16[4,2048]{1,0:T(4,128)(2,1)S(1)}, bf16[4,2048]{1,0:T(4,128)(2,1)S(1)}, u32[]{:S(2)}, u32[]{:S(2)}) collective-permute-start(bf16[4,2048]{1,0:T(4,128)(2,1)S(1)} %get-tuple-element.26), channel_id=1, source_target_pairs={{0,1},{1,0},{2,3},{3,2},{4,5},{5,4},{6,7},{7,6},{8,9},{9,8},{10,11... | collective-permute-start | bytes 49160 | tf_op jit(solution)/shard_map/ppermute | solution.py:20

commit v8 on v7

--- a/solution.py
+++ b/solution.py
@@ -1,4 +1,5 @@
 import functools
+import math
 
 import jax
 import jax.numpy as jnp
@@ -139,10 +140,25 @@
                 head += 1
 
 
-def add_body(own_ref, other_ref, out_ref, *sent_refs):
+def add_body(values, own_ref, other_ref, out_ref, *sent_refs):
     total = own_ref[...] + other_ref[...]
-    for ref in (out_ref, *sent_refs):
-        ref[...] = total.astype(ref.dtype)
+    out_ref[...] = total
+    for ref in sent_refs:
+        height = total.shape[0]
+        top = jnp.max(jnp.abs(total[height - values :]), axis=0, keepdims=True)
+        top = jnp.maximum(jnp.max(top, axis=1, keepdims=True), 1e-30)
+        exponent = jnp.ceil(jnp.log(top) * (1 / math.log(2)))
+        ref[: height - values] = total[: height - values]
+        ref[height - values : height] = total[height - values :] * jnp.exp2(-exponent)
+        ref[height:] = jnp.broadcast_to(exponent, (ref.shape[0] - height, LANES))
+
+
+def add_sent(own_ref, sent_ref, values):
+    height = own_ref.shape[0]
+    scale = jnp.exp2(sent_ref[height : height + 1])
+    sent_values = sent_ref[height - values : height] * scale
+    sent = jnp.concatenate([sent_ref[: height - values], sent_values], axis=0)
+    return own_ref[...] + sent
 
 
 def split_dot(weights, values):
@@ -216,7 +232,8 @@
     height = row_count * row_height
     contract_last = (((1,), (1,)), ((), ()))
 
-    projected = (own_ref[...] + other_ref[...]).astype(jnp.bfloat16)
+    values = (own_ref.shape[0] - height) // 2
+    projected = add_sent(own_ref, other_ref, values).astype(jnp.bfloat16)
     queries = projected[:height]
     query_ref[...] = queries.reshape(query_ref.shape)
     fresh = projected[height:]
@@ -425,10 +442,13 @@
     sent = summed
     distance = 1
     while 2 * distance < mem_count:
+        outs = [jax.ShapeDtypeStruct(summed.shape, f32)]
+        if 4 * distance == mem_count:
+            outs.append(jax.ShapeDtypeStruct((summed.shape[0] + 16, LANES), f32))
         added = kernel_call(
-            add_body,
+            functools.partial(add_body, kv_heads * token_count),
             "add",
-            [jax.ShapeDtypeStruct(summed.shape, f32)],
+            outs,
             [IN_VMEM] * 2,
             2,
             1e10,

time: 33.6 us -> 33.8 us (level)
  no operation moved by 1% of the time
where the time goes in v8:
time: 33.8 us; the launch traced here: 33.6 us
  starting transfers between devices  13 us (38%)
  waiting for transfers between devices  12.6 us (37%)
  Pallas kernels  7.05 us (21%)
  other arithmetic  0.66 us (2%)
    ppermute x7, waiting for transfers between devices, swap(): return lax.ppermute(array, axis, [(i, i ^ distance) for i in range(count)])  9.43 us
    ppermute x7, starting transfers between devices, swap(): return lax.ppermute(array, axis, [(i, i ^ distance) for i in range(count)])  7.62 us
    ppermute x3, starting transfers between devices, swap_across(): return lax.ppermute(array, ('mem', 'heads'), pairs)  5.4 us
    ppermute x3, waiting for transfers between devices, swap_across(): return lax.ppermute(array, ('mem', 'heads'), pairs)  3.18 us
    pallas_call x1, Pallas kernels, shards(): kernel_call(functools.partial(select_body, chunk, steps, per_kv), 'select...  1.82 us
    pallas_call x1, Pallas kernels, shards(): kernel_call(functools.partial(project_body, (0, *gathered), 512), 'projec...  1.46 us
    pallas_call x1, Pallas kernels, shards(): kernel_call(functools.partial(output_body, query_count, min(512, out_cols...  1.31 us
    pallas_call x1, Pallas kernels, shards(): kernel_call(functools.partial(attend_body, head_dim ** (-0.5), kv_heads *...  1.18 us
  transfers between devices with their start and end apart: 10, of which 7 were waited for; matrix products, arithmetic and copies ran while one was open for 0% of the time, Pallas kernels for 5%

profile of v8, /device:TPU:0, one launch (start us, length us, event | category | flops | bytes accessed | tf_op | source)
XLA Modules:
  0.0 33.6 jit_solution(11050291397529977125)
XLA Ops:
  0.0 1.0 %norm.1 = (bf16[4,2432]{1,0:T(4,128)(2,1)S(1)}, bf16[4,2432]{1,0:T(4,128)(2,1)S(1)}) custom-call(bf16[4,8192]{1,0:T(4,128)(2,1)} %hidden_hbm.1), custom_call_target="tpu_custom_call" | custom-call | flops 1 | bytes 1024 | tf_op jit(solution)/shard_map/norm/pallas_call | solution.py:398
  1.1 3.5 %collective-permute-start.2 = (bf16[4,2432]{1,0:T(4,128)(2,1)S(1)}, bf16[4,2432]{1,0:T(4,128)(2,1)S(1)}, u32[]{:S(2)}, u32[]{:S(2)}) collective-permute-start(bf16[4,2432]{1,0:T(4,128)(2,1)S(1)} %pass.1), channel_id=1, source_target_pairs={{0,6},{1,7},{2,4},{3,5},{4,2},{5,3},{6,0},{7,1},{8,14},{9,15},{10,... | collective-permute-start | bytes 58376 | tf_op jit(solution)/shard_map/ppermute | solution.py:32
  4.6 1.6 %collective-permute-start.1 = (bf16[4,2432]{1,0:T(4,128)(2,1)S(1)}, bf16[4,2432]{1,0:T(4,128)(2,1)S(1)}, u32[]{:S(2)}, u32[]{:S(2)}) collective-permute-start(bf16[4,2432]{1,0:T(4,128)(2,1)S(1)} %pass.1), channel_id=1, source_target_pairs={{0,7},{1,6},{2,5},{3,4},{4,3},{5,2},{6,1},{7,0},{8,15},{9,14},{10,... | collective-permute-start | bytes 58376 | tf_op jit(solution)/shard_map/ppermute | solution.py:32
  6.3 0.2 collective-permute-start
  6.5 3.2 %collective-permute-done.1.refs_2_ = bf16[4,2432]{1,0:T(4,128)(2,1)S(1)} collective-permute-done((bf16[4,2432]{1,0:T(4,128)(2,1)S(1)}, bf16[4,2432]{1,0:T(4,128)(2,1)S(1)}, u32[]{:S(2)}, u32[]{:S(2)}) %collective-permute-start.1) | collective-permute-done | bytes 19488 | tf_op jit(solution)/shard_map/ppermute | solution.py:32
  9.7 1.5 %project.1.own_ref = f32[320,128]{1,0:T(8,128)S(1)} custom-call(bf16[4,2432]{1,0:T(4,128)(2,1)S(1)} %get-tuple-element.20.refs_0_, bf16[4,2432]{1,0:T(4,128)(2,1)S(1)} %collective-permute-done.refs_1_, bf16[4,2432]{1,0:T(4,128)(2,1)S(1)} %collective-permute-done.1.refs_2_, bf16[4,2432]{1,0:T(4,128)(2,1)S(1)} %collective-permute-done.2.refs_3_, ...), custom_call_target="tpu_custom_call" | custom-call | flops 167772160 | bytes 1024 | tf_op jit(solution)/shard_map/project/pallas_call | solution.py:434
  11.2 0.8 %collective-permute-start.3 = (f32[320,128]{1,0:T(8,128)S(1)}, f32[320,128]{1,0:T(8,128)S(1)}, u32[]{:S(2)}, u32[]{:S(2)}) collective-permute-start(f32[320,128]{1,0:T(8,128)S(1)} %project.1.own_ref), channel_id=1, source_target_pairs={{0,4},{4,0},{8,12},{12,8},{1,5},{5,1},{9,13},{13,9},{2,6},{6,2},{1... | collective-permute-start | bytes 491528 | tf_op jit(solution)/shard_map/ppermute | solution.py:21
  12.0 1.0 %collective-permute-done.3.other_ref = f32[320,128]{1,0:T(8,128)S(1)} collective-permute-done((f32[320,128]{1,0:T(8,128)S(1)}, f32[320,128]{1,0:T(8,128)S(1)}, u32[]{:S(2)}, u32[]{:S(2)}) %collective-permute-start.3) | collective-permute-done | bytes 163872 | tf_op jit(solution)/shard_map/ppermute | solution.py:21
  13.2 1.5 %collective-permute-start.4 = (f16[336,128]{1,0:T(8,128)(2,1)S(1)}, f16[336,128]{1,0:T(8,128)(2,1)S(1)}, u32[]{:S(2)}, u32[]{:S(2)}) collective-permute-start(f16[336,128]{1,0:T(8,128)(2,1)S(1)} %convert_element_type.18), channel_id=1, source_target_pairs={{0,12},{4,8},{8,4},{12,0},{1,13},{5,9},{9,5},{13,1},{2,14},{6,10},... | collective-permute-start | bytes 258056 | tf_op jit(solution)/shard_map/ppermute | solution.py:21
  14.7 1.8 %select.1 = (s32[99]{0:T(128)S(4)}, f32[256,128]{1,0:T(8,128)S(1)}, bf16[32,128,256]{2,1,0:T(8,128)(2,1)S(1)}) custom-call(s32[8,24]{1,0:T(8,128)S(1)} %copy-done.5, s32[8,8]{1,0:T(8,128)S(1)} %copy-done.6, s32[8]{0:T(128)S(1)} %copy-done.7, bf16[48,2,128,128]{3,2,1,0:T(8,128)(2,1)S(1)} %copy-done.3), custom_call_target="tpu_custom_call" | custom-call | flops 10000000000 | bytes 1024 | tf_op jit(solution)/shard_map/select/pallas_call | solution.py:419
  16.6 1.1 %collective-permute-done.4 = f16[336,128]{1,0:T(8,128)(2,1)S(1)} collective-permute-done((f16[336,128]{1,0:T(8,128)(2,1)S(1)}, f16[336,128]{1,0:T(8,128)(2,1)S(1)}, u32[]{:S(2)}, u32[]{:S(2)}) %collective-permute-start.4) | collective-permute-done | bytes 86048 | tf_op jit(solution)/shard_map/ppermute | solution.py:21
  17.7 1.2 %attend.1.own_ref = f32[264,128]{1,0:T(8,128)S(1)} custom-call(s32[99]{0:T(128)S(4)} %get-tuple-element.18.chosen_ref, f32[256,128]{1,0:T(8,128)S(1)} %get-tuple-element.19.seen_ref, f32[320,128]{1,0:T(8,128)S(1)} %get-tuple-element.22.own_ref, f32[336,128]{1,0:T(8,128)S(1)} %convert_element_type.19.other_ref, ...), custom_call_target="tpu_custom_call" | custom-call | flops 10000000000 | bytes 1024 | tf_op jit(solution)/shard_map/attend/pallas_call | solution.py:460
  18.9 0.3 %collective-permute-start.5 = (f32[264,128]{1,0:T(8,128)S(1)}, f32[264,128]{1,0:T(8,128)S(1)}, u32[]{:S(2)}, u32[]{:S(2)}) collective-permute-start(f32[264,128]{1,0:T(8,128)S(1)} %attend.1.own_ref), channel_id=1, source_target_pairs={{0,4},{4,0},{8,12},{12,8},{1,5},{5,1},{9,13},{13,9},{2,6},{6,2},{1... | collective-permute-start | bytes 405512 | tf_op jit(solution)/shard_map/ppermute | solution.py:21
  19.2 1.1 %collective-permute-done.5.other_ref = f32[264,128]{1,0:T(8,128)S(1)} collective-permute-done((f32[264,128]{1,0:T(8,128)S(1)}, f32[264,128]{1,0:T(8,128)S(1)}, u32[]{:S(2)}, u32[]{:S(2)}) %collective-permute-start.5) | collective-permute-done | bytes 135200 | tf_op jit(solution)/shard_map/ppermute | solution.py:21
  20.3 0.2 combine.1
  20.5 1.4 %collective-permute-start.6 = (bf16[272,128]{1,0:T(8,128)(2,1)S(1)}, bf16[272,128]{1,0:T(8,128)(2,1)S(1)}, u32[]{:S(2)}, u32[]{:S(2)}) collective-permute-start(bf16[272,128]{1,0:T(8,128)(2,1)S(1)} %get-tuple-element.26), channel_id=1, source_target_pairs={{0,12},{4,8},{8,4},{12,0},{1,13},{5,9},{9,5},{13,1},{2,14},{6,10},... | collective-permute-start | bytes 208904 | tf_op jit(solution)/shard_map/ppermute | solution.py:21
  21.9 2.7 %collective-permute-done.6.other_ref = bf16[272,128]{1,0:T(8,128)(2,1)S(1)} collective-permute-done((bf16[272,128]{1,0:T(8,128)(2,1)S(1)}, bf16[272,128]{1,0:T(8,128)(2,1)S(1)}, u32[]{:S(2)}, u32[]{:S(2)}) %collective-permute-start.6) | collective-permute-done | bytes 69664 | tf_op jit(solution)/shard_map/ppermute | solution.py:21
  24.6 1.3 %output.1 = (f32[4,2048]{1,0:T(4,128)S(1)}, bf16[4,2048]{1,0:T(4,128)(2,1)S(1)}, bf16[4,2048]{1,0:T(4,128)(2,1)S(1)}, bf16[4,2048]{1,0:T(4,128)(2,1)S(1)}) custom-call(f32[264,128]{1,0:T(8,128)S(1)} %get-tuple-element.25.own_ref, bf16[272,128]{1,0:T(8,128)(2,1)S(1)} %collective-permute-done.6.other_ref, bf16[2048,2048]{1,0:T(8,128)(2,1)S(1)} %bitcast.1), custom_call_target="tpu_custom_call" | custom-call | flops 134217728 | bytes 1024 | tf_op jit(solution)/shard_map/output/pallas_call | solution.py:497
  25.9 1.5 %collective-permute-start.7 = (bf16[4,2048]{1,0:T(4,128)(2,1)S(1)}, bf16[4,2048]{1,0:T(4,128)(2,1)S(1)}, u32[]{:S(2)}, u32[]{:S(2)}) collective-permute-start(bf16[4,2048]{1,0:T(4,128)(2,1)S(1)} %get-tuple-element.28), channel_id=1, source_target_pairs={{0,2},{1,3},{2,0},{3,1},{4,6},{5,7},{6,4},{7,5},{8,10},{9,11},{10,... | collective-permute-start | bytes 49160 | tf_op jit(solution)/shard_map/ppermute | solution.py:21
  27.4 0.9 %collective-permute-start.8 = (bf16[4,2048]{1,0:T(4,128)(2,1)S(1)}, bf16[4,2048]{1,0:T(4,128)(2,1)S(1)}, u32[]{:S(2)}, u32[]{:S(2)}) collective-permute-start(bf16[4,2048]{1,0:T(4,128)(2,1)S(1)} %get-tuple-element.29), channel_id=1, source_target_pairs={{0,3},{1,2},{2,1},{3,0},{4,7},{5,6},{6,5},{7,4},{8,11},{9,10},{10,... | collective-permute-start | bytes 49160 | tf_op jit(solution)/shard_map/ppermute | solution.py:21
  28.4 1.1 %collective-permute-start.9 = (bf16[4,2048]{1,0:T(4,128)(2,1)S(1)}, bf16[4,2048]{1,0:T(4,128)(2,1)S(1)}, u32[]{:S(2)}, u32[]{:S(2)}) collective-permute-start(bf16[4,2048]{1,0:T(4,128)(2,1)S(1)} %get-tuple-element.30), channel_id=1, source_target_pairs={{0,1},{1,0},{2,3},{3,2},{4,5},{5,4},{6,7},{7,6},{8,9},{9,8},{10,11... | collective-permute-start | bytes 49160 | tf_op jit(solution)/shard_map/ppermute | solution.py:21
  29.4 1.1 %collective-permute-done.7 = bf16[4,2048]{1,0:T(4,128)(2,1)S(1)} collective-permute-done((bf16[4,2048]{1,0:T(4,128)(2,1)S(1)}, bf16[4,2048]{1,0:T(4,128)(2,1)S(1)}, u32[]{:S(2)}, u32[]{:S(2)}) %collective-permute-start.7) | collective-permute-done | bytes 16416 | tf_op jit(solution)/shard_map/ppermute | solution.py:21
  30.6 2.4 %collective-permute-done.8 = bf16[4,2048]{1,0:T(4,128)(2,1)S(1)} collective-permute-done((bf16[4,2048]{1,0:T(4,128)(2,1)S(1)}, bf16[4,2048]{1,0:T(4,128)(2,1)S(1)}, u32[]{:S(2)}, u32[]{:S(2)}) %collective-permute-start.8) | collective-permute-done | bytes 16416 | tf_op jit(solution)/shard_map/ppermute | solution.py:21
  33.0 0.6 %add_convert_fusion = bf16[4,2048]{1,0:T(4,128)(2,1)} fusion(bf16[4,2048]{1,0:T(4,128)(2,1)S(1)} %collective-permute-done.9, bf16[4,2048]{1,0:T(4,128)(2,1)S(1)} %collective-permute-done.8, f32[4,2048]{1,0:T(4,128)S(1)} %get-tuple-element.27, bf16[4,2048]{1,0:T(4,128)(2,1)S(1)} %collective-permute-done.7), kind=kLoop, calls=%fused_computation | loop fusion | flops 57344 | bytes 98304 | tf_op jit(solution)/shard_map/convert_element_type | solution.py:509
  (33 shorter events, 0.2 us)
Async XLA Ops:
  1.0 8.7 %slice-start.2 = ((s8[8388608]{0:T(1024)(128)(4,1)}), s8[4194304]{0:T(1024)(128)(4,1)S(1)}, s32[]{:S(2)}) async-start(s8[8388608]{0:T(1024)(128)(4,1)} %bitcast.2), calls=%async_computation.2 | async-start | bytes 8388608
  1.0 8.6 %slice-start.3 = ((s8[8388608]{0:T(1024)(128)(4,1)}), s8[4194304]{0:T(1024)(128)(4,1)S(1)}, s32[]{:S(2)}) async-start(s8[8388608]{0:T(1024)(128)(4,1)} %bitcast.2), calls=%async_computation.3 | async-start | bytes 8388608
  1.0 8.6 %copy-start = (bf16[2048,256]{1,0:T(8,128)(2,1)S(1)}, bf16[2048,256]{1,0:T(8,128)(2,1)}, u32[]{:S(2)}) copy-start(bf16[2048,256]{1,0:T(8,128)(2,1)} %refs_6_.1) | copy-start | bytes 3145732
  1.1 8.6 %copy-start.1 = (bf16[2048,256]{1,0:T(8,128)(2,1)S(1)}, bf16[2048,256]{1,0:T(8,128)(2,1)}, u32[]{:S(2)}) copy-start(bf16[2048,256]{1,0:T(8,128)(2,1)} %refs_7_.1) | copy-start | bytes 3145732
  1.1 8.6 %copy-start.2 = (bf16[2048]{0:T(1024)(128)(2,1)S(1)}, bf16[2048]{0:T(1024)(128)(2,1)}, u32[]{:S(2)}) copy-start(bf16[2048]{0:T(1024)(128)(2,1)} %refs_4_.1) | copy-start | bytes 12292
  1.1 5.4 %collective-permute-start.2 = (bf16[4,2432]{1,0:T(4,128)(2,1)S(1)}, bf16[4,2432]{1,0:T(4,128)(2,1)S(1)}, u32[]{:S(2)}, u32[]{:S(2)}) collective-permute-start(bf16[4,2432]{1,0:T(4,128)(2,1)S(1)} %pass.1), channel_id=1, source_target_pairs={{0,6},{1,7},{2,4},{3,5},{4,2},{5,3},{6,0},{7,1},{8,14},{9,15},{10,... | collective-permute-start | bytes 58376 | tf_op jit(solution)/shard_map/ppermute | solution.py:32
  4.6 5.0 %collective-permute-start.1 = (bf16[4,2432]{1,0:T(4,128)(2,1)S(1)}, bf16[4,2432]{1,0:T(4,128)(2,1)S(1)}, u32[]{:S(2)}, u32[]{:S(2)}) collective-permute-start(bf16[4,2432]{1,0:T(4,128)(2,1)S(1)} %pass.1), channel_id=1, source_target_pairs={{0,7},{1,6},{2,5},{3,4},{4,3},{5,2},{6,1},{7,0},{8,15},{9,14},{10,... | collective-permute-start | bytes 58376 | tf_op jit(solution)/shard_map/ppermute | solution.py:32
  6.3 3.4 %collective-permute-start = (bf16[4,2432]{1,0:T(4,128)(2,1)S(1)}, bf16[4,2432]{1,0:T(4,128)(2,1)S(1)}, u32[]{:S(2)}, u32[]{:S(2)}) collective-permute-start(bf16[4,2432]{1,0:T(4,128)(2,1)S(1)} %pass.1), channel_id=1, source_target_pairs={{0,5},{1,4},{2,7},{3,6},{4,1},{5,0},{6,3},{7,2},{8,13},{9,12},{10,... | collective-permute-start | bytes 58376 | tf_op jit(solution)/shard_map/ppermute | solution.py:32
  11.2 3.5 %copy-start.3 = (bf16[48,2,128,128]{3,2,1,0:T(8,128)(2,1)S(1)}, bf16[48,2,128,128]{3,2,1,0:T(8,128)(2,1)}, u32[]{:S(2)}) copy-start(bf16[48,2,128,128]{3,2,1,0:T(8,128)(2,1)} %key_ref.1) | copy-start | bytes 9437188
  11.2 3.5 %copy-start.5 = (s32[8,24]{1,0:T(8,128)S(1)}, s32[8,24]{1,0:T(8,128)}, u32[]{:S(2)}) copy-start(s32[8,24]{1,0:T(8,128)} %table_ref.1) | copy-start | bytes 2308
  11.2 3.5 %copy-start.6 = (s32[8,8]{1,0:T(8,128)S(1)}, s32[8,8]{1,0:T(8,128)}, u32[]{:S(2)}) copy-start(s32[8,8]{1,0:T(8,128)} %list_ref.1) | copy-start | bytes 772
  11.2 3.5 %copy-start.7 = (s32[8]{0:T(128)S(1)}, s32[8]{0:T(128)}, u32[]{:S(2)}) copy-start(s32[8]{0:T(128)} %lengths_ref.1) | copy-start | bytes 100
  11.2 1.8 %collective-permute-start.3 = (f32[320,128]{1,0:T(8,128)S(1)}, f32[320,128]{1,0:T(8,128)S(1)}, u32[]{:S(2)}, u32[]{:S(2)}) collective-permute-start(f32[320,128]{1,0:T(8,128)S(1)} %project.1.own_ref), channel_id=1, source_target_pairs={{0,4},{4,0},{8,12},{12,8},{1,5},{5,1},{9,13},{13,9},{2,6},{6,2},{1... | collective-permute-start | bytes 491528 | tf_op jit(solution)/shard_map/ppermute | solution.py:21
  13.2 4.5 %copy-start.4 = (bf16[48,2,128,128]{3,2,1,0:T(8,128)(2,1)S(1)}, bf16[48,2,128,128]{3,2,1,0:T(8,128)(2,1)}, u32[]{:S(2)}) copy-start(bf16[48,2,128,128]{3,2,1,0:T(8,128)(2,1)} %value_ref.1) | copy-start | bytes 9437188
  13.2 4.4 %collective-permute-start.4 = (f16[336,128]{1,0:T(8,128)(2,1)S(1)}, f16[336,128]{1,0:T(8,128)(2,1)S(1)}, u32[]{:S(2)}, u32[]{:S(2)}) collective-permute-start(f16[336,128]{1,0:T(8,128)(2,1)S(1)} %convert_element_type.18), channel_id=1, source_target_pairs={{0,12},{4,8},{8,4},{12,0},{1,13},{5,9},{9,5},{13,1},{2,14},{6,10},... | collective-permute-start | bytes 258056 | tf_op jit(solution)/shard_map/ppermute | solution.py:21
  17.7 7.0 %slice-start = ((s8[8388608]{0:T(1024)(128)(4,1)}), s8[4194304]{0:T(1024)(128)(4,1)S(1)}, s32[]{:S(2)}) async-start(s8[8388608]{0:T(1024)(128)(4,1)} %bitcast), calls=%async_computation | async-start | bytes 8388608
  18.9 5.8 %slice-start.1 = ((s8[8388608]{0:T(1024)(128)(4,1)}), s8[4194304]{0:T(1024)(128)(4,1)S(1)}, s32[]{:S(2)}) async-start(s8[8388608]{0:T(1024)(128)(4,1)} %bitcast), calls=%async_computation.1 | async-start | bytes 8388608
  18.9 1.4 %collective-permute-start.5 = (f32[264,128]{1,0:T(8,128)S(1)}, f32[264,128]{1,0:T(8,128)S(1)}, u32[]{:S(2)}, u32[]{:S(2)}) collective-permute-start(f32[264,128]{1,0:T(8,128)S(1)} %attend.1.own_ref), channel_id=1, source_target_pairs={{0,4},{4,0},{8,12},{12,8},{1,5},{5,1},{9,13},{13,9},{2,6},{6,2},{1... | collective-permute-start | bytes 405512 | tf_op jit(solution)/shard_map/ppermute | solution.py:21
  20.5 4.2 %collective-permute-start.6 = (bf16[272,128]{1,0:T(8,128)(2,1)S(1)}, bf16[272,128]{1,0:T(8,128)(2,1)S(1)}, u32[]{:S(2)}, u32[]{:S(2)}) collective-permute-start(bf16[272,128]{1,0:T(8,128)(2,1)S(1)} %get-tuple-element.26), channel_id=1, source_target_pairs={{0,12},{4,8},{8,4},{12,0},{1,13},{5,9},{9,5},{13,1},{2,14},{6,10},... | collective-permute-start | bytes 208904 | tf_op jit(solution)/shard_map/ppermute | solution.py:21
  25.9 4.6 %collective-permute-start.7 = (bf16[4,2048]{1,0:T(4,128)(2,1)S(1)}, bf16[4,2048]{1,0:T(4,128)(2,1)S(1)}, u32[]{:S(2)}, u32[]{:S(2)}) collective-permute-start(bf16[4,2048]{1,0:T(4,128)(2,1)S(1)} %get-tuple-element.28), channel_id=1, source_target_pairs={{0,2},{1,3},{2,0},{3,1},{4,6},{5,7},{6,4},{7,5},{8,10},{9,11},{10,... | collective-permute-start | bytes 49160 | tf_op jit(solution)/shard_map/ppermute | solution.py:21
  27.4 5.5 %collective-permute-start.8 = (bf16[4,2048]{1,0:T(4,128)(2,1)S(1)}, bf16[4,2048]{1,0:T(4,128)(2,1)S(1)}, u32[]{:S(2)}, u32[]{:S(2)}) collective-permute-start(bf16[4,2048]{1,0:T(4,128)(2,1)S(1)} %get-tuple-element.29), channel_id=1, source_target_pairs={{0,3},{1,2},{2,1},{3,0},{4,7},{5,6},{6,5},{7,4},{8,11},{9,10},{10,... | collective-permute-start | bytes 49160 | tf_op jit(solution)/shard_map/ppermute | solution.py:21
  28.4 4.6 %collective-permute-start.9 = (bf16[4,2048]{1,0:T(4,128)(2,1)S(1)}, bf16[4,2048]{1,0:T(4,128)(2,1)S(1)}, u32[]{:S(2)}, u32[]{:S(2)}) collective-permute-start(bf16[4,2048]{1,0:T(4,128)(2,1)S(1)} %get-tuple-element.30), channel_id=1, source_target_pairs={{0,1},{1,0},{2,3},{3,2},{4,5},{5,4},{6,7},{7,6},{8,9},{9,8},{10,11... | collective-permute-start | bytes 49160 | tf_op jit(solution)/shard_map/ppermute | solution.py:21

commit v9 on v8

--- a/solution.py
+++ b/solution.py
@@ -146,7 +146,7 @@
     for ref in sent_refs:
         height = total.shape[0]
         top = jnp.max(jnp.abs(total[height - values :]), axis=0, keepdims=True)
-        top = jnp.maximum(jnp.max(top, axis=1, keepdims=True), 1e-30)
+        top = jnp.maximum(top, 1e-30)
         exponent = jnp.ceil(jnp.log(top) * (1 / math.log(2)))
         ref[: height - values] = total[: height - values]
         ref[height - values : height] = total[height - values :] * jnp.exp2(-exponent)

time: 33.8 us -> 33.7 us (level)
  no operation moved by 1% of the time
where the time goes in v9:
time: 33.7 us; the launch traced here: 33.5 us
  starting transfers between devices  13 us (39%)
  waiting for transfers between devices  12.6 us (37%)
  Pallas kernels  6.97 us (21%)
  other arithmetic  0.66 us (2%)
    ppermute x7, waiting for transfers between devices, swap(): return lax.ppermute(array, axis, [(i, i ^ distance) for i in range(count)])  9.42 us
    ppermute x7, starting transfers between devices, swap(): return lax.ppermute(array, axis, [(i, i ^ distance) for i in range(count)])  7.62 us
    ppermute x3, starting transfers between devices, swap_across(): return lax.ppermute(array, ('mem', 'heads'), pairs)  5.4 us
    ppermute x3, waiting for transfers between devices, swap_across(): return lax.ppermute(array, ('mem', 'heads'), pairs)  3.18 us
    pallas_call x1, Pallas kernels, shards(): kernel_call(functools.partial(select_body, chunk, steps, per_kv), 'select...  1.82 us
    pallas_call x1, Pallas kernels, shards(): kernel_call(functools.partial(project_body, (0, *gathered), 512), 'projec...  1.46 us
    pallas_call x1, Pallas kernels, shards(): kernel_call(functools.partial(output_body, query_count, min(512, out_cols...  1.31 us
    pallas_call x1, Pallas kernels, shards(): kernel_call(functools.partial(attend_body, head_dim ** (-0.5), kv_heads *...  1.18 us
  transfers between devices with their start and end apart: 10, of which 7 were waited for; matrix products, arithmetic and copies ran while one was open for 0% of the time, Pallas kernels for 5%

profile of v9, /device:TPU:0, one launch (start us, length us, event | category | flops | bytes accessed | tf_op | source)
XLA Modules:
  0.0 33.5 jit_solution(7134882109089803876)
XLA Ops:
  0.0 1.0 %norm.1 = (bf16[4,2432]{1,0:T(4,128)(2,1)S(1)}, bf16[4,2432]{1,0:T(4,128)(2,1)S(1)}) custom-call(bf16[4,8192]{1,0:T(4,128)(2,1)} %hidden_hbm.1), custom_call_target="tpu_custom_call" | custom-call | flops 1 | bytes 1024 | tf_op jit(solution)/shard_map/norm/pallas_call | solution.py:398
  1.1 3.5 %collective-permute-start.2 = (bf16[4,2432]{1,0:T(4,128)(2,1)S(1)}, bf16[4,2432]{1,0:T(4,128)(2,1)S(1)}, u32[]{:S(2)}, u32[]{:S(2)}) collective-permute-start(bf16[4,2432]{1,0:T(4,128)(2,1)S(1)} %pass.1), channel_id=1, source_target_pairs={{0,6},{1,7},{2,4},{3,5},{4,2},{5,3},{6,0},{7,1},{8,14},{9,15},{10,... | collective-permute-start | bytes 58376 | tf_op jit(solution)/shard_map/ppermute | solution.py:32
  4.6 1.6 %collective-permute-start.1 = (bf16[4,2432]{1,0:T(4,128)(2,1)S(1)}, bf16[4,2432]{1,0:T(4,128)(2,1)S(1)}, u32[]{:S(2)}, u32[]{:S(2)}) collective-permute-start(bf16[4,2432]{1,0:T(4,128)(2,1)S(1)} %pass.1), channel_id=1, source_target_pairs={{0,7},{1,6},{2,5},{3,4},{4,3},{5,2},{6,1},{7,0},{8,15},{9,14},{10,... | collective-permute-start | bytes 58376 | tf_op jit(solution)/shard_map/ppermute | solution.py:32
  6.3 0.2 collective-permute-start
  6.5 3.2 %collective-permute-done.1.refs_2_ = bf16[4,2432]{1,0:T(4,128)(2,1)S(1)} collective-permute-done((bf16[4,2432]{1,0:T(4,128)(2,1)S(1)}, bf16[4,2432]{1,0:T(4,128)(2,1)S(1)}, u32[]{:S(2)}, u32[]{:S(2)}) %collective-permute-start.1) | collective-permute-done | bytes 19488 | tf_op jit(solution)/shard_map/ppermute | solution.py:32
  9.7 1.5 %project.1.own_ref = f32[320,128]{1,0:T(8,128)S(1)} custom-call(bf16[4,2432]{1,0:T(4,128)(2,1)S(1)} %get-tuple-element.20.refs_0_, bf16[4,2432]{1,0:T(4,128)(2,1)S(1)} %collective-permute-done.refs_1_, bf16[4,2432]{1,0:T(4,128)(2,1)S(1)} %collective-permute-done.1.refs_2_, bf16[4,2432]{1,0:T(4,128)(2,1)S(1)} %collective-permute-done.2.refs_3_, ...), custom_call_target="tpu_custom_call" | custom-call | flops 167772160 | bytes 1024 | tf_op jit(solution)/shard_map/project/pallas_call | solution.py:434
  11.2 0.8 %collective-permute-start.3 = (f32[320,128]{1,0:T(8,128)S(1)}, f32[320,128]{1,0:T(8,128)S(1)}, u32[]{:S(2)}, u32[]{:S(2)}) collective-permute-start(f32[320,128]{1,0:T(8,128)S(1)} %project.1.own_ref), channel_id=1, source_target_pairs={{0,4},{4,0},{8,12},{12,8},{1,5},{5,1},{9,13},{13,9},{2,6},{6,2},{1... | collective-permute-start | bytes 491528 | tf_op jit(solution)/shard_map/ppermute | solution.py:21
  12.0 1.0 %collective-permute-done.3.other_ref = f32[320,128]{1,0:T(8,128)S(1)} collective-permute-done((f32[320,128]{1,0:T(8,128)S(1)}, f32[320,128]{1,0:T(8,128)S(1)}, u32[]{:S(2)}, u32[]{:S(2)}) %collective-permute-start.3) | collective-permute-done | bytes 163872 | tf_op jit(solution)/shard_map/ppermute | solution.py:21
  13.1 1.5 %collective-permute-start.4 = (f16[336,128]{1,0:T(8,128)(2,1)S(1)}, f16[336,128]{1,0:T(8,128)(2,1)S(1)}, u32[]{:S(2)}, u32[]{:S(2)}) collective-permute-start(f16[336,128]{1,0:T(8,128)(2,1)S(1)} %convert_element_type.18), channel_id=1, source_target_pairs={{0,12},{4,8},{8,4},{12,0},{1,13},{5,9},{9,5},{13,1},{2,14},{6,10},... | collective-permute-start | bytes 258056 | tf_op jit(solution)/shard_map/ppermute | solution.py:21
  14.7 1.8 %select.1 = (s32[99]{0:T(128)S(4)}, f32[256,128]{1,0:T(8,128)S(1)}, bf16[32,128,256]{2,1,0:T(8,128)(2,1)S(1)}) custom-call(s32[8,24]{1,0:T(8,128)S(1)} %copy-done.5, s32[8,8]{1,0:T(8,128)S(1)} %copy-done.6, s32[8]{0:T(128)S(1)} %copy-done.7, bf16[48,2,128,128]{3,2,1,0:T(8,128)(2,1)S(1)} %copy-done.3), custom_call_target="tpu_custom_call" | custom-call | flops 10000000000 | bytes 1024 | tf_op jit(solution)/shard_map/select/pallas_call | solution.py:419
  16.5 1.1 %collective-permute-done.4 = f16[336,128]{1,0:T(8,128)(2,1)S(1)} collective-permute-done((f16[336,128]{1,0:T(8,128)(2,1)S(1)}, f16[336,128]{1,0:T(8,128)(2,1)S(1)}, u32[]{:S(2)}, u32[]{:S(2)}) %collective-permute-start.4) | collective-permute-done | bytes 86048 | tf_op jit(solution)/shard_map/ppermute | solution.py:21
  17.6 1.2 %attend.1.own_ref = f32[264,128]{1,0:T(8,128)S(1)} custom-call(s32[99]{0:T(128)S(4)} %get-tuple-element.18.chosen_ref, f32[256,128]{1,0:T(8,128)S(1)} %get-tuple-element.19.seen_ref, f32[320,128]{1,0:T(8,128)S(1)} %get-tuple-element.22.own_ref, f32[336,128]{1,0:T(8,128)S(1)} %convert_element_type.19.other_ref, ...), custom_call_target="tpu_custom_call" | custom-call | flops 10000000000 | bytes 1024 | tf_op jit(solution)/shard_map/attend/pallas_call | solution.py:460
  18.8 0.4 %collective-permute-start.5 = (f32[264,128]{1,0:T(8,128)S(1)}, f32[264,128]{1,0:T(8,128)S(1)}, u32[]{:S(2)}, u32[]{:S(2)}) collective-permute-start(f32[264,128]{1,0:T(8,128)S(1)} %attend.1.own_ref), channel_id=1, source_target_pairs={{0,4},{4,0},{8,12},{12,8},{1,5},{5,1},{9,13},{13,9},{2,6},{6,2},{1... | collective-permute-start | bytes 405512 | tf_op jit(solution)/shard_map/ppermute | solution.py:21
  19.2 1.1 %collective-permute-done.5.other_ref = f32[264,128]{1,0:T(8,128)S(1)} collective-permute-done((f32[264,128]{1,0:T(8,128)S(1)}, f32[264,128]{1,0:T(8,128)S(1)}, u32[]{:S(2)}, u32[]{:S(2)}) %collective-permute-start.5) | collective-permute-done | bytes 135200 | tf_op jit(solution)/shard_map/ppermute | solution.py:21
  20.2 0.2 combine.1
  20.4 1.4 %collective-permute-start.6 = (bf16[272,128]{1,0:T(8,128)(2,1)S(1)}, bf16[272,128]{1,0:T(8,128)(2,1)S(1)}, u32[]{:S(2)}, u32[]{:S(2)}) collective-permute-start(bf16[272,128]{1,0:T(8,128)(2,1)S(1)} %get-tuple-element.26), channel_id=1, source_target_pairs={{0,12},{4,8},{8,4},{12,0},{1,13},{5,9},{9,5},{13,1},{2,14},{6,10},... | collective-permute-start | bytes 208904 | tf_op jit(solution)/shard_map/ppermute | solution.py:21
  21.8 2.7 %collective-permute-done.6.other_ref = bf16[272,128]{1,0:T(8,128)(2,1)S(1)} collective-permute-done((bf16[272,128]{1,0:T(8,128)(2,1)S(1)}, bf16[272,128]{1,0:T(8,128)(2,1)S(1)}, u32[]{:S(2)}, u32[]{:S(2)}) %collective-permute-start.6) | collective-permute-done | bytes 69664 | tf_op jit(solution)/shard_map/ppermute | solution.py:21
  24.5 1.3 %output.1 = (f32[4,2048]{1,0:T(4,128)S(1)}, bf16[4,2048]{1,0:T(4,128)(2,1)S(1)}, bf16[4,2048]{1,0:T(4,128)(2,1)S(1)}, bf16[4,2048]{1,0:T(4,128)(2,1)S(1)}) custom-call(f32[264,128]{1,0:T(8,128)S(1)} %get-tuple-element.25.own_ref, bf16[272,128]{1,0:T(8,128)(2,1)S(1)} %collective-permute-done.6.other_ref, bf16[2048,2048]{1,0:T(8,128)(2,1)S(1)} %bitcast.1), custom_call_target="tpu_custom_call" | custom-call | flops 134217728 | bytes 1024 | tf_op jit(solution)/shard_map/output/pallas_call | solution.py:497
  25.9 1.5 %collective-permute-start.7 = (bf16[4,2048]{1,0:T(4,128)(2,1)S(1)}, bf16[4,2048]{1,0:T(4,128)(2,1)S(1)}, u32[]{:S(2)}, u32[]{:S(2)}) collective-permute-start(bf16[4,2048]{1,0:T(4,128)(2,1)S(1)} %get-tuple-element.28), channel_id=1, source_target_pairs={{0,2},{1,3},{2,0},{3,1},{4,6},{5,7},{6,4},{7,5},{8,10},{9,11},{10,... | collective-permute-start | bytes 49160 | tf_op jit(solution)/shard_map/ppermute | solution.py:21
  27.4 0.9 %collective-permute-start.8 = (bf16[4,2048]{1,0:T(4,128)(2,1)S(1)}, bf16[4,2048]{1,0:T(4,128)(2,1)S(1)}, u32[]{:S(2)}, u32[]{:S(2)}) collective-permute-start(bf16[4,2048]{1,0:T(4,128)(2,1)S(1)} %get-tuple-element.29), channel_id=1, source_target_pairs={{0,3},{1,2},{2,1},{3,0},{4,7},{5,6},{6,5},{7,4},{8,11},{9,10},{10,... | collective-permute-start | bytes 49160 | tf_op jit(solution)/shard_map/ppermute | solution.py:21
  28.3 1.1 %collective-permute-start.9 = (bf16[4,2048]{1,0:T(4,128)(2,1)S(1)}, bf16[4,2048]{1,0:T(4,128)(2,1)S(1)}, u32[]{:S(2)}, u32[]{:S(2)}) collective-permute-start(bf16[4,2048]{1,0:T(4,128)(2,1)S(1)} %get-tuple-element.30), channel_id=1, source_target_pairs={{0,1},{1,0},{2,3},{3,2},{4,5},{5,4},{6,7},{7,6},{8,9},{9,8},{10,11... | collective-permute-start | bytes 49160 | tf_op jit(solution)/shard_map/ppermute | solution.py:21
  29.4 1.1 %collective-permute-done.7 = bf16[4,2048]{1,0:T(4,128)(2,1)S(1)} collective-permute-done((bf16[4,2048]{1,0:T(4,128)(2,1)S(1)}, bf16[4,2048]{1,0:T(4,128)(2,1)S(1)}, u32[]{:S(2)}, u32[]{:S(2)}) %collective-permute-start.7) | collective-permute-done | bytes 16416 | tf_op jit(solution)/shard_map/ppermute | solution.py:21
  30.5 2.4 %collective-permute-done.8 = bf16[4,2048]{1,0:T(4,128)(2,1)S(1)} collective-permute-done((bf16[4,2048]{1,0:T(4,128)(2,1)S(1)}, bf16[4,2048]{1,0:T(4,128)(2,1)S(1)}, u32[]{:S(2)}, u32[]{:S(2)}) %collective-permute-start.8) | collective-permute-done | bytes 16416 | tf_op jit(solution)/shard_map/ppermute | solution.py:21
  32.9 0.6 %add_convert_fusion = bf16[4,2048]{1,0:T(4,128)(2,1)} fusion(bf16[4,2048]{1,0:T(4,128)(2,1)S(1)} %collective-permute-done.9, bf16[4,2048]{1,0:T(4,128)(2,1)S(1)} %collective-permute-done.8, f32[4,2048]{1,0:T(4,128)S(1)} %get-tuple-element.27, bf16[4,2048]{1,0:T(4,128)(2,1)S(1)} %collective-permute-done.7), kind=kLoop, calls=%fused_computation | loop fusion | flops 57344 | bytes 98304 | tf_op jit(solution)/shard_map/convert_element_type | solution.py:509
  (33 shorter events, 0.2 us)
Async XLA Ops:
  1.0 8.7 %slice-start.2 = ((s8[8388608]{0:T(1024)(128)(4,1)}), s8[4194304]{0:T(1024)(128)(4,1)S(1)}, s32[]{:S(2)}) async-start(s8[8388608]{0:T(1024)(128)(4,1)} %bitcast.2), calls=%async_computation.2 | async-start | bytes 8388608
  1.0 8.6 %slice-start.3 = ((s8[8388608]{0:T(1024)(128)(4,1)}), s8[4194304]{0:T(1024)(128)(4,1)S(1)}, s32[]{:S(2)}) async-start(s8[8388608]{0:T(1024)(128)(4,1)} %bitcast.2), calls=%async_computation.3 | async-start | bytes 8388608
  1.0 8.6 %copy-start = (bf16[2048,256]{1,0:T(8,128)(2,1)S(1)}, bf16[2048,256]{1,0:T(8,128)(2,1)}, u32[]{:S(2)}) copy-start(bf16[2048,256]{1,0:T(8,128)(2,1)} %refs_6_.1) | copy-start | bytes 3145732
  1.1 8.6 %copy-start.1 = (bf16[2048,256]{1,0:T(8,128)(2,1)S(1)}, bf16[2048,256]{1,0:T(8,128)(2,1)}, u32[]{:S(2)}) copy-start(bf16[2048,256]{1,0:T(8,128)(2,1)} %refs_7_.1) | copy-start | bytes 3145732
  1.1 8.6 %copy-start.2 = (bf16[2048]{0:T(1024)(128)(2,1)S(1)}, bf16[2048]{0:T(1024)(128)(2,1)}, u32[]{:S(2)}) copy-start(bf16[2048]{0:T(1024)(128)(2,1)} %refs_4_.1) | copy-start | bytes 12292
  1.1 5.4 %collective-permute-start.2 = (bf16[4,2432]{1,0:T(4,128)(2,1)S(1)}, bf16[4,2432]{1,0:T(4,128)(2,1)S(1)}, u32[]{:S(2)}, u32[]{:S(2)}) collective-permute-start(bf16[4,2432]{1,0:T(4,128)(2,1)S(1)} %pass.1), channel_id=1, source_target_pairs={{0,6},{1,7},{2,4},{3,5},{4,2},{5,3},{6,0},{7,1},{8,14},{9,15},{10,... | collective-permute-start | bytes 58376 | tf_op jit(solution)/shard_map/ppermute | solution.py:32
  4.6 5.0 %collective-permute-start.1 = (bf16[4,2432]{1,0:T(4,128)(2,1)S(1)}, bf16[4,2432]{1,0:T(4,128)(2,1)S(1)}, u32[]{:S(2)}, u32[]{:S(2)}) collective-permute-start(bf16[4,2432]{1,0:T(4,128)(2,1)S(1)} %pass.1), channel_id=1, source_target_pairs={{0,7},{1,6},{2,5},{3,4},{4,3},{5,2},{6,1},{7,0},{8,15},{9,14},{10,... | collective-permute-start | bytes 58376 | tf_op jit(solution)/shard_map/ppermute | solution.py:32
  6.3 3.4 %collective-permute-start = (bf16[4,2432]{1,0:T(4,128)(2,1)S(1)}, bf16[4,2432]{1,0:T(4,128)(2,1)S(1)}, u32[]{:S(2)}, u32[]{:S(2)}) collective-permute-start(bf16[4,2432]{1,0:T(4,128)(2,1)S(1)} %pass.1), channel_id=1, source_target_pairs={{0,5},{1,4},{2,7},{3,6},{4,1},{5,0},{6,3},{7,2},{8,13},{9,12},{10,... | collective-permute-start | bytes 58376 | tf_op jit(solution)/shard_map/ppermute | solution.py:32
  11.2 3.5 %copy-start.3 = (bf16[48,2,128,128]{3,2,1,0:T(8,128)(2,1)S(1)}, bf16[48,2,128,128]{3,2,1,0:T(8,128)(2,1)}, u32[]{:S(2)}) copy-start(bf16[48,2,128,128]{3,2,1,0:T(8,128)(2,1)} %key_ref.1) | copy-start | bytes 9437188
  11.2 3.5 %copy-start.5 = (s32[8,24]{1,0:T(8,128)S(1)}, s32[8,24]{1,0:T(8,128)}, u32[]{:S(2)}) copy-start(s32[8,24]{1,0:T(8,128)} %table_ref.1) | copy-start | bytes 2308
  11.2 3.5 %copy-start.6 = (s32[8,8]{1,0:T(8,128)S(1)}, s32[8,8]{1,0:T(8,128)}, u32[]{:S(2)}) copy-start(s32[8,8]{1,0:T(8,128)} %list_ref.1) | copy-start | bytes 772
  11.2 3.5 %copy-start.7 = (s32[8]{0:T(128)S(1)}, s32[8]{0:T(128)}, u32[]{:S(2)}) copy-start(s32[8]{0:T(128)} %lengths_ref.1) | copy-start | bytes 100
  11.2 1.8 %collective-permute-start.3 = (f32[320,128]{1,0:T(8,128)S(1)}, f32[320,128]{1,0:T(8,128)S(1)}, u32[]{:S(2)}, u32[]{:S(2)}) collective-permute-start(f32[320,128]{1,0:T(8,128)S(1)} %project.1.own_ref), channel_id=1, source_target_pairs={{0,4},{4,0},{8,12},{12,8},{1,5},{5,1},{9,13},{13,9},{2,6},{6,2},{1... | collective-permute-start | bytes 491528 | tf_op jit(solution)/shard_map/ppermute | solution.py:21
  13.1 4.5 %copy-start.4 = (bf16[48,2,128,128]{3,2,1,0:T(8,128)(2,1)S(1)}, bf16[48,2,128,128]{3,2,1,0:T(8,128)(2,1)}, u32[]{:S(2)}) copy-start(bf16[48,2,128,128]{3,2,1,0:T(8,128)(2,1)} %value_ref.1) | copy-start | bytes 9437188
  13.1 4.4 %collective-permute-start.4 = (f16[336,128]{1,0:T(8,128)(2,1)S(1)}, f16[336,128]{1,0:T(8,128)(2,1)S(1)}, u32[]{:S(2)}, u32[]{:S(2)}) collective-permute-start(f16[336,128]{1,0:T(8,128)(2,1)S(1)} %convert_element_type.18), channel_id=1, source_target_pairs={{0,12},{4,8},{8,4},{12,0},{1,13},{5,9},{9,5},{13,1},{2,14},{6,10},... | collective-permute-start | bytes 258056 | tf_op jit(solution)/shard_map/ppermute | solution.py:21
  17.6 7.0 %slice-start = ((s8[8388608]{0:T(1024)(128)(4,1)}), s8[4194304]{0:T(1024)(128)(4,1)S(1)}, s32[]{:S(2)}) async-start(s8[8388608]{0:T(1024)(128)(4,1)} %bitcast), calls=%async_computation | async-start | bytes 8388608
  18.8 5.8 %slice-start.1 = ((s8[8388608]{0:T(1024)(128)(4,1)}), s8[4194304]{0:T(1024)(128)(4,1)S(1)}, s32[]{:S(2)}) async-start(s8[8388608]{0:T(1024)(128)(4,1)} %bitcast), calls=%async_computation.1 | async-start | bytes 8388608
  18.8 1.4 %collective-permute-start.5 = (f32[264,128]{1,0:T(8,128)S(1)}, f32[264,128]{1,0:T(8,128)S(1)}, u32[]{:S(2)}, u32[]{:S(2)}) collective-permute-start(f32[264,128]{1,0:T(8,128)S(1)} %attend.1.own_ref), channel_id=1, source_target_pairs={{0,4},{4,0},{8,12},{12,8},{1,5},{5,1},{9,13},{13,9},{2,6},{6,2},{1... | collective-permute-start | bytes 405512 | tf_op jit(solution)/shard_map/ppermute | solution.py:21
  20.4 4.2 %collective-permute-start.6 = (bf16[272,128]{1,0:T(8,128)(2,1)S(1)}, bf16[272,128]{1,0:T(8,128)(2,1)S(1)}, u32[]{:S(2)}, u32[]{:S(2)}) collective-permute-start(bf16[272,128]{1,0:T(8,128)(2,1)S(1)} %get-tuple-element.26), channel_id=1, source_target_pairs={{0,12},{4,8},{8,4},{12,0},{1,13},{5,9},{9,5},{13,1},{2,14},{6,10},... | collective-permute-start | bytes 208904 | tf_op jit(solution)/shard_map/ppermute | solution.py:21
  25.9 4.6 %collective-permute-start.7 = (bf16[4,2048]{1,0:T(4,128)(2,1)S(1)}, bf16[4,2048]{1,0:T(4,128)(2,1)S(1)}, u32[]{:S(2)}, u32[]{:S(2)}) collective-permute-start(bf16[4,2048]{1,0:T(4,128)(2,1)S(1)} %get-tuple-element.28), channel_id=1, source_target_pairs={{0,2},{1,3},{2,0},{3,1},{4,6},{5,7},{6,4},{7,5},{8,10},{9,11},{10,... | collective-permute-start | bytes 49160 | tf_op jit(solution)/shard_map/ppermute | solution.py:21
  27.4 5.5 %collective-permute-start.8 = (bf16[4,2048]{1,0:T(4,128)(2,1)S(1)}, bf16[4,2048]{1,0:T(4,128)(2,1)S(1)}, u32[]{:S(2)}, u32[]{:S(2)}) collective-permute-start(bf16[4,2048]{1,0:T(4,128)(2,1)S(1)} %get-tuple-element.29), channel_id=1, source_target_pairs={{0,3},{1,2},{2,1},{3,0},{4,7},{5,6},{6,5},{7,4},{8,11},{9,10},{10,... | collective-permute-start | bytes 49160 | tf_op jit(solution)/shard_map/ppermute | solution.py:21
  28.3 4.6 %collective-permute-start.9 = (bf16[4,2048]{1,0:T(4,128)(2,1)S(1)}, bf16[4,2048]{1,0:T(4,128)(2,1)S(1)}, u32[]{:S(2)}, u32[]{:S(2)}) collective-permute-start(bf16[4,2048]{1,0:T(4,128)(2,1)S(1)} %get-tuple-element.30), channel_id=1, source_target_pairs={{0,1},{1,0},{2,3},{3,2},{4,5},{5,4},{6,7},{7,6},{8,9},{9,8},{10,11... | collective-permute-start | bytes 49160 | tf_op jit(solution)/shard_map/ppermute | solution.py:21

commit v10 on v9

--- a/solution.py
+++ b/solution.py
@@ -97,6 +97,9 @@
     at = lax.broadcasted_iota(jnp.int32, seen_ref.shape, 0)
     query_token = token_of(at // heads)
     query_head = at % heads // per_kv
+    place = at // heads // steps
+    half = lax.axis_size("mem") // 2
+    owner = place // (row_count // 2) * half + place % half
     lane = lax.broadcasted_iota(jnp.int32, seen_ref.shape, 1)
     key_head, key = lane // tokens, lane % tokens
     key_token = token_of(key)
@@ -104,7 +107,7 @@
         (query_head == key_head)
         & (query_token // steps == key_token // steps)
         & (key_token <= query_token)
-        & (query_token // steps % lax.axis_size("mem") == mem)
+        & (owner == mem)
     )
     seen_ref[...] = seen.astype(jnp.float32)
 
@@ -140,7 +143,7 @@
                 head += 1
 
 
-def add_body(values, own_ref, other_ref, out_ref, *sent_refs):
+def add_body(values, tokens, own_ref, other_ref, out_ref, *sent_refs):
     total = own_ref[...] + other_ref[...]
     out_ref[...] = total
     for ref in sent_refs:
@@ -148,17 +151,31 @@
         top = jnp.max(jnp.abs(total[height - values :]), axis=0, keepdims=True)
         top = jnp.maximum(top, 1e-30)
         exponent = jnp.ceil(jnp.log(top) * (1 / math.log(2)))
-        ref[: height - values] = total[: height - values]
-        ref[height - values : height] = total[height - values :] * jnp.exp2(-exponent)
-        ref[height:] = jnp.broadcast_to(exponent, (ref.shape[0] - height, LANES))
-
-
-def add_sent(own_ref, sent_ref, values):
+        mem, half = lax.axis_index("mem"), lax.axis_size("mem") // 2
+        theirs = pl.multiple_of((1 - mem // half) * (tokens // 2), tokens // 2)
+        first = height - 2 * values
+        ref[:first] = total[:first]
+        at = first
+        for block in range(first, height, tokens):
+            rows = out_ref[pl.ds(block + theirs, tokens // 2)]
+            if block >= height - values:
+                rows = rows * jnp.exp2(-exponent)
+            ref[at : at + tokens // 2] = rows
+            at += tokens // 2
+        ref[at:] = jnp.broadcast_to(exponent, (ref.shape[0] - at, LANES))
+
+
+def add_sent(own_ref, sent_ref, values, tokens):
     height = own_ref.shape[0]
-    scale = jnp.exp2(sent_ref[height : height + 1])
-    sent_values = sent_ref[height - values : height] * scale
-    sent = jnp.concatenate([sent_ref[: height - values], sent_values], axis=0)
-    return own_ref[...] + sent
+    first = height - 2 * values
+    parts = [sent_ref[:first]]
+    scale = jnp.exp2(sent_ref[first + values : first + values + 1])
+    for at in range(first, first + values, tokens // 2):
+        rows = sent_ref[at : at + tokens // 2]
+        if at >= first + values // 2:
+            rows = rows * scale
+        parts += [rows, rows]
+    return own_ref[...] + jnp.concatenate(parts, axis=0)
 
 
 def split_dot(weights, values):
@@ -233,7 +250,7 @@
     contract_last = (((1,), (1,)), ((), ()))
 
     values = (own_ref.shape[0] - height) // 2
-    projected = add_sent(own_ref, other_ref, values).astype(jnp.bfloat16)
+    projected = add_sent(own_ref, other_ref, values, values // kv_heads).astype(jnp.bfloat16)
     queries = projected[:height]
     query_ref[...] = queries.reshape(query_ref.shape)
     fresh = projected[height:]
@@ -444,9 +461,9 @@
     while 2 * distance < mem_count:
         outs = [jax.ShapeDtypeStruct(summed.shape, f32)]
         if 4 * distance == mem_count:
-            outs.append(jax.ShapeDtypeStruct((summed.shape[0] + 16, LANES), f32))
+            outs.append(jax.ShapeDtypeStruct((summed.shape[0] - kv_heads * token_count + 16, LANES), f32))
         added = kernel_call(
-            functools.partial(add_body, kv_heads * token_count),
+            functools.partial(add_body, kv_heads * token_count, token_count),
             "add",
             outs,
             [IN_VMEM] * 2,

time: 33.7 us -> 33.5 us (level)
  no operation moved by 1% of the time
where the time goes in v10:
time: 33.5 us; the launch traced here: 33.4 us
  starting transfers between devices  13 us (39%)
  waiting for transfers between devices  12.4 us (37%)
  Pallas kernels  6.99 us (21%)
  other arithmetic  0.66 us (2%)
    ppermute x7, waiting for transfers between devices, swap(): return lax.ppermute(array, axis, [(i, i ^ distance) for i in range(count)])  9.24 us
    ppermute x7, starting transfers between devices, swap(): return lax.ppermute(array, axis, [(i, i ^ distance) for i in range(count)])  7.61 us
    ppermute x3, starting transfers between devices, swap_across(): return lax.ppermute(array, ('mem', 'heads'), pairs)  5.4 us
    ppermute x3, waiting for transfers between devices, swap_across(): return lax.ppermute(array, ('mem', 'heads'), pairs)  3.18 us
    pallas_call x1, Pallas kernels, shards(): kernel_call(functools.partial(select_body, chunk, steps, per_kv), 'select...  1.83 us
    pallas_call x1, Pallas kernels, shards(): kernel_call(functools.partial(project_body, (0, *gathered), 512), 'projec...  1.46 us
    pallas_call x1, Pallas kernels, shards(): kernel_call(functools.partial(output_body, query_count, min(512, out_cols...  1.31 us
    pallas_call x1, Pallas kernels, shards(): kernel_call(functools.partial(attend_body, head_dim ** (-0.5), kv_heads *...  1.19 us
  transfers between devices with their start and end apart: 10, of which 7 were waited for; matrix products, arithmetic and copies ran while one was open for 0% of the time, Pallas kernels for 5%

profile of v10, /device:TPU:0, one launch (start us, length us, event | category | flops | bytes accessed | tf_op | source)
XLA Modules:
  0.0 33.4 jit_solution(1942036162728569531)
XLA Ops:
  0.0 1.0 %norm.1 = (bf16[4,2432]{1,0:T(4,128)(2,1)S(1)}, bf16[4,2432]{1,0:T(4,128)(2,1)S(1)}) custom-call(bf16[4,8192]{1,0:T(4,128)(2,1)} %hidden_hbm.1), custom_call_target="tpu_custom_call" | custom-call | flops 1 | bytes 1024 | tf_op jit(solution)/shard_map/norm/pallas_call | solution.py:415
  1.1 3.5 %collective-permute-start.2 = (bf16[4,2432]{1,0:T(4,128)(2,1)S(1)}, bf16[4,2432]{1,0:T(4,128)(2,1)S(1)}, u32[]{:S(2)}, u32[]{:S(2)}) collective-permute-start(bf16[4,2432]{1,0:T(4,128)(2,1)S(1)} %pass.1), channel_id=1, source_target_pairs={{0,6},{1,7},{2,4},{3,5},{4,2},{5,3},{6,0},{7,1},{8,14},{9,15},{10,... | collective-permute-start | bytes 58376 | tf_op jit(solution)/shard_map/ppermute | solution.py:32
  4.6 1.6 %collective-permute-start.1 = (bf16[4,2432]{1,0:T(4,128)(2,1)S(1)}, bf16[4,2432]{1,0:T(4,128)(2,1)S(1)}, u32[]{:S(2)}, u32[]{:S(2)}) collective-permute-start(bf16[4,2432]{1,0:T(4,128)(2,1)S(1)} %pass.1), channel_id=1, source_target_pairs={{0,7},{1,6},{2,5},{3,4},{4,3},{5,2},{6,1},{7,0},{8,15},{9,14},{10,... | collective-permute-start | bytes 58376 | tf_op jit(solution)/shard_map/ppermute | solution.py:32
  6.3 0.2 collective-permute-start
  6.5 3.2 %collective-permute-done.1.refs_2_ = bf16[4,2432]{1,0:T(4,128)(2,1)S(1)} collective-permute-done((bf16[4,2432]{1,0:T(4,128)(2,1)S(1)}, bf16[4,2432]{1,0:T(4,128)(2,1)S(1)}, u32[]{:S(2)}, u32[]{:S(2)}) %collective-permute-start.1) | collective-permute-done | bytes 19488 | tf_op jit(solution)/shard_map/ppermute | solution.py:32
  9.7 1.5 %project.1.own_ref = f32[320,128]{1,0:T(8,128)S(1)} custom-call(bf16[4,2432]{1,0:T(4,128)(2,1)S(1)} %get-tuple-element.20.refs_0_, bf16[4,2432]{1,0:T(4,128)(2,1)S(1)} %collective-permute-done.refs_1_, bf16[4,2432]{1,0:T(4,128)(2,1)S(1)} %collective-permute-done.1.refs_2_, bf16[4,2432]{1,0:T(4,128)(2,1)S(1)} %collective-permute-done.2.refs_3_, ...), custom_call_target="tpu_custom_call" | custom-call | flops 167772160 | bytes 1024 | tf_op jit(solution)/shard_map/project/pallas_call | solution.py:451
  11.2 0.8 %collective-permute-start.3 = (f32[320,128]{1,0:T(8,128)S(1)}, f32[320,128]{1,0:T(8,128)S(1)}, u32[]{:S(2)}, u32[]{:S(2)}) collective-permute-start(f32[320,128]{1,0:T(8,128)S(1)} %project.1.own_ref), channel_id=1, source_target_pairs={{0,4},{4,0},{8,12},{12,8},{1,5},{5,1},{9,13},{13,9},{2,6},{6,2},{1... | collective-permute-start | bytes 491528 | tf_op jit(solution)/shard_map/ppermute | solution.py:21
  12.0 1.0 %collective-permute-done.3.other_ref = f32[320,128]{1,0:T(8,128)S(1)} collective-permute-done((f32[320,128]{1,0:T(8,128)S(1)}, f32[320,128]{1,0:T(8,128)S(1)}, u32[]{:S(2)}, u32[]{:S(2)}) %collective-permute-start.3) | collective-permute-done | bytes 163872 | tf_op jit(solution)/shard_map/ppermute | solution.py:21
  13.1 1.5 %collective-permute-start.4 = (f16[304,128]{1,0:T(8,128)(2,1)S(1)}, f16[304,128]{1,0:T(8,128)(2,1)S(1)}, u32[]{:S(2)}, u32[]{:S(2)}) collective-permute-start(f16[304,128]{1,0:T(8,128)(2,1)S(1)} %convert_element_type.18), channel_id=1, source_target_pairs={{0,12},{4,8},{8,4},{12,0},{1,13},{5,9},{9,5},{13,1},{2,14},{6,10},... | collective-permute-start | bytes 233480 | tf_op jit(solution)/shard_map/ppermute | solution.py:21
  14.7 1.8 %select.1 = (s32[99]{0:T(128)S(4)}, f32[256,128]{1,0:T(8,128)S(1)}, bf16[32,128,256]{2,1,0:T(8,128)(2,1)S(1)}) custom-call(s32[8,24]{1,0:T(8,128)S(1)} %copy-done.5, s32[8,8]{1,0:T(8,128)S(1)} %copy-done.6, s32[8]{0:T(128)S(1)} %copy-done.7, bf16[48,2,128,128]{3,2,1,0:T(8,128)(2,1)S(1)} %copy-done.3), custom_call_target="tpu_custom_call" | custom-call | flops 10000000000 | bytes 1024 | tf_op jit(solution)/shard_map/select/pallas_call | solution.py:436
  16.5 0.9 %collective-permute-done.4 = f16[304,128]{1,0:T(8,128)(2,1)S(1)} collective-permute-done((f16[304,128]{1,0:T(8,128)(2,1)S(1)}, f16[304,128]{1,0:T(8,128)(2,1)S(1)}, u32[]{:S(2)}, u32[]{:S(2)}) %collective-permute-start.4) | collective-permute-done | bytes 77856 | tf_op jit(solution)/shard_map/ppermute | solution.py:21
  17.4 1.2 %attend.1.own_ref = f32[264,128]{1,0:T(8,128)S(1)} custom-call(s32[99]{0:T(128)S(4)} %get-tuple-element.18.chosen_ref, f32[256,128]{1,0:T(8,128)S(1)} %get-tuple-element.19.seen_ref, f32[320,128]{1,0:T(8,128)S(1)} %get-tuple-element.22.own_ref, f32[304,128]{1,0:T(8,128)S(1)} %convert_element_type.19.other_ref, ...), custom_call_target="tpu_custom_call" | custom-call | flops 10000000000 | bytes 1024 | tf_op jit(solution)/shard_map/attend/pallas_call | solution.py:477
  18.6 0.3 %collective-permute-start.5 = (f32[264,128]{1,0:T(8,128)S(1)}, f32[264,128]{1,0:T(8,128)S(1)}, u32[]{:S(2)}, u32[]{:S(2)}) collective-permute-start(f32[264,128]{1,0:T(8,128)S(1)} %attend.1.own_ref), channel_id=1, source_target_pairs={{0,4},{4,0},{8,12},{12,8},{1,5},{5,1},{9,13},{13,9},{2,6},{6,2},{1... | collective-permute-start | bytes 405512 | tf_op jit(solution)/shard_map/ppermute | solution.py:21
  19.0 1.1 %collective-permute-done.5.other_ref = f32[264,128]{1,0:T(8,128)S(1)} collective-permute-done((f32[264,128]{1,0:T(8,128)S(1)}, f32[264,128]{1,0:T(8,128)S(1)}, u32[]{:S(2)}, u32[]{:S(2)}) %collective-permute-start.5) | collective-permute-done | bytes 135200 | tf_op jit(solution)/shard_map/ppermute | solution.py:21
  20.0 0.2 combine.1
  20.2 1.4 %collective-permute-start.6 = (bf16[272,128]{1,0:T(8,128)(2,1)S(1)}, bf16[272,128]{1,0:T(8,128)(2,1)S(1)}, u32[]{:S(2)}, u32[]{:S(2)}) collective-permute-start(bf16[272,128]{1,0:T(8,128)(2,1)S(1)} %get-tuple-element.26), channel_id=1, source_target_pairs={{0,12},{4,8},{8,4},{12,0},{1,13},{5,9},{9,5},{13,1},{2,14},{6,10},... | collective-permute-start | bytes 208904 | tf_op jit(solution)/shard_map/ppermute | solution.py:21
  21.6 2.7 %collective-permute-done.6.other_ref = bf16[272,128]{1,0:T(8,128)(2,1)S(1)} collective-permute-done((bf16[272,128]{1,0:T(8,128)(2,1)S(1)}, bf16[272,128]{1,0:T(8,128)(2,1)S(1)}, u32[]{:S(2)}, u32[]{:S(2)}) %collective-permute-start.6) | collective-permute-done | bytes 69664 | tf_op jit(solution)/shard_map/ppermute | solution.py:21
  24.4 1.3 %output.1 = (f32[4,2048]{1,0:T(4,128)S(1)}, bf16[4,2048]{1,0:T(4,128)(2,1)S(1)}, bf16[4,2048]{1,0:T(4,128)(2,1)S(1)}, bf16[4,2048]{1,0:T(4,128)(2,1)S(1)}) custom-call(f32[264,128]{1,0:T(8,128)S(1)} %get-tuple-element.25.own_ref, bf16[272,128]{1,0:T(8,128)(2,1)S(1)} %collective-permute-done.6.other_ref, bf16[2048,2048]{1,0:T(8,128)(2,1)S(1)} %bitcast.1), custom_call_target="tpu_custom_call" | custom-call | flops 134217728 | bytes 1024 | tf_op jit(solution)/shard_map/output/pallas_call | solution.py:514
  25.7 1.5 %collective-permute-start.7 = (bf16[4,2048]{1,0:T(4,128)(2,1)S(1)}, bf16[4,2048]{1,0:T(4,128)(2,1)S(1)}, u32[]{:S(2)}, u32[]{:S(2)}) collective-permute-start(bf16[4,2048]{1,0:T(4,128)(2,1)S(1)} %get-tuple-element.28), channel_id=1, source_target_pairs={{0,2},{1,3},{2,0},{3,1},{4,6},{5,7},{6,4},{7,5},{8,10},{9,11},{10,... | collective-permute-start | bytes 49160 | tf_op jit(solution)/shard_map/ppermute | solution.py:21
  27.2 0.9 %collective-permute-start.8 = (bf16[4,2048]{1,0:T(4,128)(2,1)S(1)}, bf16[4,2048]{1,0:T(4,128)(2,1)S(1)}, u32[]{:S(2)}, u32[]{:S(2)}) collective-permute-start(bf16[4,2048]{1,0:T(4,128)(2,1)S(1)} %get-tuple-element.29), channel_id=1, source_target_pairs={{0,3},{1,2},{2,1},{3,0},{4,7},{5,6},{6,5},{7,4},{8,11},{9,10},{10,... | collective-permute-start | bytes 49160 | tf_op jit(solution)/shard_map/ppermute | solution.py:21
  28.1 1.1 %collective-permute-start.9 = (bf16[4,2048]{1,0:T(4,128)(2,1)S(1)}, bf16[4,2048]{1,0:T(4,128)(2,1)S(1)}, u32[]{:S(2)}, u32[]{:S(2)}) collective-permute-start(bf16[4,2048]{1,0:T(4,128)(2,1)S(1)} %get-tuple-element.30), channel_id=1, source_target_pairs={{0,1},{1,0},{2,3},{3,2},{4,5},{5,4},{6,7},{7,6},{8,9},{9,8},{10,11... | collective-permute-start | bytes 49160 | tf_op jit(solution)/shard_map/ppermute | solution.py:21
  29.2 1.1 %collective-permute-done.7 = bf16[4,2048]{1,0:T(4,128)(2,1)S(1)} collective-permute-done((bf16[4,2048]{1,0:T(4,128)(2,1)S(1)}, bf16[4,2048]{1,0:T(4,128)(2,1)S(1)}, u32[]{:S(2)}, u32[]{:S(2)}) %collective-permute-start.7) | collective-permute-done | bytes 16416 | tf_op jit(solution)/shard_map/ppermute | solution.py:21
  30.3 2.4 %collective-permute-done.8 = bf16[4,2048]{1,0:T(4,128)(2,1)S(1)} collective-permute-done((bf16[4,2048]{1,0:T(4,128)(2,1)S(1)}, bf16[4,2048]{1,0:T(4,128)(2,1)S(1)}, u32[]{:S(2)}, u32[]{:S(2)}) %collective-permute-start.8) | collective-permute-done | bytes 16416 | tf_op jit(solution)/shard_map/ppermute | solution.py:21
  32.7 0.6 %add_convert_fusion = bf16[4,2048]{1,0:T(4,128)(2,1)} fusion(bf16[4,2048]{1,0:T(4,128)(2,1)S(1)} %collective-permute-done.9, bf16[4,2048]{1,0:T(4,128)(2,1)S(1)} %collective-permute-done.8, f32[4,2048]{1,0:T(4,128)S(1)} %get-tuple-element.27, bf16[4,2048]{1,0:T(4,128)(2,1)S(1)} %collective-permute-done.7), kind=kLoop, calls=%fused_computation | loop fusion | flops 57344 | bytes 98304 | tf_op jit(solution)/shard_map/convert_element_type | solution.py:526
  (33 shorter events, 0.2 us)
Async XLA Ops:
  1.0 8.7 %slice-start.2 = ((s8[8388608]{0:T(1024)(128)(4,1)}), s8[4194304]{0:T(1024)(128)(4,1)S(1)}, s32[]{:S(2)}) async-start(s8[8388608]{0:T(1024)(128)(4,1)} %bitcast.2), calls=%async_computation.2 | async-start | bytes 8388608
  1.0 8.6 %slice-start.3 = ((s8[8388608]{0:T(1024)(128)(4,1)}), s8[4194304]{0:T(1024)(128)(4,1)S(1)}, s32[]{:S(2)}) async-start(s8[8388608]{0:T(1024)(128)(4,1)} %bitcast.2), calls=%async_computation.3 | async-start | bytes 8388608
  1.0 8.6 %copy-start = (bf16[2048,256]{1,0:T(8,128)(2,1)S(1)}, bf16[2048,256]{1,0:T(8,128)(2,1)}, u32[]{:S(2)}) copy-start(bf16[2048,256]{1,0:T(8,128)(2,1)} %refs_6_.1) | copy-start | bytes 3145732
  1.1 8.6 %copy-start.1 = (bf16[2048,256]{1,0:T(8,128)(2,1)S(1)}, bf16[2048,256]{1,0:T(8,128)(2,1)}, u32[]{:S(2)}) copy-start(bf16[2048,256]{1,0:T(8,128)(2,1)} %refs_7_.1) | copy-start | bytes 3145732
  1.1 8.6 %copy-start.2 = (bf16[2048]{0:T(1024)(128)(2,1)S(1)}, bf16[2048]{0:T(1024)(128)(2,1)}, u32[]{:S(2)}) copy-start(bf16[2048]{0:T(1024)(128)(2,1)} %refs_4_.1) | copy-start | bytes 12292
  1.1 5.4 %collective-permute-start.2 = (bf16[4,2432]{1,0:T(4,128)(2,1)S(1)}, bf16[4,2432]{1,0:T(4,128)(2,1)S(1)}, u32[]{:S(2)}, u32[]{:S(2)}) collective-permute-start(bf16[4,2432]{1,0:T(4,128)(2,1)S(1)} %pass.1), channel_id=1, source_target_pairs={{0,6},{1,7},{2,4},{3,5},{4,2},{5,3},{6,0},{7,1},{8,14},{9,15},{10,... | collective-permute-start | bytes 58376 | tf_op jit(solution)/shard_map/ppermute | solution.py:32
  4.6 5.0 %collective-permute-start.1 = (bf16[4,2432]{1,0:T(4,128)(2,1)S(1)}, bf16[4,2432]{1,0:T(4,128)(2,1)S(1)}, u32[]{:S(2)}, u32[]{:S(2)}) collective-permute-start(bf16[4,2432]{1,0:T(4,128)(2,1)S(1)} %pass.1), channel_id=1, source_target_pairs={{0,7},{1,6},{2,5},{3,4},{4,3},{5,2},{6,1},{7,0},{8,15},{9,14},{10,... | collective-permute-start | bytes 58376 | tf_op jit(solution)/shard_map/ppermute | solution.py:32
  6.3 3.4 %collective-permute-start = (bf16[4,2432]{1,0:T(4,128)(2,1)S(1)}, bf16[4,2432]{1,0:T(4,128)(2,1)S(1)}, u32[]{:S(2)}, u32[]{:S(2)}) collective-permute-start(bf16[4,2432]{1,0:T(4,128)(2,1)S(1)} %pass.1), channel_id=1, source_target_pairs={{0,5},{1,4},{2,7},{3,6},{4,1},{5,0},{6,3},{7,2},{8,13},{9,12},{10,... | collective-permute-start | bytes 58376 | tf_op jit(solution)/shard_map/ppermute | solution.py:32
  11.2 3.5 %copy-start.3 = (bf16[48,2,128,128]{3,2,1,0:T(8,128)(2,1)S(1)}, bf16[48,2,128,128]{3,2,1,0:T(8,128)(2,1)}, u32[]{:S(2)}) copy-start(bf16[48,2,128,128]{3,2,1,0:T(8,128)(2,1)} %key_ref.1) | copy-start | bytes 9437188
  11.2 3.5 %copy-start.5 = (s32[8,24]{1,0:T(8,128)S(1)}, s32[8,24]{1,0:T(8,128)}, u32[]{:S(2)}) copy-start(s32[8,24]{1,0:T(8,128)} %table_ref.1) | copy-start | bytes 2308
  11.2 3.5 %copy-start.6 = (s32[8,8]{1,0:T(8,128)S(1)}, s32[8,8]{1,0:T(8,128)}, u32[]{:S(2)}) copy-start(s32[8,8]{1,0:T(8,128)} %list_ref.1) | copy-start | bytes 772
  11.2 3.5 %copy-start.7 = (s32[8]{0:T(128)S(1)}, s32[8]{0:T(128)}, u32[]{:S(2)}) copy-start(s32[8]{0:T(128)} %lengths_ref.1) | copy-start | bytes 100
  11.2 1.8 %collective-permute-start.3 = (f32[320,128]{1,0:T(8,128)S(1)}, f32[320,128]{1,0:T(8,128)S(1)}, u32[]{:S(2)}, u32[]{:S(2)}) collective-permute-start(f32[320,128]{1,0:T(8,128)S(1)} %project.1.own_ref), channel_id=1, source_target_pairs={{0,4},{4,0},{8,12},{12,8},{1,5},{5,1},{9,13},{13,9},{2,6},{6,2},{1... | collective-permute-start | bytes 491528 | tf_op jit(solution)/shard_map/ppermute | solution.py:21
  13.1 4.3 %copy-start.4 = (bf16[48,2,128,128]{3,2,1,0:T(8,128)(2,1)S(1)}, bf16[48,2,128,128]{3,2,1,0:T(8,128)(2,1)}, u32[]{:S(2)}) copy-start(bf16[48,2,128,128]{3,2,1,0:T(8,128)(2,1)} %value_ref.1) | copy-start | bytes 9437188
  13.1 4.3 %collective-permute-start.4 = (f16[304,128]{1,0:T(8,128)(2,1)S(1)}, f16[304,128]{1,0:T(8,128)(2,1)S(1)}, u32[]{:S(2)}, u32[]{:S(2)}) collective-permute-start(f16[304,128]{1,0:T(8,128)(2,1)S(1)} %convert_element_type.18), channel_id=1, source_target_pairs={{0,12},{4,8},{8,4},{12,0},{1,13},{5,9},{9,5},{13,1},{2,14},{6,10},... | collective-permute-start | bytes 233480 | tf_op jit(solution)/shard_map/ppermute | solution.py:21
  17.4 7.0 %slice-start = ((s8[8388608]{0:T(1024)(128)(4,1)}), s8[4194304]{0:T(1024)(128)(4,1)S(1)}, s32[]{:S(2)}) async-start(s8[8388608]{0:T(1024)(128)(4,1)} %bitcast), calls=%async_computation | async-start | bytes 8388608
  18.6 5.8 %slice-start.1 = ((s8[8388608]{0:T(1024)(128)(4,1)}), s8[4194304]{0:T(1024)(128)(4,1)S(1)}, s32[]{:S(2)}) async-start(s8[8388608]{0:T(1024)(128)(4,1)} %bitcast), calls=%async_computation.1 | async-start | bytes 8388608
  18.6 1.4 %collective-permute-start.5 = (f32[264,128]{1,0:T(8,128)S(1)}, f32[264,128]{1,0:T(8,128)S(1)}, u32[]{:S(2)}, u32[]{:S(2)}) collective-permute-start(f32[264,128]{1,0:T(8,128)S(1)} %attend.1.own_ref), channel_id=1, source_target_pairs={{0,4},{4,0},{8,12},{12,8},{1,5},{5,1},{9,13},{13,9},{2,6},{6,2},{1... | collective-permute-start | bytes 405512 | tf_op jit(solution)/shard_map/ppermute | solution.py:21
  20.2 4.2 %collective-permute-start.6 = (bf16[272,128]{1,0:T(8,128)(2,1)S(1)}, bf16[272,128]{1,0:T(8,128)(2,1)S(1)}, u32[]{:S(2)}, u32[]{:S(2)}) collective-permute-start(bf16[272,128]{1,0:T(8,128)(2,1)S(1)} %get-tuple-element.26), channel_id=1, source_target_pairs={{0,12},{4,8},{8,4},{12,0},{1,13},{5,9},{9,5},{13,1},{2,14},{6,10},... | collective-permute-start | bytes 208904 | tf_op jit(solution)/shard_map/ppermute | solution.py:21
  25.7 4.6 %collective-permute-start.7 = (bf16[4,2048]{1,0:T(4,128)(2,1)S(1)}, bf16[4,2048]{1,0:T(4,128)(2,1)S(1)}, u32[]{:S(2)}, u32[]{:S(2)}) collective-permute-start(bf16[4,2048]{1,0:T(4,128)(2,1)S(1)} %get-tuple-element.28), channel_id=1, source_target_pairs={{0,2},{1,3},{2,0},{3,1},{4,6},{5,7},{6,4},{7,5},{8,10},{9,11},{10,... | collective-permute-start | bytes 49160 | tf_op jit(solution)/shard_map/ppermute | solution.py:21
  27.2 5.5 %collective-permute-start.8 = (bf16[4,2048]{1,0:T(4,128)(2,1)S(1)}, bf16[4,2048]{1,0:T(4,128)(2,1)S(1)}, u32[]{:S(2)}, u32[]{:S(2)}) collective-permute-start(bf16[4,2048]{1,0:T(4,128)(2,1)S(1)} %get-tuple-element.29), channel_id=1, source_target_pairs={{0,3},{1,2},{2,1},{3,0},{4,7},{5,6},{6,5},{7,4},{8,11},{9,10},{10,... | collective-permute-start | bytes 49160 | tf_op jit(solution)/shard_map/ppermute | solution.py:21
  28.1 4.6 %collective-permute-start.9 = (bf16[4,2048]{1,0:T(4,128)(2,1)S(1)}, bf16[4,2048]{1,0:T(4,128)(2,1)S(1)}, u32[]{:S(2)}, u32[]{:S(2)}) collective-permute-start(bf16[4,2048]{1,0:T(4,128)(2,1)S(1)} %get-tuple-element.30), channel_id=1, source_target_pairs={{0,1},{1,0},{2,3},{3,2},{4,5},{5,4},{6,7},{7,6},{8,9},{9,8},{10,11... | collective-permute-start | bytes 49160 | tf_op jit(solution)/shard_map/ppermute | solution.py:21

commit v11 on v10

--- a/solution.py
+++ b/solution.py
@@ -244,6 +244,7 @@
     *peak_refs,
 ):
     row_count, row_height, head_dim = query_ref.shape
+    row_count -= 1
     kv_heads = value_ref.shape[1]
     capacity = score_ref.shape[0]
     height = row_count * row_height
@@ -252,7 +253,8 @@
     values = (own_ref.shape[0] - height) // 2
     projected = add_sent(own_ref, other_ref, values, values // kv_heads).astype(jnp.bfloat16)
     queries = projected[:height]
-    query_ref[...] = queries.reshape(query_ref.shape)
+    query_ref[:row_count] = queries.reshape(row_count, row_height, head_dim)
+    query_ref[row_count] = jnp.zeros((row_height, head_dim), jnp.bfloat16)
     fresh = projected[height:]
     count = fresh.shape[0] // 2
     spare = jnp.zeros((LANES - count, head_dim), jnp.bfloat16)
@@ -276,7 +278,7 @@
     for c in range(capacity):
         slot, row, valid = (chosen_ref[i * stride + c] for i in range(3))
         every = jnp.dot(
-            query_ref[jnp.minimum(row, row_count - 1)],
+            query_ref[row],
             turned_ref[c],
             preferred_element_type=jnp.float32,
         )
@@ -481,8 +483,8 @@
         [IN_SMEM] + [IN_VMEM] * 5,
         4,
         1e10,
-        [pltpu.VMEM((row_count, *state), bf16), pltpu.VMEM((capacity, *state), f32)]
-        + [pltpu.VMEM((row_count + 1, *state), f32)] * 6,
+        [pltpu.VMEM((row_count + 1, *state), bf16), pltpu.VMEM((capacity, *state), f32)]
+        + [pltpu.VMEM((row_count + 1, *state), f32)] * 4,
     )(
         pltpu.with_memory_space_constraint(chosen, pltpu.SMEM),
         seen,

time: 33.5 us -> 33.5 us (level)
  no operation moved by 1% of the time
where the time goes in v11:
time: 33.5 us; the launch traced here: 33.4 us
  starting transfers between devices  13 us (39%)
  waiting for transfers between devices  12.4 us (37%)
  Pallas kernels  7 us (21%)
  other arithmetic  0.66 us (2%)
    ppermute x7, waiting for transfers between devices, swap(): return lax.ppermute(array, axis, [(i, i ^ distance) for i in range(count)])  9.23 us
    ppermute x7, starting transfers between devices, swap(): return lax.ppermute(array, axis, [(i, i ^ distance) for i in range(count)])  7.62 us
    ppermute x3, starting transfers between devices, swap_across(): return lax.ppermute(array, ('mem', 'heads'), pairs)  5.4 us
    ppermute x3, waiting for transfers between devices, swap_across(): return lax.ppermute(array, ('mem', 'heads'), pairs)  3.18 us
    pallas_call x1, Pallas kernels, shards(): kernel_call(functools.partial(select_body, chunk, steps, per_kv), 'select...  1.83 us
    pallas_call x1, Pallas kernels, shards(): kernel_call(functools.partial(project_body, (0, *gathered), 512), 'projec...  1.46 us
    pallas_call x1, Pallas kernels, shards(): kernel_call(functools.partial(output_body, query_count, min(512, out_cols...  1.31 us
    pallas_call x1, Pallas kernels, shards(): kernel_call(functools.partial(attend_body, head_dim ** (-0.5), kv_heads *...  1.19 us
  transfers between devices with their start and end apart: 10, of which 7 were waited for; matrix products, arithmetic and copies ran while one was open for 0% of the time, Pallas kernels for 5%

profile of v11, /device:TPU:0, one launch (start us, length us, event | category | flops | bytes accessed | tf_op | source)
XLA Modules:
  0.0 33.4 jit_solution(202768107612282003)
XLA Ops:
  0.0 1.0 %norm.1 = (bf16[4,2432]{1,0:T(4,128)(2,1)S(1)}, bf16[4,2432]{1,0:T(4,128)(2,1)S(1)}) custom-call(bf16[4,8192]{1,0:T(4,128)(2,1)} %hidden_hbm.1), custom_call_target="tpu_custom_call" | custom-call | flops 1 | bytes 1024 | tf_op jit(solution)/shard_map/norm/pallas_call | solution.py:417
  1.1 3.5 %collective-permute-start.2 = (bf16[4,2432]{1,0:T(4,128)(2,1)S(1)}, bf16[4,2432]{1,0:T(4,128)(2,1)S(1)}, u32[]{:S(2)}, u32[]{:S(2)}) collective-permute-start(bf16[4,2432]{1,0:T(4,128)(2,1)S(1)} %pass.1), channel_id=1, source_target_pairs={{0,6},{1,7},{2,4},{3,5},{4,2},{5,3},{6,0},{7,1},{8,14},{9,15},{10,... | collective-permute-start | bytes 58376 | tf_op jit(solution)/shard_map/ppermute | solution.py:32
  4.6 1.6 %collective-permute-start.1 = (bf16[4,2432]{1,0:T(4,128)(2,1)S(1)}, bf16[4,2432]{1,0:T(4,128)(2,1)S(1)}, u32[]{:S(2)}, u32[]{:S(2)}) collective-permute-start(bf16[4,2432]{1,0:T(4,128)(2,1)S(1)} %pass.1), channel_id=1, source_target_pairs={{0,7},{1,6},{2,5},{3,4},{4,3},{5,2},{6,1},{7,0},{8,15},{9,14},{10,... | collective-permute-start | bytes 58376 | tf_op jit(solution)/shard_map/ppermute | solution.py:32
  6.3 0.2 collective-permute-start
  6.5 3.2 %collective-permute-done.1.refs_2_ = bf16[4,2432]{1,0:T(4,128)(2,1)S(1)} collective-permute-done((bf16[4,2432]{1,0:T(4,128)(2,1)S(1)}, bf16[4,2432]{1,0:T(4,128)(2,1)S(1)}, u32[]{:S(2)}, u32[]{:S(2)}) %collective-permute-start.1) | collective-permute-done | bytes 19488 | tf_op jit(solution)/shard_map/ppermute | solution.py:32
  9.7 1.5 %project.1.own_ref = f32[320,128]{1,0:T(8,128)S(1)} custom-call(bf16[4,2432]{1,0:T(4,128)(2,1)S(1)} %get-tuple-element.20.refs_0_, bf16[4,2432]{1,0:T(4,128)(2,1)S(1)} %collective-permute-done.refs_1_, bf16[4,2432]{1,0:T(4,128)(2,1)S(1)} %collective-permute-done.1.refs_2_, bf16[4,2432]{1,0:T(4,128)(2,1)S(1)} %collective-permute-done.2.refs_3_, ...), custom_call_target="tpu_custom_call" | custom-call | flops 167772160 | bytes 1024 | tf_op jit(solution)/shard_map/project/pallas_call | solution.py:453
  11.2 0.8 %collective-permute-start.3 = (f32[320,128]{1,0:T(8,128)S(1)}, f32[320,128]{1,0:T(8,128)S(1)}, u32[]{:S(2)}, u32[]{:S(2)}) collective-permute-start(f32[320,128]{1,0:T(8,128)S(1)} %project.1.own_ref), channel_id=1, source_target_pairs={{0,4},{4,0},{8,12},{12,8},{1,5},{5,1},{9,13},{13,9},{2,6},{6,2},{1... | collective-permute-start | bytes 491528 | tf_op jit(solution)/shard_map/ppermute | solution.py:21
  12.0 1.0 %collective-permute-done.3.other_ref = f32[320,128]{1,0:T(8,128)S(1)} collective-permute-done((f32[320,128]{1,0:T(8,128)S(1)}, f32[320,128]{1,0:T(8,128)S(1)}, u32[]{:S(2)}, u32[]{:S(2)}) %collective-permute-start.3) | collective-permute-done | bytes 163872 | tf_op jit(solution)/shard_map/ppermute | solution.py:21
  13.1 1.5 %collective-permute-start.4 = (f16[304,128]{1,0:T(8,128)(2,1)S(1)}, f16[304,128]{1,0:T(8,128)(2,1)S(1)}, u32[]{:S(2)}, u32[]{:S(2)}) collective-permute-start(f16[304,128]{1,0:T(8,128)(2,1)S(1)} %convert_element_type.18), channel_id=1, source_target_pairs={{0,12},{4,8},{8,4},{12,0},{1,13},{5,9},{9,5},{13,1},{2,14},{6,10},... | collective-permute-start | bytes 233480 | tf_op jit(solution)/shard_map/ppermute | solution.py:21
  14.7 1.8 %select.1 = (s32[99]{0:T(128)S(4)}, f32[256,128]{1,0:T(8,128)S(1)}, bf16[32,128,256]{2,1,0:T(8,128)(2,1)S(1)}) custom-call(s32[8,24]{1,0:T(8,128)S(1)} %copy-done.5, s32[8,8]{1,0:T(8,128)S(1)} %copy-done.6, s32[8]{0:T(128)S(1)} %copy-done.7, bf16[48,2,128,128]{3,2,1,0:T(8,128)(2,1)S(1)} %copy-done.3), custom_call_target="tpu_custom_call" | custom-call | flops 10000000000 | bytes 1024 | tf_op jit(solution)/shard_map/select/pallas_call | solution.py:438
  16.5 0.9 %collective-permute-done.4 = f16[304,128]{1,0:T(8,128)(2,1)S(1)} collective-permute-done((f16[304,128]{1,0:T(8,128)(2,1)S(1)}, f16[304,128]{1,0:T(8,128)(2,1)S(1)}, u32[]{:S(2)}, u32[]{:S(2)}) %collective-permute-start.4) | collective-permute-done | bytes 77856 | tf_op jit(solution)/shard_map/ppermute | solution.py:21
  17.4 1.2 %attend.1.own_ref = f32[264,128]{1,0:T(8,128)S(1)} custom-call(s32[99]{0:T(128)S(4)} %get-tuple-element.18.chosen_ref, f32[256,128]{1,0:T(8,128)S(1)} %get-tuple-element.19.seen_ref, f32[320,128]{1,0:T(8,128)S(1)} %get-tuple-element.22.own_ref, f32[304,128]{1,0:T(8,128)S(1)} %convert_element_type.19.other_ref, ...), custom_call_target="tpu_custom_call" | custom-call | flops 10000000000 | bytes 1024 | tf_op jit(solution)/shard_map/attend/pallas_call | solution.py:479
  18.6 0.3 %collective-permute-start.5 = (f32[264,128]{1,0:T(8,128)S(1)}, f32[264,128]{1,0:T(8,128)S(1)}, u32[]{:S(2)}, u32[]{:S(2)}) collective-permute-start(f32[264,128]{1,0:T(8,128)S(1)} %attend.1.own_ref), channel_id=1, source_target_pairs={{0,4},{4,0},{8,12},{12,8},{1,5},{5,1},{9,13},{13,9},{2,6},{6,2},{1... | collective-permute-start | bytes 405512 | tf_op jit(solution)/shard_map/ppermute | solution.py:21
  19.0 1.1 %collective-permute-done.5.other_ref = f32[264,128]{1,0:T(8,128)S(1)} collective-permute-done((f32[264,128]{1,0:T(8,128)S(1)}, f32[264,128]{1,0:T(8,128)S(1)}, u32[]{:S(2)}, u32[]{:S(2)}) %collective-permute-start.5) | collective-permute-done | bytes 135200 | tf_op jit(solution)/shard_map/ppermute | solution.py:21
  20.1 0.2 combine.1
  20.2 1.4 %collective-permute-start.6 = (bf16[272,128]{1,0:T(8,128)(2,1)S(1)}, bf16[272,128]{1,0:T(8,128)(2,1)S(1)}, u32[]{:S(2)}, u32[]{:S(2)}) collective-permute-start(bf16[272,128]{1,0:T(8,128)(2,1)S(1)} %get-tuple-element.26), channel_id=1, source_target_pairs={{0,12},{4,8},{8,4},{12,0},{1,13},{5,9},{9,5},{13,1},{2,14},{6,10},... | collective-permute-start | bytes 208904 | tf_op jit(solution)/shard_map/ppermute | solution.py:21
  21.7 2.7 %collective-permute-done.6.other_ref = bf16[272,128]{1,0:T(8,128)(2,1)S(1)} collective-permute-done((bf16[272,128]{1,0:T(8,128)(2,1)S(1)}, bf16[272,128]{1,0:T(8,128)(2,1)S(1)}, u32[]{:S(2)}, u32[]{:S(2)}) %collective-permute-start.6) | collective-permute-done | bytes 69664 | tf_op jit(solution)/shard_map/ppermute | solution.py:21
  24.4 1.3 %output.1 = (f32[4,2048]{1,0:T(4,128)S(1)}, bf16[4,2048]{1,0:T(4,128)(2,1)S(1)}, bf16[4,2048]{1,0:T(4,128)(2,1)S(1)}, bf16[4,2048]{1,0:T(4,128)(2,1)S(1)}) custom-call(f32[264,128]{1,0:T(8,128)S(1)} %get-tuple-element.25.own_ref, bf16[272,128]{1,0:T(8,128)(2,1)S(1)} %collective-permute-done.6.other_ref, bf16[2048,2048]{1,0:T(8,128)(2,1)S(1)} %bitcast.1), custom_call_target="tpu_custom_call" | custom-call | flops 134217728 | bytes 1024 | tf_op jit(solution)/shard_map/output/pallas_call | solution.py:516
  25.7 1.5 %collective-permute-start.7 = (bf16[4,2048]{1,0:T(4,128)(2,1)S(1)}, bf16[4,2048]{1,0:T(4,128)(2,1)S(1)}, u32[]{:S(2)}, u32[]{:S(2)}) collective-permute-start(bf16[4,2048]{1,0:T(4,128)(2,1)S(1)} %get-tuple-element.28), channel_id=1, source_target_pairs={{0,2},{1,3},{2,0},{3,1},{4,6},{5,7},{6,4},{7,5},{8,10},{9,11},{10,... | collective-permute-start | bytes 49160 | tf_op jit(solution)/shard_map/ppermute | solution.py:21
  27.2 0.9 %collective-permute-start.8 = (bf16[4,2048]{1,0:T(4,128)(2,1)S(1)}, bf16[4,2048]{1,0:T(4,128)(2,1)S(1)}, u32[]{:S(2)}, u32[]{:S(2)}) collective-permute-start(bf16[4,2048]{1,0:T(4,128)(2,1)S(1)} %get-tuple-element.29), channel_id=1, source_target_pairs={{0,3},{1,2},{2,1},{3,0},{4,7},{5,6},{6,5},{7,4},{8,11},{9,10},{10,... | collective-permute-start | bytes 49160 | tf_op jit(solution)/shard_map/ppermute | solution.py:21
  28.1 1.1 %collective-permute-start.9 = (bf16[4,2048]{1,0:T(4,128)(2,1)S(1)}, bf16[4,2048]{1,0:T(4,128)(2,1)S(1)}, u32[]{:S(2)}, u32[]{:S(2)}) collective-permute-start(bf16[4,2048]{1,0:T(4,128)(2,1)S(1)} %get-tuple-element.30), channel_id=1, source_target_pairs={{0,1},{1,0},{2,3},{3,2},{4,5},{5,4},{6,7},{7,6},{8,9},{9,8},{10,11... | collective-permute-start | bytes 49160 | tf_op jit(solution)/shard_map/ppermute | solution.py:21
  29.2 1.1 %collective-permute-done.7 = bf16[4,2048]{1,0:T(4,128)(2,1)S(1)} collective-permute-done((bf16[4,2048]{1,0:T(4,128)(2,1)S(1)}, bf16[4,2048]{1,0:T(4,128)(2,1)S(1)}, u32[]{:S(2)}, u32[]{:S(2)}) %collective-permute-start.7) | collective-permute-done | bytes 16416 | tf_op jit(solution)/shard_map/ppermute | solution.py:21
  30.3 2.4 %collective-permute-done.8 = bf16[4,2048]{1,0:T(4,128)(2,1)S(1)} collective-permute-done((bf16[4,2048]{1,0:T(4,128)(2,1)S(1)}, bf16[4,2048]{1,0:T(4,128)(2,1)S(1)}, u32[]{:S(2)}, u32[]{:S(2)}) %collective-permute-start.8) | collective-permute-done | bytes 16416 | tf_op jit(solution)/shard_map/ppermute | solution.py:21
  32.7 0.6 %add_convert_fusion = bf16[4,2048]{1,0:T(4,128)(2,1)} fusion(bf16[4,2048]{1,0:T(4,128)(2,1)S(1)} %collective-permute-done.9, bf16[4,2048]{1,0:T(4,128)(2,1)S(1)} %collective-permute-done.8, f32[4,2048]{1,0:T(4,128)S(1)} %get-tuple-element.27, bf16[4,2048]{1,0:T(4,128)(2,1)S(1)} %collective-permute-done.7), kind=kLoop, calls=%fused_computation | loop fusion | flops 57344 | bytes 98304 | tf_op jit(solution)/shard_map/convert_element_type | solution.py:528
  (33 shorter events, 0.2 us)
Async XLA Ops:
  1.0 8.7 %slice-start.2 = ((s8[8388608]{0:T(1024)(128)(4,1)}), s8[4194304]{0:T(1024)(128)(4,1)S(1)}, s32[]{:S(2)}) async-start(s8[8388608]{0:T(1024)(128)(4,1)} %bitcast.2), calls=%async_computation.2 | async-start | bytes 8388608
  1.0 8.6 %slice-start.3 = ((s8[8388608]{0:T(1024)(128)(4,1)}), s8[4194304]{0:T(1024)(128)(4,1)S(1)}, s32[]{:S(2)}) async-start(s8[8388608]{0:T(1024)(128)(4,1)} %bitcast.2), calls=%async_computation.3 | async-start | bytes 8388608
  1.0 8.6 %copy-start = (bf16[2048,256]{1,0:T(8,128)(2,1)S(1)}, bf16[2048,256]{1,0:T(8,128)(2,1)}, u32[]{:S(2)}) copy-start(bf16[2048,256]{1,0:T(8,128)(2,1)} %refs_6_.1) | copy-start | bytes 3145732
  1.1 8.6 %copy-start.1 = (bf16[2048,256]{1,0:T(8,128)(2,1)S(1)}, bf16[2048,256]{1,0:T(8,128)(2,1)}, u32[]{:S(2)}) copy-start(bf16[2048,256]{1,0:T(8,128)(2,1)} %refs_7_.1) | copy-start | bytes 3145732
  1.1 8.6 %copy-start.2 = (bf16[2048]{0:T(1024)(128)(2,1)S(1)}, bf16[2048]{0:T(1024)(128)(2,1)}, u32[]{:S(2)}) copy-start(bf16[2048]{0:T(1024)(128)(2,1)} %refs_4_.1) | copy-start | bytes 12292
  1.1 5.4 %collective-permute-start.2 = (bf16[4,2432]{1,0:T(4,128)(2,1)S(1)}, bf16[4,2432]{1,0:T(4,128)(2,1)S(1)}, u32[]{:S(2)}, u32[]{:S(2)}) collective-permute-start(bf16[4,2432]{1,0:T(4,128)(2,1)S(1)} %pass.1), channel_id=1, source_target_pairs={{0,6},{1,7},{2,4},{3,5},{4,2},{5,3},{6,0},{7,1},{8,14},{9,15},{10,... | collective-permute-start | bytes 58376 | tf_op jit(solution)/shard_map/ppermute | solution.py:32
  4.6 5.0 %collective-permute-start.1 = (bf16[4,2432]{1,0:T(4,128)(2,1)S(1)}, bf16[4,2432]{1,0:T(4,128)(2,1)S(1)}, u32[]{:S(2)}, u32[]{:S(2)}) collective-permute-start(bf16[4,2432]{1,0:T(4,128)(2,1)S(1)} %pass.1), channel_id=1, source_target_pairs={{0,7},{1,6},{2,5},{3,4},{4,3},{5,2},{6,1},{7,0},{8,15},{9,14},{10,... | collective-permute-start | bytes 58376 | tf_op jit(solution)/shard_map/ppermute | solution.py:32
  6.3 3.4 %collective-permute-start = (bf16[4,2432]{1,0:T(4,128)(2,1)S(1)}, bf16[4,2432]{1,0:T(4,128)(2,1)S(1)}, u32[]{:S(2)}, u32[]{:S(2)}) collective-permute-start(bf16[4,2432]{1,0:T(4,128)(2,1)S(1)} %pass.1), channel_id=1, source_target_pairs={{0,5},{1,4},{2,7},{3,6},{4,1},{5,0},{6,3},{7,2},{8,13},{9,12},{10,... | collective-permute-start | bytes 58376 | tf_op jit(solution)/shard_map/ppermute | solution.py:32
  11.2 3.5 %copy-start.3 = (bf16[48,2,128,128]{3,2,1,0:T(8,128)(2,1)S(1)}, bf16[48,2,128,128]{3,2,1,0:T(8,128)(2,1)}, u32[]{:S(2)}) copy-start(bf16[48,2,128,128]{3,2,1,0:T(8,128)(2,1)} %key_ref.1) | copy-start | bytes 9437188
  11.2 3.5 %copy-start.5 = (s32[8,24]{1,0:T(8,128)S(1)}, s32[8,24]{1,0:T(8,128)}, u32[]{:S(2)}) copy-start(s32[8,24]{1,0:T(8,128)} %table_ref.1) | copy-start | bytes 2308
  11.2 3.5 %copy-start.6 = (s32[8,8]{1,0:T(8,128)S(1)}, s32[8,8]{1,0:T(8,128)}, u32[]{:S(2)}) copy-start(s32[8,8]{1,0:T(8,128)} %list_ref.1) | copy-start | bytes 772
  11.2 3.5 %copy-start.7 = (s32[8]{0:T(128)S(1)}, s32[8]{0:T(128)}, u32[]{:S(2)}) copy-start(s32[8]{0:T(128)} %lengths_ref.1) | copy-start | bytes 100
  11.2 1.8 %collective-permute-start.3 = (f32[320,128]{1,0:T(8,128)S(1)}, f32[320,128]{1,0:T(8,128)S(1)}, u32[]{:S(2)}, u32[]{:S(2)}) collective-permute-start(f32[320,128]{1,0:T(8,128)S(1)} %project.1.own_ref), channel_id=1, source_target_pairs={{0,4},{4,0},{8,12},{12,8},{1,5},{5,1},{9,13},{13,9},{2,6},{6,2},{1... | collective-permute-start | bytes 491528 | tf_op jit(solution)/shard_map/ppermute | solution.py:21
  13.1 4.3 %copy-start.4 = (bf16[48,2,128,128]{3,2,1,0:T(8,128)(2,1)S(1)}, bf16[48,2,128,128]{3,2,1,0:T(8,128)(2,1)}, u32[]{:S(2)}) copy-start(bf16[48,2,128,128]{3,2,1,0:T(8,128)(2,1)} %value_ref.1) | copy-start | bytes 9437188
  13.1 4.3 %collective-permute-start.4 = (f16[304,128]{1,0:T(8,128)(2,1)S(1)}, f16[304,128]{1,0:T(8,128)(2,1)S(1)}, u32[]{:S(2)}, u32[]{:S(2)}) collective-permute-start(f16[304,128]{1,0:T(8,128)(2,1)S(1)} %convert_element_type.18), channel_id=1, source_target_pairs={{0,12},{4,8},{8,4},{12,0},{1,13},{5,9},{9,5},{13,1},{2,14},{6,10},... | collective-permute-start | bytes 233480 | tf_op jit(solution)/shard_map/ppermute | solution.py:21
  17.4 7.0 %slice-start = ((s8[8388608]{0:T(1024)(128)(4,1)}), s8[4194304]{0:T(1024)(128)(4,1)S(1)}, s32[]{:S(2)}) async-start(s8[8388608]{0:T(1024)(128)(4,1)} %bitcast), calls=%async_computation | async-start | bytes 8388608
  18.6 5.8 %slice-start.1 = ((s8[8388608]{0:T(1024)(128)(4,1)}), s8[4194304]{0:T(1024)(128)(4,1)S(1)}, s32[]{:S(2)}) async-start(s8[8388608]{0:T(1024)(128)(4,1)} %bitcast), calls=%async_computation.1 | async-start | bytes 8388608
  18.6 1.4 %collective-permute-start.5 = (f32[264,128]{1,0:T(8,128)S(1)}, f32[264,128]{1,0:T(8,128)S(1)}, u32[]{:S(2)}, u32[]{:S(2)}) collective-permute-start(f32[264,128]{1,0:T(8,128)S(1)} %attend.1.own_ref), channel_id=1, source_target_pairs={{0,4},{4,0},{8,12},{12,8},{1,5},{5,1},{9,13},{13,9},{2,6},{6,2},{1... | collective-permute-start | bytes 405512 | tf_op jit(solution)/shard_map/ppermute | solution.py:21
  20.2 4.2 %collective-permute-start.6 = (bf16[272,128]{1,0:T(8,128)(2,1)S(1)}, bf16[272,128]{1,0:T(8,128)(2,1)S(1)}, u32[]{:S(2)}, u32[]{:S(2)}) collective-permute-start(bf16[272,128]{1,0:T(8,128)(2,1)S(1)} %get-tuple-element.26), channel_id=1, source_target_pairs={{0,12},{4,8},{8,4},{12,0},{1,13},{5,9},{9,5},{13,1},{2,14},{6,10},... | collective-permute-start | bytes 208904 | tf_op jit(solution)/shard_map/ppermute | solution.py:21
  25.7 4.6 %collective-permute-start.7 = (bf16[4,2048]{1,0:T(4,128)(2,1)S(1)}, bf16[4,2048]{1,0:T(4,128)(2,1)S(1)}, u32[]{:S(2)}, u32[]{:S(2)}) collective-permute-start(bf16[4,2048]{1,0:T(4,128)(2,1)S(1)} %get-tuple-element.28), channel_id=1, source_target_pairs={{0,2},{1,3},{2,0},{3,1},{4,6},{5,7},{6,4},{7,5},{8,10},{9,11},{10,... | collective-permute-start | bytes 49160 | tf_op jit(solution)/shard_map/ppermute | solution.py:21
  27.2 5.5 %collective-permute-start.8 = (bf16[4,2048]{1,0:T(4,128)(2,1)S(1)}, bf16[4,2048]{1,0:T(4,128)(2,1)S(1)}, u32[]{:S(2)}, u32[]{:S(2)}) collective-permute-start(bf16[4,2048]{1,0:T(4,128)(2,1)S(1)} %get-tuple-element.29), channel_id=1, source_target_pairs={{0,3},{1,2},{2,1},{3,0},{4,7},{5,6},{6,5},{7,4},{8,11},{9,10},{10,... | collective-permute-start | bytes 49160 | tf_op jit(solution)/shard_map/ppermute | solution.py:21
  28.1 4.6 %collective-permute-start.9 = (bf16[4,2048]{1,0:T(4,128)(2,1)S(1)}, bf16[4,2048]{1,0:T(4,128)(2,1)S(1)}, u32[]{:S(2)}, u32[]{:S(2)}) collective-permute-start(bf16[4,2048]{1,0:T(4,128)(2,1)S(1)} %get-tuple-element.30), channel_id=1, source_target_pairs={{0,1},{1,0},{2,3},{3,2},{4,5},{5,4},{6,7},{7,6},{8,9},{9,8},{10,11... | collective-permute-start | bytes 49160 | tf_op jit(solution)/shard_map/ppermute | solution.py:21

commit v12 on v11

--- a/solution.py
+++ b/solution.py
@@ -523,7 +523,7 @@
         [pltpu.VMEM((query_cols // LANES * token_count, LANES), f32)],
     )(partial, swap(sent, "mem", crossing(distance)), o_weight)
     total = projected[0]
-    for d in distances:
+    for d in range(head_count - 1, 0, -1):
         total = total + swap(projected[d], "heads", d).astype(f32)
     return total.astype(bf16)
 

time: 33.5 us -> 33.5 us (level)
  starting transfers between devices: 13 us -> 13.9 us
  waiting for transfers between devices: 12.4 us -> 11.5 us
    ppermute x7, waiting for transfers between devices: 9.23 us -> 8.33 us  [swap(): return lax.ppermute(array, axis, [(i, i ^ distance) for i in range(count)])]
    ppermute x7, starting transfers between devices: 7.62 us -> 8.52 us  [swap(): return lax.ppermute(array, axis, [(i, i ^ distance) for i in range(count)])]
  transfers between devices with their start and end apart: 10 -> 10, of which waited for: 7 -> 7; matrix products, arithmetic and copies ran while one was open for 0% -> 0% of each run, Pallas kernels for 5% -> 6%
where the time goes in v12:
time: 33.5 us; the launch traced here: 33.3 us
  starting transfers between devices  13.9 us (41%)
  waiting for transfers between devices  11.5 us (34%)
  Pallas kernels  7 us (21%)
  other arithmetic  0.66 us (2%)
    ppermute x7, starting transfers between devices, swap(): return lax.ppermute(array, axis, [(i, i ^ distance) for i in range(count)])  8.52 us
    ppermute x7, waiting for transfers between devices, swap(): return lax.ppermute(array, axis, [(i, i ^ distance) for i in range(count)])  8.33 us
    ppermute x3, starting transfers between devices, swap_across(): return lax.ppermute(array, ('mem', 'heads'), pairs)  5.4 us
    ppermute x3, waiting for transfers between devices, swap_across(): return lax.ppermute(array, ('mem', 'heads'), pairs)  3.18 us
    pallas_call x1, Pallas kernels, shards(): kernel_call(functools.partial(select_body, chunk, steps, per_kv), 'select...  1.83 us
    pallas_call x1, Pallas kernels, shards(): kernel_call(functools.partial(project_body, (0, *gathered), 512), 'projec...  1.46 us
    pallas_call x1, Pallas kernels, shards(): kernel_call(functools.partial(output_body, query_count, min(512, out_cols...  1.31 us
    pallas_call x1, Pallas kernels, shards(): kernel_call(functools.partial(attend_body, head_dim ** (-0.5), kv_heads *...  1.19 us
  transfers between devices with their start and end apart: 10, of which 7 were waited for; matrix products, arithmetic and copies ran while one was open for 0% of the time, Pallas kernels for 6%

profile of v12, /device:TPU:0, one launch (start us, length us, event | category | flops | bytes accessed | tf_op | source)
XLA Modules:
  0.0 33.3 jit_solution(2527033403711942980)
XLA Ops:
  0.0 1.0 %norm.1 = (bf16[4,2432]{1,0:T(4,128)(2,1)S(1)}, bf16[4,2432]{1,0:T(4,128)(2,1)S(1)}) custom-call(bf16[4,8192]{1,0:T(4,128)(2,1)} %hidden_hbm.1), custom_call_target="tpu_custom_call" | custom-call | flops 1 | bytes 1024 | tf_op jit(solution)/shard_map/norm/pallas_call | solution.py:417
  1.1 3.5 %collective-permute-start.2 = (bf16[4,2432]{1,0:T(4,128)(2,1)S(1)}, bf16[4,2432]{1,0:T(4,128)(2,1)S(1)}, u32[]{:S(2)}, u32[]{:S(2)}) collective-permute-start(bf16[4,2432]{1,0:T(4,128)(2,1)S(1)} %pass.1), channel_id=1, source_target_pairs={{0,6},{1,7},{2,4},{3,5},{4,2},{5,3},{6,0},{7,1},{8,14},{9,15},{10,... | collective-permute-start | bytes 58376 | tf_op jit(solution)/shard_map/ppermute | solution.py:32
  4.6 1.6 %collective-permute-start.1 = (bf16[4,2432]{1,0:T(4,128)(2,1)S(1)}, bf16[4,2432]{1,0:T(4,128)(2,1)S(1)}, u32[]{:S(2)}, u32[]{:S(2)}) collective-permute-start(bf16[4,2432]{1,0:T(4,128)(2,1)S(1)} %pass.1), channel_id=1, source_target_pairs={{0,7},{1,6},{2,5},{3,4},{4,3},{5,2},{6,1},{7,0},{8,15},{9,14},{10,... | collective-permute-start | bytes 58376 | tf_op jit(solution)/shard_map/ppermute | solution.py:32
  6.3 0.2 collective-permute-start
  6.5 3.2 %collective-permute-done.1.refs_2_ = bf16[4,2432]{1,0:T(4,128)(2,1)S(1)} collective-permute-done((bf16[4,2432]{1,0:T(4,128)(2,1)S(1)}, bf16[4,2432]{1,0:T(4,128)(2,1)S(1)}, u32[]{:S(2)}, u32[]{:S(2)}) %collective-permute-start.1) | collective-permute-done | bytes 19488 | tf_op jit(solution)/shard_map/ppermute | solution.py:32
  9.7 1.5 %project.1.own_ref = f32[320,128]{1,0:T(8,128)S(1)} custom-call(bf16[4,2432]{1,0:T(4,128)(2,1)S(1)} %get-tuple-element.20.refs_0_, bf16[4,2432]{1,0:T(4,128)(2,1)S(1)} %collective-permute-done.refs_1_, bf16[4,2432]{1,0:T(4,128)(2,1)S(1)} %collective-permute-done.1.refs_2_, bf16[4,2432]{1,0:T(4,128)(2,1)S(1)} %collective-permute-done.2.refs_3_, ...), custom_call_target="tpu_custom_call" | custom-call | flops 167772160 | bytes 1024 | tf_op jit(solution)/shard_map/project/pallas_call | solution.py:453
  11.2 0.0 copy-start.7
  11.2 0.8 %collective-permute-start.3 = (f32[320,128]{1,0:T(8,128)S(1)}, f32[320,128]{1,0:T(8,128)S(1)}, u32[]{:S(2)}, u32[]{:S(2)}) collective-permute-start(f32[320,128]{1,0:T(8,128)S(1)} %project.1.own_ref), channel_id=1, source_target_pairs={{0,4},{4,0},{8,12},{12,8},{1,5},{5,1},{9,13},{13,9},{2,6},{6,2},{1... | collective-permute-start | bytes 491528 | tf_op jit(solution)/shard_map/ppermute | solution.py:21
  12.0 1.0 %collective-permute-done.3.other_ref = f32[320,128]{1,0:T(8,128)S(1)} collective-permute-done((f32[320,128]{1,0:T(8,128)S(1)}, f32[320,128]{1,0:T(8,128)S(1)}, u32[]{:S(2)}, u32[]{:S(2)}) %collective-permute-start.3) | collective-permute-done | bytes 163872 | tf_op jit(solution)/shard_map/ppermute | solution.py:21
  13.1 1.5 %collective-permute-start.4 = (f16[304,128]{1,0:T(8,128)(2,1)S(1)}, f16[304,128]{1,0:T(8,128)(2,1)S(1)}, u32[]{:S(2)}, u32[]{:S(2)}) collective-permute-start(f16[304,128]{1,0:T(8,128)(2,1)S(1)} %convert_element_type.18), channel_id=1, source_target_pairs={{0,12},{4,8},{8,4},{12,0},{1,13},{5,9},{9,5},{13,1},{2,14},{6,10},... | collective-permute-start | bytes 233480 | tf_op jit(solution)/shard_map/ppermute | solution.py:21
  14.7 1.8 %select.1 = (s32[99]{0:T(128)S(4)}, f32[256,128]{1,0:T(8,128)S(1)}, bf16[32,128,256]{2,1,0:T(8,128)(2,1)S(1)}) custom-call(s32[8,24]{1,0:T(8,128)S(1)} %copy-done.5, s32[8,8]{1,0:T(8,128)S(1)} %copy-done.6, s32[8]{0:T(128)S(1)} %copy-done.7, bf16[48,2,128,128]{3,2,1,0:T(8,128)(2,1)S(1)} %copy-done.3), custom_call_target="tpu_custom_call" | custom-call | flops 10000000000 | bytes 1024 | tf_op jit(solution)/shard_map/select/pallas_call | solution.py:438
  16.5 0.9 %collective-permute-done.4 = f16[304,128]{1,0:T(8,128)(2,1)S(1)} collective-permute-done((f16[304,128]{1,0:T(8,128)(2,1)S(1)}, f16[304,128]{1,0:T(8,128)(2,1)S(1)}, u32[]{:S(2)}, u32[]{:S(2)}) %collective-permute-start.4) | collective-permute-done | bytes 77856 | tf_op jit(solution)/shard_map/ppermute | solution.py:21
  17.4 1.2 %attend.1.own_ref = f32[264,128]{1,0:T(8,128)S(1)} custom-call(s32[99]{0:T(128)S(4)} %get-tuple-element.18.chosen_ref, f32[256,128]{1,0:T(8,128)S(1)} %get-tuple-element.19.seen_ref, f32[320,128]{1,0:T(8,128)S(1)} %get-tuple-element.22.own_ref, f32[304,128]{1,0:T(8,128)S(1)} %convert_element_type.19.other_ref, ...), custom_call_target="tpu_custom_call" | custom-call | flops 10000000000 | bytes 1024 | tf_op jit(solution)/shard_map/attend/pallas_call | solution.py:479
  18.6 0.3 %collective-permute-start.5 = (f32[264,128]{1,0:T(8,128)S(1)}, f32[264,128]{1,0:T(8,128)S(1)}, u32[]{:S(2)}, u32[]{:S(2)}) collective-permute-start(f32[264,128]{1,0:T(8,128)S(1)} %attend.1.own_ref), channel_id=1, source_target_pairs={{0,4},{4,0},{8,12},{12,8},{1,5},{5,1},{9,13},{13,9},{2,6},{6,2},{1... | collective-permute-start | bytes 405512 | tf_op jit(solution)/shard_map/ppermute | solution.py:21
  19.0 1.1 %collective-permute-done.5.other_ref = f32[264,128]{1,0:T(8,128)S(1)} collective-permute-done((f32[264,128]{1,0:T(8,128)S(1)}, f32[264,128]{1,0:T(8,128)S(1)}, u32[]{:S(2)}, u32[]{:S(2)}) %collective-permute-start.5) | collective-permute-done | bytes 135200 | tf_op jit(solution)/shard_map/ppermute | solution.py:21
  20.1 0.2 combine.1
  20.2 1.5 %collective-permute-start.6 = (bf16[272,128]{1,0:T(8,128)(2,1)S(1)}, bf16[272,128]{1,0:T(8,128)(2,1)S(1)}, u32[]{:S(2)}, u32[]{:S(2)}) collective-permute-start(bf16[272,128]{1,0:T(8,128)(2,1)S(1)} %get-tuple-element.26), channel_id=1, source_target_pairs={{0,12},{4,8},{8,4},{12,0},{1,13},{5,9},{9,5},{13,1},{2,14},{6,10},... | collective-permute-start | bytes 208904 | tf_op jit(solution)/shard_map/ppermute | solution.py:21
  21.7 2.7 %collective-permute-done.6.other_ref = bf16[272,128]{1,0:T(8,128)(2,1)S(1)} collective-permute-done((bf16[272,128]{1,0:T(8,128)(2,1)S(1)}, bf16[272,128]{1,0:T(8,128)(2,1)S(1)}, u32[]{:S(2)}, u32[]{:S(2)}) %collective-permute-start.6) | collective-permute-done | bytes 69664 | tf_op jit(solution)/shard_map/ppermute | solution.py:21
  24.4 1.3 %output.1 = (f32[4,2048]{1,0:T(4,128)S(1)}, bf16[4,2048]{1,0:T(4,128)(2,1)S(1)}, bf16[4,2048]{1,0:T(4,128)(2,1)S(1)}, bf16[4,2048]{1,0:T(4,128)(2,1)S(1)}) custom-call(f32[264,128]{1,0:T(8,128)S(1)} %get-tuple-element.25.own_ref, bf16[272,128]{1,0:T(8,128)(2,1)S(1)} %collective-permute-done.6.other_ref, bf16[2048,2048]{1,0:T(8,128)(2,1)S(1)} %bitcast.1), custom_call_target="tpu_custom_call" | custom-call | flops 134217728 | bytes 1024 | tf_op jit(solution)/shard_map/output/pallas_call | solution.py:516
  25.7 2.4 %collective-permute-start.7 = (bf16[4,2048]{1,0:T(4,128)(2,1)S(1)}, bf16[4,2048]{1,0:T(4,128)(2,1)S(1)}, u32[]{:S(2)}, u32[]{:S(2)}) collective-permute-start(bf16[4,2048]{1,0:T(4,128)(2,1)S(1)} %get-tuple-element.28), channel_id=1, source_target_pairs={{0,3},{1,2},{2,1},{3,0},{4,7},{5,6},{6,5},{7,4},{8,11},{9,10},{10,... | collective-permute-start | bytes 49160 | tf_op jit(solution)/shard_map/ppermute | solution.py:21
  28.1 2.0 %collective-permute-start.9 = (bf16[4,2048]{1,0:T(4,128)(2,1)S(1)}, bf16[4,2048]{1,0:T(4,128)(2,1)S(1)}, u32[]{:S(2)}, u32[]{:S(2)}) collective-permute-start(bf16[4,2048]{1,0:T(4,128)(2,1)S(1)} %get-tuple-element.30), channel_id=1, source_target_pairs={{0,1},{1,0},{2,3},{3,2},{4,5},{5,4},{6,7},{7,6},{8,9},{9,8},{10,11... | collective-permute-start | bytes 49160 | tf_op jit(solution)/shard_map/ppermute | solution.py:21
  30.1 1.1 %collective-permute-done.7 = bf16[4,2048]{1,0:T(4,128)(2,1)S(1)} collective-permute-done((bf16[4,2048]{1,0:T(4,128)(2,1)S(1)}, bf16[4,2048]{1,0:T(4,128)(2,1)S(1)}, u32[]{:S(2)}, u32[]{:S(2)}) %collective-permute-start.7) | collective-permute-done | bytes 16416 | tf_op jit(solution)/shard_map/ppermute | solution.py:21
  31.2 1.5 %collective-permute-done.8 = bf16[4,2048]{1,0:T(4,128)(2,1)S(1)} collective-permute-done((bf16[4,2048]{1,0:T(4,128)(2,1)S(1)}, bf16[4,2048]{1,0:T(4,128)(2,1)S(1)}, u32[]{:S(2)}, u32[]{:S(2)}) %collective-permute-start.8) | collective-permute-done | bytes 16416 | tf_op jit(solution)/shard_map/ppermute | solution.py:21
  32.7 0.6 %add_convert_fusion = bf16[4,2048]{1,0:T(4,128)(2,1)} fusion(bf16[4,2048]{1,0:T(4,128)(2,1)S(1)} %collective-permute-done.9, bf16[4,2048]{1,0:T(4,128)(2,1)S(1)} %collective-permute-done.8, f32[4,2048]{1,0:T(4,128)S(1)} %get-tuple-element.27, bf16[4,2048]{1,0:T(4,128)(2,1)S(1)} %collective-permute-done.7), kind=kLoop, calls=%fused_computation | loop fusion | flops 57344 | bytes 98304 | tf_op jit(solution)/shard_map/convert_element_type | solution.py:528
  (33 shorter events, 0.1 us)
Async XLA Ops:
  1.0 8.7 %slice-start.2 = ((s8[8388608]{0:T(1024)(128)(4,1)}), s8[4194304]{0:T(1024)(128)(4,1)S(1)}, s32[]{:S(2)}) async-start(s8[8388608]{0:T(1024)(128)(4,1)} %bitcast.2), calls=%async_computation.2 | async-start | bytes 8388608
  1.0 8.6 %slice-start.3 = ((s8[8388608]{0:T(1024)(128)(4,1)}), s8[4194304]{0:T(1024)(128)(4,1)S(1)}, s32[]{:S(2)}) async-start(s8[8388608]{0:T(1024)(128)(4,1)} %bitcast.2), calls=%async_computation.3 | async-start | bytes 8388608
  1.0 8.6 %copy-start = (bf16[2048,256]{1,0:T(8,128)(2,1)S(1)}, bf16[2048,256]{1,0:T(8,128)(2,1)}, u32[]{:S(2)}) copy-start(bf16[2048,256]{1,0:T(8,128)(2,1)} %refs_6_.1) | copy-start | bytes 3145732
  1.1 8.6 %copy-start.1 = (bf16[2048,256]{1,0:T(8,128)(2,1)S(1)}, bf16[2048,256]{1,0:T(8,128)(2,1)}, u32[]{:S(2)}) copy-start(bf16[2048,256]{1,0:T(8,128)(2,1)} %refs_7_.1) | copy-start | bytes 3145732
  1.1 8.6 %copy-start.2 = (bf16[2048]{0:T(1024)(128)(2,1)S(1)}, bf16[2048]{0:T(1024)(128)(2,1)}, u32[]{:S(2)}) copy-start(bf16[2048]{0:T(1024)(128)(2,1)} %refs_4_.1) | copy-start | bytes 12292
  1.1 5.4 %collective-permute-start.2 = (bf16[4,2432]{1,0:T(4,128)(2,1)S(1)}, bf16[4,2432]{1,0:T(4,128)(2,1)S(1)}, u32[]{:S(2)}, u32[]{:S(2)}) collective-permute-start(bf16[4,2432]{1,0:T(4,128)(2,1)S(1)} %pass.1), channel_id=1, source_target_pairs={{0,6},{1,7},{2,4},{3,5},{4,2},{5,3},{6,0},{7,1},{8,14},{9,15},{10,... | collective-permute-start | bytes 58376 | tf_op jit(solution)/shard_map/ppermute | solution.py:32
  4.6 5.0 %collective-permute-start.1 = (bf16[4,2432]{1,0:T(4,128)(2,1)S(1)}, bf16[4,2432]{1,0:T(4,128)(2,1)S(1)}, u32[]{:S(2)}, u32[]{:S(2)}) collective-permute-start(bf16[4,2432]{1,0:T(4,128)(2,1)S(1)} %pass.1), channel_id=1, source_target_pairs={{0,7},{1,6},{2,5},{3,4},{4,3},{5,2},{6,1},{7,0},{8,15},{9,14},{10,... | collective-permute-start | bytes 58376 | tf_op jit(solution)/shard_map/ppermute | solution.py:32
  6.3 3.4 %collective-permute-start = (bf16[4,2432]{1,0:T(4,128)(2,1)S(1)}, bf16[4,2432]{1,0:T(4,128)(2,1)S(1)}, u32[]{:S(2)}, u32[]{:S(2)}) collective-permute-start(bf16[4,2432]{1,0:T(4,128)(2,1)S(1)} %pass.1), channel_id=1, source_target_pairs={{0,5},{1,4},{2,7},{3,6},{4,1},{5,0},{6,3},{7,2},{8,13},{9,12},{10,... | collective-permute-start | bytes 58376 | tf_op jit(solution)/shard_map/ppermute | solution.py:32
  11.2 3.5 %copy-start.3 = (bf16[48,2,128,128]{3,2,1,0:T(8,128)(2,1)S(1)}, bf16[48,2,128,128]{3,2,1,0:T(8,128)(2,1)}, u32[]{:S(2)}) copy-start(bf16[48,2,128,128]{3,2,1,0:T(8,128)(2,1)} %key_ref.1) | copy-start | bytes 9437188
  11.2 3.5 %copy-start.5 = (s32[8,24]{1,0:T(8,128)S(1)}, s32[8,24]{1,0:T(8,128)}, u32[]{:S(2)}) copy-start(s32[8,24]{1,0:T(8,128)} %table_ref.1) | copy-start | bytes 2308
  11.2 3.5 %copy-start.6 = (s32[8,8]{1,0:T(8,128)S(1)}, s32[8,8]{1,0:T(8,128)}, u32[]{:S(2)}) copy-start(s32[8,8]{1,0:T(8,128)} %list_ref.1) | copy-start | bytes 772
  11.2 3.5 %copy-start.7 = (s32[8]{0:T(128)S(1)}, s32[8]{0:T(128)}, u32[]{:S(2)}) copy-start(s32[8]{0:T(128)} %lengths_ref.1) | copy-start | bytes 100
  11.2 1.8 %collective-permute-start.3 = (f32[320,128]{1,0:T(8,128)S(1)}, f32[320,128]{1,0:T(8,128)S(1)}, u32[]{:S(2)}, u32[]{:S(2)}) collective-permute-start(f32[320,128]{1,0:T(8,128)S(1)} %project.1.own_ref), channel_id=1, source_target_pairs={{0,4},{4,0},{8,12},{12,8},{1,5},{5,1},{9,13},{13,9},{2,6},{6,2},{1... | collective-permute-start | bytes 491528 | tf_op jit(solution)/shard_map/ppermute | solution.py:21
  13.1 4.3 %copy-start.4 = (bf16[48,2,128,128]{3,2,1,0:T(8,128)(2,1)S(1)}, bf16[48,2,128,128]{3,2,1,0:T(8,128)(2,1)}, u32[]{:S(2)}) copy-start(bf16[48,2,128,128]{3,2,1,0:T(8,128)(2,1)} %value_ref.1) | copy-start | bytes 9437188
  13.1 4.3 %collective-permute-start.4 = (f16[304,128]{1,0:T(8,128)(2,1)S(1)}, f16[304,128]{1,0:T(8,128)(2,1)S(1)}, u32[]{:S(2)}, u32[]{:S(2)}) collective-permute-start(f16[304,128]{1,0:T(8,128)(2,1)S(1)} %convert_element_type.18), channel_id=1, source_target_pairs={{0,12},{4,8},{8,4},{12,0},{1,13},{5,9},{9,5},{13,1},{2,14},{6,10},... | collective-permute-start | bytes 233480 | tf_op jit(solution)/shard_map/ppermute | solution.py:21
  17.4 7.0 %slice-start = ((s8[8388608]{0:T(1024)(128)(4,1)}), s8[4194304]{0:T(1024)(128)(4,1)S(1)}, s32[]{:S(2)}) async-start(s8[8388608]{0:T(1024)(128)(4,1)} %bitcast), calls=%async_computation | async-start | bytes 8388608
  18.6 5.8 %slice-start.1 = ((s8[8388608]{0:T(1024)(128)(4,1)}), s8[4194304]{0:T(1024)(128)(4,1)S(1)}, s32[]{:S(2)}) async-start(s8[8388608]{0:T(1024)(128)(4,1)} %bitcast), calls=%async_computation.1 | async-start | bytes 8388608
  18.6 1.4 %collective-permute-start.5 = (f32[264,128]{1,0:T(8,128)S(1)}, f32[264,128]{1,0:T(8,128)S(1)}, u32[]{:S(2)}, u32[]{:S(2)}) collective-permute-start(f32[264,128]{1,0:T(8,128)S(1)} %attend.1.own_ref), channel_id=1, source_target_pairs={{0,4},{4,0},{8,12},{12,8},{1,5},{5,1},{9,13},{13,9},{2,6},{6,2},{1... | collective-permute-start | bytes 405512 | tf_op jit(solution)/shard_map/ppermute | solution.py:21
  20.2 4.2 %collective-permute-start.6 = (bf16[272,128]{1,0:T(8,128)(2,1)S(1)}, bf16[272,128]{1,0:T(8,128)(2,1)S(1)}, u32[]{:S(2)}, u32[]{:S(2)}) collective-permute-start(bf16[272,128]{1,0:T(8,128)(2,1)S(1)} %get-tuple-element.26), channel_id=1, source_target_pairs={{0,12},{4,8},{8,4},{12,0},{1,13},{5,9},{9,5},{13,1},{2,14},{6,10},... | collective-permute-start | bytes 208904 | tf_op jit(solution)/shard_map/ppermute | solution.py:21
  25.7 5.5 %collective-permute-start.7 = (bf16[4,2048]{1,0:T(4,128)(2,1)S(1)}, bf16[4,2048]{1,0:T(4,128)(2,1)S(1)}, u32[]{:S(2)}, u32[]{:S(2)}) collective-permute-start(bf16[4,2048]{1,0:T(4,128)(2,1)S(1)} %get-tuple-element.28), channel_id=1, source_target_pairs={{0,3},{1,2},{2,1},{3,0},{4,7},{5,6},{6,5},{7,4},{8,11},{9,10},{10,... | collective-permute-start | bytes 49160 | tf_op jit(solution)/shard_map/ppermute | solution.py:21
  28.1 4.6 %collective-permute-start.8 = (bf16[4,2048]{1,0:T(4,128)(2,1)S(1)}, bf16[4,2048]{1,0:T(4,128)(2,1)S(1)}, u32[]{:S(2)}, u32[]{:S(2)}) collective-permute-start(bf16[4,2048]{1,0:T(4,128)(2,1)S(1)} %get-tuple-element.29), channel_id=1, source_target_pairs={{0,2},{1,3},{2,0},{3,1},{4,6},{5,7},{6,4},{7,5},{8,10},{9,11},{10,... | collective-permute-start | bytes 49160 | tf_op jit(solution)/shard_map/ppermute | solution.py:21
  28.1 4.6 %collective-permute-start.9 = (bf16[4,2048]{1,0:T(4,128)(2,1)S(1)}, bf16[4,2048]{1,0:T(4,128)(2,1)S(1)}, u32[]{:S(2)}, u32[]{:S(2)}) collective-permute-start(bf16[4,2048]{1,0:T(4,128)(2,1)S(1)} %get-tuple-element.30), channel_id=1, source_target_pairs={{0,1},{1,0},{2,3},{3,2},{4,5},{5,4},{6,7},{7,6},{8,9},{9,8},{10,11... | collective-permute-start | bytes 49160 | tf_op jit(solution)/shard_map/ppermute | solution.py:21
